TPU v7x, 32 devices: a whole 2x2x4 slice. The times are simulated.
32 devices in a mesh: shift: 2 (over y), row: 8 (over z, x), col: 2 (over core).
Axes of the slice: x: 2, y: 2, z: 4, core: 2. Of those that a mesh axis runs over, the one named last changes fastest.
Arguments:
- krylov_basis: float32 [128, 3, 8, 8, 128], P('shift', None, 'row', 'col'), parts along dimension 0, may hold values from -4000 to 4000, as said below
- regions: int32 [8, 8, 128], P('row', 'col'), may hold values from 0 to 7
- mu_table: float32 [8], replicated, may hold values from 0.5 to 2
- eps_table: float32 [8], replicated, may hold values from 1 to 4
- shift_value: float32 [2], P('shift'), parts along dimension 0, may hold values from 0.5 to 2
Outputs:
- orthonormal: float32 [128, 3, 8, 8, 128], P('shift', None, 'row', 'col'), parts along dimension 0
- upper_factor: float32 [128, 64], P('shift'), parts along dimension 0
- applied: float32 [128, 3, 8, 8, 128], P('shift', None, 'row', 'col'), parts along dimension 0
- projected: float32 [128, 64], P('shift'), parts along dimension 0
There are 2 independent parts, one for each index of `shift`. A program takes and returns all parts, laid end to end along the dimension named above; an argument that names none is the same for every part. Nothing has to cross between parts.
Inputs may be any that keep to these rules, and one draw needn't show every extreme that they name: `krylov_basis`: Real-valued entries.
All inputs are finite; a program needn't handle non-finite values.
Results may differ from a plain program's by a relative error of at most 0.000071.
Values sent between devices are 32-bit elements; how exact they have to be, the bound alone decides.
No kernel may reach another device: no remote copies, remote signals or barrier semaphores. Data moves between devices by JAX's collectives and lax.ppermute only.
A program may use at most 64 MiB of HBM per device.

v0:
```python
import jax
import jax.numpy as jnp
from jax import lax
from jax.sharding import PartitionSpec as P


def shifted(x, axis, by):
    peers = lax.axis_size(axis)
    pairs = [(i, i + by) for i in range(peers) if 0 <= i + by < peers]
    return lax.ppermute(x, axis, pairs)


def padded(x, sides, width):
    for axis, dim in sides:
        peers, length = (lax.axis_size(axis), x.shape[dim])
        up = [(i, (i + 1) % peers) for i in range(peers - 1)]
        down = [(j, i) for i, j in up]
        last = lax.slice_in_dim(x, length - width, length, axis=dim)
        leading = lax.slice_in_dim(x, 0, width, axis=dim)
        before = lax.ppermute(last, axis, up)
        after = lax.ppermute(leading, axis, down)
        x = jnp.concatenate([before, x, after], axis=dim)
    return x


def forward_z(values):
    return jnp.pad(values[..., 1:], ((0, 0), (0, 0), (0, 0), (0, 1))) - values


def backward_z(values):
    return values - jnp.pad(values[..., :-1], ((0, 0), (0, 0), (0, 0), (1, 0)))


def operator_block(padded_field, coupling, permittivity, shift_scalar):
    cells_x = padded_field.shape[2] - 2
    cells_y = padded_field.shape[3] - 2
    field_x = padded_field[:, 0]
    field_y = padded_field[:, 1]
    field_z = padded_field[:, 2]

    def corner_part(values):
        return values[:, : cells_x + 1, : cells_y + 1]

    def forward_x(values):
        return values[:, 1 : cells_x + 2, : cells_y + 1] - corner_part(values)

    def forward_y(values):
        return values[:, : cells_x + 1, 1 : cells_y + 2] - corner_part(values)

    def forward_dz(values):
        return forward_z(corner_part(values))

    curl_x = forward_y(field_z) - forward_dz(field_y)
    curl_y = forward_dz(field_x) - forward_x(field_z)
    curl_z = forward_x(field_y) - forward_y(field_x)
    weighted_x = coupling * curl_x
    weighted_y = coupling * curl_y
    weighted_z = coupling * curl_z

    def backward_x(values):
        return values[:, 1:, 1:] - values[:, :-1, 1:]

    def backward_y(values):
        return values[:, 1:, 1:] - values[:, 1:, :-1]

    def backward_dz(values):
        return backward_z(values[:, 1:, 1:])

    result_x = backward_y(weighted_z) - backward_dz(weighted_y)
    result_y = backward_dz(weighted_x) - backward_x(weighted_z)
    result_z = backward_x(weighted_y) - backward_y(weighted_x)
    interior = padded_field[:, :, 1 : cells_x + 1, 1 : cells_y + 1]
    stacked = jnp.stack([result_x, result_y, result_z], axis=1)
    return stacked - shift_scalar * permittivity * interior


def lookup(labels, table):
    result = jnp.zeros(labels.shape, jnp.float32)
    for region in range(table.shape[0]):
        result = result + jnp.where(labels == region, table[region], 0.0)
    return result


def inner_products(left, right):
    return jnp.dot(
        left, right.T, precision=lax.Precision.HIGHEST, preferred_element_type=jnp.float32
    )


def apply_operator(padded_basis, coupling, permittivity, shift_scalar):
    columns = padded_basis.shape[0]
    blocks = padded_basis.reshape((columns // 16, 16) + padded_basis.shape[1:])

    def apply_block(column_block):
        return operator_block(column_block, coupling, permittivity, shift_scalar)

    images = lax.map(apply_block, blocks)
    return images.reshape((columns,) + images.shape[2:])


def factor_inverse(gram_matrix):
    lower_factor = jnp.linalg.cholesky(gram_matrix)
    inverse = lax.linalg.triangular_solve(
        lower_factor, jnp.eye(gram_matrix.shape[0], dtype=jnp.float32), left_side=True, lower=True
    )
    return (lower_factor.T, inverse)


def local(krylov_basis, regions, mu_table, eps_table, shift_value):
    columns = krylov_basis.shape[0]
    flattened = krylov_basis.reshape(columns, -1)
    total_rows = flattened.shape[1] * lax.axis_size("row") * lax.axis_size("col")
    cells_y = regions.shape[1]
    labels = regions + 1
    from_lower_row = shifted(labels, "row", 1)
    from_lower_col = shifted(labels[:, cells_y - 1 :], "col", 1)
    corner_zero = jnp.zeros((1, 1, labels.shape[2]), jnp.int32)
    top_layer = jnp.concatenate([corner_zero, from_lower_row], axis=1)
    rest_layers = jnp.concatenate([from_lower_col, labels], axis=1)
    padded_ids = jnp.concatenate([top_layer, rest_layers], axis=0)
    mu_extended = jnp.concatenate([jnp.zeros((1,), jnp.float32), mu_table])
    coupling = lookup(padded_ids, mu_extended)
    permittivity = lookup(regions, eps_table)
    shift_scalar = shift_value[0]
    padded_basis = padded(krylov_basis, (("row", 2), ("col", 3)), 1)
    image_basis = apply_operator(padded_basis, coupling, permittivity, shift_scalar)
    image_flat = image_basis.reshape(columns, -1)
    gram_matrix, raw_proj = lax.psum(
        (
            inner_products(flattened, flattened) / total_rows,
            inner_products(flattened, image_flat) / total_rows,
        ),
        ("row", "col"),
    )
    upper_factor, inverse = factor_inverse(gram_matrix)
    orthonormal = jnp.dot(
        inverse, flattened, precision=lax.Precision.HIGHEST, preferred_element_type=jnp.float32
    ).reshape(krylov_basis.shape)
    applied = jnp.dot(
        inverse, image_flat, precision=lax.Precision.HIGHEST, preferred_element_type=jnp.float32
    ).reshape(krylov_basis.shape)
    half_proj = jnp.dot(
        inverse, raw_proj, precision=lax.Precision.HIGHEST, preferred_element_type=jnp.float32
    )
    projected = inner_products(half_proj, inverse)
    return (orthonormal, upper_factor, applied, projected)


def solution(mesh):
    placed = (P("shift", None, "row", "col", None), P("row", "col", None), P(), P(), P("shift"))
    return jax.shard_map(
        local,
        mesh=mesh,
        in_specs=placed,
        out_specs=(
            P("shift", None, "row", "col", None),
            P("shift", None),
            P("shift", None, "row", "col", None),
            P("shift", None),
        ),
        check_vma=False,
    )
```

profile of v0, /device:TPU:0, one launch (start us, length us, event | category | flops | bytes accessed | tf_op | source)
XLA Modules:
  0.0 131.0 jit_solution(15011954159071276242)
XLA Ops:
  0.7 1.1 copy.27
  1.7 4.9 %collective-permute-start.2 = (f32[64,3,1,4,128]{4,0,3,2,1:T(8,128)S(1)}, f32[64,3,1,4,128]{4,0,3,2,1:T(8,128)S(1)}, u32[]{:S(2)}, u32[]{:S(2)}) collective-permute-start(f32[64,3,1,4,128]{4,0,3,2,1:T(8,128)S(1)} %copy.27), channel_id=1, source_target_pairs={{0,2},{2,4},{4,6},{6,8},{8,10},{10,12},{12,14},{1,3},{3,5},{5,7},{... | collective-permute-start | bytes 1179656 | tf_op jit(solution)/shard_map/ppermute | solution.py:20
  6.6 1.3 collective-permute-start.3
  7.9 0.7 broadcast_add_fusion
  8.6 4.5 %collective-permute-start = (s32[1,4,128]{2,1,0:T(4,128)S(1)}, s32[1,4,128]{2,1,0:T(4,128)S(1)}, u32[]{:S(2)}, u32[]{:S(2)}) collective-permute-start(s32[1,4,128]{2,1,0:T(4,128)S(1)} %broadcast_add_fusion), channel_id=1, source_target_pairs={{0,2},{2,4},{4,6},{6,8},{8,10},{10,12},{12,14},{1,3},{3,5},{5,7},{... | collective-permute-start | bytes 6152 | tf_op jit(solution)/shard_map/ppermute | solution.py:10
  13.2 1.3 collective-permute-start.1
  14.5 1.6 %fusion.16 = f32[64,64]{0,1:T(8,128)S(1)} fusion(f32[64,3,4,128]{3,2,1,0:T(4,128)} %bitcast.98), kind=kOutput, calls=%fused_computation.37 | convolution fusion | flops 75501568 | bytes 409600 | tf_op jit(solution)/shard_map/dot_general | solution.py:85
  16.1 0.7 fusion.27
  16.7 6.7 %collective-permute-done.2 = f32[64,3,1,4,128]{4,0,3,2,1:T(8,128)S(1)} collective-permute-done((f32[64,3,1,4,128]{4,0,3,2,1:T(8,128)S(1)}, f32[64,3,1,4,128]{4,0,3,2,1:T(8,128)S(1)}, u32[]{:S(2)}, u32[]{:S(2)}) %collective-permute-start.2) | collective-permute-done | bytes 393248 | tf_op jit(solution)/shard_map/ppermute | solution.py:20
  23.6 1.3 collective-permute-start.4
  24.9 1.3 collective-permute-start.5
  26.2 5.1 %select_add_fusion.1 = f32[1,4,128]{2,1,0:T(4,128)S(1)} fusion(s32[1,4,128]{2,1,0:T(4,128)S(1)} %copy-done.5, f32[]{:T(128)} %bitcast.37, f32[]{:T(128)} %bitcast.36, f32[]{:T(128)} %bitcast.35, f32[]{:T(128)} %bitcast.34, f32[]{:T(128)} %bitcast.33, f32[]{:T(128)} %bitcast.32, f32[]{:T(128)} %bitcast.31, f32[]{:T(128)} %bitcast.30), kind=kLoop, calls=%fused_computation.58 | loop fusion | flops 11776 | bytes 4128 | tf_op jit(solution)/shard_map/add | solution.py:80
  31.3 0.7 fusion.28
  32.0 0.2 reshape.58
  32.2 0.9 reshape.59
  33.1 5.0 %select_add_fusion = f32[2,5,128]{2,1,0:T(8,128)S(1)} fusion(s32[1,4,128]{2,1,0:T(4,128)S(1)} %broadcast_add_fusion, s32[1,1,128]{2,1,0:T(1,128)S(1)} %collective-permute-done.1, s32[1,4,128]{2,1,0:T(4,128)S(1)} %collective-permute-done, f32[]{:T(128)} %bitcast.27, f32[]{:T(128)} %bitcast.26, f32[]{:T(128)} %bitcast.25, f32[]{:T(128)} %bitcast.24, ...), kind=kLoop, calls=%fused_computation.57 | loop fusion | flops 32000 | bytes 9760 | tf_op jit(solution)/shard_map/add | solution.py:80
  38.1 0.7 copy-done.2
  38.8 1.2 pad_maximum_fusion.1
  40.0 8.1 %while.12 = (s32[]{:T(128)}, f32[4,16,3,1,4,128]{5,4,3,2,1,0:T(4,128)}, f32[2,5,128]{2,1,0:T(8,128)S(1)}, f32[4,16,3,3,6,128]{5,1,0,4,3,2:T(8,128)S(1)}, f32[]{:T(128)}, /*index=5*/f32[1,4,128]{2,1,0:T(4,128)S(1)}, s32[]{:T(128)}) while((s32[]{:T(128)}, f32[4,16,3,1,4,128]{5,4,3,2,1,0:T(4,128)}, f32[2,5,128]{2,1,0:T(8,128)S(1)}, ...), condition=%wide.region_4.5_spmd, body=%wide.region_3.4_spmd.sunk | while | flops 418306 | bytes 4790613 | solution.py:97
  40.0 0.1 copy.55
  40.5 0.1 fusion.41
  40.7 0.6 multiply_bitcast_fusion.2
  41.3 0.7 fusion.42
  42.0 0.1 copy.55
  42.7 0.6 multiply_bitcast_fusion.2
  43.3 0.7 fusion.42
  44.1 0.1 copy.55
  44.7 0.6 multiply_bitcast_fusion.2
  45.4 0.7 fusion.42
  46.1 0.1 copy.55
  46.7 0.6 multiply_bitcast_fusion.2
  47.4 0.7 fusion.42
  48.1 1.2 reshape_reshape.3
  49.2 0.5 fusion.15
  49.7 64.1 %all-reduce.5 = (f32[64,64]{0,1:T(8,128)S(1)}, f32[64,64]{1,0:T(8,128)S(1)}) all-reduce(f32[64,64]{0,1:T(8,128)S(1)} %fusion.16, f32[64,64]{1,0:T(8,128)S(1)} %fusion.15), channel_id=1, replica_groups=mesh['shift'=2,'row'=8,'col'=2] {'row','col'}, use_global_device_ids=true, to_apply=%region_0.1 | all-reduce | flops 8192 | bytes 65536 | tf_op jit(solution)/shard_map/psum | solution.py:128
  113.9 5.8 %cholesky.17 = f32[64,64]{1,0:T(8,128)S(1)} custom-call(f32[64,64]{1,0:T(8,128)S(1)} %fusion.24), custom_call_target="Cholesky" | custom-call | tf_op jit(solution)/shard_map/jit(cholesky)/cholesky | solution.py:102
  119.7 0.6 compare_reduce_fusion
  120.4 0.7 fusion.25
  121.1 4.9 %custom-call.6 = f32[1,64,64]{1,2,0:T(8,128)S(1)} custom-call(f32[1,64,64]{2,1,0:T(8,128)S(1)} %get-tuple-element.122), custom_call_target="InvertDiagBlocksLowerTriangular" | custom-call | tf_op jit(solution)/shard_map/triangular_solve | solution.py:103
  125.9 0.2 fusion.22
  126.2 0.2 fusion.29
  126.4 0.8 fusion.30
  127.2 0.1 reshape.61
  127.3 0.5 convolution_bitcast_fusion
  127.8 1.0 copy.34
  128.8 0.5 convolution_bitcast_fusion.1
  129.3 1.0 copy.32
  130.3 0.7 copy.33
  (56 shorter events, 2.1 us)
Async XLA Ops:
  0.6 22.8 %copy-start = (f32[64,3,1,4,128]{4,3,2,1,0:T(4,128)S(1)}, f32[64,3,1,4,128]{4,3,2,1,0:T(4,128)}, u32[]{:S(2)}) copy-start(f32[64,3,1,4,128]{4,3,2,1,0:T(4,128)} %param.7) | copy-start | bytes 1179652
  0.6 15.4 %copy-start.3 = (f32[8]{0:T(128)S(1)}, f32[8]{0:T(128)}, u32[]{:S(2)}) copy-start(f32[8]{0:T(128)} %param.10) | copy-start | bytes 100
  1.7 21.7 %collective-permute-start.2 = (f32[64,3,1,4,128]{4,0,3,2,1:T(8,128)S(1)}, f32[64,3,1,4,128]{4,0,3,2,1:T(8,128)S(1)}, u32[]{:S(2)}, u32[]{:S(2)}) collective-permute-start(f32[64,3,1,4,128]{4,0,3,2,1:T(8,128)S(1)} %copy.27), channel_id=1, source_target_pairs={{0,2},{2,4},{4,6},{6,8},{8,10},{10,12},{12,14},{1,3},{3,5},{5,7},{... | collective-permute-start | bytes 1179656 | tf_op jit(solution)/shard_map/ppermute | solution.py:20
  6.6 16.9 %collective-permute-start.3 = (f32[64,3,1,4,128]{4,0,3,2,1:T(8,128)S(1)}, f32[64,3,1,4,128]{4,0,3,2,1:T(8,128)S(1)}, u32[]{:S(2)}, u32[]{:S(2)}) collective-permute-start(f32[64,3,1,4,128]{4,0,3,2,1:T(8,128)S(1)} %copy.27), channel_id=1, source_target_pairs={{2,0},{4,2},{6,4},{8,6},{10,8},{12,10},{14,12},{3,1},{5,3},{7,5},{... | collective-permute-start | bytes 1179656 | tf_op jit(solution)/shard_map/ppermute | solution.py:21
  8.6 24.5 %collective-permute-start = (s32[1,4,128]{2,1,0:T(4,128)S(1)}, s32[1,4,128]{2,1,0:T(4,128)S(1)}, u32[]{:S(2)}, u32[]{:S(2)}) collective-permute-start(s32[1,4,128]{2,1,0:T(4,128)S(1)} %broadcast_add_fusion), channel_id=1, source_target_pairs={{0,2},{2,4},{4,6},{6,8},{8,10},{10,12},{12,14},{1,3},{3,5},{5,7},{... | collective-permute-start | bytes 6152 | tf_op jit(solution)/shard_map/ppermute | solution.py:10
  13.2 19.9 %collective-permute-start.1 = (s32[1,1,128]{2,1,0:T(1,128)S(1)}, s32[1,1,128]{2,1,0:T(1,128)S(1)}, u32[]{:S(2)}, u32[]{:S(2)}) collective-permute-start(s32[1,1,128]{2,1,0:T(1,128)S(1)} %slice.209), channel_id=1, source_target_pairs={{0,1},{2,3},{4,5},{6,7},{8,9},{10,11},{12,13},{14,15},{16,17},{18,... | collective-permute-start | bytes 1544 | tf_op jit(solution)/shard_map/ppermute | solution.py:10
  23.5 2.7 %copy-start.5 = (s32[1,4,128]{2,1,0:T(4,128)S(1)}, s32[1,4,128]{2,1,0:T(4,128)}, u32[]{:S(2)}) copy-start(s32[1,4,128]{2,1,0:T(4,128)} %param.8) | copy-start | bytes 6148
  23.5 7.8 %copy-start.4 = (f32[8]{0:T(128)S(1)}, f32[8]{0:T(128)}, u32[]{:S(2)}) copy-start(f32[8]{0:T(128)} %param.9) | copy-start | bytes 100
  23.6 14.5 %collective-permute-start.4 = (f32[64,3,3,1,128]{4,0,3,2,1:T(8,128)S(1)}, f32[64,3,3,1,128]{4,0,3,2,1:T(8,128)S(1)}, u32[]{:S(2)}, u32[]{:S(2)}) collective-permute-start(f32[64,3,3,1,128]{4,0,3,2,1:T(8,128)S(1)} %get-tuple-element.119), channel_id=1, source_target_pairs={{0,1},{2,3},{4,5},{6,7},{8,9},{10,11},{12,13},{14,15},{16,17},{18,... | collective-permute-start | bytes 884744 | tf_op jit(solution)/shard_map/ppermute | solution.py:20
  24.9 13.9 %collective-permute-start.5 = (f32[64,3,3,1,128]{4,0,3,2,1:T(8,128)S(1)}, f32[64,3,3,1,128]{4,0,3,2,1:T(8,128)}, u32[]{:S(2)}, u32[]{:S(2)}) collective-permute-start(f32[64,3,3,1,128]{4,0,3,2,1:T(8,128)S(1)} %get-tuple-element.120), channel_id=1, source_target_pairs={{1,0},{3,2},{5,4},{7,6},{9,8},{11,10},{13,12},{15,14},{17,16},{19,... | collective-permute-start | bytes 884744 | tf_op jit(solution)/shard_map/ppermute | solution.py:21
  38.1 0.7 copy-start.2
  127.2 1.6 %copy-start.1 = (f32[3,4,128,64]{2,1,0,3:T(4,128)S(1)}, f32[3,4,128,64]{2,1,0,3:T(4,128)}, u32[]{:S(2)}) copy-start(f32[3,4,128,64]{2,1,0,3:T(4,128)} %reshape.59) | copy-start | bytes 1179652
where the time goes:
time: 132 us; the launch traced here: 131 us
  blocking collectives  64.1 us (49%)
  other arithmetic  30.2 us (23%)
  starting transfers between devices  14.6 us (11%)
  local copies, waits for them, and re-layouts  10.1 us (8%)
  waiting for transfers between devices  6.67 us (5%)
  matrix products  4.18 us (3%)
    psum x1, blocking collectives, local(): lax.psum((inner_products(flattened, flattened) / total_rows, inner_produc...  64.1 us
    add x2, other arithmetic, lookup(): result = result + jnp.where(labels == region, table[region], 0.0)  10.1 us
    ppermute x2, waiting for transfers between devices, padded(): before = lax.ppermute(last, axis, up)  6.66 us
    another operation x3, other arithmetic, factor_inverse(): lower_factor = jnp.linalg.cholesky(gram_matrix)  6.52 us
    ppermute x2, starting transfers between devices, padded(): before = lax.ppermute(last, axis, up)  6.17 us
    ppermute x2, starting transfers between devices, shifted(): return lax.ppermute(x, axis, pairs)  5.82 us
    another operation x1, other arithmetic, factor_inverse(): lax.linalg.triangular_solve(lower_factor, jnp.eye(gram_matrix.shape[0], d...  4.9 us
    unnamed x18, local copies, waits for them, and re-layouts  4.56 us
  transfers between devices with their start and end apart: 6, of which 1 were waited for; matrix products, arithmetic and copies ran while one was open for 11% of the time, Pallas kernels for 0%

commit v1 on v0

v1 whole, which is shorter than its diff:
```python
import functools

import jax
import jax.numpy as jnp
from jax import lax
from jax.experimental import pallas as pl
from jax.experimental.pallas import tpu as pltpu
from jax.sharding import PartitionSpec as P

F32 = jnp.float32
HIGHEST = lax.Precision.HIGHEST


def shifted(x, axis, by):
    peers = lax.axis_size(axis)
    pairs = [(i, i + by) for i in range(peers) if 0 <= i + by < peers]
    return lax.ppermute(x, axis, pairs)


def exchanged_sum(x, axes):
    for axis in axes:
        peers = lax.axis_size(axis)
        if peers & (peers - 1):
            x = lax.psum(x, axis)
            continue
        step = 1
        while step < peers:
            x = x + lax.ppermute(x, axis, [(i, i ^ step) for i in range(peers)])
            step *= 2
    return x


def wide(chunks):
    return jnp.concatenate(chunks, axis=1)


def inner(left, right):
    return lax.dot_general(
        left, right, (((1,), (1,)), ((), ())), precision=HIGHEST, preferred_element_type=F32
    )


def table_rows(labels, table_ref):
    result = jnp.zeros(labels.shape, F32)
    for region in range(table_ref.shape[0]):
        result = jnp.where(labels == region, table_ref[region], result)
    return result


def forward_z(values):
    lanes = values.shape[1]
    lane = lax.broadcasted_iota(jnp.int32, values.shape, 1)
    ahead = jnp.where(lane == lanes - 1, 0.0, pltpu.roll(values, lanes - 1, 1))
    return ahead - values


def backward_z(values):
    lane = lax.broadcasted_iota(jnp.int32, values.shape, 1)
    return values - jnp.where(lane == 0, 0.0, pltpu.roll(values, 1, 1))


def part(ref, index, columns):
    return ref[index * columns : (index + 1) * columns, :]


def pack_kernel(columns, cells, basis, out_x, out_yz, out_edge):
    stride = 3 * cells
    for k in range(stride):
        chunk = basis[pl.ds(k, columns, stride=stride), :]
        ref, at = (out_x, k) if k < cells else (out_yz, k - cells)
        ref[at * columns : (at + 1) * columns, :] = chunk
        if k == 0:
            out_edge[:columns, :] = chunk
        if k == 2 * cells:
            out_edge[columns:, :] = chunk


def gram_kernel(columns, cells, field_x, field_yz, out):
    chunks = [part(field_x, k, columns) for k in range(cells)]
    chunks += [part(field_yz, k, columns) for k in range(2 * cells)]
    flat = wide(chunks)
    out[...] = inner(flat, flat)


def curl_kernel(
    columns, cells, mu_table, eps_table, shift, field_x, field_yz, ahead_x, ahead_y, regions,
    out_x, out_yz, out_edge, out_proj,
):
    coupling = table_rows(regions[...], mu_table)
    scaled_eps = -shift[0] * table_rows(regions[...], eps_table)
    left, right = [], []
    for y in range(cells):
        e_x = part(field_x, y, columns)
        e_y = part(field_yz, y, columns)
        e_z = part(field_yz, cells + y, columns)
        inside = y + 1 < cells
        e_x_up = part(field_x, y + 1, columns) if inside else part(ahead_y, 0, columns)
        e_z_up = part(field_yz, cells + y + 1, columns) if inside else part(ahead_y, 1, columns)
        e_y_next = part(ahead_x, y, columns)
        e_z_next = part(ahead_x, cells + y, columns)
        curl_x = (e_z_up - e_z) - forward_z(e_y)
        curl_y = forward_z(e_x) - (e_z_next - e_z)
        curl_z = (e_y_next - e_y) - (e_x_up - e_x)
        mu = coupling[y : y + 1, :]
        eps = scaled_eps[y : y + 1, :]
        m_x, m_y, m_z = mu * curl_x, mu * curl_y, mu * curl_z
        out_x[y * columns : (y + 1) * columns, :] = m_x
        out_yz[y * columns : (y + 1) * columns, :] = m_y
        out_yz[(cells + y) * columns : (cells + y + 1) * columns, :] = m_z
        if not inside:
            out_edge[:columns, :] = m_x
            out_edge[columns:, :] = m_z
        left += [curl_x, curl_y, curl_z, e_x, e_y, e_z]
        right += [m_x, m_y, m_z, eps * e_x, eps * e_y, eps * e_z]
    out_proj[...] = inner(wide(left), wide(right))


def factor(gram):
    columns = gram.shape[0]
    row = lax.broadcasted_iota(jnp.int32, (columns, 2 * columns), 0)
    lane = lax.broadcasted_iota(jnp.int32, (columns, 2 * columns), 1)
    work = jnp.concatenate([gram, jnp.zeros_like(gram)], axis=1)
    work = jnp.where(lane == row + columns, 1.0, work)
    for j in range(columns):
        pivot_row = work[j : j + 1, :]
        column = work[:, j : j + 1]
        scale = jnp.where(row > j, column / work[j : j + 1, j : j + 1], 0.0)
        work = work - scale * pivot_row
    diagonal = jnp.sum(jnp.where(lane == row, work, 0.0), axis=1, keepdims=True)
    work = work * lax.rsqrt(diagonal)
    work = jnp.where((lane >= row) & (lane <= row + columns), work, 0.0)
    return work[:, :columns], work[:, columns:]


def finish_kernel(
    columns, cells, total, eps_table, shift, field_x, field_yz, m_x, m_yz, behind_x, behind_y,
    regions, gram, proj, out_basis, out_upper, out_image, out_proj,
):
    upper, inverse = factor(gram[...] / total)
    out_upper[...] = upper
    half = lax.dot_general(
        inverse, proj[...] / total, (((1,), (0,)), ((), ())), precision=HIGHEST,
        preferred_element_type=F32,
    )
    out_proj[...] = inner(half, inverse)
    scaled_eps = shift[0] * table_rows(regions[...], eps_table)
    stride = 3 * cells
    for y in range(cells):
        e = [part(field_x, y, columns), part(field_yz, y, columns), part(field_yz, cells + y, columns)]
        m = [part(m_x, y, columns), part(m_yz, y, columns), part(m_yz, cells + y, columns)]
        inside = y > 0
        m_x_down = part(m_x, y - 1, columns) if inside else part(behind_y, 0, columns)
        m_z_down = part(m_yz, cells + y - 1, columns) if inside else part(behind_y, 1, columns)
        m_y_last = part(behind_x, y, columns)
        m_z_last = part(behind_x, cells + y, columns)
        eps = scaled_eps[y : y + 1, :]
        image = [
            (m[2] - m_z_down) - backward_z(m[1]) - eps * e[0],
            backward_z(m[0]) - (m[2] - m_z_last) - eps * e[1],
            (m[1] - m_y_last) - (m[0] - m_x_down) - eps * e[2],
        ]
        both = lax.dot_general(
            inverse, wide(e + image), (((1,), (0,)), ((), ())), precision=HIGHEST,
            preferred_element_type=F32,
        )
        lanes = e[0].shape[1]
        for c in range(3):
            place = pl.ds(c * cells + y, columns, stride=stride)
            out_basis[place, :] = both[:, c * lanes : (c + 1) * lanes]
            out_image[place, :] = both[:, (3 + c) * lanes : (4 + c) * lanes]


SMEM = pl.BlockSpec(memory_space=pltpu.SMEM)
VMEM = pl.BlockSpec(memory_space=pltpu.VMEM)


def call(body, scalars, arrays, outs):
    shapes = [jax.ShapeDtypeStruct(shape, F32) for shape in outs]
    return pl.pallas_call(
        body,
        out_shape=shapes,
        in_specs=[SMEM] * len(scalars) + [VMEM] * len(arrays),
        out_specs=[VMEM] * len(shapes),
        compiler_params=pltpu.CompilerParams(vmem_limit_bytes=32 * 1024 * 1024),
    )(*scalars, *arrays)


def local(krylov_basis, regions, mu_table, eps_table, shift_value):
    columns, parts, layers, cells, lanes = krylov_basis.shape
    assert layers == 1 and parts == 3
    total = 3 * cells * lanes * lax.axis_size("row") * lax.axis_size("col")
    basis = krylov_basis.reshape(-1, lanes)
    labels = regions[0]
    small, large, edge = (cells * columns, lanes), (2 * cells * columns, lanes), (2 * columns, lanes)
    square = (columns, columns)

    field_x, field_yz, edge_e = call(
        functools.partial(pack_kernel, columns, cells), (), (basis,), (small, large, edge)
    )
    ahead_x = shifted(field_yz, "row", -1)
    ahead_y = shifted(edge_e, "col", -1)
    (gram,) = call(
        functools.partial(gram_kernel, columns, cells), (), (field_x, field_yz), (square,)
    )
    m_x, m_yz, edge_m, proj = call(
        functools.partial(curl_kernel, columns, cells),
        (mu_table, eps_table, shift_value),
        (field_x, field_yz, ahead_x, ahead_y, labels),
        (small, large, edge, square),
    )
    behind_x = shifted(m_yz, "row", 1)
    behind_y = shifted(edge_m, "col", 1)
    gram = exchanged_sum(gram, ("col", "row"))
    proj = exchanged_sum(proj, ("col", "row"))
    basis_out, upper, image_out, projected = call(
        functools.partial(finish_kernel, columns, cells, total),
        (eps_table, shift_value),
        (field_x, field_yz, m_x, m_yz, behind_x, behind_y, labels, gram, proj),
        (basis.shape, square, basis.shape, square),
    )
    return (
        basis_out.reshape(krylov_basis.shape),
        upper,
        image_out.reshape(krylov_basis.shape),
        projected,
    )


def solution(mesh):
    placed = (P("shift", None, "row", "col", None), P("row", "col", None), P(), P(), P("shift"))
    return jax.shard_map(
        local,
        mesh=mesh,
        in_specs=placed,
        out_specs=(
            P("shift", None, "row", "col", None),
            P("shift", None),
            P("shift", None, "row", "col", None),
            P("shift", None),
        ),
        check_vma=False,
    )
```

time: 132 us -> 46 us (0.35)
  blocking collectives: 64.1 us -> 0 us
  other arithmetic: 30.2 us -> 0.04 us
  Pallas kernels: 0 us -> 9.66 us
  local copies, waits for them, and re-layouts: 10.1 us -> 1.66 us
  waiting for transfers between devices: 6.67 us -> 15 us
  matrix products: 4.18 us -> 0 us
  starting transfers between devices: 14.6 us -> 18 us
    psum x1 -> x0, blocking collectives: 64.1 us -> none  [local(): lax.psum((inner_products(flattened, flattened) / total_rows, inner_produc...]
    another operation x8 -> x0, other arithmetic: 11.9 us -> none  [the longest x3 6.52 us: factor_inverse(): lower_factor = jnp.linalg.cholesky(gram_matrix)]
    add x3 -> x8, other arithmetic: 10.8 us -> 0.04 us  [exchanged_sum(): x = x + lax.ppermute(x, axis, [(i, i ^ step) for i in range(peers)])]
    pallas_call x0 -> x4, Pallas kernels: none -> 9.66 us  [call(): pl.pallas_call(body, out_shape=shapes, in_specs=[SMEM] * len(scalars) + [...]
    ppermute x2 -> x4, waiting for transfers between devices: 0.01 us -> 7.89 us  [shifted(): return lax.ppermute(x, axis, pairs)]
    dot_general x6 -> x0, matrix products: 3.95 us -> none  [the longest x3 2.85 us: inner_products(): jnp.dot(left, right.T, precision=lax.Precision.HIGHEST, preferred_element...]
    ppermute x2 -> x4, starting transfers between devices: 5.82 us -> 9.11 us  [shifted(): return lax.ppermute(x, axis, pairs)]
    mul x8 -> x0, other arithmetic: 2.94 us -> none  [the longest x4 2.6 us: operator_block(): return stacked - shift_scalar * permittivity * interior]
  transfers between devices with their start and end apart: 6 -> 12, of which waited for: 1 -> 6; matrix products, arithmetic and copies ran while one was open for 11% -> 0% of each run, Pallas kernels for 0% -> 1%
where the time goes in v1:
time: 46 us; the launch traced here: 45.8 us
  starting transfers between devices  18 us (39%)
  waiting for transfers between devices  15 us (33%)
  Pallas kernels  9.66 us (21%)
  local copies, waits for them, and re-layouts  1.66 us (4%)
  between operations  1.4 us (3%)
    pallas_call x4, Pallas kernels, call(): pl.pallas_call(body, out_shape=shapes, in_specs=[SMEM] * len(scalars) + [...  9.66 us
    ppermute x4, starting transfers between devices, shifted(): return lax.ppermute(x, axis, pairs)  9.11 us
    ppermute x8, starting transfers between devices, exchanged_sum(): x = x + lax.ppermute(x, axis, [(i, i ^ step) for i in range(peers)])  8.91 us
    ppermute x4, waiting for transfers between devices, shifted(): return lax.ppermute(x, axis, pairs)  7.89 us
    ppermute x8, waiting for transfers between devices, exchanged_sum(): x = x + lax.ppermute(x, axis, [(i, i ^ step) for i in range(peers)])  7.11 us
    unnamed x8, local copies, waits for them, and re-layouts  1.66 us
  transfers between devices with their start and end apart: 12, of which 6 were waited for; matrix products, arithmetic and copies ran while one was open for 0% of the time, Pallas kernels for 1%

profile of v1, /device:TPU:0, one launch (start us, length us, event | category | flops | bytes accessed | tf_op | source)
XLA Modules:
  0.0 45.8 jit_solution(9172049858849623035)
XLA Ops:
  0.6 0.0 copy-start
  0.6 1.0 %copy-done = f32[64,3,1,4,128]{4,3,2,1,0:T(4,128)S(1)} copy-done((f32[64,3,1,4,128]{4,3,2,1,0:T(4,128)S(1)}, f32[64,3,1,4,128]{4,3,2,1,0:T(4,128)}, u32[]{:S(2)}) %copy-start) | copy-done | bytes 393240
  1.7 1.3 %collective-permute-start = (f32[512,128]{1,0:T(8,128)S(1)}, f32[512,128]{1,0:T(8,128)S(1)}, u32[]{:S(2)}, u32[]{:S(2)}) collective-permute-start(f32[512,128]{1,0:T(8,128)S(1)} %get-tuple-element.16.field_yz), channel_id=1, source_target_pairs={{2,0},{4,2},{6,4},{8,6},{10,8},{12,10},{14,12},{3,1},{5,3},{7,5},{... | collective-permute-start | bytes 786440 | tf_op jit(solution)/shard_map/ppermute | solution.py:17
  3.0 1.3 %collective-permute-start.1 = (f32[128,128]{1,0:T(8,128)S(1)}, f32[128,128]{1,0:T(8,128)S(1)}, u32[]{:S(2)}, u32[]{:S(2)}) collective-permute-start(f32[128,128]{1,0:T(8,128)S(1)} %get-tuple-element.17), channel_id=1, source_target_pairs={{1,0},{3,2},{5,4},{7,6},{9,8},{11,10},{13,12},{15,14},{17,16},{19,... | collective-permute-start | bytes 196616 | tf_op jit(solution)/shard_map/ppermute | solution.py:17
  4.9 0.0 copy-start.1
  4.9 1.2 %collective-permute-done.1.ahead_y = f32[128,128]{1,0:T(8,128)S(1)} collective-permute-done((f32[128,128]{1,0:T(8,128)S(1)}, f32[128,128]{1,0:T(8,128)S(1)}, u32[]{:S(2)}, u32[]{:S(2)}) %collective-permute-start.1) | collective-permute-done | bytes 65568 | tf_op jit(solution)/shard_map/ppermute | solution.py:17
  6.1 6.7 %collective-permute-done.ahead_x = f32[512,128]{1,0:T(8,128)S(1)} collective-permute-done((f32[512,128]{1,0:T(8,128)S(1)}, f32[512,128]{1,0:T(8,128)S(1)}, u32[]{:S(2)}, u32[]{:S(2)}) %collective-permute-start) | collective-permute-done | bytes 262176 | tf_op jit(solution)/shard_map/ppermute | solution.py:17
  12.8 0.0 copy-start.2
  12.8 0.0 copy-start.3
  12.8 0.0 copy-done.1
  12.8 0.6 %copy-done.2 = f32[8]{0:T(128)S(1)} copy-done((f32[8]{0:T(128)S(1)}, f32[8]{0:T(128)}, u32[]{:S(2)}) %copy-start.2) | copy-done | bytes 56
  13.5 0.0 copy-done.3
  13.5 1.5 %shard_map.85 = (f32[256,128]{1,0:T(8,128)S(1)}, f32[512,128]{1,0:T(8,128)S(1)}, f32[128,128]{1,0:T(8,128)S(1)}, f32[64,64]{1,0:T(8,128)S(1)}) custom-call(f32[8]{0:T(128)S(1)} %copy-done.3, f32[8]{0:T(128)S(1)} %copy-done.2, f32[1]{0:T(128)S(6)} %copy.11.shift, f32[256,128]{1,0:T(8,128)S(1)} %get-tuple-element.15.field_x, ...), custom_call_target="tpu_custom_call" | custom-call | tf_op jit(solution)/shard_map/pallas_call | solution.py:179
  14.9 4.6 %collective-permute-start.2 = (f32[512,128]{1,0:T(8,128)S(1)}, f32[512,128]{1,0:T(8,128)S(1)}, u32[]{:S(2)}, u32[]{:S(2)}) collective-permute-start(f32[512,128]{1,0:T(8,128)S(1)} %get-tuple-element.19.m_yz), channel_id=1, source_target_pairs={{0,2},{2,4},{4,6},{6,8},{8,10},{10,12},{12,14},{1,3},{3,5},{5,7},{... | collective-permute-start | bytes 786440 | tf_op jit(solution)/shard_map/ppermute | solution.py:17
  19.5 0.5 shard_map.86
  20.0 0.1 collective-permute-start.4
  20.0 0.5 %collective-permute-start.8 = (f32[64,64]{1,0:T(8,128)S(1)}, f32[64,64]{1,0:T(8,128)S(1)}, u32[]{:S(2)}, u32[]{:S(2)}) collective-permute-start(f32[64,64]{1,0:T(8,128)S(1)} %get-tuple-element.21), channel_id=1, source_target_pairs={{0,1},{1,0},{2,3},{3,2},{4,5},{5,4},{6,7},{7,6},{8,9},{9,8},{10,11... | collective-permute-start | bytes 49160 | tf_op jit(solution)/shard_map/ppermute | solution.py:28
  20.5 2.0 %collective-permute-start.3 = (f32[128,128]{1,0:T(8,128)S(1)}, f32[128,128]{1,0:T(8,128)S(1)}, u32[]{:S(2)}, u32[]{:S(2)}) collective-permute-start(f32[128,128]{1,0:T(8,128)S(1)} %get-tuple-element.20), channel_id=1, source_target_pairs={{0,1},{2,3},{4,5},{6,7},{8,9},{10,11},{12,13},{14,15},{16,17},{18,... | collective-permute-start | bytes 196616 | tf_op jit(solution)/shard_map/ppermute | solution.py:17
  22.5 0.0 collective-permute-done.4
  22.6 0.7 %collective-permute-start.5 = (f32[64,64]{1,0:T(8,128)S(1)}, f32[64,64]{1,0:T(8,128)S(1)}, u32[]{:S(2)}, u32[]{:S(2)}) collective-permute-start(f32[64,64]{1,0:T(8,128)S(1)} %add.24), channel_id=1, source_target_pairs={{0,2},{2,0},{4,6},{6,4},{8,10},{10,8},{12,14},{14,12},{1,3},{3,1},... | collective-permute-start | bytes 49160 | tf_op jit(solution)/shard_map/ppermute | solution.py:28
  23.3 0.0 collective-permute-done.8
  23.3 1.5 %collective-permute-start.9 = (f32[64,64]{1,0:T(8,128)S(1)}, f32[64,64]{1,0:T(8,128)S(1)}, u32[]{:S(2)}, u32[]{:S(2)}) collective-permute-start(f32[64,64]{1,0:T(8,128)S(1)} %add.28), channel_id=1, source_target_pairs={{0,2},{2,0},{4,6},{6,4},{8,10},{10,8},{12,14},{14,12},{1,3},{3,1},... | collective-permute-start | bytes 49160 | tf_op jit(solution)/shard_map/ppermute | solution.py:28
  24.7 1.8 %collective-permute-done.5 = f32[64,64]{1,0:T(8,128)S(1)} collective-permute-done((f32[64,64]{1,0:T(8,128)S(1)}, f32[64,64]{1,0:T(8,128)S(1)}, u32[]{:S(2)}, u32[]{:S(2)}) %collective-permute-start.5) | collective-permute-done | bytes 16416 | tf_op jit(solution)/shard_map/ppermute | solution.py:28
  26.5 1.6 %collective-permute-start.6 = (f32[64,64]{1,0:T(8,128)S(1)}, f32[64,64]{1,0:T(8,128)S(1)}, u32[]{:S(2)}, u32[]{:S(2)}) collective-permute-start(f32[64,64]{1,0:T(8,128)S(1)} %add.25), channel_id=1, source_target_pairs={{0,4},{2,6},{4,0},{6,2},{8,12},{10,14},{12,8},{14,10},{1,5},{3,7},... | collective-permute-start | bytes 49160 | tf_op jit(solution)/shard_map/ppermute | solution.py:28
  28.1 0.0 collective-permute-done.9
  28.1 0.7 %collective-permute-start.10 = (f32[64,64]{1,0:T(8,128)S(1)}, f32[64,64]{1,0:T(8,128)S(1)}, u32[]{:S(2)}, u32[]{:S(2)}) collective-permute-start(f32[64,64]{1,0:T(8,128)S(1)} %add.29), channel_id=1, source_target_pairs={{0,4},{2,6},{4,0},{6,2},{8,12},{10,14},{12,8},{14,10},{1,5},{3,7},... | collective-permute-start | bytes 49160 | tf_op jit(solution)/shard_map/ppermute | solution.py:28
  28.8 1.6 %collective-permute-done.6 = f32[64,64]{1,0:T(8,128)S(1)} collective-permute-done((f32[64,64]{1,0:T(8,128)S(1)}, f32[64,64]{1,0:T(8,128)S(1)}, u32[]{:S(2)}, u32[]{:S(2)}) %collective-permute-start.6) | collective-permute-done | bytes 16416 | tf_op jit(solution)/shard_map/ppermute | solution.py:28
  30.5 2.7 %collective-permute-start.7 = (f32[64,64]{1,0:T(8,128)S(1)}, f32[64,64]{1,0:T(8,128)S(1)}, u32[]{:S(2)}, u32[]{:S(2)}) collective-permute-start(f32[64,64]{1,0:T(8,128)S(1)} %add.26), channel_id=1, source_target_pairs={{0,8},{2,10},{4,12},{6,14},{8,0},{10,2},{12,4},{14,6},{1,9},{3,11}... | collective-permute-start | bytes 49160 | tf_op jit(solution)/shard_map/ppermute | solution.py:28
  33.1 0.0 collective-permute-done.10
  33.2 1.2 %collective-permute-start.11 = (f32[64,64]{1,0:T(8,128)S(1)}, f32[64,64]{1,0:T(8,128)S(1)}, u32[]{:S(2)}, u32[]{:S(2)}) collective-permute-start(f32[64,64]{1,0:T(8,128)S(1)} %add.30), channel_id=1, source_target_pairs={{0,8},{2,10},{4,12},{6,14},{8,0},{10,2},{12,4},{14,6},{1,9},{3,11}... | collective-permute-start | bytes 49160 | tf_op jit(solution)/shard_map/ppermute | solution.py:28
  34.4 0.9 %collective-permute-done.7 = f32[64,64]{1,0:T(8,128)S(1)} collective-permute-done((f32[64,64]{1,0:T(8,128)S(1)}, f32[64,64]{1,0:T(8,128)S(1)}, u32[]{:S(2)}, u32[]{:S(2)}) %collective-permute-start.7) | collective-permute-done | bytes 16416 | tf_op jit(solution)/shard_map/ppermute | solution.py:28
  35.3 2.8 %collective-permute-done.11 = f32[64,64]{1,0:T(8,128)S(1)} collective-permute-done((f32[64,64]{1,0:T(8,128)S(1)}, f32[64,64]{1,0:T(8,128)S(1)}, u32[]{:S(2)}, u32[]{:S(2)}) %collective-permute-start.11) | collective-permute-done | bytes 16416 | tf_op jit(solution)/shard_map/ppermute | solution.py:28
  38.1 0.0 collective-permute-done.3.behind_y
  38.1 0.0 collective-permute-done.2.behind_x
  38.1 7.7 %shard_map.87 = (f32[768,128]{1,0:T(8,128)}, f32[64,64]{1,0:T(8,128)}, f32[768,128]{1,0:T(8,128)}, f32[64,64]{1,0:T(8,128)}) custom-call(f32[8]{0:T(128)S(1)} %copy-done.2, f32[1]{0:T(128)S(6)} %copy.11.shift, f32[256,128]{1,0:T(8,128)S(1)} %get-tuple-element.15.field_x, f32[512,128]{1,0:T(8,128)S(1)} %get-tuple-element.16.field_yz, ...), custom_call_target="tpu_custom_call" | custom-call | tf_op jit(solution)/shard_map/pallas_call | solution.py:179
  (9 shorter events, 0.1 us)
Async XLA Ops:
  0.6 1.0 %copy-start = (f32[64,3,1,4,128]{4,3,2,1,0:T(4,128)S(1)}, f32[64,3,1,4,128]{4,3,2,1,0:T(4,128)}, u32[]{:S(2)}) copy-start(f32[64,3,1,4,128]{4,3,2,1,0:T(4,128)} %param.5) | copy-start | bytes 1179652
  1.7 11.1 %collective-permute-start = (f32[512,128]{1,0:T(8,128)S(1)}, f32[512,128]{1,0:T(8,128)S(1)}, u32[]{:S(2)}, u32[]{:S(2)}) collective-permute-start(f32[512,128]{1,0:T(8,128)S(1)} %get-tuple-element.16.field_yz), channel_id=1, source_target_pairs={{2,0},{4,2},{6,4},{8,6},{10,8},{12,10},{14,12},{3,1},{5,3},{7,5},{... | collective-permute-start | bytes 786440 | tf_op jit(solution)/shard_map/ppermute | solution.py:17
  3.0 3.1 %collective-permute-start.1 = (f32[128,128]{1,0:T(8,128)S(1)}, f32[128,128]{1,0:T(8,128)S(1)}, u32[]{:S(2)}, u32[]{:S(2)}) collective-permute-start(f32[128,128]{1,0:T(8,128)S(1)} %get-tuple-element.17), channel_id=1, source_target_pairs={{1,0},{3,2},{5,4},{7,6},{9,8},{11,10},{13,12},{15,14},{17,16},{19,... | collective-permute-start | bytes 196616 | tf_op jit(solution)/shard_map/ppermute | solution.py:17
  4.9 7.9 %copy-start.1 = (s32[1,4,128]{2,1,0:T(4,128)S(1)}, s32[1,4,128]{2,1,0:T(4,128)}, u32[]{:S(2)}) copy-start(s32[1,4,128]{2,1,0:T(4,128)} %param.6) | copy-start | bytes 6148
  12.8 0.7 %copy-start.2 = (f32[8]{0:T(128)S(1)}, f32[8]{0:T(128)}, u32[]{:S(2)}) copy-start(f32[8]{0:T(128)} %eps_table.3) | copy-start | bytes 100
  12.8 0.7 %copy-start.3 = (f32[8]{0:T(128)S(1)}, f32[8]{0:T(128)}, u32[]{:S(2)}) copy-start(f32[8]{0:T(128)} %mu_table.1) | copy-start | bytes 100
  14.9 23.1 %collective-permute-start.2 = (f32[512,128]{1,0:T(8,128)S(1)}, f32[512,128]{1,0:T(8,128)S(1)}, u32[]{:S(2)}, u32[]{:S(2)}) collective-permute-start(f32[512,128]{1,0:T(8,128)S(1)} %get-tuple-element.19.m_yz), channel_id=1, source_target_pairs={{0,2},{2,4},{4,6},{6,8},{8,10},{10,12},{12,14},{1,3},{3,5},{5,7},{... | collective-permute-start | bytes 786440 | tf_op jit(solution)/shard_map/ppermute | solution.py:17
  20.0 2.6 %collective-permute-start.4 = (f32[64,64]{1,0:T(8,128)S(1)}, f32[64,64]{1,0:T(8,128)S(1)}, u32[]{:S(2)}, u32[]{:S(2)}) collective-permute-start(f32[64,64]{1,0:T(8,128)S(1)} %shard_map.86), channel_id=1, source_target_pairs={{0,1},{1,0},{2,3},{3,2},{4,5},{5,4},{6,7},{7,6},{8,9},{9,8},{10,11... | collective-permute-start | bytes 49160 | tf_op jit(solution)/shard_map/ppermute | solution.py:28
  20.0 3.2 %collective-permute-start.8 = (f32[64,64]{1,0:T(8,128)S(1)}, f32[64,64]{1,0:T(8,128)S(1)}, u32[]{:S(2)}, u32[]{:S(2)}) collective-permute-start(f32[64,64]{1,0:T(8,128)S(1)} %get-tuple-element.21), channel_id=1, source_target_pairs={{0,1},{1,0},{2,3},{3,2},{4,5},{5,4},{6,7},{7,6},{8,9},{9,8},{10,11... | collective-permute-start | bytes 49160 | tf_op jit(solution)/shard_map/ppermute | solution.py:28
  20.5 17.5 %collective-permute-start.3 = (f32[128,128]{1,0:T(8,128)S(1)}, f32[128,128]{1,0:T(8,128)S(1)}, u32[]{:S(2)}, u32[]{:S(2)}) collective-permute-start(f32[128,128]{1,0:T(8,128)S(1)} %get-tuple-element.20), channel_id=1, source_target_pairs={{0,1},{2,3},{4,5},{6,7},{8,9},{10,11},{12,13},{14,15},{16,17},{18,... | collective-permute-start | bytes 196616 | tf_op jit(solution)/shard_map/ppermute | solution.py:17
  22.6 4.0 %collective-permute-start.5 = (f32[64,64]{1,0:T(8,128)S(1)}, f32[64,64]{1,0:T(8,128)S(1)}, u32[]{:S(2)}, u32[]{:S(2)}) collective-permute-start(f32[64,64]{1,0:T(8,128)S(1)} %add.24), channel_id=1, source_target_pairs={{0,2},{2,0},{4,6},{6,4},{8,10},{10,8},{12,14},{14,12},{1,3},{3,1},... | collective-permute-start | bytes 49160 | tf_op jit(solution)/shard_map/ppermute | solution.py:28
  23.3 4.8 %collective-permute-start.9 = (f32[64,64]{1,0:T(8,128)S(1)}, f32[64,64]{1,0:T(8,128)S(1)}, u32[]{:S(2)}, u32[]{:S(2)}) collective-permute-start(f32[64,64]{1,0:T(8,128)S(1)} %add.28), channel_id=1, source_target_pairs={{0,2},{2,0},{4,6},{6,4},{8,10},{10,8},{12,14},{14,12},{1,3},{3,1},... | collective-permute-start | bytes 49160 | tf_op jit(solution)/shard_map/ppermute | solution.py:28
  26.5 3.9 %collective-permute-start.6 = (f32[64,64]{1,0:T(8,128)S(1)}, f32[64,64]{1,0:T(8,128)S(1)}, u32[]{:S(2)}, u32[]{:S(2)}) collective-permute-start(f32[64,64]{1,0:T(8,128)S(1)} %add.25), channel_id=1, source_target_pairs={{0,4},{2,6},{4,0},{6,2},{8,12},{10,14},{12,8},{14,10},{1,5},{3,7},... | collective-permute-start | bytes 49160 | tf_op jit(solution)/shard_map/ppermute | solution.py:28
  28.1 5.0 %collective-permute-start.10 = (f32[64,64]{1,0:T(8,128)S(1)}, f32[64,64]{1,0:T(8,128)S(1)}, u32[]{:S(2)}, u32[]{:S(2)}) collective-permute-start(f32[64,64]{1,0:T(8,128)S(1)} %add.29), channel_id=1, source_target_pairs={{0,4},{2,6},{4,0},{6,2},{8,12},{10,14},{12,8},{14,10},{1,5},{3,7},... | collective-permute-start | bytes 49160 | tf_op jit(solution)/shard_map/ppermute | solution.py:28
  30.5 4.8 %collective-permute-start.7 = (f32[64,64]{1,0:T(8,128)S(1)}, f32[64,64]{1,0:T(8,128)S(1)}, u32[]{:S(2)}, u32[]{:S(2)}) collective-permute-start(f32[64,64]{1,0:T(8,128)S(1)} %add.26), channel_id=1, source_target_pairs={{0,8},{2,10},{4,12},{6,14},{8,0},{10,2},{12,4},{14,6},{1,9},{3,11}... | collective-permute-start | bytes 49160 | tf_op jit(solution)/shard_map/ppermute | solution.py:28
  33.2 4.9 %collective-permute-start.11 = (f32[64,64]{1,0:T(8,128)S(1)}, f32[64,64]{1,0:T(8,128)S(1)}, u32[]{:S(2)}, u32[]{:S(2)}) collective-permute-start(f32[64,64]{1,0:T(8,128)S(1)} %add.30), channel_id=1, source_target_pairs={{0,8},{2,10},{4,12},{6,14},{8,0},{10,2},{12,4},{14,6},{1,9},{3,11}... | collective-permute-start | bytes 49160 | tf_op jit(solution)/shard_map/ppermute | solution.py:28

commit v2 on v1

v2 whole, which is shorter than its diff:
```python
import functools

import jax
import jax.numpy as jnp
from jax import lax
from jax.experimental import pallas as pl
from jax.experimental.pallas import tpu as pltpu
from jax.sharding import PartitionSpec as P

F32 = jnp.float32
HIGHEST = lax.Precision.HIGHEST


def shifted(x, axis, by):
    peers = lax.axis_size(axis)
    pairs = [(i, i + by) for i in range(peers) if 0 <= i + by < peers]
    return lax.ppermute(x, axis, pairs)


def wide(chunks):
    return jnp.concatenate(chunks, axis=1)


def inner(left, right):
    return lax.dot_general(
        left, right, (((1,), (1,)), ((), ())), precision=HIGHEST, preferred_element_type=F32
    )


def table_rows(labels, table_ref):
    result = jnp.zeros(labels.shape, F32)
    for region in range(table_ref.shape[0]):
        result = jnp.where(labels == region, table_ref[region], result)
    return result


def forward_z(values):
    lanes = values.shape[1]
    lane = lax.broadcasted_iota(jnp.int32, values.shape, 1)
    ahead = jnp.where(lane == lanes - 1, 0.0, pltpu.roll(values, lanes - 1, 1))
    return ahead - values


def backward_z(values):
    lane = lax.broadcasted_iota(jnp.int32, values.shape, 1)
    return values - jnp.where(lane == 0, 0.0, pltpu.roll(values, 1, 1))


def part(ref, index, columns):
    return ref[index * columns : (index + 1) * columns, :]


def packed(square):
    half = square.shape[0] // 2
    return jnp.concatenate([square[:half, :], square[half:, :]], axis=1)


def unpacked(pair):
    half = pair.shape[1] // 2
    return jnp.concatenate([pair[:, :half], pair[:, half:]], axis=0)


def pack_kernel(columns, cells, basis, out_x, out_yz):
    stride = 3 * cells
    for k in range(stride):
        ref, at = (out_x, k) if k < cells else (out_yz, k - cells)
        ref[at * columns : (at + 1) * columns, :] = basis[pl.ds(k, columns, stride=stride), :]


def material_kernel(mu_table, eps_table, shift, regions, out):
    labels = regions[...]
    cells = labels.shape[0]
    out[:cells, :] = table_rows(labels, mu_table)
    out[cells:, :] = shift[0] * table_rows(labels, eps_table)


def gram_kernel(columns, cells, field_x, field_yz, out):
    half = columns // 2
    chunks = [part(field_x, k, columns) for k in range(cells)]
    chunks += [part(field_yz, k, columns) for k in range(2 * cells)]
    flat = wide(chunks)
    out[half : half + columns, :] = chunks[0]
    out[half + columns :, :] = chunks[2 * cells]
    out[:half, :] = packed(inner(flat, flat))


def curl_kernel(
    columns, cells, has_next, field_x, field_yz, ahead_x, ahead_y, material, gram, gram_other,
    out_x, out_yz, out_edge, out_gram,
):
    half = columns // 2
    out_gram[...] = gram[...] + gram_other[...]
    coupling = material[:cells, :]
    scaled_eps = -material[cells:, :]
    inside_next = has_next[0] > 0
    left, right = [], []
    for y in range(cells):
        e_x = part(field_x, y, columns)
        e_y = part(field_yz, y, columns)
        e_z = part(field_yz, cells + y, columns)
        inside = y + 1 < cells
        if inside:
            e_x_up, e_z_up = part(field_x, y + 1, columns), part(field_yz, cells + y + 1, columns)
        else:
            e_x_up = jnp.where(inside_next, ahead_y[half : half + columns, :], 0.0)
            e_z_up = jnp.where(inside_next, ahead_y[half + columns :, :], 0.0)
        e_y_next = part(ahead_x, y, columns)
        e_z_next = part(ahead_x, cells + y, columns)
        curl_x = (e_z_up - e_z) - forward_z(e_y)
        curl_y = forward_z(e_x) - (e_z_next - e_z)
        curl_z = (e_y_next - e_y) - (e_x_up - e_x)
        mu = coupling[y : y + 1, :]
        eps = scaled_eps[y : y + 1, :]
        m_x, m_y, m_z = mu * curl_x, mu * curl_y, mu * curl_z
        out_x[y * columns : (y + 1) * columns, :] = m_x
        out_yz[y * columns : (y + 1) * columns, :] = m_y
        out_yz[(cells + y) * columns : (cells + y + 1) * columns, :] = m_z
        if not inside:
            out_edge[half : half + columns, :] = m_x
            out_edge[half + columns :, :] = m_z
        left += [curl_x, curl_y, curl_z, e_x, e_y, e_z]
        right += [m_x, m_y, m_z, eps * e_x, eps * e_y, eps * e_z]
    out_edge[:half, :] = packed(inner(wide(left), wide(right)))


def join_kernel(gram, edge, edge_other, out):
    half, columns = gram.shape[0], 2 * gram.shape[0]
    proj = edge[:half, :] + edge_other[:half, :]
    out[:, :columns] = unpacked(gram[...])
    out[:, columns:] = unpacked(proj)


def factor(gram):
    columns = gram.shape[0]
    span, tile = 2 * columns, 8
    count = columns // tile
    spread = lambda values: jnp.broadcast_to(values, (tile, span))
    sublane = lax.broadcasted_iota(jnp.int32, (tile, span), 0)
    lane = lax.broadcasted_iota(jnp.int32, (tile, span), 1)
    blocks = []
    for b in range(count):
        rows = gram[b * tile : (b + 1) * tile, :]
        rows = jnp.concatenate([rows, jnp.zeros_like(rows)], axis=1)
        blocks.append(jnp.where(lane == sublane + b * tile + columns, 1.0, rows))
    scales = [None] * count
    for first in range(count):
        panel = [
            [spread(rows[:, first * tile + k : first * tile + k + 1]) for rows in blocks[first:]]
            for k in range(tile)
        ]
        for k in range(tile):
            pivot = spread(panel[k][0][k : k + 1, :])
            inverse = 1.0 / pivot
            ratio = [rows * inverse for rows in panel[k]]
            ratio[0] = jnp.where(sublane > k, ratio[0], 0.0)
            root = lax.rsqrt(pivot)
            scales[first] = root if k == 0 else jnp.where(sublane == k, root, scales[first])
            for later in range(k + 1, tile):
                entry = spread(panel[k][0][later : later + 1, :])
                panel[later] = [rows - f * entry for rows, f in zip(panel[later], ratio)]
            pivot_row = spread(blocks[first][k : k + 1, :])
            for b in range(first, count):
                blocks[b] = blocks[b] - ratio[b - first] * pivot_row
    kept = []
    for b in range(count):
        row = sublane + b * tile
        kept.append(jnp.where((lane >= row) & (lane <= row + columns), blocks[b] * scales[b], 0.0))
    both = jnp.concatenate(kept, axis=0)
    return both[:, :columns], both[:, columns:]


def factor_kernel(total, sums, out_upper, out_inverse):
    columns = sums.shape[0]
    upper, inverse = factor(sums[:, :columns] / total)
    out_upper[...] = upper
    out_inverse[...] = inverse


def finish_kernel(
    columns, cells, total, has_last, field_x, field_yz, m_x, m_yz, behind_x, behind_y, material,
    inverse_ref, proj, proj_other, out_basis, out_image, out_proj,
):
    half = columns // 2
    inverse = inverse_ref[...]
    raw = unpacked(proj[...] + proj_other[...]) / total
    left = lax.dot_general(
        inverse, raw, (((1,), (0,)), ((), ())), precision=HIGHEST, preferred_element_type=F32
    )
    out_proj[...] = inner(left, inverse)
    inside_last = has_last[0] > 0
    scaled_eps = material[cells:, :]
    stride = 3 * cells
    for y in range(cells):
        e = [part(field_x, y, columns), part(field_yz, y, columns), part(field_yz, cells + y, columns)]
        m = [part(m_x, y, columns), part(m_yz, y, columns), part(m_yz, cells + y, columns)]
        if y > 0:
            m_x_down, m_z_down = part(m_x, y - 1, columns), part(m_yz, cells + y - 1, columns)
        else:
            m_x_down = jnp.where(inside_last, behind_y[half : half + columns, :], 0.0)
            m_z_down = jnp.where(inside_last, behind_y[half + columns :, :], 0.0)
        m_y_last = part(behind_x, y, columns)
        m_z_last = part(behind_x, cells + y, columns)
        eps = scaled_eps[y : y + 1, :]
        image = [
            (m[2] - m_z_down) - backward_z(m[1]) - eps * e[0],
            backward_z(m[0]) - (m[2] - m_z_last) - eps * e[1],
            (m[1] - m_y_last) - (m[0] - m_x_down) - eps * e[2],
        ]
        both = lax.dot_general(
            inverse, wide(e + image), (((1,), (0,)), ((), ())), precision=HIGHEST,
            preferred_element_type=F32,
        )
        lanes = e[0].shape[1]
        for c in range(3):
            place = pl.ds(c * cells + y, columns, stride=stride)
            out_basis[place, :] = both[:, c * lanes : (c + 1) * lanes]
            out_image[place, :] = both[:, (3 + c) * lanes : (4 + c) * lanes]


def split_kernel(sums, out):
    columns = sums.shape[0]
    out[...] = packed(sums[:, columns:])


SMEM = pl.BlockSpec(memory_space=pltpu.SMEM)
VMEM = pl.BlockSpec(memory_space=pltpu.VMEM)


def call(body, scalars, arrays, outs, flops=None):
    shapes = [jax.ShapeDtypeStruct(shape, F32) for shape in outs]
    cost = None
    if flops is not None:
        cost = pl.CostEstimate(flops=flops, bytes_accessed=0, transcendentals=0)
    return pl.pallas_call(
        body,
        out_shape=shapes,
        in_specs=[SMEM] * len(scalars) + [VMEM] * len(arrays),
        out_specs=[VMEM] * len(shapes),
        cost_estimate=cost,
        compiler_params=pltpu.CompilerParams(vmem_limit_bytes=32 * 1024 * 1024),
    )(*scalars, *arrays)


def swapped(x, axis, step):
    return lax.ppermute(x, axis, [(i, i ^ step) for i in range(lax.axis_size(axis))])


def local(krylov_basis, regions, mu_table, eps_table, shift_value):
    columns, parts, layers, cells, lanes = krylov_basis.shape
    rows, cols = lax.axis_size("row"), lax.axis_size("col")
    assert layers == 1 and parts == 3 and cols == 2 and rows & (rows - 1) == 0
    total = 3 * cells * lanes * rows * cols
    basis = krylov_basis.reshape(-1, lanes)
    labels = regions[0]
    half = columns // 2
    small, large = (cells * columns, lanes), (2 * cells * columns, lanes)
    edge, pair = (half + 2 * columns, lanes), (half, 2 * columns)
    square = (columns, columns)
    place = lax.axis_index("col")
    has_next = jnp.where(place == 0, 1, 0).astype(jnp.int32)[None]
    has_last = 1 - has_next

    (material,) = call(
        material_kernel, (mu_table, eps_table, shift_value), (labels,), ((2 * cells, lanes),),
        flops=0,
    )
    field_x, field_yz = call(
        functools.partial(pack_kernel, columns, cells), (), (basis,), (small, large), flops=0
    )
    ahead_x = shifted(field_yz, "row", -1)
    (gram_edge,) = call(
        functools.partial(gram_kernel, columns, cells), (), (field_x, field_yz), (edge,), flops=0
    )
    ahead_y = swapped(gram_edge, "col", 1)
    gram = gram_edge[:half] + ahead_y[:half]
    gram_other = swapped(gram, "row", 1)
    m_x, m_yz, proj_edge, gram = call(
        functools.partial(curl_kernel, columns, cells),
        (has_next,),
        (field_x, field_yz, ahead_x, ahead_y, material, gram, gram_other),
        (small, large, edge, pair),
        flops=0,
    )
    behind_y = swapped(proj_edge, "col", 1)
    behind_x = shifted(m_yz, "row", 1)
    (sums,) = call(
        join_kernel, (), (gram, proj_edge, behind_y), ((columns, 2 * columns),), flops=0
    )
    step = 2
    while step < rows:
        sums = sums + swapped(sums, "row", step)
        step *= 2
    (proj,) = call(split_kernel, (), (sums,), (pair,), flops=0)
    proj_other = swapped(proj, "row", 1)
    upper, inverse = call(
        functools.partial(factor_kernel, total), (), (sums,), (square, square), flops=0
    )
    basis_out, image_out, projected = call(
        functools.partial(finish_kernel, columns, cells, total),
        (has_last,),
        (field_x, field_yz, m_x, m_yz, behind_x, behind_y, material, inverse, proj, proj_other),
        (basis.shape, basis.shape, square),
        flops=0,
    )
    return (
        basis_out.reshape(krylov_basis.shape),
        upper,
        image_out.reshape(krylov_basis.shape),
        projected,
    )


def solution(mesh):
    placed = (P("shift", None, "row", "col", None), P("row", "col", None), P(), P(), P("shift"))
    return jax.shard_map(
        local,
        mesh=mesh,
        in_specs=placed,
        out_specs=(
            P("shift", None, "row", "col", None),
            P("shift", None),
            P("shift", None, "row", "col", None),
            P("shift", None),
        ),
        check_vma=False,
    )
```

time: 46 us -> 36.1 us (0.78)
  waiting for transfers between devices: 15 us -> 10.8 us
  Pallas kernels: 9.66 us -> 6.5 us
  starting transfers between devices: 18 us -> 15.5 us
    ppermute x4 -> x2, waiting for transfers between devices: 7.89 us -> 0.01 us  [shifted(): return lax.ppermute(x, axis, pairs)]
    ppermute x8 -> x6, waiting for transfers between devices: 7.11 us -> 10.8 us  [swapped(): lax.ppermute(x, axis, [(i, i ^ step) for i in range(lax.axis_size(axis))])]
    ppermute x4 -> x2, starting transfers between devices: 9.11 us -> 5.48 us  [shifted(): return lax.ppermute(x, axis, pairs)]
    pallas_call x4 -> x8, Pallas kernels: 9.66 us -> 6.5 us  [call(): pl.pallas_call(body, out_shape=shapes, in_specs=[SMEM] * len(scalars) + [...]
    ppermute x8 -> x6, starting transfers between devices: 8.91 us -> 10.1 us  [swapped(): lax.ppermute(x, axis, [(i, i ^ step) for i in range(lax.axis_size(axis))])]
  transfers between devices with their start and end apart: 12 -> 8, of which waited for: 6 -> 4; matrix products, arithmetic and copies ran while one was open for 0% -> 0% of each run, Pallas kernels for 1% -> 9%
where the time goes in v2:
time: 36.1 us; the launch traced here: 35.9 us
  starting transfers between devices  15.5 us (43%)
  waiting for transfers between devices  10.8 us (30%)
  Pallas kernels  6.5 us (18%)
  local copies, waits for them, and re-layouts  1.65 us (5%)
  between operations  1.38 us (4%)
    ppermute x6, waiting for transfers between devices, swapped(): lax.ppermute(x, axis, [(i, i ^ step) for i in range(lax.axis_size(axis))])  10.8 us
    ppermute x6, starting transfers between devices, swapped(): lax.ppermute(x, axis, [(i, i ^ step) for i in range(lax.axis_size(axis))])  10.1 us
    pallas_call x8, Pallas kernels, call(): pl.pallas_call(body, out_shape=shapes, in_specs=[SMEM] * len(scalars) + [...  6.5 us
    ppermute x2, starting transfers between devices, shifted(): return lax.ppermute(x, axis, pairs)  5.48 us
    unnamed x8, local copies, waits for them, and re-layouts  1.65 us
  transfers between devices with their start and end apart: 8, of which 4 were waited for; matrix products, arithmetic and copies ran while one was open for 0% of the time, Pallas kernels for 9%

profile of v2, /device:TPU:0, one launch (start us, length us, event | category | flops | bytes accessed | tf_op | source)
XLA Modules:
  0.0 35.9 jit_solution(11234817362713115366)
XLA Ops:
  0.6 0.0 copy-start
  0.6 1.0 %copy-done = f32[64,3,1,4,128]{4,3,2,1,0:T(4,128)S(1)} copy-done((f32[64,3,1,4,128]{4,3,2,1,0:T(4,128)S(1)}, f32[64,3,1,4,128]{4,3,2,1,0:T(4,128)}, u32[]{:S(2)}) %copy-start) | copy-done | bytes 393240
  1.7 0.5 %shard_map.85 = f32[160,128]{1,0:T(8,128)S(1)} custom-call(f32[256,128]{1,0:T(8,128)S(1)} %get-tuple-element.15.field_x, f32[512,128]{1,0:T(8,128)S(1)} %get-tuple-element.16.field_yz), custom_call_target="tpu_custom_call" | custom-call | tf_op jit(solution)/shard_map/pallas_call | solution.py:234
  2.2 0.5 %collective-permute-start.1 = (f32[160,128]{1,0:T(8,128)S(1)}, f32[160,128]{1,0:T(8,128)S(1)}, u32[]{:S(2)}, u32[]{:S(2)}) collective-permute-start(f32[160,128]{1,0:T(8,128)S(1)} %shard_map.85), channel_id=1, source_target_pairs={{0,1},{1,0},{2,3},{3,2},{4,5},{5,4},{6,7},{7,6},{8,9},{9,8},{10,11... | collective-permute-start | bytes 245768 | tf_op jit(solution)/shard_map/ppermute | solution.py:245
  2.7 1.3 %collective-permute-start = (f32[512,128]{1,0:T(8,128)S(1)}, f32[512,128]{1,0:T(8,128)S(1)}, u32[]{:S(2)}, u32[]{:S(2)}) collective-permute-start(f32[512,128]{1,0:T(8,128)S(1)} %get-tuple-element.16.field_yz), channel_id=1, source_target_pairs={{2,0},{4,2},{6,4},{8,6},{10,8},{12,10},{14,12},{3,1},{5,3},{7,5},{... | collective-permute-start | bytes 786440 | tf_op jit(solution)/shard_map/ppermute | solution.py:17
  3.9 0.0 collective-permute-done.1.ahead_y
  4.0 3.2 %collective-permute-start.2 = (f32[32,128]{1,0:T(8,128)S(1)}, f32[32,128]{1,0:T(8,128)S(1)}, u32[]{:S(2)}, u32[]{:S(2)}) collective-permute-start(f32[32,128]{1,0:T(8,128)S(1)} %slice_add_fusion.gram), channel_id=1, source_target_pairs={{0,2},{2,0},{4,6},{6,4},{8,10},{10,8},{12,14},{14,12},{1,3},{3,1},... | collective-permute-start | bytes 49160 | tf_op jit(solution)/shard_map/ppermute | solution.py:245
  7.8 0.0 copy-start.1
  7.8 0.0 copy-start.2
  7.9 0.0 copy-start.3
  7.9 0.6 %copy-done.1 = s32[1,4,128]{2,1,0:T(4,128)S(1)} copy-done((s32[1,4,128]{2,1,0:T(4,128)S(1)}, s32[1,4,128]{2,1,0:T(4,128)}, u32[]{:S(2)}) %copy-start.1) | copy-done | bytes 2072
  8.5 0.0 copy-done.2
  8.5 0.0 copy-done.3
  8.5 0.6 %shard_map.86.material = f32[8,128]{1,0:T(8,128)S(1)} custom-call(f32[8]{0:T(128)S(1)} %copy-done.2, f32[8]{0:T(128)S(1)} %copy-done.3, f32[1]{0:T(128)S(6)} %copy.11.shift, s32[4,128]{1,0:T(4,128)S(1)} %bitcast.10), custom_call_target="tpu_custom_call" | custom-call | tf_op jit(solution)/shard_map/pallas_call | solution.py:234
  9.1 5.3 %collective-permute-done.2.gram_other = f32[32,128]{1,0:T(8,128)S(1)} collective-permute-done((f32[32,128]{1,0:T(8,128)S(1)}, f32[32,128]{1,0:T(8,128)S(1)}, u32[]{:S(2)}, u32[]{:S(2)}) %collective-permute-start.2) | collective-permute-done | bytes 16416 | tf_op jit(solution)/shard_map/ppermute | solution.py:245
  14.4 0.0 collective-permute-done.ahead_x
  14.4 1.0 %shard_map.87 = (f32[256,128]{1,0:T(8,128)S(1)}, f32[512,128]{1,0:T(8,128)S(1)}, f32[160,128]{1,0:T(8,128)S(1)}, f32[32,128]{1,0:T(8,128)S(1)}) custom-call(s32[1]{0:T(128)} %bitcast.has_next, f32[256,128]{1,0:T(8,128)S(1)} %get-tuple-element.15.field_x, f32[512,128]{1,0:T(8,128)S(1)} %get-tuple-element.16.field_yz, ...), custom_call_target="tpu_custom_call" | custom-call | tf_op jit(solution)/shard_map/pallas_call | solution.py:234
  15.3 4.2 %collective-permute-start.3 = (f32[512,128]{1,0:T(8,128)S(1)}, f32[512,128]{1,0:T(8,128)S(1)}, u32[]{:S(2)}, u32[]{:S(2)}) collective-permute-start(f32[512,128]{1,0:T(8,128)S(1)} %get-tuple-element.18.m_yz), channel_id=1, source_target_pairs={{0,2},{2,4},{4,6},{6,8},{8,10},{10,12},{12,14},{1,3},{3,5},{5,7},{... | collective-permute-start | bytes 786440 | tf_op jit(solution)/shard_map/ppermute | solution.py:17
  19.5 0.1 collective-permute-start.4
  19.6 1.3 %collective-permute-done.4.edge_other.behind_y = f32[160,128]{1,0:T(8,128)S(1)} collective-permute-done((f32[160,128]{1,0:T(8,128)S(1)}, f32[160,128]{1,0:T(8,128)S(1)}, u32[]{:S(2)}, u32[]{:S(2)}) %collective-permute-start.4) | collective-permute-done | bytes 81952 | tf_op jit(solution)/shard_map/ppermute | solution.py:245
  20.9 0.1 shard_map.88
  21.0 1.7 %collective-permute-start.5 = (f32[64,128]{1,0:T(8,128)S(1)}, f32[64,128]{1,0:T(8,128)S(1)}, u32[]{:S(2)}, u32[]{:S(2)}) collective-permute-start(f32[64,128]{1,0:T(8,128)S(1)} %shard_map.88), channel_id=1, source_target_pairs={{0,4},{2,6},{4,0},{6,2},{8,12},{10,14},{12,8},{14,10},{1,5},{3,7},... | collective-permute-start | bytes 98312 | tf_op jit(solution)/shard_map/ppermute | solution.py:245
  22.7 2.2 %collective-permute-done.5 = f32[64,128]{1,0:T(8,128)S(1)} collective-permute-done((f32[64,128]{1,0:T(8,128)S(1)}, f32[64,128]{1,0:T(8,128)S(1)}, u32[]{:S(2)}, u32[]{:S(2)}) %collective-permute-start.5) | collective-permute-done | bytes 32800 | tf_op jit(solution)/shard_map/ppermute | solution.py:245
  24.9 2.8 %collective-permute-start.6 = (f32[64,128]{1,0:T(8,128)S(1)}, f32[64,128]{1,0:T(8,128)S(1)}, u32[]{:S(2)}, u32[]{:S(2)}) collective-permute-start(f32[64,128]{1,0:T(8,128)S(1)} %add.10), channel_id=1, source_target_pairs={{0,8},{2,10},{4,12},{6,14},{8,0},{10,2},{12,4},{14,6},{1,9},{3,11}... | collective-permute-start | bytes 98312 | tf_op jit(solution)/shard_map/ppermute | solution.py:245
  27.7 2.1 %collective-permute-done.6 = f32[64,128]{1,0:T(8,128)S(1)} collective-permute-done((f32[64,128]{1,0:T(8,128)S(1)}, f32[64,128]{1,0:T(8,128)S(1)}, u32[]{:S(2)}, u32[]{:S(2)}) %collective-permute-start.6) | collective-permute-done | bytes 32800 | tf_op jit(solution)/shard_map/ppermute | solution.py:245
  29.7 0.1 shard_map.90.proj
  29.8 1.8 %collective-permute-start.7 = (f32[32,128]{1,0:T(8,128)S(1)}, f32[32,128]{1,0:T(8,128)S(1)}, u32[]{:S(2)}, u32[]{:S(2)}) collective-permute-start(f32[32,128]{1,0:T(8,128)S(1)} %shard_map.90.proj), channel_id=1, source_target_pairs={{0,2},{2,0},{4,6},{6,4},{8,10},{10,8},{12,14},{14,12},{1,3},{3,1},... | collective-permute-start | bytes 49160 | tf_op jit(solution)/shard_map/ppermute | solution.py:245
  31.6 2.3 %shard_map.89 = (f32[64,64]{1,0:T(8,128)}, f32[64,64]{1,0:T(8,128)S(1)}) custom-call(f32[64,128]{1,0:T(8,128)S(1)} %add.11.sums), custom_call_target="tpu_custom_call" | custom-call | tf_op jit(solution)/shard_map/pallas_call | solution.py:234
  34.0 0.0 collective-permute-done.7.proj_other
  34.0 0.0 collective-permute-done.3.behind_x
  34.0 1.9 %shard_map.91 = (f32[768,128]{1,0:T(8,128)}, f32[768,128]{1,0:T(8,128)}, f32[64,64]{1,0:T(8,128)}) custom-call(s32[1]{0:T(128)S(6)} %sub.3.has_last, f32[256,128]{1,0:T(8,128)S(1)} %get-tuple-element.15.field_x, f32[512,128]{1,0:T(8,128)S(1)} %get-tuple-element.16.field_yz, f32[256,128]{1,0:T(8,128)S(1)} %get-tuple-element.17.m_x, ...), custom_call_target="tpu_custom_call" | custom-call | tf_op jit(solution)/shard_map/pallas_call | solution.py:234
  (4 shorter events, 0.0 us)
Async XLA Ops:
  0.6 1.0 %copy-start = (f32[64,3,1,4,128]{4,3,2,1,0:T(4,128)S(1)}, f32[64,3,1,4,128]{4,3,2,1,0:T(4,128)}, u32[]{:S(2)}) copy-start(f32[64,3,1,4,128]{4,3,2,1,0:T(4,128)} %param.5) | copy-start | bytes 1179652
  2.2 1.8 %collective-permute-start.1 = (f32[160,128]{1,0:T(8,128)S(1)}, f32[160,128]{1,0:T(8,128)S(1)}, u32[]{:S(2)}, u32[]{:S(2)}) collective-permute-start(f32[160,128]{1,0:T(8,128)S(1)} %shard_map.85), channel_id=1, source_target_pairs={{0,1},{1,0},{2,3},{3,2},{4,5},{5,4},{6,7},{7,6},{8,9},{9,8},{10,11... | collective-permute-start | bytes 245768 | tf_op jit(solution)/shard_map/ppermute | solution.py:245
  2.7 11.7 %collective-permute-start = (f32[512,128]{1,0:T(8,128)S(1)}, f32[512,128]{1,0:T(8,128)S(1)}, u32[]{:S(2)}, u32[]{:S(2)}) collective-permute-start(f32[512,128]{1,0:T(8,128)S(1)} %get-tuple-element.16.field_yz), channel_id=1, source_target_pairs={{2,0},{4,2},{6,4},{8,6},{10,8},{12,10},{14,12},{3,1},{5,3},{7,5},{... | collective-permute-start | bytes 786440 | tf_op jit(solution)/shard_map/ppermute | solution.py:17
  4.0 10.4 %collective-permute-start.2 = (f32[32,128]{1,0:T(8,128)S(1)}, f32[32,128]{1,0:T(8,128)S(1)}, u32[]{:S(2)}, u32[]{:S(2)}) collective-permute-start(f32[32,128]{1,0:T(8,128)S(1)} %slice_add_fusion.gram), channel_id=1, source_target_pairs={{0,2},{2,0},{4,6},{6,4},{8,10},{10,8},{12,14},{14,12},{1,3},{3,1},... | collective-permute-start | bytes 49160 | tf_op jit(solution)/shard_map/ppermute | solution.py:245
  7.8 0.7 %copy-start.1 = (s32[1,4,128]{2,1,0:T(4,128)S(1)}, s32[1,4,128]{2,1,0:T(4,128)}, u32[]{:S(2)}) copy-start(s32[1,4,128]{2,1,0:T(4,128)} %param.6) | copy-start | bytes 6148
  7.8 0.7 %copy-start.2 = (f32[8]{0:T(128)S(1)}, f32[8]{0:T(128)}, u32[]{:S(2)}) copy-start(f32[8]{0:T(128)} %mu_table.1) | copy-start | bytes 100
  7.9 0.7 %copy-start.3 = (f32[8]{0:T(128)S(1)}, f32[8]{0:T(128)}, u32[]{:S(2)}) copy-start(f32[8]{0:T(128)} %eps_table.1) | copy-start | bytes 100
  15.3 18.7 %collective-permute-start.3 = (f32[512,128]{1,0:T(8,128)S(1)}, f32[512,128]{1,0:T(8,128)S(1)}, u32[]{:S(2)}, u32[]{:S(2)}) collective-permute-start(f32[512,128]{1,0:T(8,128)S(1)} %get-tuple-element.18.m_yz), channel_id=1, source_target_pairs={{0,2},{2,4},{4,6},{6,8},{8,10},{10,12},{12,14},{1,3},{3,5},{5,7},{... | collective-permute-start | bytes 786440 | tf_op jit(solution)/shard_map/ppermute | solution.py:17
  19.5 1.3 %collective-permute-start.4 = (f32[160,128]{1,0:T(8,128)S(1)}, f32[160,128]{1,0:T(8,128)S(1)}, u32[]{:S(2)}, u32[]{:S(2)}) collective-permute-start(f32[160,128]{1,0:T(8,128)S(1)} %get-tuple-element.19.edge), channel_id=1, source_target_pairs={{0,1},{1,0},{2,3},{3,2},{4,5},{5,4},{6,7},{7,6},{8,9},{9,8},{10,11... | collective-permute-start | bytes 245768 | tf_op jit(solution)/shard_map/ppermute | solution.py:245
  21.0 3.9 %collective-permute-start.5 = (f32[64,128]{1,0:T(8,128)S(1)}, f32[64,128]{1,0:T(8,128)S(1)}, u32[]{:S(2)}, u32[]{:S(2)}) collective-permute-start(f32[64,128]{1,0:T(8,128)S(1)} %shard_map.88), channel_id=1, source_target_pairs={{0,4},{2,6},{4,0},{6,2},{8,12},{10,14},{12,8},{14,10},{1,5},{3,7},... | collective-permute-start | bytes 98312 | tf_op jit(solution)/shard_map/ppermute | solution.py:245
  24.9 4.8 %collective-permute-start.6 = (f32[64,128]{1,0:T(8,128)S(1)}, f32[64,128]{1,0:T(8,128)S(1)}, u32[]{:S(2)}, u32[]{:S(2)}) collective-permute-start(f32[64,128]{1,0:T(8,128)S(1)} %add.10), channel_id=1, source_target_pairs={{0,8},{2,10},{4,12},{6,14},{8,0},{10,2},{12,4},{14,6},{1,9},{3,11}... | collective-permute-start | bytes 98312 | tf_op jit(solution)/shard_map/ppermute | solution.py:245
  29.8 4.2 %collective-permute-start.7 = (f32[32,128]{1,0:T(8,128)S(1)}, f32[32,128]{1,0:T(8,128)S(1)}, u32[]{:S(2)}, u32[]{:S(2)}) collective-permute-start(f32[32,128]{1,0:T(8,128)S(1)} %shard_map.90.proj), channel_id=1, source_target_pairs={{0,2},{2,0},{4,6},{6,4},{8,10},{10,8},{12,14},{14,12},{1,3},{3,1},... | collective-permute-start | bytes 49160 | tf_op jit(solution)/shard_map/ppermute | solution.py:245

commit v3 on v2

--- a/solution.py
+++ b/solution.py
@@ -84,12 +84,30 @@
     out[:half, :] = packed(inner(flat, flat))
 
 
+def behind_kernel(columns, cells, has_next, field_x, field_yz, ahead_y, material, out):
+    half = columns // 2
+    inside_next = has_next[0] > 0
+    mu = material[:cells, :]
+    for y in range(cells):
+        e_x = part(field_x, y, columns)
+        if y + 1 < cells:
+            e_x_up = part(field_x, y + 1, columns)
+        else:
+            e_x_up = jnp.where(inside_next, ahead_y[half : half + columns, :], 0.0)
+        e_y, e_z = part(field_yz, y, columns), part(field_yz, cells + y, columns)
+        mu_row = mu[y : y + 1, :]
+        out[y * columns : (y + 1) * columns, :] = mu_row * (forward_z(e_x) + e_z)
+        out[(cells + y) * columns : (cells + y + 1) * columns, :] = -mu_row * (e_y + (e_x_up - e_x))
+    out[2 * cells * columns :, :] = jnp.concatenate(
+        [mu, jnp.zeros((out.shape[0] - 2 * cells * columns - cells, mu.shape[1]), F32)], axis=0
+    )
+
+
 def curl_kernel(
-    columns, cells, has_next, field_x, field_yz, ahead_x, ahead_y, material, gram, gram_other,
-    out_x, out_yz, out_edge, out_gram,
+    columns, cells, has_next, field_x, field_yz, ahead_x, ahead_y, material, out_x,
+    out_yz, out_edge,
 ):
     half = columns // 2
-    out_gram[...] = gram[...] + gram_other[...]
     coupling = material[:cells, :]
     scaled_eps = -material[cells:, :]
     inside_next = has_next[0] > 0
@@ -121,6 +139,10 @@
         left += [curl_x, curl_y, curl_z, e_x, e_y, e_z]
         right += [m_x, m_y, m_z, eps * e_x, eps * e_y, eps * e_z]
     out_edge[:half, :] = packed(inner(wide(left), wide(right)))
+
+
+def add_kernel(left, right, out):
+    out[...] = left[...] + right[...]
 
 
 def join_kernel(gram, edge, edge_other, out):
@@ -198,8 +220,9 @@
         else:
             m_x_down = jnp.where(inside_last, behind_y[half : half + columns, :], 0.0)
             m_z_down = jnp.where(inside_last, behind_y[half + columns :, :], 0.0)
-        m_y_last = part(behind_x, y, columns)
-        m_z_last = part(behind_x, cells + y, columns)
+        mu_last = behind_x[2 * cells * columns + y : 2 * cells * columns + y + 1, :]
+        m_y_last = part(behind_x, y, columns) - mu_last * e[2]
+        m_z_last = part(behind_x, cells + y, columns) + mu_last * e[1]
         eps = scaled_eps[y : y + 1, :]
         image = [
             (m[2] - m_z_down) - backward_z(m[1]) - eps * e[0],
@@ -274,15 +297,23 @@
     ahead_y = swapped(gram_edge, "col", 1)
     gram = gram_edge[:half] + ahead_y[:half]
     gram_other = swapped(gram, "row", 1)
-    m_x, m_yz, proj_edge, gram = call(
+    (sent,) = call(
+        functools.partial(behind_kernel, columns, cells),
+        (has_next,),
+        (field_x, field_yz, ahead_y, material),
+        ((2 * cells * columns + -(-cells // 8) * 8, lanes),),
+        flops=0,
+    )
+    behind_x = shifted(sent, "row", 1)
+    m_x, m_yz, proj_edge = call(
         functools.partial(curl_kernel, columns, cells),
         (has_next,),
-        (field_x, field_yz, ahead_x, ahead_y, material, gram, gram_other),
-        (small, large, edge, pair),
-        flops=0,
-    )
+        (field_x, field_yz, ahead_x, ahead_y, material),
+        (small, large, edge),
+        flops=10**10,
+    )
+    (gram,) = call(add_kernel, (), (gram, gram_other), (pair,), flops=10**10)
     behind_y = swapped(proj_edge, "col", 1)
-    behind_x = shifted(m_yz, "row", 1)
     (sums,) = call(
         join_kernel, (), (gram, proj_edge, behind_y), ((columns, 2 * columns),), flops=0
     )

time: 36.1 us -> 32.4 us (0.90)
  waiting for transfers between devices: 10.8 us -> 8.4 us
  starting transfers between devices: 15.5 us -> 14.1 us
    ppermute x6, waiting for transfers between devices: 10.8 us -> 5.34 us  [swapped(): lax.ppermute(x, axis, [(i, i ^ step) for i in range(lax.axis_size(axis))])]
    ppermute x2, waiting for transfers between devices: 0.01 us -> 3.06 us  [shifted(): return lax.ppermute(x, axis, pairs)]
    ppermute x2, starting transfers between devices: 5.48 us -> 3.22 us  [shifted(): return lax.ppermute(x, axis, pairs)]
    ppermute x6, starting transfers between devices: 10.1 us -> 10.9 us  [swapped(): lax.ppermute(x, axis, [(i, i ^ step) for i in range(lax.axis_size(axis))])]
    pallas_call x8 -> x10, Pallas kernels: 6.5 us -> 6.62 us  [call(): pl.pallas_call(body, out_shape=shapes, in_specs=[SMEM] * len(scalars) + [...]
  transfers between devices with their start and end apart: 8 -> 8, of which waited for: 4 -> 4; matrix products, arithmetic and copies ran while one was open for 0% -> 0% of each run, Pallas kernels for 9% -> 13%
where the time goes in v3:
time: 32.4 us; the launch traced here: 32.2 us
  starting transfers between devices  14.1 us (44%)
  waiting for transfers between devices  8.4 us (26%)
  Pallas kernels  6.62 us (20%)
  local copies, waits for them, and re-layouts  1.65 us (5%)
  between operations  1.4 us (4%)
    ppermute x6, starting transfers between devices, swapped(): lax.ppermute(x, axis, [(i, i ^ step) for i in range(lax.axis_size(axis))])  10.9 us
    pallas_call x10, Pallas kernels, call(): pl.pallas_call(body, out_shape=shapes, in_specs=[SMEM] * len(scalars) + [...  6.62 us
    ppermute x6, waiting for transfers between devices, swapped(): lax.ppermute(x, axis, [(i, i ^ step) for i in range(lax.axis_size(axis))])  5.34 us
    ppermute x2, starting transfers between devices, shifted(): return lax.ppermute(x, axis, pairs)  3.22 us
    ppermute x2, waiting for transfers between devices, shifted(): return lax.ppermute(x, axis, pairs)  3.06 us
    unnamed x8, local copies, waits for them, and re-layouts  1.65 us
  transfers between devices with their start and end apart: 8, of which 4 were waited for; matrix products, arithmetic and copies ran while one was open for 0% of the time, Pallas kernels for 13%

profile of v3, /device:TPU:0, one launch (start us, length us, event | category | flops | bytes accessed | tf_op | source)
XLA Modules:
  0.0 32.2 jit_solution(1995501418669676327)
XLA Ops:
  0.6 0.0 copy-start
  0.6 1.0 %copy-done = f32[64,3,1,4,128]{4,3,2,1,0:T(4,128)S(1)} copy-done((f32[64,3,1,4,128]{4,3,2,1,0:T(4,128)S(1)}, f32[64,3,1,4,128]{4,3,2,1,0:T(4,128)}, u32[]{:S(2)}) %copy-start) | copy-done | bytes 393240
  1.7 0.5 %shard_map.85 = f32[160,128]{1,0:T(8,128)S(1)} custom-call(f32[256,128]{1,0:T(8,128)S(1)} %get-tuple-element.14.field_x, f32[512,128]{1,0:T(8,128)S(1)} %get-tuple-element.15.field_yz), custom_call_target="tpu_custom_call" | custom-call | tf_op jit(solution)/shard_map/pallas_call | solution.py:257
  2.2 0.5 %collective-permute-start.1 = (f32[160,128]{1,0:T(8,128)S(1)}, f32[160,128]{1,0:T(8,128)S(1)}, u32[]{:S(2)}, u32[]{:S(2)}) collective-permute-start(f32[160,128]{1,0:T(8,128)S(1)} %shard_map.85), channel_id=1, source_target_pairs={{0,1},{1,0},{2,3},{3,2},{4,5},{5,4},{6,7},{7,6},{8,9},{9,8},{10,11... | collective-permute-start | bytes 245768 | tf_op jit(solution)/shard_map/ppermute | solution.py:268
  2.7 1.3 %collective-permute-start = (f32[512,128]{1,0:T(8,128)S(1)}, f32[512,128]{1,0:T(8,128)S(1)}, u32[]{:S(2)}, u32[]{:S(2)}) collective-permute-start(f32[512,128]{1,0:T(8,128)S(1)} %get-tuple-element.15.field_yz), channel_id=1, source_target_pairs={{2,0},{4,2},{6,4},{8,6},{10,8},{12,10},{14,12},{3,1},{5,3},{7,5},{... | collective-permute-start | bytes 786440 | tf_op jit(solution)/shard_map/ppermute | solution.py:17
  4.6 0.0 copy-start.1
  4.6 0.0 copy-start.2
  4.6 0.0 copy-start.3
  4.6 0.6 %copy-done.1 = s32[1,4,128]{2,1,0:T(4,128)S(1)} copy-done((s32[1,4,128]{2,1,0:T(4,128)S(1)}, s32[1,4,128]{2,1,0:T(4,128)}, u32[]{:S(2)}) %copy-start.1) | copy-done | bytes 2072
  5.3 0.0 copy-done.2
  5.3 0.0 copy-done.3
  5.3 0.6 %shard_map.86.material = f32[8,128]{1,0:T(8,128)S(1)} custom-call(f32[8]{0:T(128)S(1)} %copy-done.2, f32[8]{0:T(128)S(1)} %copy-done.3, f32[1]{0:T(128)S(6)} %copy.11.shift, s32[4,128]{1,0:T(4,128)S(1)} %bitcast.10), custom_call_target="tpu_custom_call" | custom-call | tf_op jit(solution)/shard_map/pallas_call | solution.py:257
  5.8 0.0 collective-permute-done.1.ahead_y
  5.9 3.2 %collective-permute-start.4 = (f32[32,128]{1,0:T(8,128)S(1)}, f32[32,128]{1,0:T(8,128)S(1)}, u32[]{:S(2)}, u32[]{:S(2)}) collective-permute-start(f32[32,128]{1,0:T(8,128)S(1)} %slice_add_fusion.left), channel_id=1, source_target_pairs={{0,2},{2,0},{4,6},{6,4},{8,10},{10,8},{12,14},{14,12},{1,3},{3,1},... | collective-permute-start | bytes 49160 | tf_op jit(solution)/shard_map/ppermute | solution.py:268
  9.1 0.1 shard_map.88
  9.2 1.9 %collective-permute-start.2 = (f32[520,128]{1,0:T(8,128)S(1)}, f32[520,128]{1,0:T(8,128)S(1)}, u32[]{:S(2)}, u32[]{:S(2)}) collective-permute-start(f32[520,128]{1,0:T(8,128)S(1)} %shard_map.88), channel_id=1, source_target_pairs={{0,2},{2,4},{4,6},{6,8},{8,10},{10,12},{12,14},{1,3},{3,5},{5,7},{... | collective-permute-start | bytes 798728 | tf_op jit(solution)/shard_map/ppermute | solution.py:17
  11.1 3.1 %collective-permute-done.ahead_x = f32[512,128]{1,0:T(8,128)S(1)} collective-permute-done((f32[512,128]{1,0:T(8,128)S(1)}, f32[512,128]{1,0:T(8,128)S(1)}, u32[]{:S(2)}, u32[]{:S(2)}) %collective-permute-start) | collective-permute-done | bytes 262176 | tf_op jit(solution)/shard_map/ppermute | solution.py:17
  14.2 1.0 %shard_map.87 = (f32[256,128]{1,0:T(8,128)S(1)}, f32[512,128]{1,0:T(8,128)S(1)}, f32[160,128]{1,0:T(8,128)S(1)}) custom-call(s32[1]{0:T(128)} %bitcast.has_next, f32[256,128]{1,0:T(8,128)S(1)} %get-tuple-element.14.field_x, f32[512,128]{1,0:T(8,128)S(1)} %get-tuple-element.15.field_yz, f32[512,128]{1,0:T(8,128)S(1)} %collective-permute-done.ahead_x, ...), custom_call_target="tpu_custom_call" | custom-call | flops 10000000000 | tf_op jit(solution)/shard_map/pallas_call | solution.py:257
  15.2 0.0 collective-permute-start.3
  15.2 0.0 collective-permute-done.4.right
  15.2 1.2 %collective-permute-done.3.edge_other.behind_y = f32[160,128]{1,0:T(8,128)S(1)} collective-permute-done((f32[160,128]{1,0:T(8,128)S(1)}, f32[160,128]{1,0:T(8,128)S(1)}, u32[]{:S(2)}, u32[]{:S(2)}) %collective-permute-start.3) | collective-permute-done | bytes 81952 | tf_op jit(solution)/shard_map/ppermute | solution.py:268
  16.4 0.1 shard_map.90
  16.6 1.8 %collective-permute-start.5 = (f32[64,128]{1,0:T(8,128)S(1)}, f32[64,128]{1,0:T(8,128)S(1)}, u32[]{:S(2)}, u32[]{:S(2)}) collective-permute-start(f32[64,128]{1,0:T(8,128)S(1)} %shard_map.90), channel_id=1, source_target_pairs={{0,4},{2,6},{4,0},{6,2},{8,12},{10,14},{12,8},{14,10},{1,5},{3,7},... | collective-permute-start | bytes 98312 | tf_op jit(solution)/shard_map/ppermute | solution.py:268
  18.4 2.1 %collective-permute-done.5 = f32[64,128]{1,0:T(8,128)S(1)} collective-permute-done((f32[64,128]{1,0:T(8,128)S(1)}, f32[64,128]{1,0:T(8,128)S(1)}, u32[]{:S(2)}, u32[]{:S(2)}) %collective-permute-start.5) | collective-permute-done | bytes 32800 | tf_op jit(solution)/shard_map/ppermute | solution.py:268
  20.5 2.8 %collective-permute-start.6 = (f32[64,128]{1,0:T(8,128)S(1)}, f32[64,128]{1,0:T(8,128)S(1)}, u32[]{:S(2)}, u32[]{:S(2)}) collective-permute-start(f32[64,128]{1,0:T(8,128)S(1)} %add.10), channel_id=1, source_target_pairs={{0,8},{2,10},{4,12},{6,14},{8,0},{10,2},{12,4},{14,6},{1,9},{3,11}... | collective-permute-start | bytes 98312 | tf_op jit(solution)/shard_map/ppermute | solution.py:268
  23.3 2.0 %collective-permute-done.6 = f32[64,128]{1,0:T(8,128)S(1)} collective-permute-done((f32[64,128]{1,0:T(8,128)S(1)}, f32[64,128]{1,0:T(8,128)S(1)}, u32[]{:S(2)}, u32[]{:S(2)}) %collective-permute-start.6) | collective-permute-done | bytes 32800 | tf_op jit(solution)/shard_map/ppermute | solution.py:268
  25.3 0.1 shard_map.92.proj
  25.4 2.6 %collective-permute-start.7 = (f32[32,128]{1,0:T(8,128)S(1)}, f32[32,128]{1,0:T(8,128)S(1)}, u32[]{:S(2)}, u32[]{:S(2)}) collective-permute-start(f32[32,128]{1,0:T(8,128)S(1)} %shard_map.92.proj), channel_id=1, source_target_pairs={{0,2},{2,0},{4,6},{6,4},{8,10},{10,8},{12,14},{14,12},{1,3},{3,1},... | collective-permute-start | bytes 49160 | tf_op jit(solution)/shard_map/ppermute | solution.py:268
  28.0 2.3 %shard_map.91 = (f32[64,64]{1,0:T(8,128)}, f32[64,64]{1,0:T(8,128)S(1)}) custom-call(f32[64,128]{1,0:T(8,128)S(1)} %add.11.sums), custom_call_target="tpu_custom_call" | custom-call | tf_op jit(solution)/shard_map/pallas_call | solution.py:257
  30.3 0.0 collective-permute-done.2.behind_x
  30.3 0.0 collective-permute-done.7.proj_other
  30.3 1.9 %shard_map.93 = (f32[768,128]{1,0:T(8,128)}, f32[768,128]{1,0:T(8,128)}, f32[64,64]{1,0:T(8,128)}) custom-call(s32[1]{0:T(128)S(6)} %sub.3.has_last, f32[256,128]{1,0:T(8,128)S(1)} %get-tuple-element.14.field_x, f32[512,128]{1,0:T(8,128)S(1)} %get-tuple-element.15.field_yz, f32[256,128]{1,0:T(8,128)S(1)} %get-tuple-element.16.m_x, ...), custom_call_target="tpu_custom_call" | custom-call | tf_op jit(solution)/shard_map/pallas_call | solution.py:257
  (5 shorter events, 0.0 us)
Async XLA Ops:
  0.6 1.0 %copy-start = (f32[64,3,1,4,128]{4,3,2,1,0:T(4,128)S(1)}, f32[64,3,1,4,128]{4,3,2,1,0:T(4,128)}, u32[]{:S(2)}) copy-start(f32[64,3,1,4,128]{4,3,2,1,0:T(4,128)} %param.5) | copy-start | bytes 1179652
  2.2 3.7 %collective-permute-start.1 = (f32[160,128]{1,0:T(8,128)S(1)}, f32[160,128]{1,0:T(8,128)S(1)}, u32[]{:S(2)}, u32[]{:S(2)}) collective-permute-start(f32[160,128]{1,0:T(8,128)S(1)} %shard_map.85), channel_id=1, source_target_pairs={{0,1},{1,0},{2,3},{3,2},{4,5},{5,4},{6,7},{7,6},{8,9},{9,8},{10,11... | collective-permute-start | bytes 245768 | tf_op jit(solution)/shard_map/ppermute | solution.py:268
  2.7 11.5 %collective-permute-start = (f32[512,128]{1,0:T(8,128)S(1)}, f32[512,128]{1,0:T(8,128)S(1)}, u32[]{:S(2)}, u32[]{:S(2)}) collective-permute-start(f32[512,128]{1,0:T(8,128)S(1)} %get-tuple-element.15.field_yz), channel_id=1, source_target_pairs={{2,0},{4,2},{6,4},{8,6},{10,8},{12,10},{14,12},{3,1},{5,3},{7,5},{... | collective-permute-start | bytes 786440 | tf_op jit(solution)/shard_map/ppermute | solution.py:17
  4.6 0.7 %copy-start.1 = (s32[1,4,128]{2,1,0:T(4,128)S(1)}, s32[1,4,128]{2,1,0:T(4,128)}, u32[]{:S(2)}) copy-start(s32[1,4,128]{2,1,0:T(4,128)} %param.6) | copy-start | bytes 6148
  4.6 0.7 %copy-start.2 = (f32[8]{0:T(128)S(1)}, f32[8]{0:T(128)}, u32[]{:S(2)}) copy-start(f32[8]{0:T(128)} %mu_table.1) | copy-start | bytes 100
  4.6 0.7 %copy-start.3 = (f32[8]{0:T(128)S(1)}, f32[8]{0:T(128)}, u32[]{:S(2)}) copy-start(f32[8]{0:T(128)} %eps_table.1) | copy-start | bytes 100
  5.9 9.3 %collective-permute-start.4 = (f32[32,128]{1,0:T(8,128)S(1)}, f32[32,128]{1,0:T(8,128)S(1)}, u32[]{:S(2)}, u32[]{:S(2)}) collective-permute-start(f32[32,128]{1,0:T(8,128)S(1)} %slice_add_fusion.left), channel_id=1, source_target_pairs={{0,2},{2,0},{4,6},{6,4},{8,10},{10,8},{12,14},{14,12},{1,3},{3,1},... | collective-permute-start | bytes 49160 | tf_op jit(solution)/shard_map/ppermute | solution.py:268
  9.2 21.1 %collective-permute-start.2 = (f32[520,128]{1,0:T(8,128)S(1)}, f32[520,128]{1,0:T(8,128)S(1)}, u32[]{:S(2)}, u32[]{:S(2)}) collective-permute-start(f32[520,128]{1,0:T(8,128)S(1)} %shard_map.88), channel_id=1, source_target_pairs={{0,2},{2,4},{4,6},{6,8},{8,10},{10,12},{12,14},{1,3},{3,5},{5,7},{... | collective-permute-start | bytes 798728 | tf_op jit(solution)/shard_map/ppermute | solution.py:17
  15.2 1.3 %collective-permute-start.3 = (f32[160,128]{1,0:T(8,128)S(1)}, f32[160,128]{1,0:T(8,128)S(1)}, u32[]{:S(2)}, u32[]{:S(2)}) collective-permute-start(f32[160,128]{1,0:T(8,128)S(1)} %get-tuple-element.18.edge), channel_id=1, source_target_pairs={{0,1},{1,0},{2,3},{3,2},{4,5},{5,4},{6,7},{7,6},{8,9},{9,8},{10,11... | collective-permute-start | bytes 245768 | tf_op jit(solution)/shard_map/ppermute | solution.py:268
  16.6 3.9 %collective-permute-start.5 = (f32[64,128]{1,0:T(8,128)S(1)}, f32[64,128]{1,0:T(8,128)S(1)}, u32[]{:S(2)}, u32[]{:S(2)}) collective-permute-start(f32[64,128]{1,0:T(8,128)S(1)} %shard_map.90), channel_id=1, source_target_pairs={{0,4},{2,6},{4,0},{6,2},{8,12},{10,14},{12,8},{14,10},{1,5},{3,7},... | collective-permute-start | bytes 98312 | tf_op jit(solution)/shard_map/ppermute | solution.py:268
  20.5 4.8 %collective-permute-start.6 = (f32[64,128]{1,0:T(8,128)S(1)}, f32[64,128]{1,0:T(8,128)S(1)}, u32[]{:S(2)}, u32[]{:S(2)}) collective-permute-start(f32[64,128]{1,0:T(8,128)S(1)} %add.10), channel_id=1, source_target_pairs={{0,8},{2,10},{4,12},{6,14},{8,0},{10,2},{12,4},{14,6},{1,9},{3,11}... | collective-permute-start | bytes 98312 | tf_op jit(solution)/shard_map/ppermute | solution.py:268
  25.4 4.9 %collective-permute-start.7 = (f32[32,128]{1,0:T(8,128)S(1)}, f32[32,128]{1,0:T(8,128)S(1)}, u32[]{:S(2)}, u32[]{:S(2)}) collective-permute-start(f32[32,128]{1,0:T(8,128)S(1)} %shard_map.92.proj), channel_id=1, source_target_pairs={{0,2},{2,0},{4,6},{6,4},{8,10},{10,8},{12,14},{14,12},{1,3},{3,1},... | collective-permute-start | bytes 49160 | tf_op jit(solution)/shard_map/ppermute | solution.py:268

commit v4 on v3

--- a/solution.py
+++ b/solution.py
@@ -84,8 +84,11 @@
     out[:half, :] = packed(inner(flat, flat))
 
 
-def behind_kernel(columns, cells, has_next, field_x, field_yz, ahead_y, material, out):
-    half = columns // 2
+def behind_kernel(
+    columns, cells, has_next, field_x, field_yz, gram_edge, ahead_y, material, out, out_gram
+):
+    half = columns // 2
+    out_gram[...] = gram_edge[:half, :] + ahead_y[:half, :]
     inside_next = has_next[0] > 0
     mu = material[:cells, :]
     for y in range(cells):
@@ -103,42 +106,54 @@
     )
 
 
-def curl_kernel(
-    columns, cells, has_next, field_x, field_yz, ahead_x, ahead_y, material, out_x,
-    out_yz, out_edge,
-):
-    half = columns // 2
-    coupling = material[:cells, :]
-    scaled_eps = -material[cells:, :]
+def near_kernel(columns, cells, has_next, field_x, field_yz, ahead_y, material, out_x, out_proj):
+    half = columns // 2
     inside_next = has_next[0] > 0
     left, right = [], []
     for y in range(cells):
         e_x = part(field_x, y, columns)
         e_y = part(field_yz, y, columns)
         e_z = part(field_yz, cells + y, columns)
-        inside = y + 1 < cells
-        if inside:
-            e_x_up, e_z_up = part(field_x, y + 1, columns), part(field_yz, cells + y + 1, columns)
+        if y + 1 < cells:
+            e_z_up = part(field_yz, cells + y + 1, columns)
+        else:
+            e_z_up = jnp.where(inside_next, ahead_y[half + columns :, :], 0.0)
+        curl_x = (e_z_up - e_z) - forward_z(e_y)
+        m_x = material[y : y + 1, :] * curl_x
+        eps = -material[cells + y : cells + y + 1, :]
+        out_x[y * columns : (y + 1) * columns, :] = m_x
+        left += [curl_x, e_x, e_y, e_z]
+        right += [m_x, eps * e_x, eps * e_y, eps * e_z]
+    out_proj[...] = packed(inner(wide(left), wide(right)))
+
+
+def curl_kernel(
+    columns, cells, has_next, field_x, field_yz, ahead_x, ahead_y, material, m_x, near, out_yz,
+    out_edge,
+):
+    half = columns // 2
+    inside_next = has_next[0] > 0
+    left, right = [], []
+    for y in range(cells):
+        e_x = part(field_x, y, columns)
+        e_y = part(field_yz, y, columns)
+        e_z = part(field_yz, cells + y, columns)
+        if y + 1 < cells:
+            e_x_up = part(field_x, y + 1, columns)
         else:
             e_x_up = jnp.where(inside_next, ahead_y[half : half + columns, :], 0.0)
-            e_z_up = jnp.where(inside_next, ahead_y[half + columns :, :], 0.0)
-        e_y_next = part(ahead_x, y, columns)
-        e_z_next = part(ahead_x, cells + y, columns)
-        curl_x = (e_z_up - e_z) - forward_z(e_y)
-        curl_y = forward_z(e_x) - (e_z_next - e_z)
-        curl_z = (e_y_next - e_y) - (e_x_up - e_x)
-        mu = coupling[y : y + 1, :]
-        eps = scaled_eps[y : y + 1, :]
-        m_x, m_y, m_z = mu * curl_x, mu * curl_y, mu * curl_z
-        out_x[y * columns : (y + 1) * columns, :] = m_x
+        curl_y = forward_z(e_x) - (part(ahead_x, cells + y, columns) - e_z)
+        curl_z = (part(ahead_x, y, columns) - e_y) - (e_x_up - e_x)
+        mu = material[y : y + 1, :]
+        m_y, m_z = mu * curl_y, mu * curl_z
         out_yz[y * columns : (y + 1) * columns, :] = m_y
         out_yz[(cells + y) * columns : (cells + y + 1) * columns, :] = m_z
-        if not inside:
-            out_edge[half : half + columns, :] = m_x
+        if y + 1 == cells:
             out_edge[half + columns :, :] = m_z
-        left += [curl_x, curl_y, curl_z, e_x, e_y, e_z]
-        right += [m_x, m_y, m_z, eps * e_x, eps * e_y, eps * e_z]
-    out_edge[:half, :] = packed(inner(wide(left), wide(right)))
+        left += [curl_y, curl_z]
+        right += [m_y, m_z]
+    out_edge[half : half + columns, :] = part(m_x, cells - 1, columns)
+    out_edge[:half, :] = near[...] + packed(inner(wide(left), wide(right)))
 
 
 def add_kernel(left, right, out):
@@ -154,7 +169,7 @@
 
 def factor(gram):
     columns = gram.shape[0]
-    span, tile = 2 * columns, 8
+    span, tile, width = 2 * columns, 8, 16
     count = columns // tile
     spread = lambda values: jnp.broadcast_to(values, (tile, span))
     sublane = lax.broadcasted_iota(jnp.int32, (tile, span), 0)
@@ -165,45 +180,47 @@
         rows = jnp.concatenate([rows, jnp.zeros_like(rows)], axis=1)
         blocks.append(jnp.where(lane == sublane + b * tile + columns, 1.0, rows))
     scales = [None] * count
-    for first in range(count):
+    for start in range(0, columns, width):
+        top = start // tile
         panel = [
-            [spread(rows[:, first * tile + k : first * tile + k + 1]) for rows in blocks[first:]]
-            for k in range(tile)
+            {b: spread(blocks[b][:, start + k : start + k + 1]) for b in range(top, count)}
+            for k in range(width)
         ]
-        for k in range(tile):
-            pivot = spread(panel[k][0][k : k + 1, :])
+        for k in range(width):
+            at, row = divmod(start + k, tile)
+            pivot = spread(panel[k][at][row : row + 1, :])
             inverse = 1.0 / pivot
-            ratio = [rows * inverse for rows in panel[k]]
-            ratio[0] = jnp.where(sublane > k, ratio[0], 0.0)
+            ratio = {b: panel[k][b] * inverse for b in range(at, count)}
+            ratio[at] = jnp.where(sublane > row, ratio[at], 0.0)
             root = lax.rsqrt(pivot)
-            scales[first] = root if k == 0 else jnp.where(sublane == k, root, scales[first])
-            for later in range(k + 1, tile):
-                entry = spread(panel[k][0][later : later + 1, :])
-                panel[later] = [rows - f * entry for rows, f in zip(panel[later], ratio)]
-            pivot_row = spread(blocks[first][k : k + 1, :])
-            for b in range(first, count):
-                blocks[b] = blocks[b] - ratio[b - first] * pivot_row
+            scales[at] = root if row == 0 else jnp.where(sublane == row, root, scales[at])
+            for later in range(k + 1, width):
+                to, below = divmod(start + later, tile)
+                entry = spread(panel[k][to][below : below + 1, :])
+                for b in range(at, count):
+                    panel[later][b] = panel[later][b] - ratio[b] * entry
+            pivot_row = spread(blocks[at][row : row + 1, :])
+            for b in range(at, count):
+                blocks[b] = blocks[b] - ratio[b] * pivot_row
     kept = []
     for b in range(count):
         row = sublane + b * tile
         kept.append(jnp.where((lane >= row) & (lane <= row + columns), blocks[b] * scales[b], 0.0))
-    both = jnp.concatenate(kept, axis=0)
-    return both[:, :columns], both[:, columns:]
-
-
-def factor_kernel(total, sums, out_upper, out_inverse):
+    return jnp.concatenate(kept, axis=0)
+
+
+def factor_kernel(total, sums, out):
     columns = sums.shape[0]
-    upper, inverse = factor(sums[:, :columns] / total)
-    out_upper[...] = upper
-    out_inverse[...] = inverse
+    out[...] = factor(sums[:, :columns] / total)
 
 
 def finish_kernel(
     columns, cells, total, has_last, field_x, field_yz, m_x, m_yz, behind_x, behind_y, material,
-    inverse_ref, proj, proj_other, out_basis, out_image, out_proj,
+    factors, proj, proj_other, out_basis, out_image, out_proj, out_upper,
 ):
     half = columns // 2
-    inverse = inverse_ref[...]
+    inverse = factors[:, columns:]
+    out_upper[...] = factors[:, :columns]
     raw = unpacked(proj[...] + proj_other[...]) / total
     left = lax.dot_general(
         inverse, raw, (((1,), (0,)), ((), ())), precision=HIGHEST, preferred_element_type=F32
@@ -295,21 +312,27 @@
         functools.partial(gram_kernel, columns, cells), (), (field_x, field_yz), (edge,), flops=0
     )
     ahead_y = swapped(gram_edge, "col", 1)
-    gram = gram_edge[:half] + ahead_y[:half]
-    gram_other = swapped(gram, "row", 1)
-    (sent,) = call(
+    sent, gram = call(
         functools.partial(behind_kernel, columns, cells),
         (has_next,),
+        (field_x, field_yz, gram_edge, ahead_y, material),
+        ((2 * cells * columns + -(-cells // 8) * 8, lanes), pair),
+        flops=0,
+    )
+    gram_other = swapped(gram, "row", 1)
+    behind_x = shifted(sent, "row", 1)
+    m_x, near = call(
+        functools.partial(near_kernel, columns, cells),
+        (has_next,),
         (field_x, field_yz, ahead_y, material),
-        ((2 * cells * columns + -(-cells // 8) * 8, lanes),),
+        (small, pair),
         flops=0,
     )
-    behind_x = shifted(sent, "row", 1)
-    m_x, m_yz, proj_edge = call(
+    m_yz, proj_edge = call(
         functools.partial(curl_kernel, columns, cells),
         (has_next,),
-        (field_x, field_yz, ahead_x, ahead_y, material),
-        (small, large, edge),
+        (field_x, field_yz, ahead_x, ahead_y, material, m_x, near),
+        (large, edge),
         flops=10**10,
     )
     (gram,) = call(add_kernel, (), (gram, gram_other), (pair,), flops=10**10)
@@ -323,14 +346,14 @@
         step *= 2
     (proj,) = call(split_kernel, (), (sums,), (pair,), flops=0)
     proj_other = swapped(proj, "row", 1)
-    upper, inverse = call(
-        functools.partial(factor_kernel, total), (), (sums,), (square, square), flops=0
-    )
-    basis_out, image_out, projected = call(
+    (factors,) = call(
+        functools.partial(factor_kernel, total), (), (sums,), ((columns, 2 * columns),), flops=0
+    )
+    basis_out, image_out, projected, upper = call(
         functools.partial(finish_kernel, columns, cells, total),
         (has_last,),
-        (field_x, field_yz, m_x, m_yz, behind_x, behind_y, material, inverse, proj, proj_other),
-        (basis.shape, basis.shape, square),
+        (field_x, field_yz, m_x, m_yz, behind_x, behind_y, material, factors, proj, proj_other),
+        (basis.shape, basis.shape, square, square),
         flops=0,
     )
     return (

time: 32.4 us -> 30.1 us (0.929)
  waiting for transfers between devices: 8.4 us -> 6.49 us
  Pallas kernels: 6.62 us -> 5.95 us
    ppermute x2, waiting for transfers between devices: 3.06 us -> 1.14 us  [shifted(): return lax.ppermute(x, axis, pairs)]
    pallas_call x10 -> x11, Pallas kernels: 6.62 us -> 5.95 us  [call(): pl.pallas_call(body, out_shape=shapes, in_specs=[SMEM] * len(scalars) + [...]
  transfers between devices with their start and end apart: 8 -> 8, of which waited for: 4 -> 5; matrix products, arithmetic and copies ran while one was open for 0% -> 0% of each run, Pallas kernels for 13% -> 14%
where the time goes in v4:
time: 30.1 us; the launch traced here: 29.9 us
  starting transfers between devices  14.4 us (48%)
  waiting for transfers between devices  6.49 us (22%)
  Pallas kernels  5.95 us (20%)
  local copies, waits for them, and re-layouts  1.65 us (5%)
  between operations  1.41 us (5%)
    ppermute x6, starting transfers between devices, swapped(): lax.ppermute(x, axis, [(i, i ^ step) for i in range(lax.axis_size(axis))])  11.2 us
    pallas_call x11, Pallas kernels, call(): pl.pallas_call(body, out_shape=shapes, in_specs=[SMEM] * len(scalars) + [...  5.95 us
    ppermute x6, waiting for transfers between devices, swapped(): lax.ppermute(x, axis, [(i, i ^ step) for i in range(lax.axis_size(axis))])  5.35 us
    ppermute x2, starting transfers between devices, shifted(): return lax.ppermute(x, axis, pairs)  3.23 us
    unnamed x8, local copies, waits for them, and re-layouts  1.65 us
    ppermute x2, waiting for transfers between devices, shifted(): return lax.ppermute(x, axis, pairs)  1.14 us
  transfers between devices with their start and end apart: 8, of which 5 were waited for; matrix products, arithmetic and copies ran while one was open for 0% of the time, Pallas kernels for 14%

profile of v4, /device:TPU:0, one launch (start us, length us, event | category | flops | bytes accessed | tf_op | source)
XLA Modules:
  0.0 29.9 jit_solution(198978819997628704)
XLA Ops:
  0.6 0.0 copy-start
  0.6 1.0 %copy-done = f32[64,3,1,4,128]{4,3,2,1,0:T(4,128)S(1)} copy-done((f32[64,3,1,4,128]{4,3,2,1,0:T(4,128)S(1)}, f32[64,3,1,4,128]{4,3,2,1,0:T(4,128)}, u32[]{:S(2)}) %copy-start) | copy-done | bytes 393240
  1.7 1.3 %collective-permute-start.1 = (f32[512,128]{1,0:T(8,128)S(1)}, f32[512,128]{1,0:T(8,128)S(1)}, u32[]{:S(2)}, u32[]{:S(2)}) collective-permute-start(f32[512,128]{1,0:T(8,128)S(1)} %get-tuple-element.17.field_yz), channel_id=1, source_target_pairs={{2,0},{4,2},{6,4},{8,6},{10,8},{12,10},{14,12},{3,1},{5,3},{7,5},{... | collective-permute-start | bytes 786440 | tf_op jit(solution)/shard_map/ppermute | solution.py:17
  3.0 0.5 %shard_map.85.gram_edge = f32[160,128]{1,0:T(8,128)S(1)} custom-call(f32[256,128]{1,0:T(8,128)S(1)} %get-tuple-element.16.field_x, f32[512,128]{1,0:T(8,128)S(1)} %get-tuple-element.17.field_yz), custom_call_target="tpu_custom_call" | custom-call | tf_op jit(solution)/shard_map/pallas_call | solution.py:274
  3.5 0.5 %collective-permute-start = (f32[160,128]{1,0:T(8,128)S(1)}, f32[160,128]{1,0:T(8,128)S(1)}, u32[]{:S(2)}, u32[]{:S(2)}) collective-permute-start(f32[160,128]{1,0:T(8,128)S(1)} %shard_map.85.gram_edge), channel_id=1, source_target_pairs={{0,1},{1,0},{2,3},{3,2},{4,5},{5,4},{6,7},{7,6},{8,9},{9,8},{10,11... | collective-permute-start | bytes 245768 | tf_op jit(solution)/shard_map/ppermute | solution.py:285
  4.6 0.0 copy-start.1
  4.6 0.0 copy-start.2
  4.6 0.0 copy-start.3
  4.6 0.6 %copy-done.1 = s32[1,4,128]{2,1,0:T(4,128)S(1)} copy-done((s32[1,4,128]{2,1,0:T(4,128)S(1)}, s32[1,4,128]{2,1,0:T(4,128)}, u32[]{:S(2)}) %copy-start.1) | copy-done | bytes 2072
  5.3 0.0 copy-done.2
  5.3 0.0 copy-done.3
  5.3 0.6 %shard_map.86.material = f32[8,128]{1,0:T(8,128)S(1)} custom-call(f32[8]{0:T(128)S(1)} %copy-done.2, f32[8]{0:T(128)S(1)} %copy-done.3, f32[1]{0:T(128)S(6)} %copy.11.shift, s32[4,128]{1,0:T(4,128)S(1)} %bitcast.10), custom_call_target="tpu_custom_call" | custom-call | tf_op jit(solution)/shard_map/pallas_call | solution.py:274
  5.9 0.0 collective-permute-done.ahead_y
  5.9 0.1 shard_map.89
  6.0 3.2 %collective-permute-start.4 = (f32[32,128]{1,0:T(8,128)S(1)}, f32[32,128]{1,0:T(8,128)S(1)}, u32[]{:S(2)}, u32[]{:S(2)}) collective-permute-start(f32[32,128]{1,0:T(8,128)S(1)} %get-tuple-element.23.left), channel_id=1, source_target_pairs={{0,2},{2,0},{4,6},{6,4},{8,10},{10,8},{12,14},{14,12},{1,3},{3,1},... | collective-permute-start | bytes 49160 | tf_op jit(solution)/shard_map/ppermute | solution.py:285
  9.2 1.9 %collective-permute-start.2 = (f32[520,128]{1,0:T(8,128)S(1)}, f32[520,128]{1,0:T(8,128)S(1)}, u32[]{:S(2)}, u32[]{:S(2)}) collective-permute-start(f32[520,128]{1,0:T(8,128)S(1)} %get-tuple-element.21), channel_id=1, source_target_pairs={{0,2},{2,4},{4,6},{6,8},{8,10},{10,12},{12,14},{1,3},{3,5},{5,7},{... | collective-permute-start | bytes 798728 | tf_op jit(solution)/shard_map/ppermute | solution.py:17
  11.1 0.7 %shard_map.87 = (f32[256,128]{1,0:T(8,128)S(1)}, f32[32,128]{1,0:T(8,128)S(1)}) custom-call(s32[1]{0:T(128)} %bitcast.has_next, f32[256,128]{1,0:T(8,128)S(1)} %get-tuple-element.16.field_x, f32[512,128]{1,0:T(8,128)S(1)} %get-tuple-element.17.field_yz, f32[160,128]{1,0:T(8,128)S(1)} %collective-permute-done.ahead_y, f32[8,128]{1,0:T(8,128)S(1)} %shard_map.86.material), custom_call_target="tpu_custom_call" | custom-call | tf_op jit(solution)/shard_map/pallas_call | solution.py:274
  11.8 1.1 %collective-permute-done.1.ahead_x = f32[512,128]{1,0:T(8,128)S(1)} collective-permute-done((f32[512,128]{1,0:T(8,128)S(1)}, f32[512,128]{1,0:T(8,128)S(1)}, u32[]{:S(2)}, u32[]{:S(2)}) %collective-permute-start.1) | collective-permute-done | bytes 262176 | tf_op jit(solution)/shard_map/ppermute | solution.py:17
  13.0 0.5 %shard_map.88 = (f32[512,128]{1,0:T(8,128)S(1)}, f32[160,128]{1,0:T(8,128)S(1)}) custom-call(s32[1]{0:T(128)} %bitcast.has_next, f32[256,128]{1,0:T(8,128)S(1)} %get-tuple-element.16.field_x, f32[512,128]{1,0:T(8,128)S(1)} %get-tuple-element.17.field_yz, f32[512,128]{1,0:T(8,128)S(1)} %collective-permute-done.1.ahead_x, ...), custom_call_target="tpu_custom_call" | custom-call | flops 10000000000 | tf_op jit(solution)/shard_map/pallas_call | solution.py:274
  13.5 0.0 collective-permute-start.3
  13.5 0.0 collective-permute-done.4.right
  13.5 1.2 %collective-permute-done.3.edge_other.behind_y = f32[160,128]{1,0:T(8,128)S(1)} collective-permute-done((f32[160,128]{1,0:T(8,128)S(1)}, f32[160,128]{1,0:T(8,128)S(1)}, u32[]{:S(2)}, u32[]{:S(2)}) %collective-permute-start.3) | collective-permute-done | bytes 81952 | tf_op jit(solution)/shard_map/ppermute | solution.py:285
  14.8 0.1 shard_map.91
  14.9 2.3 %collective-permute-start.5 = (f32[64,128]{1,0:T(8,128)S(1)}, f32[64,128]{1,0:T(8,128)S(1)}, u32[]{:S(2)}, u32[]{:S(2)}) collective-permute-start(f32[64,128]{1,0:T(8,128)S(1)} %shard_map.91), channel_id=1, source_target_pairs={{0,4},{2,6},{4,0},{6,2},{8,12},{10,14},{12,8},{14,10},{1,5},{3,7},... | collective-permute-start | bytes 98312 | tf_op jit(solution)/shard_map/ppermute | solution.py:285
  17.2 1.9 %collective-permute-done.5 = f32[64,128]{1,0:T(8,128)S(1)} collective-permute-done((f32[64,128]{1,0:T(8,128)S(1)}, f32[64,128]{1,0:T(8,128)S(1)}, u32[]{:S(2)}, u32[]{:S(2)}) %collective-permute-start.5) | collective-permute-done | bytes 32800 | tf_op jit(solution)/shard_map/ppermute | solution.py:285
  19.1 3.0 %collective-permute-start.6 = (f32[64,128]{1,0:T(8,128)S(1)}, f32[64,128]{1,0:T(8,128)S(1)}, u32[]{:S(2)}, u32[]{:S(2)}) collective-permute-start(f32[64,128]{1,0:T(8,128)S(1)} %add.6), channel_id=1, source_target_pairs={{0,8},{2,10},{4,12},{6,14},{8,0},{10,2},{12,4},{14,6},{1,9},{3,11}... | collective-permute-start | bytes 98312 | tf_op jit(solution)/shard_map/ppermute | solution.py:285
  22.2 1.9 %collective-permute-done.6 = f32[64,128]{1,0:T(8,128)S(1)} collective-permute-done((f32[64,128]{1,0:T(8,128)S(1)}, f32[64,128]{1,0:T(8,128)S(1)}, u32[]{:S(2)}, u32[]{:S(2)}) %collective-permute-start.6) | collective-permute-done | bytes 32800 | tf_op jit(solution)/shard_map/ppermute | solution.py:285
  24.1 0.1 shard_map.93.proj
  24.2 2.2 %collective-permute-start.7 = (f32[32,128]{1,0:T(8,128)S(1)}, f32[32,128]{1,0:T(8,128)S(1)}, u32[]{:S(2)}, u32[]{:S(2)}) collective-permute-start(f32[32,128]{1,0:T(8,128)S(1)} %shard_map.93.proj), channel_id=1, source_target_pairs={{0,2},{2,0},{4,6},{6,4},{8,10},{10,8},{12,14},{14,12},{1,3},{3,1},... | collective-permute-start | bytes 49160 | tf_op jit(solution)/shard_map/ppermute | solution.py:285
  26.3 1.4 %shard_map.92.factors = f32[64,128]{1,0:T(8,128)S(1)} custom-call(f32[64,128]{1,0:T(8,128)S(1)} %add.7.sums), custom_call_target="tpu_custom_call" | custom-call | tf_op jit(solution)/shard_map/pallas_call | solution.py:274
  27.7 0.0 collective-permute-done.2.behind_x
  27.7 0.3 collective-permute-done.7.proj_other
  28.0 1.9 %shard_map.94 = (f32[768,128]{1,0:T(8,128)}, f32[768,128]{1,0:T(8,128)}, f32[64,64]{1,0:T(8,128)}, f32[64,64]{1,0:T(8,128)}) custom-call(s32[1]{0:T(128)S(6)} %sub.3.has_last, f32[256,128]{1,0:T(8,128)S(1)} %get-tuple-element.16.field_x, f32[512,128]{1,0:T(8,128)S(1)} %get-tuple-element.17.field_yz, f32[256,128]{1,0:T(8,128)S(1)} %get-tuple-element.18.m_x, ...), custom_call_target="tpu_custom_call" | custom-call | tf_op jit(solution)/shard_map/pallas_call | solution.py:274
  (4 shorter events, 0.0 us)
Async XLA Ops:
  0.6 1.0 %copy-start = (f32[64,3,1,4,128]{4,3,2,1,0:T(4,128)S(1)}, f32[64,3,1,4,128]{4,3,2,1,0:T(4,128)}, u32[]{:S(2)}) copy-start(f32[64,3,1,4,128]{4,3,2,1,0:T(4,128)} %param.5) | copy-start | bytes 1179652
  1.7 11.3 %collective-permute-start.1 = (f32[512,128]{1,0:T(8,128)S(1)}, f32[512,128]{1,0:T(8,128)S(1)}, u32[]{:S(2)}, u32[]{:S(2)}) collective-permute-start(f32[512,128]{1,0:T(8,128)S(1)} %get-tuple-element.17.field_yz), channel_id=1, source_target_pairs={{2,0},{4,2},{6,4},{8,6},{10,8},{12,10},{14,12},{3,1},{5,3},{7,5},{... | collective-permute-start | bytes 786440 | tf_op jit(solution)/shard_map/ppermute | solution.py:17
  3.5 2.4 %collective-permute-start = (f32[160,128]{1,0:T(8,128)S(1)}, f32[160,128]{1,0:T(8,128)S(1)}, u32[]{:S(2)}, u32[]{:S(2)}) collective-permute-start(f32[160,128]{1,0:T(8,128)S(1)} %shard_map.85.gram_edge), channel_id=1, source_target_pairs={{0,1},{1,0},{2,3},{3,2},{4,5},{5,4},{6,7},{7,6},{8,9},{9,8},{10,11... | collective-permute-start | bytes 245768 | tf_op jit(solution)/shard_map/ppermute | solution.py:285
  4.6 0.7 %copy-start.1 = (s32[1,4,128]{2,1,0:T(4,128)S(1)}, s32[1,4,128]{2,1,0:T(4,128)}, u32[]{:S(2)}) copy-start(s32[1,4,128]{2,1,0:T(4,128)} %param.6) | copy-start | bytes 6148
  4.6 0.7 %copy-start.2 = (f32[8]{0:T(128)S(1)}, f32[8]{0:T(128)}, u32[]{:S(2)}) copy-start(f32[8]{0:T(128)} %mu_table.1) | copy-start | bytes 100
  4.6 0.7 %copy-start.3 = (f32[8]{0:T(128)S(1)}, f32[8]{0:T(128)}, u32[]{:S(2)}) copy-start(f32[8]{0:T(128)} %eps_table.1) | copy-start | bytes 100
  6.0 7.5 %collective-permute-start.4 = (f32[32,128]{1,0:T(8,128)S(1)}, f32[32,128]{1,0:T(8,128)S(1)}, u32[]{:S(2)}, u32[]{:S(2)}) collective-permute-start(f32[32,128]{1,0:T(8,128)S(1)} %get-tuple-element.23.left), channel_id=1, source_target_pairs={{0,2},{2,0},{4,6},{6,4},{8,10},{10,8},{12,14},{14,12},{1,3},{3,1},... | collective-permute-start | bytes 49160 | tf_op jit(solution)/shard_map/ppermute | solution.py:285
  9.2 18.5 %collective-permute-start.2 = (f32[520,128]{1,0:T(8,128)S(1)}, f32[520,128]{1,0:T(8,128)S(1)}, u32[]{:S(2)}, u32[]{:S(2)}) collective-permute-start(f32[520,128]{1,0:T(8,128)S(1)} %get-tuple-element.21), channel_id=1, source_target_pairs={{0,2},{2,4},{4,6},{6,8},{8,10},{10,12},{12,14},{1,3},{3,5},{5,7},{... | collective-permute-start | bytes 798728 | tf_op jit(solution)/shard_map/ppermute | solution.py:17
  13.5 1.3 %collective-permute-start.3 = (f32[160,128]{1,0:T(8,128)S(1)}, f32[160,128]{1,0:T(8,128)S(1)}, u32[]{:S(2)}, u32[]{:S(2)}) collective-permute-start(f32[160,128]{1,0:T(8,128)S(1)} %get-tuple-element.22.edge), channel_id=1, source_target_pairs={{0,1},{1,0},{2,3},{3,2},{4,5},{5,4},{6,7},{7,6},{8,9},{9,8},{10,11... | collective-permute-start | bytes 245768 | tf_op jit(solution)/shard_map/ppermute | solution.py:285
  14.9 4.2 %collective-permute-start.5 = (f32[64,128]{1,0:T(8,128)S(1)}, f32[64,128]{1,0:T(8,128)S(1)}, u32[]{:S(2)}, u32[]{:S(2)}) collective-permute-start(f32[64,128]{1,0:T(8,128)S(1)} %shard_map.91), channel_id=1, source_target_pairs={{0,4},{2,6},{4,0},{6,2},{8,12},{10,14},{12,8},{14,10},{1,5},{3,7},... | collective-permute-start | bytes 98312 | tf_op jit(solution)/shard_map/ppermute | solution.py:285
  19.1 5.0 %collective-permute-start.6 = (f32[64,128]{1,0:T(8,128)S(1)}, f32[64,128]{1,0:T(8,128)S(1)}, u32[]{:S(2)}, u32[]{:S(2)}) collective-permute-start(f32[64,128]{1,0:T(8,128)S(1)} %add.6), channel_id=1, source_target_pairs={{0,8},{2,10},{4,12},{6,14},{8,0},{10,2},{12,4},{14,6},{1,9},{3,11}... | collective-permute-start | bytes 98312 | tf_op jit(solution)/shard_map/ppermute | solution.py:285
  24.2 3.9 %collective-permute-start.7 = (f32[32,128]{1,0:T(8,128)S(1)}, f32[32,128]{1,0:T(8,128)S(1)}, u32[]{:S(2)}, u32[]{:S(2)}) collective-permute-start(f32[32,128]{1,0:T(8,128)S(1)} %shard_map.93.proj), channel_id=1, source_target_pairs={{0,2},{2,0},{4,6},{6,4},{8,10},{10,8},{12,14},{14,12},{1,3},{3,1},... | collective-permute-start | bytes 49160 | tf_op jit(solution)/shard_map/ppermute | solution.py:285

commit v5 on v4

--- a/solution.py
+++ b/solution.py
@@ -8,7 +8,7 @@
 from jax.sharding import PartitionSpec as P
 
 F32 = jnp.float32
-HIGHEST = lax.Precision.HIGHEST
+BF16 = jnp.bfloat16
 
 
 def shifted(x, axis, by):
@@ -21,10 +21,33 @@
     return jnp.concatenate(chunks, axis=1)
 
 
+def three(values):
+    high = values.astype(BF16)
+    rest = values - high.astype(F32)
+    middle = rest.astype(BF16)
+    low = (rest - middle.astype(F32)).astype(BF16)
+    return [high, middle, low]
+
+
 def inner(left, right):
     return lax.dot_general(
-        left, right, (((1,), (1,)), ((), ())), precision=HIGHEST, preferred_element_type=F32
-    )
+        left, right, (((1,), (1,)), ((), ())), precision=lax.Precision.HIGHEST,
+        preferred_element_type=F32,
+    )
+
+
+def product(left, right):
+    rows = left.shape[0]
+    high, middle, low = three(left)
+    none = jnp.zeros_like(high)
+    stacked = jnp.concatenate(
+        [wide([high, high, high]), wide([middle, middle, none]), wide([low, none, none])], axis=0
+    )
+    blocks = lax.dot_general(
+        stacked, jnp.concatenate(three(right), axis=0), (((1,), (0,)), ((), ())),
+        preferred_element_type=F32,
+    )
+    return blocks[:rows, :] + (blocks[rows : 2 * rows, :] + blocks[2 * rows :, :])
 
 
 def table_rows(labels, table_ref):
@@ -214,21 +237,33 @@
     out[...] = factor(sums[:, :columns] / total)
 
 
-def finish_kernel(
+def basis_kernel(
     columns, cells, total, has_last, field_x, field_yz, m_x, m_yz, behind_x, behind_y, material,
-    factors, proj, proj_other, out_basis, out_image, out_proj, out_upper,
+    factors, proj, proj_other, out_basis, out_image, out_upper, out_proj, basis, image, upper,
+    projected, sems,
 ):
     half = columns // 2
+    stride = 3 * cells
     inverse = factors[:, columns:]
-    out_upper[...] = factors[:, :columns]
-    raw = unpacked(proj[...] + proj_other[...]) / total
-    left = lax.dot_general(
-        inverse, raw, (((1,), (0,)), ((), ())), precision=HIGHEST, preferred_element_type=F32
-    )
-    out_proj[...] = inner(left, inverse)
+    upper[...] = factors[:, :columns]
+    third = pltpu.make_async_copy(upper, out_upper, sems.at[2])
+    third.start()
+
+    def write(chunks, places, held, target, sem):
+        lanes = chunks[0].shape[1]
+        whole = product(inverse, wide(chunks))
+        for i, k in enumerate(places):
+            held[pl.ds(k, columns, stride=stride), :] = whole[:, i * lanes : (i + 1) * lanes]
+        copy = pltpu.make_async_copy(held, target, sem)
+        copy.start()
+        return copy
+
+    fields = [part(field_x, y, columns) for y in range(cells)]
+    fields += [part(field_yz, k, columns) for k in range(2 * cells)]
+    first = write(fields, range(stride), basis, out_basis, sems.at[0])
     inside_last = has_last[0] > 0
     scaled_eps = material[cells:, :]
-    stride = 3 * cells
+    images, places = [], []
     for y in range(cells):
         e = [part(field_x, y, columns), part(field_yz, y, columns), part(field_yz, cells + y, columns)]
         m = [part(m_x, y, columns), part(m_yz, y, columns), part(m_yz, cells + y, columns)]
@@ -241,20 +276,25 @@
         m_y_last = part(behind_x, y, columns) - mu_last * e[2]
         m_z_last = part(behind_x, cells + y, columns) + mu_last * e[1]
         eps = scaled_eps[y : y + 1, :]
-        image = [
+        images += [
             (m[2] - m_z_down) - backward_z(m[1]) - eps * e[0],
             backward_z(m[0]) - (m[2] - m_z_last) - eps * e[1],
             (m[1] - m_y_last) - (m[0] - m_x_down) - eps * e[2],
         ]
-        both = lax.dot_general(
-            inverse, wide(e + image), (((1,), (0,)), ((), ())), precision=HIGHEST,
-            preferred_element_type=F32,
-        )
-        lanes = e[0].shape[1]
-        for c in range(3):
-            place = pl.ds(c * cells + y, columns, stride=stride)
-            out_basis[place, :] = both[:, c * lanes : (c + 1) * lanes]
-            out_image[place, :] = both[:, (3 + c) * lanes : (4 + c) * lanes]
+        places += [y, cells + y, 2 * cells + y]
+    second = write(images, places, image, out_image, sems.at[1])
+    raw = unpacked(proj[...] + proj_other[...]) / total
+    left = lax.dot_general(
+        inverse, raw, (((1,), (0,)), ((), ())), precision=lax.Precision.HIGHEST,
+        preferred_element_type=F32,
+    )
+    projected[...] = inner(left, inverse)
+    fourth = pltpu.make_async_copy(projected, out_proj, sems.at[3])
+    fourth.start()
+    first.wait()
+    second.wait()
+    third.wait()
+    fourth.wait()
 
 
 def split_kernel(sums, out):
@@ -264,9 +304,10 @@
 
 SMEM = pl.BlockSpec(memory_space=pltpu.SMEM)
 VMEM = pl.BlockSpec(memory_space=pltpu.VMEM)
-
-
-def call(body, scalars, arrays, outs, flops=None):
+ANY = pl.BlockSpec(memory_space=pl.ANY)
+
+
+def call(body, scalars, arrays, outs, flops=None, far=0, scratch=()):
     shapes = [jax.ShapeDtypeStruct(shape, F32) for shape in outs]
     cost = None
     if flops is not None:
@@ -275,7 +316,8 @@
         body,
         out_shape=shapes,
         in_specs=[SMEM] * len(scalars) + [VMEM] * len(arrays),
-        out_specs=[VMEM] * len(shapes),
+        out_specs=[ANY] * far + [VMEM] * (len(shapes) - far),
+        scratch_shapes=scratch,
         cost_estimate=cost,
         compiler_params=pltpu.CompilerParams(vmem_limit_bytes=32 * 1024 * 1024),
     )(*scalars, *arrays)
@@ -349,12 +391,23 @@
     (factors,) = call(
         functools.partial(factor_kernel, total), (), (sums,), ((columns, 2 * columns),), flops=0
     )
-    basis_out, image_out, projected, upper = call(
-        functools.partial(finish_kernel, columns, cells, total),
+    basis_out, image_out, upper, projected = call(
+        functools.partial(basis_kernel, columns, cells, total),
         (has_last,),
-        (field_x, field_yz, m_x, m_yz, behind_x, behind_y, material, factors, proj, proj_other),
+        (
+            field_x, field_yz, m_x, m_yz, behind_x, behind_y, material, factors, proj,
+            proj_other,
+        ),
         (basis.shape, basis.shape, square, square),
         flops=0,
+        far=4,
+        scratch=[
+            pltpu.VMEM(basis.shape, F32),
+            pltpu.VMEM(basis.shape, F32),
+            pltpu.VMEM(square, F32),
+            pltpu.VMEM(square, F32),
+            pltpu.SemaphoreType.DMA((4,)),
+        ],
     )
     return (
         basis_out.reshape(krylov_basis.shape),

time: 30.1 us -> 29.7 us (0.987)
  Pallas kernels: 5.95 us -> 5.56 us
    pallas_call x11, Pallas kernels: 5.95 us -> 5.56 us  [call(): pl.pallas_call(body, out_shape=shapes, in_specs=[SMEM] * len(scalars) + [...]
where the time goes in v5:
time: 29.7 us; the launch traced here: 29.5 us
  starting transfers between devices  14.4 us (48%)
  waiting for transfers between devices  6.49 us (22%)
  Pallas kernels  5.56 us (19%)
  local copies, waits for them, and re-layouts  1.65 us (6%)
  between operations  1.41 us (5%)
    ppermute x6, starting transfers between devices, swapped(): lax.ppermute(x, axis, [(i, i ^ step) for i in range(lax.axis_size(axis))])  11.2 us
    pallas_call x11, Pallas kernels, call(): pl.pallas_call(body, out_shape=shapes, in_specs=[SMEM] * len(scalars) + [...  5.56 us
    ppermute x6, waiting for transfers between devices, swapped(): lax.ppermute(x, axis, [(i, i ^ step) for i in range(lax.axis_size(axis))])  5.35 us
    ppermute x2, starting transfers between devices, shifted(): return lax.ppermute(x, axis, pairs)  3.23 us
    unnamed x8, local copies, waits for them, and re-layouts  1.65 us
    ppermute x2, waiting for transfers between devices, shifted(): return lax.ppermute(x, axis, pairs)  1.14 us
  transfers between devices with their start and end apart: 8, of which 5 were waited for; matrix products, arithmetic and copies ran while one was open for 0% of the time, Pallas kernels for 14%

profile of v5, /device:TPU:0, one launch (start us, length us, event | category | flops | bytes accessed | tf_op | source)
XLA Modules:
  0.0 29.5 jit_solution(12807181530280867428)
XLA Ops:
  0.6 0.0 copy-start
  0.6 1.0 %copy-done = f32[64,3,1,4,128]{4,3,2,1,0:T(4,128)S(1)} copy-done((f32[64,3,1,4,128]{4,3,2,1,0:T(4,128)S(1)}, f32[64,3,1,4,128]{4,3,2,1,0:T(4,128)}, u32[]{:S(2)}) %copy-start) | copy-done | bytes 393240
  1.7 1.3 %collective-permute-start.1 = (f32[512,128]{1,0:T(8,128)S(1)}, f32[512,128]{1,0:T(8,128)S(1)}, u32[]{:S(2)}, u32[]{:S(2)}) collective-permute-start(f32[512,128]{1,0:T(8,128)S(1)} %get-tuple-element.17.field_yz), channel_id=1, source_target_pairs={{2,0},{4,2},{6,4},{8,6},{10,8},{12,10},{14,12},{3,1},{5,3},{7,5},{... | collective-permute-start | bytes 786440 | tf_op jit(solution)/shard_map/ppermute | solution.py:17
  3.0 0.5 %shard_map.85.gram_edge = f32[160,128]{1,0:T(8,128)S(1)} custom-call(f32[256,128]{1,0:T(8,128)S(1)} %get-tuple-element.16.field_x, f32[512,128]{1,0:T(8,128)S(1)} %get-tuple-element.17.field_yz), custom_call_target="tpu_custom_call" | custom-call | tf_op jit(solution)/shard_map/pallas_call | solution.py:315
  3.5 0.5 %collective-permute-start = (f32[160,128]{1,0:T(8,128)S(1)}, f32[160,128]{1,0:T(8,128)S(1)}, u32[]{:S(2)}, u32[]{:S(2)}) collective-permute-start(f32[160,128]{1,0:T(8,128)S(1)} %shard_map.85.gram_edge), channel_id=1, source_target_pairs={{0,1},{1,0},{2,3},{3,2},{4,5},{5,4},{6,7},{7,6},{8,9},{9,8},{10,11... | collective-permute-start | bytes 245768 | tf_op jit(solution)/shard_map/ppermute | solution.py:327
  4.6 0.0 copy-start.1
  4.6 0.0 copy-start.2
  4.6 0.0 copy-start.3
  4.6 0.6 %copy-done.1 = s32[1,4,128]{2,1,0:T(4,128)S(1)} copy-done((s32[1,4,128]{2,1,0:T(4,128)S(1)}, s32[1,4,128]{2,1,0:T(4,128)}, u32[]{:S(2)}) %copy-start.1) | copy-done | bytes 2072
  5.3 0.0 copy-done.2
  5.3 0.0 copy-done.3
  5.3 0.6 %shard_map.86.material = f32[8,128]{1,0:T(8,128)S(1)} custom-call(f32[8]{0:T(128)S(1)} %copy-done.2, f32[8]{0:T(128)S(1)} %copy-done.3, f32[1]{0:T(128)S(6)} %copy.11.shift, s32[4,128]{1,0:T(4,128)S(1)} %bitcast.10), custom_call_target="tpu_custom_call" | custom-call | tf_op jit(solution)/shard_map/pallas_call | solution.py:315
  5.9 0.0 collective-permute-done.ahead_y
  5.9 0.1 shard_map.89
  6.0 3.2 %collective-permute-start.4 = (f32[32,128]{1,0:T(8,128)S(1)}, f32[32,128]{1,0:T(8,128)S(1)}, u32[]{:S(2)}, u32[]{:S(2)}) collective-permute-start(f32[32,128]{1,0:T(8,128)S(1)} %get-tuple-element.23.left), channel_id=1, source_target_pairs={{0,2},{2,0},{4,6},{6,4},{8,10},{10,8},{12,14},{14,12},{1,3},{3,1},... | collective-permute-start | bytes 49160 | tf_op jit(solution)/shard_map/ppermute | solution.py:327
  9.2 1.9 %collective-permute-start.2 = (f32[520,128]{1,0:T(8,128)S(1)}, f32[520,128]{1,0:T(8,128)S(1)}, u32[]{:S(2)}, u32[]{:S(2)}) collective-permute-start(f32[520,128]{1,0:T(8,128)S(1)} %get-tuple-element.21), channel_id=1, source_target_pairs={{0,2},{2,4},{4,6},{6,8},{8,10},{10,12},{12,14},{1,3},{3,5},{5,7},{... | collective-permute-start | bytes 798728 | tf_op jit(solution)/shard_map/ppermute | solution.py:17
  11.1 0.7 %shard_map.87 = (f32[256,128]{1,0:T(8,128)S(1)}, f32[32,128]{1,0:T(8,128)S(1)}) custom-call(s32[1]{0:T(128)} %bitcast.has_next, f32[256,128]{1,0:T(8,128)S(1)} %get-tuple-element.16.field_x, f32[512,128]{1,0:T(8,128)S(1)} %get-tuple-element.17.field_yz, f32[160,128]{1,0:T(8,128)S(1)} %collective-permute-done.ahead_y, f32[8,128]{1,0:T(8,128)S(1)} %shard_map.86.material), custom_call_target="tpu_custom_call" | custom-call | tf_op jit(solution)/shard_map/pallas_call | solution.py:315
  11.8 1.1 %collective-permute-done.1.ahead_x = f32[512,128]{1,0:T(8,128)S(1)} collective-permute-done((f32[512,128]{1,0:T(8,128)S(1)}, f32[512,128]{1,0:T(8,128)S(1)}, u32[]{:S(2)}, u32[]{:S(2)}) %collective-permute-start.1) | collective-permute-done | bytes 262176 | tf_op jit(solution)/shard_map/ppermute | solution.py:17
  13.0 0.5 %shard_map.88 = (f32[512,128]{1,0:T(8,128)S(1)}, f32[160,128]{1,0:T(8,128)S(1)}) custom-call(s32[1]{0:T(128)} %bitcast.has_next, f32[256,128]{1,0:T(8,128)S(1)} %get-tuple-element.16.field_x, f32[512,128]{1,0:T(8,128)S(1)} %get-tuple-element.17.field_yz, f32[512,128]{1,0:T(8,128)S(1)} %collective-permute-done.1.ahead_x, ...), custom_call_target="tpu_custom_call" | custom-call | flops 10000000000 | tf_op jit(solution)/shard_map/pallas_call | solution.py:315
  13.5 0.0 collective-permute-start.3
  13.5 0.0 collective-permute-done.4.right
  13.5 1.2 %collective-permute-done.3.edge_other.behind_y = f32[160,128]{1,0:T(8,128)S(1)} collective-permute-done((f32[160,128]{1,0:T(8,128)S(1)}, f32[160,128]{1,0:T(8,128)S(1)}, u32[]{:S(2)}, u32[]{:S(2)}) %collective-permute-start.3) | collective-permute-done | bytes 81952 | tf_op jit(solution)/shard_map/ppermute | solution.py:327
  14.8 0.1 shard_map.91
  14.9 2.3 %collective-permute-start.5 = (f32[64,128]{1,0:T(8,128)S(1)}, f32[64,128]{1,0:T(8,128)S(1)}, u32[]{:S(2)}, u32[]{:S(2)}) collective-permute-start(f32[64,128]{1,0:T(8,128)S(1)} %shard_map.91), channel_id=1, source_target_pairs={{0,4},{2,6},{4,0},{6,2},{8,12},{10,14},{12,8},{14,10},{1,5},{3,7},... | collective-permute-start | bytes 98312 | tf_op jit(solution)/shard_map/ppermute | solution.py:327
  17.2 1.9 %collective-permute-done.5 = f32[64,128]{1,0:T(8,128)S(1)} collective-permute-done((f32[64,128]{1,0:T(8,128)S(1)}, f32[64,128]{1,0:T(8,128)S(1)}, u32[]{:S(2)}, u32[]{:S(2)}) %collective-permute-start.5) | collective-permute-done | bytes 32800 | tf_op jit(solution)/shard_map/ppermute | solution.py:327
  19.1 3.0 %collective-permute-start.6 = (f32[64,128]{1,0:T(8,128)S(1)}, f32[64,128]{1,0:T(8,128)S(1)}, u32[]{:S(2)}, u32[]{:S(2)}) collective-permute-start(f32[64,128]{1,0:T(8,128)S(1)} %add.6), channel_id=1, source_target_pairs={{0,8},{2,10},{4,12},{6,14},{8,0},{10,2},{12,4},{14,6},{1,9},{3,11}... | collective-permute-start | bytes 98312 | tf_op jit(solution)/shard_map/ppermute | solution.py:327
  22.2 1.9 %collective-permute-done.6 = f32[64,128]{1,0:T(8,128)S(1)} collective-permute-done((f32[64,128]{1,0:T(8,128)S(1)}, f32[64,128]{1,0:T(8,128)S(1)}, u32[]{:S(2)}, u32[]{:S(2)}) %collective-permute-start.6) | collective-permute-done | bytes 32800 | tf_op jit(solution)/shard_map/ppermute | solution.py:327
  24.1 0.1 shard_map.93.proj
  24.2 2.2 %collective-permute-start.7 = (f32[32,128]{1,0:T(8,128)S(1)}, f32[32,128]{1,0:T(8,128)S(1)}, u32[]{:S(2)}, u32[]{:S(2)}) collective-permute-start(f32[32,128]{1,0:T(8,128)S(1)} %shard_map.93.proj), channel_id=1, source_target_pairs={{0,2},{2,0},{4,6},{6,4},{8,10},{10,8},{12,14},{14,12},{1,3},{3,1},... | collective-permute-start | bytes 49160 | tf_op jit(solution)/shard_map/ppermute | solution.py:327
  26.3 1.4 %shard_map.92.factors = f32[64,128]{1,0:T(8,128)S(1)} custom-call(f32[64,128]{1,0:T(8,128)S(1)} %add.7.sums), custom_call_target="tpu_custom_call" | custom-call | tf_op jit(solution)/shard_map/pallas_call | solution.py:315
  27.7 0.0 collective-permute-done.2.behind_x
  27.7 0.3 collective-permute-done.7.proj_other
  28.0 1.5 %shard_map.94 = (f32[768,128]{1,0:T(8,128)}, f32[768,128]{1,0:T(8,128)}, f32[64,64]{1,0:T(8,128)}, f32[64,64]{1,0:T(8,128)}) custom-call(s32[1]{0:T(128)S(6)} %sub.3.has_last, f32[256,128]{1,0:T(8,128)S(1)} %get-tuple-element.16.field_x, f32[512,128]{1,0:T(8,128)S(1)} %get-tuple-element.17.field_yz, f32[256,128]{1,0:T(8,128)S(1)} %get-tuple-element.18.m_x, ...), custom_call_target="tpu_custom_call" | custom-call | tf_op jit(solution)/shard_map/pallas_call | solution.py:315
  (4 shorter events, 0.0 us)
Async XLA Ops:
  0.6 1.0 %copy-start = (f32[64,3,1,4,128]{4,3,2,1,0:T(4,128)S(1)}, f32[64,3,1,4,128]{4,3,2,1,0:T(4,128)}, u32[]{:S(2)}) copy-start(f32[64,3,1,4,128]{4,3,2,1,0:T(4,128)} %param.5) | copy-start | bytes 1179652
  1.7 11.3 %collective-permute-start.1 = (f32[512,128]{1,0:T(8,128)S(1)}, f32[512,128]{1,0:T(8,128)S(1)}, u32[]{:S(2)}, u32[]{:S(2)}) collective-permute-start(f32[512,128]{1,0:T(8,128)S(1)} %get-tuple-element.17.field_yz), channel_id=1, source_target_pairs={{2,0},{4,2},{6,4},{8,6},{10,8},{12,10},{14,12},{3,1},{5,3},{7,5},{... | collective-permute-start | bytes 786440 | tf_op jit(solution)/shard_map/ppermute | solution.py:17
  3.5 2.4 %collective-permute-start = (f32[160,128]{1,0:T(8,128)S(1)}, f32[160,128]{1,0:T(8,128)S(1)}, u32[]{:S(2)}, u32[]{:S(2)}) collective-permute-start(f32[160,128]{1,0:T(8,128)S(1)} %shard_map.85.gram_edge), channel_id=1, source_target_pairs={{0,1},{1,0},{2,3},{3,2},{4,5},{5,4},{6,7},{7,6},{8,9},{9,8},{10,11... | collective-permute-start | bytes 245768 | tf_op jit(solution)/shard_map/ppermute | solution.py:327
  4.6 0.7 %copy-start.1 = (s32[1,4,128]{2,1,0:T(4,128)S(1)}, s32[1,4,128]{2,1,0:T(4,128)}, u32[]{:S(2)}) copy-start(s32[1,4,128]{2,1,0:T(4,128)} %param.6) | copy-start | bytes 6148
  4.6 0.7 %copy-start.2 = (f32[8]{0:T(128)S(1)}, f32[8]{0:T(128)}, u32[]{:S(2)}) copy-start(f32[8]{0:T(128)} %mu_table.1) | copy-start | bytes 100
  4.6 0.7 %copy-start.3 = (f32[8]{0:T(128)S(1)}, f32[8]{0:T(128)}, u32[]{:S(2)}) copy-start(f32[8]{0:T(128)} %eps_table.1) | copy-start | bytes 100
  6.0 7.5 %collective-permute-start.4 = (f32[32,128]{1,0:T(8,128)S(1)}, f32[32,128]{1,0:T(8,128)S(1)}, u32[]{:S(2)}, u32[]{:S(2)}) collective-permute-start(f32[32,128]{1,0:T(8,128)S(1)} %get-tuple-element.23.left), channel_id=1, source_target_pairs={{0,2},{2,0},{4,6},{6,4},{8,10},{10,8},{12,14},{14,12},{1,3},{3,1},... | collective-permute-start | bytes 49160 | tf_op jit(solution)/shard_map/ppermute | solution.py:327
  9.2 18.5 %collective-permute-start.2 = (f32[520,128]{1,0:T(8,128)S(1)}, f32[520,128]{1,0:T(8,128)S(1)}, u32[]{:S(2)}, u32[]{:S(2)}) collective-permute-start(f32[520,128]{1,0:T(8,128)S(1)} %get-tuple-element.21), channel_id=1, source_target_pairs={{0,2},{2,4},{4,6},{6,8},{8,10},{10,12},{12,14},{1,3},{3,5},{5,7},{... | collective-permute-start | bytes 798728 | tf_op jit(solution)/shard_map/ppermute | solution.py:17
  13.5 1.3 %collective-permute-start.3 = (f32[160,128]{1,0:T(8,128)S(1)}, f32[160,128]{1,0:T(8,128)S(1)}, u32[]{:S(2)}, u32[]{:S(2)}) collective-permute-start(f32[160,128]{1,0:T(8,128)S(1)} %get-tuple-element.22.edge), channel_id=1, source_target_pairs={{0,1},{1,0},{2,3},{3,2},{4,5},{5,4},{6,7},{7,6},{8,9},{9,8},{10,11... | collective-permute-start | bytes 245768 | tf_op jit(solution)/shard_map/ppermute | solution.py:327
  14.9 4.2 %collective-permute-start.5 = (f32[64,128]{1,0:T(8,128)S(1)}, f32[64,128]{1,0:T(8,128)S(1)}, u32[]{:S(2)}, u32[]{:S(2)}) collective-permute-start(f32[64,128]{1,0:T(8,128)S(1)} %shard_map.91), channel_id=1, source_target_pairs={{0,4},{2,6},{4,0},{6,2},{8,12},{10,14},{12,8},{14,10},{1,5},{3,7},... | collective-permute-start | bytes 98312 | tf_op jit(solution)/shard_map/ppermute | solution.py:327
  19.1 5.0 %collective-permute-start.6 = (f32[64,128]{1,0:T(8,128)S(1)}, f32[64,128]{1,0:T(8,128)S(1)}, u32[]{:S(2)}, u32[]{:S(2)}) collective-permute-start(f32[64,128]{1,0:T(8,128)S(1)} %add.6), channel_id=1, source_target_pairs={{0,8},{2,10},{4,12},{6,14},{8,0},{10,2},{12,4},{14,6},{1,9},{3,11}... | collective-permute-start | bytes 98312 | tf_op jit(solution)/shard_map/ppermute | solution.py:327
  24.2 3.9 %collective-permute-start.7 = (f32[32,128]{1,0:T(8,128)S(1)}, f32[32,128]{1,0:T(8,128)S(1)}, u32[]{:S(2)}, u32[]{:S(2)}) collective-permute-start(f32[32,128]{1,0:T(8,128)S(1)} %shard_map.93.proj), channel_id=1, source_target_pairs={{0,2},{2,0},{4,6},{6,4},{8,10},{10,8},{12,14},{14,12},{1,3},{3,1},... | collective-permute-start | bytes 49160 | tf_op jit(solution)/shard_map/ppermute | solution.py:327

commit v6 on v5

--- a/solution.py
+++ b/solution.py
@@ -184,10 +184,16 @@
 
 
 def join_kernel(gram, edge, edge_other, out):
-    half, columns = gram.shape[0], 2 * gram.shape[0]
-    proj = edge[:half, :] + edge_other[:half, :]
-    out[:, :columns] = unpacked(gram[...])
-    out[:, columns:] = unpacked(proj)
+    half = gram.shape[0]
+    out[:half, :] = gram[...]
+    out[half:, :] = edge[:half, :] + edge_other[:half, :]
+
+
+def sum_kernel(own, both, out, out_proj):
+    half = out_proj.shape[0]
+    total = own[...] + both[...]
+    out[...] = total
+    out_proj[...] = total[half:, :]
 
 
 def factor(gram):
@@ -232,19 +238,19 @@
     return jnp.concatenate(kept, axis=0)
 
 
-def factor_kernel(total, sums, out):
-    columns = sums.shape[0]
-    out[...] = factor(sums[:, :columns] / total)
+def factor_kernel(total, sums, far, out):
+    half = sums.shape[0] // 2
+    out[...] = factor(unpacked(sums[:half, :] + far[:half, :]) / total)
 
 
 def basis_kernel(
-    columns, cells, total, has_last, field_x, field_yz, m_x, m_yz, behind_x, behind_y, material,
-    factors, proj, proj_other, out_basis, out_image, out_upper, out_proj, basis, image, upper,
-    projected, sems,
+    columns, cells, has_last, field_x, field_yz, m_x, m_yz, behind_x, behind_y, material, factors,
+    out_basis, out_image, out_upper, out_inverse, basis, image, upper, sems,
 ):
     half = columns // 2
     stride = 3 * cells
     inverse = factors[:, columns:]
+    out_inverse[...] = inverse
     upper[...] = factors[:, :columns]
     third = pltpu.make_async_copy(upper, out_upper, sems.at[2])
     third.start()
@@ -283,23 +289,19 @@
         ]
         places += [y, cells + y, 2 * cells + y]
     second = write(images, places, image, out_image, sems.at[1])
-    raw = unpacked(proj[...] + proj_other[...]) / total
-    left = lax.dot_general(
-        inverse, raw, (((1,), (0,)), ((), ())), precision=lax.Precision.HIGHEST,
-        preferred_element_type=F32,
-    )
-    projected[...] = inner(left, inverse)
-    fourth = pltpu.make_async_copy(projected, out_proj, sems.at[3])
-    fourth.start()
     first.wait()
     second.wait()
     third.wait()
-    fourth.wait()
-
-
-def split_kernel(sums, out):
-    columns = sums.shape[0]
-    out[...] = packed(sums[:, columns:])
+
+
+def proj_kernel(total, inverse, proj, far_cross, far, near, out):
+    half = proj.shape[0]
+    raw = (proj[...] + near[...]) + (far[half:, :] + far_cross[...])
+    left = lax.dot_general(
+        inverse[...], unpacked(raw) / total, (((1,), (0,)), ((), ())),
+        precision=lax.Precision.HIGHEST, preferred_element_type=F32,
+    )
+    out[...] = inner(left, inverse[...])
 
 
 SMEM = pl.BlockSpec(memory_space=pltpu.SMEM)
@@ -330,11 +332,11 @@
 def local(krylov_basis, regions, mu_table, eps_table, shift_value):
     columns, parts, layers, cells, lanes = krylov_basis.shape
     rows, cols = lax.axis_size("row"), lax.axis_size("col")
-    assert layers == 1 and parts == 3 and cols == 2 and rows & (rows - 1) == 0
+    assert layers == 1 and parts == 3 and cols == 2 and rows >= 8 and rows & (rows - 1) == 0
     total = 3 * cells * lanes * rows * cols
     basis = krylov_basis.reshape(-1, lanes)
     labels = regions[0]
-    half = columns // 2
+    half, outer = columns // 2, rows // 2
     small, large = (cells * columns, lanes), (2 * cells * columns, lanes)
     edge, pair = (half + 2 * columns, lanes), (half, 2 * columns)
     square = (columns, columns)
@@ -377,37 +379,43 @@
         (large, edge),
         flops=10**10,
     )
+    both = (2 * half, 2 * columns)
     (gram,) = call(add_kernel, (), (gram, gram_other), (pair,), flops=10**10)
     behind_y = swapped(proj_edge, "col", 1)
-    (sums,) = call(
-        join_kernel, (), (gram, proj_edge, behind_y), ((columns, 2 * columns),), flops=0
-    )
-    step = 2
-    while step < rows:
+    (own,) = call(join_kernel, (), (gram, proj_edge, behind_y), (both,), flops=0)
+    next_both = swapped(own, "row", 2)
+    sums, proj = call(sum_kernel, (), (own, next_both), (both, pair), flops=0)
+    step = 4
+    while step < outer:
         sums = sums + swapped(sums, "row", step)
+        proj = sums[half:]
         step *= 2
-    (proj,) = call(split_kernel, (), (sums,), (pair,), flops=0)
-    proj_other = swapped(proj, "row", 1)
+    far = swapped(sums, "row", outer)
+    proj_near = swapped(proj, "row", 1)
+    far_cross = swapped(proj, "row", outer + 1)
     (factors,) = call(
-        functools.partial(factor_kernel, total), (), (sums,), ((columns, 2 * columns),), flops=0
-    )
-    basis_out, image_out, upper, projected = call(
-        functools.partial(basis_kernel, columns, cells, total),
+        functools.partial(factor_kernel, total), (), (sums, far), ((columns, 2 * columns),), flops=0
+    )
+    basis_out, image_out, upper, inverse = call(
+        functools.partial(basis_kernel, columns, cells),
         (has_last,),
-        (
-            field_x, field_yz, m_x, m_yz, behind_x, behind_y, material, factors, proj,
-            proj_other,
-        ),
+        (field_x, field_yz, m_x, m_yz, behind_x, behind_y, material, factors),
         (basis.shape, basis.shape, square, square),
         flops=0,
-        far=4,
+        far=3,
         scratch=[
             pltpu.VMEM(basis.shape, F32),
             pltpu.VMEM(basis.shape, F32),
             pltpu.VMEM(square, F32),
-            pltpu.VMEM(square, F32),
-            pltpu.SemaphoreType.DMA((4,)),
+            pltpu.SemaphoreType.DMA((3,)),
         ],
+    )
+    (projected,) = call(
+        functools.partial(proj_kernel, total),
+        (),
+        (inverse, proj, far_cross, far, proj_near),
+        (square,),
+        flops=0,
     )
     return (
         basis_out.reshape(krylov_basis.shape),

time: 29.7 us -> 29 us (0.976)
  waiting for transfers between devices: 6.49 us -> 5.24 us
  Pallas kernels: 5.56 us -> 6.25 us
    ppermute x6 -> x7, waiting for transfers between devices: 5.35 us -> 4.1 us  [swapped(): lax.ppermute(x, axis, [(i, i ^ step) for i in range(lax.axis_size(axis))])]
    pallas_call x11 -> x12, Pallas kernels: 5.56 us -> 6.25 us  [call(): pl.pallas_call(body, out_shape=shapes, in_specs=[SMEM] * len(scalars) + [...]
    ppermute x6 -> x7, starting transfers between devices: 11.2 us -> 11 us  [swapped(): lax.ppermute(x, axis, [(i, i ^ step) for i in range(lax.axis_size(axis))])]
  transfers between devices with their start and end apart: 8 -> 9, of which waited for: 5 -> 4; matrix products, arithmetic and copies ran while one was open for 0% -> 0% of each run, Pallas kernels for 14% -> 18%
where the time goes in v6:
time: 29 us; the launch traced here: 28.8 us
  starting transfers between devices  14.2 us (49%)
  Pallas kernels  6.25 us (22%)
  waiting for transfers between devices  5.24 us (18%)
  local copies, waits for them, and re-layouts  1.65 us (6%)
  between operations  1.42 us (5%)
    ppermute x7, starting transfers between devices, swapped(): lax.ppermute(x, axis, [(i, i ^ step) for i in range(lax.axis_size(axis))])  11 us
    pallas_call x12, Pallas kernels, call(): pl.pallas_call(body, out_shape=shapes, in_specs=[SMEM] * len(scalars) + [...  6.25 us
    ppermute x7, waiting for transfers between devices, swapped(): lax.ppermute(x, axis, [(i, i ^ step) for i in range(lax.axis_size(axis))])  4.1 us
    ppermute x2, starting transfers between devices, shifted(): return lax.ppermute(x, axis, pairs)  3.23 us
    unnamed x8, local copies, waits for them, and re-layouts  1.65 us
    ppermute x2, waiting for transfers between devices, shifted(): return lax.ppermute(x, axis, pairs)  1.14 us
  transfers between devices with their start and end apart: 9, of which 4 were waited for; matrix products, arithmetic and copies ran while one was open for 0% of the time, Pallas kernels for 18%

profile of v6, /device:TPU:0, one launch (start us, length us, event | category | flops | bytes accessed | tf_op | source)
XLA Modules:
  0.0 28.8 jit_solution(7752963104551934153)
XLA Ops:
  0.6 0.0 copy-start
  0.6 1.0 %copy-done = f32[64,3,1,4,128]{4,3,2,1,0:T(4,128)S(1)} copy-done((f32[64,3,1,4,128]{4,3,2,1,0:T(4,128)S(1)}, f32[64,3,1,4,128]{4,3,2,1,0:T(4,128)}, u32[]{:S(2)}) %copy-start) | copy-done | bytes 393240
  1.7 1.3 %collective-permute-start.1 = (f32[512,128]{1,0:T(8,128)S(1)}, f32[512,128]{1,0:T(8,128)S(1)}, u32[]{:S(2)}, u32[]{:S(2)}) collective-permute-start(f32[512,128]{1,0:T(8,128)S(1)} %get-tuple-element.19.field_yz), channel_id=1, source_target_pairs={{2,0},{4,2},{6,4},{8,6},{10,8},{12,10},{14,12},{3,1},{5,3},{7,5},{... | collective-permute-start | bytes 786440 | tf_op jit(solution)/shard_map/ppermute | solution.py:17
  3.0 0.5 %shard_map.85.gram_edge = f32[160,128]{1,0:T(8,128)S(1)} custom-call(f32[256,128]{1,0:T(8,128)S(1)} %get-tuple-element.18.field_x, f32[512,128]{1,0:T(8,128)S(1)} %get-tuple-element.19.field_yz), custom_call_target="tpu_custom_call" | custom-call | tf_op jit(solution)/shard_map/pallas_call | solution.py:317
  3.5 0.5 %collective-permute-start = (f32[160,128]{1,0:T(8,128)S(1)}, f32[160,128]{1,0:T(8,128)S(1)}, u32[]{:S(2)}, u32[]{:S(2)}) collective-permute-start(f32[160,128]{1,0:T(8,128)S(1)} %shard_map.85.gram_edge), channel_id=1, source_target_pairs={{0,1},{1,0},{2,3},{3,2},{4,5},{5,4},{6,7},{7,6},{8,9},{9,8},{10,11... | collective-permute-start | bytes 245768 | tf_op jit(solution)/shard_map/ppermute | solution.py:329
  4.6 0.0 copy-start.1
  4.6 0.0 copy-start.2
  4.6 0.0 copy-start.3
  4.6 0.6 %copy-done.1 = s32[1,4,128]{2,1,0:T(4,128)S(1)} copy-done((s32[1,4,128]{2,1,0:T(4,128)S(1)}, s32[1,4,128]{2,1,0:T(4,128)}, u32[]{:S(2)}) %copy-start.1) | copy-done | bytes 2072
  5.3 0.0 copy-done.2
  5.3 0.0 copy-done.3
  5.3 0.6 %shard_map.86.material = f32[8,128]{1,0:T(8,128)S(1)} custom-call(f32[8]{0:T(128)S(1)} %copy-done.2, f32[8]{0:T(128)S(1)} %copy-done.3, f32[1]{0:T(128)S(6)} %copy.11.shift, s32[4,128]{1,0:T(4,128)S(1)} %bitcast.10), custom_call_target="tpu_custom_call" | custom-call | tf_op jit(solution)/shard_map/pallas_call | solution.py:317
  5.9 0.0 collective-permute-done.ahead_y
  5.9 0.1 shard_map.89
  6.0 3.2 %collective-permute-start.4 = (f32[32,128]{1,0:T(8,128)S(1)}, f32[32,128]{1,0:T(8,128)S(1)}, u32[]{:S(2)}, u32[]{:S(2)}) collective-permute-start(f32[32,128]{1,0:T(8,128)S(1)} %get-tuple-element.25.left), channel_id=1, source_target_pairs={{0,2},{2,0},{4,6},{6,4},{8,10},{10,8},{12,14},{14,12},{1,3},{3,1},... | collective-permute-start | bytes 49160 | tf_op jit(solution)/shard_map/ppermute | solution.py:329
  9.2 1.9 %collective-permute-start.2 = (f32[520,128]{1,0:T(8,128)S(1)}, f32[520,128]{1,0:T(8,128)S(1)}, u32[]{:S(2)}, u32[]{:S(2)}) collective-permute-start(f32[520,128]{1,0:T(8,128)S(1)} %get-tuple-element.23), channel_id=1, source_target_pairs={{0,2},{2,4},{4,6},{6,8},{8,10},{10,12},{12,14},{1,3},{3,5},{5,7},{... | collective-permute-start | bytes 798728 | tf_op jit(solution)/shard_map/ppermute | solution.py:17
  11.1 0.7 %shard_map.87 = (f32[256,128]{1,0:T(8,128)S(1)}, f32[32,128]{1,0:T(8,128)S(1)}) custom-call(s32[1]{0:T(128)} %bitcast.has_next, f32[256,128]{1,0:T(8,128)S(1)} %get-tuple-element.18.field_x, f32[512,128]{1,0:T(8,128)S(1)} %get-tuple-element.19.field_yz, f32[160,128]{1,0:T(8,128)S(1)} %collective-permute-done.ahead_y, f32[8,128]{1,0:T(8,128)S(1)} %shard_map.86.material), custom_call_target="tpu_custom_call" | custom-call | tf_op jit(solution)/shard_map/pallas_call | solution.py:317
  11.8 1.1 %collective-permute-done.1.ahead_x = f32[512,128]{1,0:T(8,128)S(1)} collective-permute-done((f32[512,128]{1,0:T(8,128)S(1)}, f32[512,128]{1,0:T(8,128)S(1)}, u32[]{:S(2)}, u32[]{:S(2)}) %collective-permute-start.1) | collective-permute-done | bytes 262176 | tf_op jit(solution)/shard_map/ppermute | solution.py:17
  13.0 0.5 %shard_map.88 = (f32[512,128]{1,0:T(8,128)S(1)}, f32[160,128]{1,0:T(8,128)S(1)}) custom-call(s32[1]{0:T(128)} %bitcast.has_next, f32[256,128]{1,0:T(8,128)S(1)} %get-tuple-element.18.field_x, f32[512,128]{1,0:T(8,128)S(1)} %get-tuple-element.19.field_yz, f32[512,128]{1,0:T(8,128)S(1)} %collective-permute-done.1.ahead_x, ...), custom_call_target="tpu_custom_call" | custom-call | flops 10000000000 | tf_op jit(solution)/shard_map/pallas_call | solution.py:317
  13.5 0.0 collective-permute-start.3
  13.5 0.0 collective-permute-done.4.right
  13.5 1.2 %collective-permute-done.3.edge_other.behind_y = f32[160,128]{1,0:T(8,128)S(1)} collective-permute-done((f32[160,128]{1,0:T(8,128)S(1)}, f32[160,128]{1,0:T(8,128)S(1)}, u32[]{:S(2)}, u32[]{:S(2)}) %collective-permute-start.3) | collective-permute-done | bytes 81952 | tf_op jit(solution)/shard_map/ppermute | solution.py:329
  14.8 2.3 %collective-permute-start.5 = (f32[64,128]{1,0:T(8,128)S(1)}, f32[64,128]{1,0:T(8,128)S(1)}, u32[]{:S(2)}, u32[]{:S(2)}) collective-permute-start(f32[64,128]{1,0:T(8,128)S(1)} %shard_map.91.own), channel_id=1, source_target_pairs={{0,4},{2,6},{4,0},{6,2},{8,12},{10,14},{12,8},{14,10},{1,5},{3,7},... | collective-permute-start | bytes 98312 | tf_op jit(solution)/shard_map/ppermute | solution.py:329
  17.1 1.9 %collective-permute-done.5.both = f32[64,128]{1,0:T(8,128)S(1)} collective-permute-done((f32[64,128]{1,0:T(8,128)S(1)}, f32[64,128]{1,0:T(8,128)S(1)}, u32[]{:S(2)}, u32[]{:S(2)}) %collective-permute-start.5) | collective-permute-done | bytes 32800 | tf_op jit(solution)/shard_map/ppermute | solution.py:329
  19.0 3.0 %collective-permute-start.6 = (f32[64,128]{1,0:T(8,128)S(1)}, f32[64,128]{1,0:T(8,128)S(1)}, u32[]{:S(2)}, u32[]{:S(2)}) collective-permute-start(f32[64,128]{1,0:T(8,128)S(1)} %get-tuple-element.26.sums), channel_id=1, source_target_pairs={{0,8},{2,10},{4,12},{6,14},{8,0},{10,2},{12,4},{14,6},{1,9},{3,11}... | collective-permute-start | bytes 98312 | tf_op jit(solution)/shard_map/ppermute | solution.py:329
  22.0 1.7 %collective-permute-start.7 = (f32[32,128]{1,0:T(8,128)S(1)}, f32[32,128]{1,0:T(8,128)S(1)}, u32[]{:S(2)}, u32[]{:S(2)}) collective-permute-start(f32[32,128]{1,0:T(8,128)S(1)} %get-tuple-element.31.proj), channel_id=1, source_target_pairs={{0,10},{2,8},{4,14},{6,12},{8,2},{10,0},{12,6},{14,4},{1,11},{3,9}... | collective-permute-start | bytes 49160 | tf_op jit(solution)/shard_map/ppermute | solution.py:329
  23.7 0.2 collective-permute-start.8
  24.0 0.0 collective-permute-done.6.far
  24.0 1.4 %shard_map.93.factors = f32[64,128]{1,0:T(8,128)S(1)} custom-call(f32[64,128]{1,0:T(8,128)S(1)} %get-tuple-element.26.sums, f32[64,128]{1,0:T(8,128)S(1)} %collective-permute-done.6.far), custom_call_target="tpu_custom_call" | custom-call | tf_op jit(solution)/shard_map/pallas_call | solution.py:317
  25.4 0.0 collective-permute-done.2.behind_x
  25.4 1.3 %shard_map.94 = (f32[768,128]{1,0:T(8,128)}, f32[768,128]{1,0:T(8,128)}, f32[64,64]{1,0:T(8,128)}, f32[64,64]{1,0:T(8,128)S(1)}) custom-call(s32[1]{0:T(128)S(6)} %sub.3.has_last, f32[256,128]{1,0:T(8,128)S(1)} %get-tuple-element.18.field_x, f32[512,128]{1,0:T(8,128)S(1)} %get-tuple-element.19.field_yz, f32[256,128]{1,0:T(8,128)S(1)} %get-tuple-element.20.m_x, ...), custom_call_target="tpu_custom_call" | custom-call | tf_op jit(solution)/shard_map/pallas_call | solution.py:317
  26.7 1.0 %collective-permute-done.7.far_cross = f32[32,128]{1,0:T(8,128)S(1)} collective-permute-done((f32[32,128]{1,0:T(8,128)S(1)}, f32[32,128]{1,0:T(8,128)S(1)}, u32[]{:S(2)}, u32[]{:S(2)}) %collective-permute-start.7) | collective-permute-done | bytes 16416 | tf_op jit(solution)/shard_map/ppermute | solution.py:329
  27.7 0.0 collective-permute-done.8.near
  27.7 1.0 %shard_map.95 = f32[64,64]{1,0:T(8,128)} custom-call(f32[64,64]{1,0:T(8,128)S(1)} %get-tuple-element.30.inverse, f32[32,128]{1,0:T(8,128)S(1)} %get-tuple-element.31.proj, f32[32,128]{1,0:T(8,128)S(1)} %collective-permute-done.7.far_cross, f32[64,128]{1,0:T(8,128)S(1)} %collective-permute-done.6.far, f32[32,128]{1,0:T(8,128)S(1)} %collective-permute-done.8.near), custom_call_target="tpu_custom_call" | custom-call | tf_op jit(solution)/shard_map/pallas_call | solution.py:317
  (4 shorter events, 0.0 us)
Async XLA Ops:
  0.6 1.0 %copy-start = (f32[64,3,1,4,128]{4,3,2,1,0:T(4,128)S(1)}, f32[64,3,1,4,128]{4,3,2,1,0:T(4,128)}, u32[]{:S(2)}) copy-start(f32[64,3,1,4,128]{4,3,2,1,0:T(4,128)} %param.5) | copy-start | bytes 1179652
  1.7 11.3 %collective-permute-start.1 = (f32[512,128]{1,0:T(8,128)S(1)}, f32[512,128]{1,0:T(8,128)S(1)}, u32[]{:S(2)}, u32[]{:S(2)}) collective-permute-start(f32[512,128]{1,0:T(8,128)S(1)} %get-tuple-element.19.field_yz), channel_id=1, source_target_pairs={{2,0},{4,2},{6,4},{8,6},{10,8},{12,10},{14,12},{3,1},{5,3},{7,5},{... | collective-permute-start | bytes 786440 | tf_op jit(solution)/shard_map/ppermute | solution.py:17
  3.5 2.4 %collective-permute-start = (f32[160,128]{1,0:T(8,128)S(1)}, f32[160,128]{1,0:T(8,128)S(1)}, u32[]{:S(2)}, u32[]{:S(2)}) collective-permute-start(f32[160,128]{1,0:T(8,128)S(1)} %shard_map.85.gram_edge), channel_id=1, source_target_pairs={{0,1},{1,0},{2,3},{3,2},{4,5},{5,4},{6,7},{7,6},{8,9},{9,8},{10,11... | collective-permute-start | bytes 245768 | tf_op jit(solution)/shard_map/ppermute | solution.py:329
  4.6 0.7 %copy-start.1 = (s32[1,4,128]{2,1,0:T(4,128)S(1)}, s32[1,4,128]{2,1,0:T(4,128)}, u32[]{:S(2)}) copy-start(s32[1,4,128]{2,1,0:T(4,128)} %param.6) | copy-start | bytes 6148
  4.6 0.7 %copy-start.2 = (f32[8]{0:T(128)S(1)}, f32[8]{0:T(128)}, u32[]{:S(2)}) copy-start(f32[8]{0:T(128)} %mu_table.1) | copy-start | bytes 100
  4.6 0.7 %copy-start.3 = (f32[8]{0:T(128)S(1)}, f32[8]{0:T(128)}, u32[]{:S(2)}) copy-start(f32[8]{0:T(128)} %eps_table.1) | copy-start | bytes 100
  6.0 7.5 %collective-permute-start.4 = (f32[32,128]{1,0:T(8,128)S(1)}, f32[32,128]{1,0:T(8,128)S(1)}, u32[]{:S(2)}, u32[]{:S(2)}) collective-permute-start(f32[32,128]{1,0:T(8,128)S(1)} %get-tuple-element.25.left), channel_id=1, source_target_pairs={{0,2},{2,0},{4,6},{6,4},{8,10},{10,8},{12,14},{14,12},{1,3},{3,1},... | collective-permute-start | bytes 49160 | tf_op jit(solution)/shard_map/ppermute | solution.py:329
  9.2 16.2 %collective-permute-start.2 = (f32[520,128]{1,0:T(8,128)S(1)}, f32[520,128]{1,0:T(8,128)S(1)}, u32[]{:S(2)}, u32[]{:S(2)}) collective-permute-start(f32[520,128]{1,0:T(8,128)S(1)} %get-tuple-element.23), channel_id=1, source_target_pairs={{0,2},{2,4},{4,6},{6,8},{8,10},{10,12},{12,14},{1,3},{3,5},{5,7},{... | collective-permute-start | bytes 798728 | tf_op jit(solution)/shard_map/ppermute | solution.py:17
  13.5 1.3 %collective-permute-start.3 = (f32[160,128]{1,0:T(8,128)S(1)}, f32[160,128]{1,0:T(8,128)S(1)}, u32[]{:S(2)}, u32[]{:S(2)}) collective-permute-start(f32[160,128]{1,0:T(8,128)S(1)} %get-tuple-element.24.edge), channel_id=1, source_target_pairs={{0,1},{1,0},{2,3},{3,2},{4,5},{5,4},{6,7},{7,6},{8,9},{9,8},{10,11... | collective-permute-start | bytes 245768 | tf_op jit(solution)/shard_map/ppermute | solution.py:329
  14.8 4.2 %collective-permute-start.5 = (f32[64,128]{1,0:T(8,128)S(1)}, f32[64,128]{1,0:T(8,128)S(1)}, u32[]{:S(2)}, u32[]{:S(2)}) collective-permute-start(f32[64,128]{1,0:T(8,128)S(1)} %shard_map.91.own), channel_id=1, source_target_pairs={{0,4},{2,6},{4,0},{6,2},{8,12},{10,14},{12,8},{14,10},{1,5},{3,7},... | collective-permute-start | bytes 98312 | tf_op jit(solution)/shard_map/ppermute | solution.py:329
  19.0 5.0 %collective-permute-start.6 = (f32[64,128]{1,0:T(8,128)S(1)}, f32[64,128]{1,0:T(8,128)S(1)}, u32[]{:S(2)}, u32[]{:S(2)}) collective-permute-start(f32[64,128]{1,0:T(8,128)S(1)} %get-tuple-element.26.sums), channel_id=1, source_target_pairs={{0,8},{2,10},{4,12},{6,14},{8,0},{10,2},{12,4},{14,6},{1,9},{3,11}... | collective-permute-start | bytes 98312 | tf_op jit(solution)/shard_map/ppermute | solution.py:329
  22.0 5.7 %collective-permute-start.7 = (f32[32,128]{1,0:T(8,128)S(1)}, f32[32,128]{1,0:T(8,128)S(1)}, u32[]{:S(2)}, u32[]{:S(2)}) collective-permute-start(f32[32,128]{1,0:T(8,128)S(1)} %get-tuple-element.31.proj), channel_id=1, source_target_pairs={{0,10},{2,8},{4,14},{6,12},{8,2},{10,0},{12,6},{14,4},{1,11},{3,9}... | collective-permute-start | bytes 49160 | tf_op jit(solution)/shard_map/ppermute | solution.py:329
  23.7 4.0 %collective-permute-start.8 = (f32[32,128]{1,0:T(8,128)S(1)}, f32[32,128]{1,0:T(8,128)S(1)}, u32[]{:S(2)}, u32[]{:S(2)}) collective-permute-start(f32[32,128]{1,0:T(8,128)S(1)} %get-tuple-element.31.proj), channel_id=1, source_target_pairs={{0,2},{2,0},{4,6},{6,4},{8,10},{10,8},{12,14},{14,12},{1,3},{3,1},... | collective-permute-start | bytes 49160 | tf_op jit(solution)/shard_map/ppermute | solution.py:329

commit v7 on v6

--- a/solution.py
+++ b/solution.py
@@ -15,6 +15,11 @@
     peers = lax.axis_size(axis)
     pairs = [(i, i + by) for i in range(peers) if 0 <= i + by < peers]
     return lax.ppermute(x, axis, pairs)
+
+
+def ringed(x, axis, by):
+    peers = lax.axis_size(axis)
+    return lax.ppermute(x, axis, [(i, (i + by) % peers) for i in range(peers)])
 
 
 def wide(chunks):
@@ -108,11 +113,11 @@
 
 
 def behind_kernel(
-    columns, cells, has_next, field_x, field_yz, gram_edge, ahead_y, material, out, out_gram
+    columns, cells, field_x, field_yz, gram_edge, ahead_y, material, out, out_gram
 ):
     half = columns // 2
     out_gram[...] = gram_edge[:half, :] + ahead_y[:half, :]
-    inside_next = has_next[0] > 0
+    inside_next = lax.axis_index("col") + 1 < lax.axis_size("col")
     mu = material[:cells, :]
     for y in range(cells):
         e_x = part(field_x, y, columns)
@@ -129,9 +134,9 @@
     )
 
 
-def near_kernel(columns, cells, has_next, field_x, field_yz, ahead_y, material, out_x, out_proj):
+def near_kernel(columns, cells, field_x, field_yz, ahead_y, material, out_x, out_proj):
     half = columns // 2
-    inside_next = has_next[0] > 0
+    inside_next = lax.axis_index("col") + 1 < lax.axis_size("col")
     left, right = [], []
     for y in range(cells):
         e_x = part(field_x, y, columns)
@@ -151,11 +156,11 @@
 
 
 def curl_kernel(
-    columns, cells, has_next, field_x, field_yz, ahead_x, ahead_y, material, m_x, near, out_yz,
+    columns, cells, field_x, field_yz, ahead_x, ahead_y, material, m_x, near, out_yz,
     out_edge,
 ):
     half = columns // 2
-    inside_next = has_next[0] > 0
+    inside_next = lax.axis_index("col") + 1 < lax.axis_size("col")
     left, right = [], []
     for y in range(cells):
         e_x = part(field_x, y, columns)
@@ -244,7 +249,7 @@
 
 
 def basis_kernel(
-    columns, cells, has_last, field_x, field_yz, m_x, m_yz, behind_x, behind_y, material, factors,
+    columns, cells, field_x, field_yz, m_x, m_yz, behind_x, behind_y, material, factors,
     out_basis, out_image, out_upper, out_inverse, basis, image, upper, sems,
 ):
     half = columns // 2
@@ -267,7 +272,7 @@
     fields = [part(field_x, y, columns) for y in range(cells)]
     fields += [part(field_yz, k, columns) for k in range(2 * cells)]
     first = write(fields, range(stride), basis, out_basis, sems.at[0])
-    inside_last = has_last[0] > 0
+    inside_last = lax.axis_index("col") > 0
     scaled_eps = material[cells:, :]
     images, places = [], []
     for y in range(cells):
@@ -340,9 +345,6 @@
     small, large = (cells * columns, lanes), (2 * cells * columns, lanes)
     edge, pair = (half + 2 * columns, lanes), (half, 2 * columns)
     square = (columns, columns)
-    place = lax.axis_index("col")
-    has_next = jnp.where(place == 0, 1, 0).astype(jnp.int32)[None]
-    has_last = 1 - has_next
 
     (material,) = call(
         material_kernel, (mu_table, eps_table, shift_value), (labels,), ((2 * cells, lanes),),
@@ -358,7 +360,7 @@
     ahead_y = swapped(gram_edge, "col", 1)
     sent, gram = call(
         functools.partial(behind_kernel, columns, cells),
-        (has_next,),
+        (),
         (field_x, field_yz, gram_edge, ahead_y, material),
         ((2 * cells * columns + -(-cells // 8) * 8, lanes), pair),
         flops=0,
@@ -367,14 +369,14 @@
     behind_x = shifted(sent, "row", 1)
     m_x, near = call(
         functools.partial(near_kernel, columns, cells),
-        (has_next,),
+        (),
         (field_x, field_yz, ahead_y, material),
         (small, pair),
         flops=0,
     )
     m_yz, proj_edge = call(
         functools.partial(curl_kernel, columns, cells),
-        (has_next,),
+        (),
         (field_x, field_yz, ahead_x, ahead_y, material, m_x, near),
         (large, edge),
         flops=10**10,
@@ -398,7 +400,7 @@
     )
     basis_out, image_out, upper, inverse = call(
         functools.partial(basis_kernel, columns, cells),
-        (has_last,),
+        (),
         (field_x, field_yz, m_x, m_yz, behind_x, behind_y, material, factors),
         (basis.shape, basis.shape, square, square),
         flops=0,

time: 29 us -> 29 us (level)
  no operation moved by 1% of the time
where the time goes in v7:
time: 29 us; the launch traced here: 28.8 us
  starting transfers between devices  14.2 us (49%)
  Pallas kernels  6.28 us (22%)
  waiting for transfers between devices  5.23 us (18%)
  local copies, waits for them, and re-layouts  1.64 us (6%)
  between operations  1.41 us (5%)
    ppermute x7, starting transfers between devices, swapped(): lax.ppermute(x, axis, [(i, i ^ step) for i in range(lax.axis_size(axis))])  11 us
    pallas_call x12, Pallas kernels, call(): pl.pallas_call(body, out_shape=shapes, in_specs=[SMEM] * len(scalars) + [...  6.28 us
    ppermute x7, waiting for transfers between devices, swapped(): lax.ppermute(x, axis, [(i, i ^ step) for i in range(lax.axis_size(axis))])  4.09 us
    ppermute x2, starting transfers between devices, shifted(): return lax.ppermute(x, axis, pairs)  3.23 us
    unnamed x8, local copies, waits for them, and re-layouts  1.64 us
    ppermute x2, waiting for transfers between devices, shifted(): return lax.ppermute(x, axis, pairs)  1.13 us
  transfers between devices with their start and end apart: 9, of which 4 were waited for; matrix products, arithmetic and copies ran while one was open for 0% of the time, Pallas kernels for 18%

profile of v7, /device:TPU:0, one launch (start us, length us, event | category | flops | bytes accessed | tf_op | source)
XLA Modules:
  0.0 28.8 jit_solution(18022963241942472087)
XLA Ops:
  0.6 0.0 copy-start
  0.6 1.0 %copy-done = f32[64,3,1,4,128]{4,3,2,1,0:T(4,128)S(1)} copy-done((f32[64,3,1,4,128]{4,3,2,1,0:T(4,128)S(1)}, f32[64,3,1,4,128]{4,3,2,1,0:T(4,128)}, u32[]{:S(2)}) %copy-start) | copy-done | bytes 393240
  1.7 1.3 %collective-permute-start.1 = (f32[512,128]{1,0:T(8,128)S(1)}, f32[512,128]{1,0:T(8,128)S(1)}, u32[]{:S(2)}, u32[]{:S(2)}) collective-permute-start(f32[512,128]{1,0:T(8,128)S(1)} %get-tuple-element.19.field_yz), channel_id=1, source_target_pairs={{2,0},{4,2},{6,4},{8,6},{10,8},{12,10},{14,12},{3,1},{5,3},{7,5},{... | collective-permute-start | bytes 786440 | tf_op jit(solution)/shard_map/ppermute | solution.py:17
  3.0 0.5 %shard_map.85.gram_edge = f32[160,128]{1,0:T(8,128)S(1)} custom-call(f32[256,128]{1,0:T(8,128)S(1)} %get-tuple-element.18.field_x, f32[512,128]{1,0:T(8,128)S(1)} %get-tuple-element.19.field_yz), custom_call_target="tpu_custom_call" | custom-call | tf_op jit(solution)/shard_map/pallas_call | solution.py:322
  3.5 0.0 copy-start.1
  3.5 0.5 %collective-permute-start = (f32[160,128]{1,0:T(8,128)S(1)}, f32[160,128]{1,0:T(8,128)S(1)}, u32[]{:S(2)}, u32[]{:S(2)}) collective-permute-start(f32[160,128]{1,0:T(8,128)S(1)} %shard_map.85.gram_edge), channel_id=1, source_target_pairs={{0,1},{1,0},{2,3},{3,2},{4,5},{5,4},{6,7},{7,6},{8,9},{9,8},{10,11... | collective-permute-start | bytes 245768 | tf_op jit(solution)/shard_map/ppermute | solution.py:334
  4.6 0.0 copy-start.2
  4.6 0.0 copy-start.3
  4.7 0.0 copy-done.1
  4.7 0.6 %copy-done.2 = f32[8]{0:T(128)S(1)} copy-done((f32[8]{0:T(128)S(1)}, f32[8]{0:T(128)}, u32[]{:S(2)}) %copy-start.2) | copy-done | bytes 56
  5.3 0.0 copy-done.3
  5.3 0.6 %shard_map.86.material = f32[8,128]{1,0:T(8,128)S(1)} custom-call(f32[8]{0:T(128)S(1)} %copy-done.2, f32[8]{0:T(128)S(1)} %copy-done.3, f32[1]{0:T(128)S(6)} %copy.11.shift, s32[4,128]{1,0:T(4,128)S(1)} %bitcast.9), custom_call_target="tpu_custom_call" | custom-call | tf_op jit(solution)/shard_map/pallas_call | solution.py:322
  5.9 0.0 collective-permute-done.ahead_y
  5.9 0.1 shard_map.89
  6.0 3.2 %collective-permute-start.4 = (f32[32,128]{1,0:T(8,128)S(1)}, f32[32,128]{1,0:T(8,128)S(1)}, u32[]{:S(2)}, u32[]{:S(2)}) collective-permute-start(f32[32,128]{1,0:T(8,128)S(1)} %get-tuple-element.25.left), channel_id=1, source_target_pairs={{0,2},{2,0},{4,6},{6,4},{8,10},{10,8},{12,14},{14,12},{1,3},{3,1},... | collective-permute-start | bytes 49160 | tf_op jit(solution)/shard_map/ppermute | solution.py:334
  9.2 1.9 %collective-permute-start.2 = (f32[520,128]{1,0:T(8,128)S(1)}, f32[520,128]{1,0:T(8,128)S(1)}, u32[]{:S(2)}, u32[]{:S(2)}) collective-permute-start(f32[520,128]{1,0:T(8,128)S(1)} %get-tuple-element.23), channel_id=1, source_target_pairs={{0,2},{2,4},{4,6},{6,8},{8,10},{10,12},{12,14},{1,3},{3,5},{5,7},{... | collective-permute-start | bytes 798728 | tf_op jit(solution)/shard_map/ppermute | solution.py:17
  11.1 0.7 %shard_map.87 = (f32[256,128]{1,0:T(8,128)S(1)}, f32[32,128]{1,0:T(8,128)S(1)}) custom-call(f32[256,128]{1,0:T(8,128)S(1)} %get-tuple-element.18.field_x, f32[512,128]{1,0:T(8,128)S(1)} %get-tuple-element.19.field_yz, f32[160,128]{1,0:T(8,128)S(1)} %collective-permute-done.ahead_y, f32[8,128]{1,0:T(8,128)S(1)} %shard_map.86.material), custom_call_target="tpu_custom_call" | custom-call | tf_op jit(solution)/shard_map/pallas_call | solution.py:322
  11.8 1.1 %collective-permute-done.1.ahead_x = f32[512,128]{1,0:T(8,128)S(1)} collective-permute-done((f32[512,128]{1,0:T(8,128)S(1)}, f32[512,128]{1,0:T(8,128)S(1)}, u32[]{:S(2)}, u32[]{:S(2)}) %collective-permute-start.1) | collective-permute-done | bytes 262176 | tf_op jit(solution)/shard_map/ppermute | solution.py:17
  13.0 0.5 %shard_map.88 = (f32[512,128]{1,0:T(8,128)S(1)}, f32[160,128]{1,0:T(8,128)S(1)}) custom-call(f32[256,128]{1,0:T(8,128)S(1)} %get-tuple-element.18.field_x, f32[512,128]{1,0:T(8,128)S(1)} %get-tuple-element.19.field_yz, f32[512,128]{1,0:T(8,128)S(1)} %collective-permute-done.1.ahead_x, f32[160,128]{1,0:T(8,128)S(1)} %collective-permute-done.ahead_y, ...), custom_call_target="tpu_custom_call" | custom-call | flops 10000000000 | tf_op jit(solution)/shard_map/pallas_call | solution.py:322
  13.5 0.0 collective-permute-start.3
  13.5 0.0 collective-permute-done.4.right
  13.5 1.2 %collective-permute-done.3.edge_other.behind_y = f32[160,128]{1,0:T(8,128)S(1)} collective-permute-done((f32[160,128]{1,0:T(8,128)S(1)}, f32[160,128]{1,0:T(8,128)S(1)}, u32[]{:S(2)}, u32[]{:S(2)}) %collective-permute-start.3) | collective-permute-done | bytes 81952 | tf_op jit(solution)/shard_map/ppermute | solution.py:334
  14.8 2.3 %collective-permute-start.5 = (f32[64,128]{1,0:T(8,128)S(1)}, f32[64,128]{1,0:T(8,128)S(1)}, u32[]{:S(2)}, u32[]{:S(2)}) collective-permute-start(f32[64,128]{1,0:T(8,128)S(1)} %shard_map.91.own), channel_id=1, source_target_pairs={{0,4},{2,6},{4,0},{6,2},{8,12},{10,14},{12,8},{14,10},{1,5},{3,7},... | collective-permute-start | bytes 98312 | tf_op jit(solution)/shard_map/ppermute | solution.py:334
  17.1 1.9 %collective-permute-done.5.both = f32[64,128]{1,0:T(8,128)S(1)} collective-permute-done((f32[64,128]{1,0:T(8,128)S(1)}, f32[64,128]{1,0:T(8,128)S(1)}, u32[]{:S(2)}, u32[]{:S(2)}) %collective-permute-start.5) | collective-permute-done | bytes 32800 | tf_op jit(solution)/shard_map/ppermute | solution.py:334
  19.0 3.0 %collective-permute-start.6 = (f32[64,128]{1,0:T(8,128)S(1)}, f32[64,128]{1,0:T(8,128)S(1)}, u32[]{:S(2)}, u32[]{:S(2)}) collective-permute-start(f32[64,128]{1,0:T(8,128)S(1)} %get-tuple-element.26.sums), channel_id=1, source_target_pairs={{0,8},{2,10},{4,12},{6,14},{8,0},{10,2},{12,4},{14,6},{1,9},{3,11}... | collective-permute-start | bytes 98312 | tf_op jit(solution)/shard_map/ppermute | solution.py:334
  22.0 1.7 %collective-permute-start.7 = (f32[32,128]{1,0:T(8,128)S(1)}, f32[32,128]{1,0:T(8,128)S(1)}, u32[]{:S(2)}, u32[]{:S(2)}) collective-permute-start(f32[32,128]{1,0:T(8,128)S(1)} %get-tuple-element.31.proj), channel_id=1, source_target_pairs={{0,10},{2,8},{4,14},{6,12},{8,2},{10,0},{12,6},{14,4},{1,11},{3,9}... | collective-permute-start | bytes 49160 | tf_op jit(solution)/shard_map/ppermute | solution.py:334
  23.7 0.2 collective-permute-start.8
  24.0 0.0 collective-permute-done.6.far
  24.0 1.4 %shard_map.93.factors = f32[64,128]{1,0:T(8,128)S(1)} custom-call(f32[64,128]{1,0:T(8,128)S(1)} %get-tuple-element.26.sums, f32[64,128]{1,0:T(8,128)S(1)} %collective-permute-done.6.far), custom_call_target="tpu_custom_call" | custom-call | tf_op jit(solution)/shard_map/pallas_call | solution.py:322
  25.4 0.0 collective-permute-done.2.behind_x
  25.4 1.3 %shard_map.94 = (f32[768,128]{1,0:T(8,128)}, f32[768,128]{1,0:T(8,128)}, f32[64,64]{1,0:T(8,128)}, f32[64,64]{1,0:T(8,128)S(1)}) custom-call(f32[256,128]{1,0:T(8,128)S(1)} %get-tuple-element.18.field_x, f32[512,128]{1,0:T(8,128)S(1)} %get-tuple-element.19.field_yz, f32[256,128]{1,0:T(8,128)S(1)} %get-tuple-element.20.m_x, ...), custom_call_target="tpu_custom_call" | custom-call | tf_op jit(solution)/shard_map/pallas_call | solution.py:322
  26.8 0.9 %collective-permute-done.7.far_cross = f32[32,128]{1,0:T(8,128)S(1)} collective-permute-done((f32[32,128]{1,0:T(8,128)S(1)}, f32[32,128]{1,0:T(8,128)S(1)}, u32[]{:S(2)}, u32[]{:S(2)}) %collective-permute-start.7) | collective-permute-done | bytes 16416 | tf_op jit(solution)/shard_map/ppermute | solution.py:334
  27.7 0.0 collective-permute-done.8.near
  27.7 1.0 %shard_map.95 = f32[64,64]{1,0:T(8,128)} custom-call(f32[64,64]{1,0:T(8,128)S(1)} %get-tuple-element.30.inverse, f32[32,128]{1,0:T(8,128)S(1)} %get-tuple-element.31.proj, f32[32,128]{1,0:T(8,128)S(1)} %collective-permute-done.7.far_cross, f32[64,128]{1,0:T(8,128)S(1)} %collective-permute-done.6.far, f32[32,128]{1,0:T(8,128)S(1)} %collective-permute-done.8.near), custom_call_target="tpu_custom_call" | custom-call | tf_op jit(solution)/shard_map/pallas_call | solution.py:322
  (4 shorter events, 0.0 us)
Async XLA Ops:
  0.6 1.0 %copy-start = (f32[64,3,1,4,128]{4,3,2,1,0:T(4,128)S(1)}, f32[64,3,1,4,128]{4,3,2,1,0:T(4,128)}, u32[]{:S(2)}) copy-start(f32[64,3,1,4,128]{4,3,2,1,0:T(4,128)} %param.5) | copy-start | bytes 1179652
  1.7 11.3 %collective-permute-start.1 = (f32[512,128]{1,0:T(8,128)S(1)}, f32[512,128]{1,0:T(8,128)S(1)}, u32[]{:S(2)}, u32[]{:S(2)}) collective-permute-start(f32[512,128]{1,0:T(8,128)S(1)} %get-tuple-element.19.field_yz), channel_id=1, source_target_pairs={{2,0},{4,2},{6,4},{8,6},{10,8},{12,10},{14,12},{3,1},{5,3},{7,5},{... | collective-permute-start | bytes 786440 | tf_op jit(solution)/shard_map/ppermute | solution.py:17
  3.5 1.2 %copy-start.1 = (s32[1,4,128]{2,1,0:T(4,128)S(1)}, s32[1,4,128]{2,1,0:T(4,128)}, u32[]{:S(2)}) copy-start(s32[1,4,128]{2,1,0:T(4,128)} %param.6) | copy-start | bytes 6148
  3.5 2.4 %collective-permute-start = (f32[160,128]{1,0:T(8,128)S(1)}, f32[160,128]{1,0:T(8,128)S(1)}, u32[]{:S(2)}, u32[]{:S(2)}) collective-permute-start(f32[160,128]{1,0:T(8,128)S(1)} %shard_map.85.gram_edge), channel_id=1, source_target_pairs={{0,1},{1,0},{2,3},{3,2},{4,5},{5,4},{6,7},{7,6},{8,9},{9,8},{10,11... | collective-permute-start | bytes 245768 | tf_op jit(solution)/shard_map/ppermute | solution.py:334
  4.6 0.7 %copy-start.2 = (f32[8]{0:T(128)S(1)}, f32[8]{0:T(128)}, u32[]{:S(2)}) copy-start(f32[8]{0:T(128)} %mu_table.1) | copy-start | bytes 100
  4.6 0.7 %copy-start.3 = (f32[8]{0:T(128)S(1)}, f32[8]{0:T(128)}, u32[]{:S(2)}) copy-start(f32[8]{0:T(128)} %eps_table.1) | copy-start | bytes 100
  6.0 7.5 %collective-permute-start.4 = (f32[32,128]{1,0:T(8,128)S(1)}, f32[32,128]{1,0:T(8,128)S(1)}, u32[]{:S(2)}, u32[]{:S(2)}) collective-permute-start(f32[32,128]{1,0:T(8,128)S(1)} %get-tuple-element.25.left), channel_id=1, source_target_pairs={{0,2},{2,0},{4,6},{6,4},{8,10},{10,8},{12,14},{14,12},{1,3},{3,1},... | collective-permute-start | bytes 49160 | tf_op jit(solution)/shard_map/ppermute | solution.py:334
  9.2 16.2 %collective-permute-start.2 = (f32[520,128]{1,0:T(8,128)S(1)}, f32[520,128]{1,0:T(8,128)S(1)}, u32[]{:S(2)}, u32[]{:S(2)}) collective-permute-start(f32[520,128]{1,0:T(8,128)S(1)} %get-tuple-element.23), channel_id=1, source_target_pairs={{0,2},{2,4},{4,6},{6,8},{8,10},{10,12},{12,14},{1,3},{3,5},{5,7},{... | collective-permute-start | bytes 798728 | tf_op jit(solution)/shard_map/ppermute | solution.py:17
  13.5 1.3 %collective-permute-start.3 = (f32[160,128]{1,0:T(8,128)S(1)}, f32[160,128]{1,0:T(8,128)S(1)}, u32[]{:S(2)}, u32[]{:S(2)}) collective-permute-start(f32[160,128]{1,0:T(8,128)S(1)} %get-tuple-element.24.edge), channel_id=1, source_target_pairs={{0,1},{1,0},{2,3},{3,2},{4,5},{5,4},{6,7},{7,6},{8,9},{9,8},{10,11... | collective-permute-start | bytes 245768 | tf_op jit(solution)/shard_map/ppermute | solution.py:334
  14.8 4.2 %collective-permute-start.5 = (f32[64,128]{1,0:T(8,128)S(1)}, f32[64,128]{1,0:T(8,128)S(1)}, u32[]{:S(2)}, u32[]{:S(2)}) collective-permute-start(f32[64,128]{1,0:T(8,128)S(1)} %shard_map.91.own), channel_id=1, source_target_pairs={{0,4},{2,6},{4,0},{6,2},{8,12},{10,14},{12,8},{14,10},{1,5},{3,7},... | collective-permute-start | bytes 98312 | tf_op jit(solution)/shard_map/ppermute | solution.py:334
  19.0 5.0 %collective-permute-start.6 = (f32[64,128]{1,0:T(8,128)S(1)}, f32[64,128]{1,0:T(8,128)S(1)}, u32[]{:S(2)}, u32[]{:S(2)}) collective-permute-start(f32[64,128]{1,0:T(8,128)S(1)} %get-tuple-element.26.sums), channel_id=1, source_target_pairs={{0,8},{2,10},{4,12},{6,14},{8,0},{10,2},{12,4},{14,6},{1,9},{3,11}... | collective-permute-start | bytes 98312 | tf_op jit(solution)/shard_map/ppermute | solution.py:334
  22.0 5.7 %collective-permute-start.7 = (f32[32,128]{1,0:T(8,128)S(1)}, f32[32,128]{1,0:T(8,128)S(1)}, u32[]{:S(2)}, u32[]{:S(2)}) collective-permute-start(f32[32,128]{1,0:T(8,128)S(1)} %get-tuple-element.31.proj), channel_id=1, source_target_pairs={{0,10},{2,8},{4,14},{6,12},{8,2},{10,0},{12,6},{14,4},{1,11},{3,9}... | collective-permute-start | bytes 49160 | tf_op jit(solution)/shard_map/ppermute | solution.py:334
  23.7 4.0 %collective-permute-start.8 = (f32[32,128]{1,0:T(8,128)S(1)}, f32[32,128]{1,0:T(8,128)S(1)}, u32[]{:S(2)}, u32[]{:S(2)}) collective-permute-start(f32[32,128]{1,0:T(8,128)S(1)} %get-tuple-element.31.proj), channel_id=1, source_target_pairs={{0,2},{2,0},{4,6},{6,4},{8,10},{10,8},{12,14},{14,12},{1,3},{3,1},... | collective-permute-start | bytes 49160 | tf_op jit(solution)/shard_map/ppermute | solution.py:334

commit v8 on v7

--- a/solution.py
+++ b/solution.py
@@ -11,15 +11,11 @@
 BF16 = jnp.bfloat16
 
 
-def shifted(x, axis, by):
-    peers = lax.axis_size(axis)
-    pairs = [(i, i + by) for i in range(peers) if 0 <= i + by < peers]
-    return lax.ppermute(x, axis, pairs)
-
-
-def ringed(x, axis, by):
-    peers = lax.axis_size(axis)
-    return lax.ppermute(x, axis, [(i, (i + by) % peers) for i in range(peers)])
+def halo_ring(rows, back):
+    ahead = [((r, 0), (r - 1, 0)) for r in range(1, rows)] + [((0, 0), (0, 1))]
+    ahead += [((r, 1), (r + 1, 1)) for r in range(rows - 1)] + [((rows - 1, 1), (rows - 1, 0))]
+    pairs = [(2 * r + c, 2 * to_r + to_c) for (r, c), (to_r, to_c) in ahead]
+    return [(j, i) for i, j in pairs] if back else pairs
 
 
 def wide(chunks):
@@ -88,11 +84,23 @@
     return jnp.concatenate([pair[:, :half], pair[:, half:]], axis=0)
 
 
-def pack_kernel(columns, cells, basis, out_x, out_yz):
+def first_core():
+    return lax.axis_index("col") == 0
+
+
+def pack_kernel(columns, cells, basis, out_x, out_yz, out_send):
     stride = 3 * cells
-    for k in range(stride):
-        ref, at = (out_x, k) if k < cells else (out_yz, k - cells)
-        ref[at * columns : (at + 1) * columns, :] = basis[pl.ds(k, columns, stride=stride), :]
+    chunks = [basis[pl.ds(k, columns, stride=stride), :] for k in range(stride)]
+    down = first_core()
+    for y in range(cells):
+        e_x, e_y, e_z = chunks[y], chunks[cells + y], chunks[2 * cells + y]
+        e_x_up = chunks[y + 1] if y + 1 < cells else jnp.zeros_like(e_x)
+        at, other = y * columns, (cells + y) * columns
+        out_x[at : at + columns, :] = e_x
+        out_yz[at : at + columns, :] = e_y
+        out_yz[other : other + columns, :] = e_z
+        out_send[at : at + columns, :] = jnp.where(down, e_y, forward_z(e_x) + e_z)
+        out_send[other : other + columns, :] = jnp.where(down, e_z, (e_x - e_x_up) - e_y)
 
 
 def material_kernel(mu_table, eps_table, shift, regions, out):
@@ -112,31 +120,25 @@
     out[:half, :] = packed(inner(flat, flat))
 
 
-def behind_kernel(
-    columns, cells, field_x, field_yz, gram_edge, ahead_y, material, out, out_gram
-):
+def open_kernel(columns, cells, field_x, field_yz, gram_edge, ahead_y, out_open, out_gram):
     half = columns // 2
     out_gram[...] = gram_edge[:half, :] + ahead_y[:half, :]
-    inside_next = lax.axis_index("col") + 1 < lax.axis_size("col")
-    mu = material[:cells, :]
+    inside = first_core()
     for y in range(cells):
         e_x = part(field_x, y, columns)
         if y + 1 < cells:
             e_x_up = part(field_x, y + 1, columns)
         else:
-            e_x_up = jnp.where(inside_next, ahead_y[half : half + columns, :], 0.0)
+            e_x_up = jnp.where(inside, ahead_y[half : half + columns, :], 0.0)
         e_y, e_z = part(field_yz, y, columns), part(field_yz, cells + y, columns)
-        mu_row = mu[y : y + 1, :]
-        out[y * columns : (y + 1) * columns, :] = mu_row * (forward_z(e_x) + e_z)
-        out[(cells + y) * columns : (cells + y + 1) * columns, :] = -mu_row * (e_y + (e_x_up - e_x))
-    out[2 * cells * columns :, :] = jnp.concatenate(
-        [mu, jnp.zeros((out.shape[0] - 2 * cells * columns - cells, mu.shape[1]), F32)], axis=0
-    )
-
-
-def near_kernel(columns, cells, field_x, field_yz, ahead_y, material, out_x, out_proj):
+        at, other = y * columns, (cells + y) * columns
+        out_open[at : at + columns, :] = forward_z(e_x) + e_z
+        out_open[other : other + columns, :] = (e_x - e_x_up) - e_y
+
+
+def near_kernel(columns, cells, field_x, field_yz, ahead_y, material, open_yz, out_x, out_proj):
     half = columns // 2
-    inside_next = lax.axis_index("col") + 1 < lax.axis_size("col")
+    inside = first_core()
     left, right = [], []
     for y in range(cells):
         e_x = part(field_x, y, columns)
@@ -145,43 +147,55 @@
         if y + 1 < cells:
             e_z_up = part(field_yz, cells + y + 1, columns)
         else:
-            e_z_up = jnp.where(inside_next, ahead_y[half + columns :, :], 0.0)
+            e_z_up = jnp.where(inside, ahead_y[half + columns :, :], 0.0)
         curl_x = (e_z_up - e_z) - forward_z(e_y)
-        m_x = material[y : y + 1, :] * curl_x
+        mu = material[y : y + 1, :]
         eps = -material[cells + y : cells + y + 1, :]
+        m_x = mu * curl_x
+        open_y, open_z = part(open_yz, y, columns), part(open_yz, cells + y, columns)
         out_x[y * columns : (y + 1) * columns, :] = m_x
-        left += [curl_x, e_x, e_y, e_z]
-        right += [m_x, eps * e_x, eps * e_y, eps * e_z]
+        left += [curl_x, e_x, e_y, e_z, open_y, open_z]
+        right += [m_x, eps * e_x, eps * e_y, eps * e_z, mu * open_y, mu * open_z]
     out_proj[...] = packed(inner(wide(left), wide(right)))
 
 
+def below_top():
+    return lax.axis_index("row") + 1 < lax.axis_size("row")
+
+
+def above_bottom():
+    return lax.axis_index("row") > 0
+
+
 def curl_kernel(
-    columns, cells, field_x, field_yz, ahead_x, ahead_y, material, m_x, near, out_yz,
-    out_edge,
+    columns, cells, field_yz, received, mu_received, open_yz, material, m_x, near, out_edge, out_send
 ):
     half = columns // 2
-    inside_next = lax.axis_index("col") + 1 < lax.axis_size("col")
+    ahead = first_core()
+    behind = jnp.logical_and(jnp.logical_not(ahead), above_bottom())
+    ahead_here = jnp.logical_and(ahead, below_top())
     left, right = [], []
     for y in range(cells):
-        e_x = part(field_x, y, columns)
-        e_y = part(field_yz, y, columns)
-        e_z = part(field_yz, cells + y, columns)
-        if y + 1 < cells:
-            e_x_up = part(field_x, y + 1, columns)
-        else:
-            e_x_up = jnp.where(inside_next, ahead_y[half : half + columns, :], 0.0)
-        curl_y = forward_z(e_x) - (part(ahead_x, cells + y, columns) - e_z)
-        curl_z = (part(ahead_x, y, columns) - e_y) - (e_x_up - e_x)
-        mu = material[y : y + 1, :]
-        m_y, m_z = mu * curl_y, mu * curl_z
-        out_yz[y * columns : (y + 1) * columns, :] = m_y
-        out_yz[(cells + y) * columns : (cells + y + 1) * columns, :] = m_z
+        at, other = y * columns, (cells + y) * columns
+        got_y, got_z = part(received, y, columns), part(received, cells + y, columns)
+        own_y, own_z = part(field_yz, y, columns), part(field_yz, cells + y, columns)
+        open_y, open_z = part(open_yz, y, columns), part(open_yz, cells + y, columns)
+        mu_got = jnp.where(behind, mu_received[y : y + 1, :], 0.0)
+        mu = jnp.where(ahead, material[y : y + 1, :], mu_got)
+        out_send[at : at + columns, :] = jnp.where(ahead, open_y, own_y)
+        out_send[other : other + columns, :] = jnp.where(ahead, open_z, own_z)
+        open_y = jnp.where(ahead, open_y, jnp.where(behind, got_y, 0.0))
+        open_z = jnp.where(ahead, open_z, jnp.where(behind, got_z, 0.0))
+        e_y = jnp.where(ahead, jnp.where(ahead_here, got_y, 0.0), own_y)
+        e_z = jnp.where(ahead, jnp.where(ahead_here, got_z, 0.0), own_z)
+        left += [e_z, e_y]
+        right += [mu * (0.5 * e_z - open_y), mu * (0.5 * e_y + open_z)]
         if y + 1 == cells:
-            out_edge[half + columns :, :] = m_z
-        left += [curl_y, curl_z]
-        right += [m_y, m_z]
+            out_edge[half + columns :, :] = mu * (open_z + e_y)
+    out_send[2 * cells * columns :, :] = material[...]
     out_edge[half : half + columns, :] = part(m_x, cells - 1, columns)
-    out_edge[:half, :] = near[...] + packed(inner(wide(left), wide(right)))
+    crossing = inner(wide(left), wide(right))
+    out_edge[:half, :] = near[...] + packed(crossing + crossing.T)
 
 
 def add_kernel(left, right, out):
@@ -249,7 +263,8 @@
 
 
 def basis_kernel(
-    columns, cells, field_x, field_yz, m_x, m_yz, behind_x, behind_y, material, factors,
+    columns, cells, field_x, field_yz, m_x, open_yz, first_got, mu_received, second_got, behind_y,
+    material, factors,
     out_basis, out_image, out_upper, out_inverse, basis, image, upper, sems,
 ):
     half = columns // 2
@@ -271,21 +286,33 @@
 
     fields = [part(field_x, y, columns) for y in range(cells)]
     fields += [part(field_yz, k, columns) for k in range(2 * cells)]
-    first = write(fields, range(stride), basis, out_basis, sems.at[0])
-    inside_last = lax.axis_index("col") > 0
+    first_copy = write(fields, range(stride), basis, out_basis, sems.at[0])
+    ahead = first_core()
+    top, bottom = below_top(), above_bottom()
     scaled_eps = material[cells:, :]
     images, places = [], []
+    m_z_down = None
     for y in range(cells):
         e = [part(field_x, y, columns), part(field_yz, y, columns), part(field_yz, cells + y, columns)]
-        m = [part(m_x, y, columns), part(m_yz, y, columns), part(m_yz, cells + y, columns)]
+        last = 2 * cells * columns + y
+        mu = material[y : y + 1, :]
+        first = part(first_got, y, columns), part(first_got, cells + y, columns)
+        second = part(second_got, y, columns), part(second_got, cells + y, columns)
+        e_y_next = jnp.where(top, jnp.where(ahead, first[0], second[0]), 0.0)
+        e_z_next = jnp.where(top, jnp.where(ahead, first[1], second[1]), 0.0)
+        m = [
+            part(m_x, y, columns),
+            mu * (part(open_yz, y, columns) - e_z_next),
+            mu * (part(open_yz, cells + y, columns) + e_y_next),
+        ]
         if y > 0:
-            m_x_down, m_z_down = part(m_x, y - 1, columns), part(m_yz, cells + y - 1, columns)
+            m_x_down = part(m_x, y - 1, columns)
         else:
-            m_x_down = jnp.where(inside_last, behind_y[half : half + columns, :], 0.0)
-            m_z_down = jnp.where(inside_last, behind_y[half + columns :, :], 0.0)
-        mu_last = behind_x[2 * cells * columns + y : 2 * cells * columns + y + 1, :]
-        m_y_last = part(behind_x, y, columns) - mu_last * e[2]
-        m_z_last = part(behind_x, cells + y, columns) + mu_last * e[1]
+            m_x_down = jnp.where(ahead, 0.0, behind_y[half : half + columns, :])
+            m_z_down = jnp.where(ahead, 0.0, behind_y[half + columns :, :])
+        mu_last = jnp.where(ahead, second_got[last : last + 1, :], mu_received[y : y + 1, :])
+        m_y_last = jnp.where(bottom, mu_last * (jnp.where(ahead, second[0], first[0]) - e[2]), 0.0)
+        m_z_last = jnp.where(bottom, mu_last * (jnp.where(ahead, second[1], first[1]) + e[1]), 0.0)
         eps = scaled_eps[y : y + 1, :]
         images += [
             (m[2] - m_z_down) - backward_z(m[1]) - eps * e[0],
@@ -293,9 +320,10 @@
             (m[1] - m_y_last) - (m[0] - m_x_down) - eps * e[2],
         ]
         places += [y, cells + y, 2 * cells + y]
-    second = write(images, places, image, out_image, sems.at[1])
-    first.wait()
-    second.wait()
+        m_z_down = m[2]
+    second_copy = write(images, places, image, out_image, sems.at[1])
+    first_copy.wait()
+    second_copy.wait()
     third.wait()
 
 
@@ -350,40 +378,41 @@
         material_kernel, (mu_table, eps_table, shift_value), (labels,), ((2 * cells, lanes),),
         flops=0,
     )
-    field_x, field_yz = call(
-        functools.partial(pack_kernel, columns, cells), (), (basis,), (small, large), flops=0
-    )
-    ahead_x = shifted(field_yz, "row", -1)
+    field_x, field_yz, send = call(
+        functools.partial(pack_kernel, columns, cells), (), (basis,), (small, large, large), flops=0
+    )
+    first_got = lax.ppermute(send, ("row", "col"), halo_ring(rows, False))
     (gram_edge,) = call(
         functools.partial(gram_kernel, columns, cells), (), (field_x, field_yz), (edge,), flops=0
     )
     ahead_y = swapped(gram_edge, "col", 1)
-    sent, gram = call(
-        functools.partial(behind_kernel, columns, cells),
+    mu_received = lax.ppermute(material, ("row", "col"), halo_ring(rows, False))
+    open_yz, gram = call(
+        functools.partial(open_kernel, columns, cells),
         (),
-        (field_x, field_yz, gram_edge, ahead_y, material),
-        ((2 * cells * columns + -(-cells // 8) * 8, lanes), pair),
+        (field_x, field_yz, gram_edge, ahead_y),
+        (large, pair),
         flops=0,
     )
     gram_other = swapped(gram, "row", 1)
-    behind_x = shifted(sent, "row", 1)
     m_x, near = call(
         functools.partial(near_kernel, columns, cells),
         (),
-        (field_x, field_yz, ahead_y, material),
+        (field_x, field_yz, ahead_y, material, open_yz),
         (small, pair),
         flops=0,
     )
-    m_yz, proj_edge = call(
+    proj_edge, send = call(
         functools.partial(curl_kernel, columns, cells),
         (),
-        (field_x, field_yz, ahead_x, ahead_y, material, m_x, near),
-        (large, edge),
+        (field_yz, first_got, mu_received, open_yz, material, m_x, near),
+        (edge, (2 * cells * (columns + 1), lanes)),
         flops=10**10,
     )
-    both = (2 * half, 2 * columns)
+    second_got = lax.ppermute(send, ("row", "col"), halo_ring(rows, True))
     (gram,) = call(add_kernel, (), (gram, gram_other), (pair,), flops=10**10)
     behind_y = swapped(proj_edge, "col", 1)
+    both = (2 * half, 2 * columns)
     (own,) = call(join_kernel, (), (gram, proj_edge, behind_y), (both,), flops=0)
     next_both = swapped(own, "row", 2)
     sums, proj = call(sum_kernel, (), (own, next_both), (both, pair), flops=0)
@@ -401,7 +430,10 @@
     basis_out, image_out, upper, inverse = call(
         functools.partial(basis_kernel, columns, cells),
         (),
-        (field_x, field_yz, m_x, m_yz, behind_x, behind_y, material, factors),
+        (
+            field_x, field_yz, m_x, open_yz, first_got, mu_received, second_got, behind_y, material,
+            factors,
+        ),
         (basis.shape, basis.shape, square, square),
         flops=0,
         far=3,

time: 29 us -> 28.3 us (0.976)
  waiting for transfers between devices: 5.23 us -> 3.79 us
  starting transfers between devices: 14.2 us -> 14.7 us
  Pallas kernels: 6.28 us -> 6.64 us
    ppermute x7, starting transfers between devices: 11 us -> 12.2 us  [swapped(): lax.ppermute(x, axis, [(i, i ^ step) for i in range(lax.axis_size(axis))])]
    ppermute x7, waiting for transfers between devices: 4.09 us -> 3.32 us  [swapped(): lax.ppermute(x, axis, [(i, i ^ step) for i in range(lax.axis_size(axis))])]
    ppermute x2 -> x3, starting transfers between devices: 3.23 us -> 2.47 us  [the longest x1 1.89 us: local(): second_got = lax.ppermute(send, ('row', 'col'), halo_ring(rows, True))]
    ppermute x2 -> x3, waiting for transfers between devices: 1.13 us -> 0.47 us  [the longest x1 0.46 us: local(): mu_received = lax.ppermute(material, ('row', 'col'), halo_ring(rows, False))]
    pallas_call x12, Pallas kernels: 6.28 us -> 6.64 us  [call(): pl.pallas_call(body, out_shape=shapes, in_specs=[SMEM] * len(scalars) + [...]
  transfers between devices with their start and end apart: 9 -> 10, of which waited for: 4 -> 3; matrix products, arithmetic and copies ran while one was open for 0% -> 0% of each run, Pallas kernels for 18% -> 19%
where the time goes in v8:
time: 28.3 us; the launch traced here: 28.2 us
  starting transfers between devices  14.7 us (52%)
  Pallas kernels  6.64 us (23%)
  waiting for transfers between devices  3.79 us (13%)
  local copies, waits for them, and re-layouts  1.64 us (6%)
  between operations  1.39 us (5%)
    ppermute x7, starting transfers between devices, swapped(): lax.ppermute(x, axis, [(i, i ^ step) for i in range(lax.axis_size(axis))])  12.2 us
    pallas_call x12, Pallas kernels, call(): pl.pallas_call(body, out_shape=shapes, in_specs=[SMEM] * len(scalars) + [...  6.64 us
    ppermute x7, waiting for transfers between devices, swapped(): lax.ppermute(x, axis, [(i, i ^ step) for i in range(lax.axis_size(axis))])  3.32 us
    ppermute x1, starting transfers between devices, local(): second_got = lax.ppermute(send, ('row', 'col'), halo_ring(rows, True))  1.89 us
    unnamed x8, local copies, waits for them, and re-layouts  1.64 us
  transfers between devices with their start and end apart: 10, of which 3 were waited for; matrix products, arithmetic and copies ran while one was open for 0% of the time, Pallas kernels for 19%

profile of v8, /device:TPU:0, one launch (start us, length us, event | category | flops | bytes accessed | tf_op | source)
XLA Modules:
  0.0 28.2 jit_solution(11054805113882681695)
XLA Ops:
  0.6 0.0 copy-start
  0.6 1.0 %copy-done = f32[64,3,1,4,128]{4,3,2,1,0:T(4,128)S(1)} copy-done((f32[64,3,1,4,128]{4,3,2,1,0:T(4,128)S(1)}, f32[64,3,1,4,128]{4,3,2,1,0:T(4,128)}, u32[]{:S(2)}) %copy-start) | copy-done | bytes 393240
  1.6 0.1 shard_map.84
  1.7 0.5 %collective-permute-start.1 = (f32[512,128]{1,0:T(8,128)S(1)}, f32[512,128]{1,0:T(8,128)S(1)}, u32[]{:S(2)}, u32[]{:S(2)}) collective-permute-start(f32[512,128]{1,0:T(8,128)S(1)} %get-tuple-element.23), channel_id=1, source_target_pairs={{2,0},{4,2},{6,4},{8,6},{10,8},{12,10},{14,12},{0,1},{1,3},{3,5},{... | collective-permute-start | bytes 786440 | tf_op jit(solution)/shard_map/ppermute | solution.py:384
  2.2 0.5 %shard_map.85.gram_edge = f32[160,128]{1,0:T(8,128)S(1)} custom-call(f32[256,128]{1,0:T(8,128)S(1)} %get-tuple-element.19.field_x, f32[512,128]{1,0:T(8,128)S(1)} %get-tuple-element.20.field_yz), custom_call_target="tpu_custom_call" | custom-call | tf_op jit(solution)/shard_map/pallas_call | solution.py:350
  2.8 0.0 copy-start.1
  2.8 2.1 %collective-permute-start = (f32[160,128]{1,0:T(8,128)S(1)}, f32[160,128]{1,0:T(8,128)S(1)}, u32[]{:S(2)}, u32[]{:S(2)}) collective-permute-start(f32[160,128]{1,0:T(8,128)S(1)} %shard_map.85.gram_edge), channel_id=1, source_target_pairs={{0,1},{1,0},{2,3},{3,2},{4,5},{5,4},{6,7},{7,6},{8,9},{9,8},{10,11... | collective-permute-start | bytes 245768 | tf_op jit(solution)/shard_map/ppermute | solution.py:362
  5.5 0.0 copy-start.2
  5.5 0.0 copy-start.3
  5.5 0.0 copy-done.1
  5.5 0.6 %copy-done.2 = f32[8]{0:T(128)S(1)} copy-done((f32[8]{0:T(128)S(1)}, f32[8]{0:T(128)}, u32[]{:S(2)}) %copy-start.2) | copy-done | bytes 56
  6.2 0.0 copy-done.3
  6.2 0.6 %shard_map.86.material = f32[8,128]{1,0:T(8,128)S(1)} custom-call(f32[8]{0:T(128)S(1)} %copy-done.2, f32[8]{0:T(128)S(1)} %copy-done.3, f32[1]{0:T(128)S(6)} %copy.11.shift, s32[4,128]{1,0:T(4,128)S(1)} %bitcast.9), custom_call_target="tpu_custom_call" | custom-call | tf_op jit(solution)/shard_map/pallas_call | solution.py:350
  6.7 0.1 collective-permute-start.2
  6.8 0.0 collective-permute-done.ahead_y
  6.8 0.1 shard_map.87
  6.9 2.1 %collective-permute-start.5 = (f32[32,128]{1,0:T(8,128)S(1)}, f32[32,128]{1,0:T(8,128)S(1)}, u32[]{:S(2)}, u32[]{:S(2)}) collective-permute-start(f32[32,128]{1,0:T(8,128)S(1)} %get-tuple-element.27.left), channel_id=1, source_target_pairs={{0,2},{2,0},{4,6},{6,4},{8,10},{10,8},{12,14},{14,12},{1,3},{3,1},... | collective-permute-start | bytes 49160 | tf_op jit(solution)/shard_map/ppermute | solution.py:362
  9.0 0.9 %shard_map.88 = (f32[256,128]{1,0:T(8,128)S(1)}, f32[32,128]{1,0:T(8,128)S(1)}) custom-call(f32[256,128]{1,0:T(8,128)S(1)} %get-tuple-element.19.field_x, f32[512,128]{1,0:T(8,128)S(1)} %get-tuple-element.20.field_yz, f32[160,128]{1,0:T(8,128)S(1)} %collective-permute-done.ahead_y, f32[8,128]{1,0:T(8,128)S(1)} %shard_map.86.material, ...), custom_call_target="tpu_custom_call" | custom-call | tf_op jit(solution)/shard_map/pallas_call | solution.py:350
  9.9 0.5 %collective-permute-done.2.mu_received = f32[8,128]{1,0:T(8,128)S(1)} collective-permute-done((f32[8,128]{1,0:T(8,128)S(1)}, f32[8,128]{1,0:T(8,128)S(1)}, u32[]{:S(2)}, u32[]{:S(2)}) %collective-permute-start.2) | collective-permute-done | bytes 4128 | tf_op jit(solution)/shard_map/ppermute | solution.py:389
  10.4 0.0 collective-permute-done.1.received.first_got
  10.4 0.6 %shard_map.89 = (f32[160,128]{1,0:T(8,128)S(1)}, f32[520,128]{1,0:T(8,128)S(1)}) custom-call(f32[512,128]{1,0:T(8,128)S(1)} %get-tuple-element.20.field_yz, f32[512,128]{1,0:T(8,128)S(1)} %collective-permute-done.1.received.first_got, f32[8,128]{1,0:T(8,128)S(1)} %collective-permute-done.2.mu_received, f32[512,128]{1,0:T(8,128)S(1)} %get-tuple-element.21.open_yz, ...), custom_call_target="tpu_custom_call" | custom-call | flops 10000000000 | tf_op jit(solution)/shard_map/pallas_call | solution.py:350
  11.0 0.9 %collective-permute-start.4 = (f32[160,128]{1,0:T(8,128)S(1)}, f32[160,128]{1,0:T(8,128)S(1)}, u32[]{:S(2)}, u32[]{:S(2)}) collective-permute-start(f32[160,128]{1,0:T(8,128)S(1)} %get-tuple-element.26.edge), channel_id=1, source_target_pairs={{0,1},{1,0},{2,3},{3,2},{4,5},{5,4},{6,7},{7,6},{8,9},{9,8},{10,11... | collective-permute-start | bytes 245768 | tf_op jit(solution)/shard_map/ppermute | solution.py:362
  11.8 1.9 %collective-permute-start.3 = (f32[520,128]{1,0:T(8,128)S(1)}, f32[520,128]{1,0:T(8,128)S(1)}, u32[]{:S(2)}, u32[]{:S(2)}) collective-permute-start(f32[520,128]{1,0:T(8,128)S(1)} %get-tuple-element.25), channel_id=1, source_target_pairs={{0,2},{2,4},{4,6},{6,8},{8,10},{10,12},{12,14},{1,0},{3,1},{5,3},{... | collective-permute-start | bytes 798728 | tf_op jit(solution)/shard_map/ppermute | solution.py:412
  13.7 0.0 collective-permute-done.5.right
  13.7 0.0 collective-permute-done.4.edge_other.behind_y
  13.8 2.1 %collective-permute-start.6 = (f32[64,128]{1,0:T(8,128)S(1)}, f32[64,128]{1,0:T(8,128)S(1)}, u32[]{:S(2)}, u32[]{:S(2)}) collective-permute-start(f32[64,128]{1,0:T(8,128)S(1)} %shard_map.91.own), channel_id=1, source_target_pairs={{0,4},{2,6},{4,0},{6,2},{8,12},{10,14},{12,8},{14,10},{1,5},{3,7},... | collective-permute-start | bytes 98312 | tf_op jit(solution)/shard_map/ppermute | solution.py:362
  15.9 2.3 %collective-permute-done.6.both = f32[64,128]{1,0:T(8,128)S(1)} collective-permute-done((f32[64,128]{1,0:T(8,128)S(1)}, f32[64,128]{1,0:T(8,128)S(1)}, u32[]{:S(2)}, u32[]{:S(2)}) %collective-permute-start.6) | collective-permute-done | bytes 32800 | tf_op jit(solution)/shard_map/ppermute | solution.py:362
  18.2 3.0 %collective-permute-start.7 = (f32[64,128]{1,0:T(8,128)S(1)}, f32[64,128]{1,0:T(8,128)S(1)}, u32[]{:S(2)}, u32[]{:S(2)}) collective-permute-start(f32[64,128]{1,0:T(8,128)S(1)} %get-tuple-element.28.sums), channel_id=1, source_target_pairs={{0,8},{2,10},{4,12},{6,14},{8,0},{10,2},{12,4},{14,6},{1,9},{3,11}... | collective-permute-start | bytes 98312 | tf_op jit(solution)/shard_map/ppermute | solution.py:362
  21.2 1.8 %collective-permute-start.8 = (f32[32,128]{1,0:T(8,128)S(1)}, f32[32,128]{1,0:T(8,128)S(1)}, u32[]{:S(2)}, u32[]{:S(2)}) collective-permute-start(f32[32,128]{1,0:T(8,128)S(1)} %get-tuple-element.33.proj), channel_id=1, source_target_pairs={{0,10},{2,8},{4,14},{6,12},{8,2},{10,0},{12,6},{14,4},{1,11},{3,9}... | collective-permute-start | bytes 49160 | tf_op jit(solution)/shard_map/ppermute | solution.py:362
  23.0 0.2 collective-permute-start.9
  23.3 0.0 collective-permute-done.7.far
  23.3 1.4 %shard_map.93.factors = f32[64,128]{1,0:T(8,128)S(1)} custom-call(f32[64,128]{1,0:T(8,128)S(1)} %get-tuple-element.28.sums, f32[64,128]{1,0:T(8,128)S(1)} %collective-permute-done.7.far), custom_call_target="tpu_custom_call" | custom-call | tf_op jit(solution)/shard_map/pallas_call | solution.py:350
  24.7 0.0 collective-permute-done.3.second_got
  24.7 1.4 %shard_map.94 = (f32[768,128]{1,0:T(8,128)}, f32[768,128]{1,0:T(8,128)}, f32[64,64]{1,0:T(8,128)}, f32[64,64]{1,0:T(8,128)S(1)}) custom-call(f32[256,128]{1,0:T(8,128)S(1)} %get-tuple-element.19.field_x, f32[512,128]{1,0:T(8,128)S(1)} %get-tuple-element.20.field_yz, f32[256,128]{1,0:T(8,128)S(1)} %get-tuple-element.22.m_x, ...), custom_call_target="tpu_custom_call" | custom-call | tf_op jit(solution)/shard_map/pallas_call | solution.py:350
  26.1 1.0 %collective-permute-done.8.far_cross = f32[32,128]{1,0:T(8,128)S(1)} collective-permute-done((f32[32,128]{1,0:T(8,128)S(1)}, f32[32,128]{1,0:T(8,128)S(1)}, u32[]{:S(2)}, u32[]{:S(2)}) %collective-permute-start.8) | collective-permute-done | bytes 16416 | tf_op jit(solution)/shard_map/ppermute | solution.py:362
  27.1 0.0 collective-permute-done.9.near
  27.1 1.0 %shard_map.95 = f32[64,64]{1,0:T(8,128)} custom-call(f32[64,64]{1,0:T(8,128)S(1)} %get-tuple-element.32.inverse, f32[32,128]{1,0:T(8,128)S(1)} %get-tuple-element.33.proj, f32[32,128]{1,0:T(8,128)S(1)} %collective-permute-done.8.far_cross, f32[64,128]{1,0:T(8,128)S(1)} %collective-permute-done.7.far, f32[32,128]{1,0:T(8,128)S(1)} %collective-permute-done.9.near), custom_call_target="tpu_custom_call" | custom-call | tf_op jit(solution)/shard_map/pallas_call | solution.py:350
  (3 shorter events, 0.0 us)
Async XLA Ops:
  0.6 1.0 %copy-start = (f32[64,3,1,4,128]{4,3,2,1,0:T(4,128)S(1)}, f32[64,3,1,4,128]{4,3,2,1,0:T(4,128)}, u32[]{:S(2)}) copy-start(f32[64,3,1,4,128]{4,3,2,1,0:T(4,128)} %param.5) | copy-start | bytes 1179652
  1.7 8.7 %collective-permute-start.1 = (f32[512,128]{1,0:T(8,128)S(1)}, f32[512,128]{1,0:T(8,128)S(1)}, u32[]{:S(2)}, u32[]{:S(2)}) collective-permute-start(f32[512,128]{1,0:T(8,128)S(1)} %get-tuple-element.23), channel_id=1, source_target_pairs={{2,0},{4,2},{6,4},{8,6},{10,8},{12,10},{14,12},{0,1},{1,3},{3,5},{... | collective-permute-start | bytes 786440 | tf_op jit(solution)/shard_map/ppermute | solution.py:384
  2.8 2.8 %copy-start.1 = (s32[1,4,128]{2,1,0:T(4,128)S(1)}, s32[1,4,128]{2,1,0:T(4,128)}, u32[]{:S(2)}) copy-start(s32[1,4,128]{2,1,0:T(4,128)} %param.6) | copy-start | bytes 6148
  2.8 4.0 %collective-permute-start = (f32[160,128]{1,0:T(8,128)S(1)}, f32[160,128]{1,0:T(8,128)S(1)}, u32[]{:S(2)}, u32[]{:S(2)}) collective-permute-start(f32[160,128]{1,0:T(8,128)S(1)} %shard_map.85.gram_edge), channel_id=1, source_target_pairs={{0,1},{1,0},{2,3},{3,2},{4,5},{5,4},{6,7},{7,6},{8,9},{9,8},{10,11... | collective-permute-start | bytes 245768 | tf_op jit(solution)/shard_map/ppermute | solution.py:362
  5.5 0.7 %copy-start.2 = (f32[8]{0:T(128)S(1)}, f32[8]{0:T(128)}, u32[]{:S(2)}) copy-start(f32[8]{0:T(128)} %mu_table.1) | copy-start | bytes 100
  5.5 0.7 %copy-start.3 = (f32[8]{0:T(128)S(1)}, f32[8]{0:T(128)}, u32[]{:S(2)}) copy-start(f32[8]{0:T(128)} %eps_table.1) | copy-start | bytes 100
  6.7 3.7 %collective-permute-start.2 = (f32[8,128]{1,0:T(8,128)S(1)}, f32[8,128]{1,0:T(8,128)S(1)}, u32[]{:S(2)}, u32[]{:S(2)}) collective-permute-start(f32[8,128]{1,0:T(8,128)S(1)} %shard_map.86.material), channel_id=1, source_target_pairs={{2,0},{4,2},{6,4},{8,6},{10,8},{12,10},{14,12},{0,1},{1,3},{3,5},{... | collective-permute-start | bytes 12296 | tf_op jit(solution)/shard_map/ppermute | solution.py:389
  6.9 6.8 %collective-permute-start.5 = (f32[32,128]{1,0:T(8,128)S(1)}, f32[32,128]{1,0:T(8,128)S(1)}, u32[]{:S(2)}, u32[]{:S(2)}) collective-permute-start(f32[32,128]{1,0:T(8,128)S(1)} %get-tuple-element.27.left), channel_id=1, source_target_pairs={{0,2},{2,0},{4,6},{6,4},{8,10},{10,8},{12,14},{14,12},{1,3},{3,1},... | collective-permute-start | bytes 49160 | tf_op jit(solution)/shard_map/ppermute | solution.py:362
  11.0 2.8 %collective-permute-start.4 = (f32[160,128]{1,0:T(8,128)S(1)}, f32[160,128]{1,0:T(8,128)S(1)}, u32[]{:S(2)}, u32[]{:S(2)}) collective-permute-start(f32[160,128]{1,0:T(8,128)S(1)} %get-tuple-element.26.edge), channel_id=1, source_target_pairs={{0,1},{1,0},{2,3},{3,2},{4,5},{5,4},{6,7},{7,6},{8,9},{9,8},{10,11... | collective-permute-start | bytes 245768 | tf_op jit(solution)/shard_map/ppermute | solution.py:362
  11.8 12.9 %collective-permute-start.3 = (f32[520,128]{1,0:T(8,128)S(1)}, f32[520,128]{1,0:T(8,128)S(1)}, u32[]{:S(2)}, u32[]{:S(2)}) collective-permute-start(f32[520,128]{1,0:T(8,128)S(1)} %get-tuple-element.25), channel_id=1, source_target_pairs={{0,2},{2,4},{4,6},{6,8},{8,10},{10,12},{12,14},{1,0},{3,1},{5,3},{... | collective-permute-start | bytes 798728 | tf_op jit(solution)/shard_map/ppermute | solution.py:412
  13.8 4.4 %collective-permute-start.6 = (f32[64,128]{1,0:T(8,128)S(1)}, f32[64,128]{1,0:T(8,128)S(1)}, u32[]{:S(2)}, u32[]{:S(2)}) collective-permute-start(f32[64,128]{1,0:T(8,128)S(1)} %shard_map.91.own), channel_id=1, source_target_pairs={{0,4},{2,6},{4,0},{6,2},{8,12},{10,14},{12,8},{14,10},{1,5},{3,7},... | collective-permute-start | bytes 98312 | tf_op jit(solution)/shard_map/ppermute | solution.py:362
  18.2 5.1 %collective-permute-start.7 = (f32[64,128]{1,0:T(8,128)S(1)}, f32[64,128]{1,0:T(8,128)S(1)}, u32[]{:S(2)}, u32[]{:S(2)}) collective-permute-start(f32[64,128]{1,0:T(8,128)S(1)} %get-tuple-element.28.sums), channel_id=1, source_target_pairs={{0,8},{2,10},{4,12},{6,14},{8,0},{10,2},{12,4},{14,6},{1,9},{3,11}... | collective-permute-start | bytes 98312 | tf_op jit(solution)/shard_map/ppermute | solution.py:362
  21.2 5.9 %collective-permute-start.8 = (f32[32,128]{1,0:T(8,128)S(1)}, f32[32,128]{1,0:T(8,128)S(1)}, u32[]{:S(2)}, u32[]{:S(2)}) collective-permute-start(f32[32,128]{1,0:T(8,128)S(1)} %get-tuple-element.33.proj), channel_id=1, source_target_pairs={{0,10},{2,8},{4,14},{6,12},{8,2},{10,0},{12,6},{14,4},{1,11},{3,9}... | collective-permute-start | bytes 49160 | tf_op jit(solution)/shard_map/ppermute | solution.py:362
  23.0 4.1 %collective-permute-start.9 = (f32[32,128]{1,0:T(8,128)S(1)}, f32[32,128]{1,0:T(8,128)S(1)}, u32[]{:S(2)}, u32[]{:S(2)}) collective-permute-start(f32[32,128]{1,0:T(8,128)S(1)} %get-tuple-element.33.proj), channel_id=1, source_target_pairs={{0,2},{2,0},{4,6},{6,4},{8,10},{10,8},{12,14},{14,12},{1,3},{3,1},... | collective-permute-start | bytes 49160 | tf_op jit(solution)/shard_map/ppermute | solution.py:362

commit v9 on v8

--- a/solution.py
+++ b/solution.py
@@ -136,7 +136,9 @@
         out_open[other : other + columns, :] = (e_x - e_x_up) - e_y
 
 
-def near_kernel(columns, cells, field_x, field_yz, ahead_y, material, open_yz, out_x, out_proj):
+def near_kernel(
+    columns, cells, field_x, field_yz, ahead_y, material, open_yz, out_x, out_proj, out_send
+):
     half = columns // 2
     inside = first_core()
     left, right = [], []
@@ -153,9 +155,13 @@
         eps = -material[cells + y : cells + y + 1, :]
         m_x = mu * curl_x
         open_y, open_z = part(open_yz, y, columns), part(open_yz, cells + y, columns)
-        out_x[y * columns : (y + 1) * columns, :] = m_x
+        at, other = y * columns, (cells + y) * columns
+        out_x[at : at + columns, :] = m_x
+        out_send[at : at + columns, :] = jnp.where(inside, open_y, e_y)
+        out_send[other : other + columns, :] = jnp.where(inside, open_z, e_z)
         left += [curl_x, e_x, e_y, e_z, open_y, open_z]
         right += [m_x, eps * e_x, eps * e_y, eps * e_z, mu * open_y, mu * open_z]
+    out_send[2 * cells * columns :, :] = material[...]
     out_proj[...] = packed(inner(wide(left), wide(right)))
 
 
@@ -168,7 +174,7 @@
 
 
 def curl_kernel(
-    columns, cells, field_yz, received, mu_received, open_yz, material, m_x, near, out_edge, out_send
+    columns, cells, field_yz, received, mu_received, open_yz, material, m_x, near, out_edge
 ):
     half = columns // 2
     ahead = first_core()
@@ -176,14 +182,11 @@
     ahead_here = jnp.logical_and(ahead, below_top())
     left, right = [], []
     for y in range(cells):
-        at, other = y * columns, (cells + y) * columns
         got_y, got_z = part(received, y, columns), part(received, cells + y, columns)
         own_y, own_z = part(field_yz, y, columns), part(field_yz, cells + y, columns)
         open_y, open_z = part(open_yz, y, columns), part(open_yz, cells + y, columns)
         mu_got = jnp.where(behind, mu_received[y : y + 1, :], 0.0)
         mu = jnp.where(ahead, material[y : y + 1, :], mu_got)
-        out_send[at : at + columns, :] = jnp.where(ahead, open_y, own_y)
-        out_send[other : other + columns, :] = jnp.where(ahead, open_z, own_z)
         open_y = jnp.where(ahead, open_y, jnp.where(behind, got_y, 0.0))
         open_z = jnp.where(ahead, open_z, jnp.where(behind, got_z, 0.0))
         e_y = jnp.where(ahead, jnp.where(ahead_here, got_y, 0.0), own_y)
@@ -192,7 +195,6 @@
         right += [mu * (0.5 * e_z - open_y), mu * (0.5 * e_y + open_z)]
         if y + 1 == cells:
             out_edge[half + columns :, :] = mu * (open_z + e_y)
-    out_send[2 * cells * columns :, :] = material[...]
     out_edge[half : half + columns, :] = part(m_x, cells - 1, columns)
     crossing = inner(wide(left), wide(right))
     out_edge[:half, :] = near[...] + packed(crossing + crossing.T)
@@ -395,21 +397,21 @@
         flops=0,
     )
     gram_other = swapped(gram, "row", 1)
-    m_x, near = call(
+    m_x, near, send = call(
         functools.partial(near_kernel, columns, cells),
         (),
         (field_x, field_yz, ahead_y, material, open_yz),
-        (small, pair),
+        (small, pair, (2 * cells * (columns + 1), lanes)),
         flops=0,
     )
-    proj_edge, send = call(
+    second_got = lax.ppermute(send, ("row", "col"), halo_ring(rows, True))
+    (proj_edge,) = call(
         functools.partial(curl_kernel, columns, cells),
         (),
         (field_yz, first_got, mu_received, open_yz, material, m_x, near),
-        (edge, (2 * cells * (columns + 1), lanes)),
+        (edge,),
         flops=10**10,
     )
-    second_got = lax.ppermute(send, ("row", "col"), halo_ring(rows, True))
     (gram,) = call(add_kernel, (), (gram, gram_other), (pair,), flops=10**10)
     behind_y = swapped(proj_edge, "col", 1)
     both = (2 * half, 2 * columns)

time: 28.3 us -> 27.7 us (0.979)
  starting transfers between devices: 14.7 us -> 13.4 us
  waiting for transfers between devices: 3.79 us -> 4.38 us
    ppermute x1, starting transfers between devices: 1.89 us -> 0.03 us  [local(): second_got = lax.ppermute(send, ('row', 'col'), halo_ring(rows, True))]
    ppermute x7, waiting for transfers between devices: 3.32 us -> 3.98 us  [swapped(): lax.ppermute(x, axis, [(i, i ^ step) for i in range(lax.axis_size(axis))])]
    ppermute x7, starting transfers between devices: 12.2 us -> 12.8 us  [swapped(): lax.ppermute(x, axis, [(i, i ^ step) for i in range(lax.axis_size(axis))])]
  transfers between devices with their start and end apart: 10 -> 10, of which waited for: 3 -> 5; matrix products, arithmetic and copies ran while one was open for 0% -> 0% of each run, Pallas kernels for 19% -> 20%
where the time goes in v9:
time: 27.7 us; the launch traced here: 27.5 us
  starting transfers between devices  13.4 us (48%)
  Pallas kernels  6.69 us (24%)
  waiting for transfers between devices  4.38 us (16%)
  local copies, waits for them, and re-layouts  1.64 us (6%)
  between operations  1.38 us (5%)
    ppermute x7, starting transfers between devices, swapped(): lax.ppermute(x, axis, [(i, i ^ step) for i in range(lax.axis_size(axis))])  12.8 us
    pallas_call x12, Pallas kernels, call(): pl.pallas_call(body, out_shape=shapes, in_specs=[SMEM] * len(scalars) + [...  6.69 us
    ppermute x7, waiting for transfers between devices, swapped(): lax.ppermute(x, axis, [(i, i ^ step) for i in range(lax.axis_size(axis))])  3.98 us
    unnamed x8, local copies, waits for them, and re-layouts  1.64 us
  transfers between devices with their start and end apart: 10, of which 5 were waited for; matrix products, arithmetic and copies ran while one was open for 0% of the time, Pallas kernels for 20%

profile of v9, /device:TPU:0, one launch (start us, length us, event | category | flops | bytes accessed | tf_op | source)
XLA Modules:
  0.0 27.5 jit_solution(12993942545820630389)
XLA Ops:
  0.6 0.0 copy-start
  0.6 1.0 %copy-done = f32[64,3,1,4,128]{4,3,2,1,0:T(4,128)S(1)} copy-done((f32[64,3,1,4,128]{4,3,2,1,0:T(4,128)S(1)}, f32[64,3,1,4,128]{4,3,2,1,0:T(4,128)}, u32[]{:S(2)}) %copy-start) | copy-done | bytes 393240
  1.6 0.1 shard_map.84
  1.7 0.5 %collective-permute-start.1 = (f32[512,128]{1,0:T(8,128)S(1)}, f32[512,128]{1,0:T(8,128)S(1)}, u32[]{:S(2)}, u32[]{:S(2)}) collective-permute-start(f32[512,128]{1,0:T(8,128)S(1)} %get-tuple-element.22), channel_id=1, source_target_pairs={{2,0},{4,2},{6,4},{8,6},{10,8},{12,10},{14,12},{0,1},{1,3},{3,5},{... | collective-permute-start | bytes 786440 | tf_op jit(solution)/shard_map/ppermute | solution.py:386
  2.2 0.5 %shard_map.85.gram_edge = f32[160,128]{1,0:T(8,128)S(1)} custom-call(f32[256,128]{1,0:T(8,128)S(1)} %get-tuple-element.18.field_x, f32[512,128]{1,0:T(8,128)S(1)} %get-tuple-element.19.field_yz), custom_call_target="tpu_custom_call" | custom-call | tf_op jit(solution)/shard_map/pallas_call | solution.py:352
  2.8 0.0 copy-start.1
  2.8 2.1 %collective-permute-start = (f32[160,128]{1,0:T(8,128)S(1)}, f32[160,128]{1,0:T(8,128)S(1)}, u32[]{:S(2)}, u32[]{:S(2)}) collective-permute-start(f32[160,128]{1,0:T(8,128)S(1)} %shard_map.85.gram_edge), channel_id=1, source_target_pairs={{0,1},{1,0},{2,3},{3,2},{4,5},{5,4},{6,7},{7,6},{8,9},{9,8},{10,11... | collective-permute-start | bytes 245768 | tf_op jit(solution)/shard_map/ppermute | solution.py:364
  5.5 0.0 copy-start.2
  5.5 0.0 copy-start.3
  5.5 0.0 copy-done.1
  5.5 0.6 %copy-done.2 = f32[8]{0:T(128)S(1)} copy-done((f32[8]{0:T(128)S(1)}, f32[8]{0:T(128)}, u32[]{:S(2)}) %copy-start.2) | copy-done | bytes 56
  6.2 0.0 copy-done.3
  6.2 0.6 %shard_map.86.material = f32[8,128]{1,0:T(8,128)S(1)} custom-call(f32[8]{0:T(128)S(1)} %copy-done.2, f32[8]{0:T(128)S(1)} %copy-done.3, f32[1]{0:T(128)S(6)} %copy.11.shift, s32[4,128]{1,0:T(4,128)S(1)} %bitcast.9), custom_call_target="tpu_custom_call" | custom-call | tf_op jit(solution)/shard_map/pallas_call | solution.py:352
  6.7 0.1 collective-permute-start.2
  6.8 0.0 collective-permute-done.ahead_y
  6.8 0.1 shard_map.87
  6.9 2.1 %collective-permute-start.5 = (f32[32,128]{1,0:T(8,128)S(1)}, f32[32,128]{1,0:T(8,128)S(1)}, u32[]{:S(2)}, u32[]{:S(2)}) collective-permute-start(f32[32,128]{1,0:T(8,128)S(1)} %get-tuple-element.25.left), channel_id=1, source_target_pairs={{0,2},{2,0},{4,6},{6,4},{8,10},{10,8},{12,14},{14,12},{1,3},{3,1},... | collective-permute-start | bytes 49160 | tf_op jit(solution)/shard_map/ppermute | solution.py:364
  9.0 1.0 %shard_map.88 = (f32[256,128]{1,0:T(8,128)S(1)}, f32[32,128]{1,0:T(8,128)S(1)}, f32[520,128]{1,0:T(8,128)S(1)}) custom-call(f32[256,128]{1,0:T(8,128)S(1)} %get-tuple-element.18.field_x, f32[512,128]{1,0:T(8,128)S(1)} %get-tuple-element.19.field_yz, f32[160,128]{1,0:T(8,128)S(1)} %collective-permute-done.ahead_y, f32[8,128]{1,0:T(8,128)S(1)} %shard_map.86.material, ...), custom_call_target="tpu_custom_call" | custom-call | tf_op jit(solution)/shard_map/pallas_call | solution.py:352
  10.0 0.0 collective-permute-start.3
  10.0 0.4 %collective-permute-done.2.mu_received = f32[8,128]{1,0:T(8,128)S(1)} collective-permute-done((f32[8,128]{1,0:T(8,128)S(1)}, f32[8,128]{1,0:T(8,128)S(1)}, u32[]{:S(2)}, u32[]{:S(2)}) %collective-permute-start.2) | collective-permute-done | bytes 4128 | tf_op jit(solution)/shard_map/ppermute | solution.py:391
  10.4 0.0 collective-permute-done.1.received.first_got
  10.4 0.6 %shard_map.89.edge = f32[160,128]{1,0:T(8,128)S(1)} custom-call(f32[512,128]{1,0:T(8,128)S(1)} %get-tuple-element.19.field_yz, f32[512,128]{1,0:T(8,128)S(1)} %collective-permute-done.1.received.first_got, f32[8,128]{1,0:T(8,128)S(1)} %collective-permute-done.2.mu_received, f32[512,128]{1,0:T(8,128)S(1)} %get-tuple-element.20.open_yz, ...), custom_call_target="tpu_custom_call" | custom-call | flops 10000000000 | tf_op jit(solution)/shard_map/pallas_call | solution.py:352
  11.0 0.9 %collective-permute-start.4 = (f32[160,128]{1,0:T(8,128)S(1)}, f32[160,128]{1,0:T(8,128)S(1)}, u32[]{:S(2)}, u32[]{:S(2)}) collective-permute-start(f32[160,128]{1,0:T(8,128)S(1)} %shard_map.89.edge), channel_id=1, source_target_pairs={{0,1},{1,0},{2,3},{3,2},{4,5},{5,4},{6,7},{7,6},{8,9},{9,8},{10,11... | collective-permute-start | bytes 245768 | tf_op jit(solution)/shard_map/ppermute | solution.py:364
  11.9 0.0 collective-permute-done.5.right
  11.9 0.9 %collective-permute-done.4.edge_other.behind_y = f32[160,128]{1,0:T(8,128)S(1)} collective-permute-done((f32[160,128]{1,0:T(8,128)S(1)}, f32[160,128]{1,0:T(8,128)S(1)}, u32[]{:S(2)}, u32[]{:S(2)}) %collective-permute-start.4) | collective-permute-done | bytes 81952 | tf_op jit(solution)/shard_map/ppermute | solution.py:364
  12.8 3.1 %collective-permute-start.6 = (f32[64,128]{1,0:T(8,128)S(1)}, f32[64,128]{1,0:T(8,128)S(1)}, u32[]{:S(2)}, u32[]{:S(2)}) collective-permute-start(f32[64,128]{1,0:T(8,128)S(1)} %shard_map.91.own), channel_id=1, source_target_pairs={{0,4},{2,6},{4,0},{6,2},{8,12},{10,14},{12,8},{14,10},{1,5},{3,7},... | collective-permute-start | bytes 98312 | tf_op jit(solution)/shard_map/ppermute | solution.py:364
  15.9 1.9 %collective-permute-done.6.both = f32[64,128]{1,0:T(8,128)S(1)} collective-permute-done((f32[64,128]{1,0:T(8,128)S(1)}, f32[64,128]{1,0:T(8,128)S(1)}, u32[]{:S(2)}, u32[]{:S(2)}) %collective-permute-start.6) | collective-permute-done | bytes 32800 | tf_op jit(solution)/shard_map/ppermute | solution.py:364
  17.8 3.2 %collective-permute-start.7 = (f32[64,128]{1,0:T(8,128)S(1)}, f32[64,128]{1,0:T(8,128)S(1)}, u32[]{:S(2)}, u32[]{:S(2)}) collective-permute-start(f32[64,128]{1,0:T(8,128)S(1)} %get-tuple-element.26.sums), channel_id=1, source_target_pairs={{0,8},{2,10},{4,12},{6,14},{8,0},{10,2},{12,4},{14,6},{1,9},{3,11}... | collective-permute-start | bytes 98312 | tf_op jit(solution)/shard_map/ppermute | solution.py:364
  21.0 0.6 %collective-permute-start.8 = (f32[32,128]{1,0:T(8,128)S(1)}, f32[32,128]{1,0:T(8,128)S(1)}, u32[]{:S(2)}, u32[]{:S(2)}) collective-permute-start(f32[32,128]{1,0:T(8,128)S(1)} %get-tuple-element.31.proj), channel_id=1, source_target_pairs={{0,10},{2,8},{4,14},{6,12},{8,2},{10,0},{12,6},{14,4},{1,11},{3,9}... | collective-permute-start | bytes 49160 | tf_op jit(solution)/shard_map/ppermute | solution.py:364
  21.5 1.0 %collective-permute-start.9 = (f32[32,128]{1,0:T(8,128)S(1)}, f32[32,128]{1,0:T(8,128)S(1)}, u32[]{:S(2)}, u32[]{:S(2)}) collective-permute-start(f32[32,128]{1,0:T(8,128)S(1)} %get-tuple-element.31.proj), channel_id=1, source_target_pairs={{0,2},{2,0},{4,6},{6,4},{8,10},{10,8},{12,14},{14,12},{1,3},{3,1},... | collective-permute-start | bytes 49160 | tf_op jit(solution)/shard_map/ppermute | solution.py:364
  22.5 0.7 %collective-permute-done.7.far = f32[64,128]{1,0:T(8,128)S(1)} collective-permute-done((f32[64,128]{1,0:T(8,128)S(1)}, f32[64,128]{1,0:T(8,128)S(1)}, u32[]{:S(2)}, u32[]{:S(2)}) %collective-permute-start.7) | collective-permute-done | bytes 32800 | tf_op jit(solution)/shard_map/ppermute | solution.py:364
  23.2 1.4 %shard_map.93.factors = f32[64,128]{1,0:T(8,128)S(1)} custom-call(f32[64,128]{1,0:T(8,128)S(1)} %get-tuple-element.26.sums, f32[64,128]{1,0:T(8,128)S(1)} %collective-permute-done.7.far), custom_call_target="tpu_custom_call" | custom-call | tf_op jit(solution)/shard_map/pallas_call | solution.py:352
  24.6 0.0 collective-permute-done.3.second_got
  24.6 1.4 %shard_map.94 = (f32[768,128]{1,0:T(8,128)}, f32[768,128]{1,0:T(8,128)}, f32[64,64]{1,0:T(8,128)}, f32[64,64]{1,0:T(8,128)S(1)}) custom-call(f32[256,128]{1,0:T(8,128)S(1)} %get-tuple-element.18.field_x, f32[512,128]{1,0:T(8,128)S(1)} %get-tuple-element.19.field_yz, f32[256,128]{1,0:T(8,128)S(1)} %get-tuple-element.21.m_x, ...), custom_call_target="tpu_custom_call" | custom-call | tf_op jit(solution)/shard_map/pallas_call | solution.py:352
  26.0 0.5 %collective-permute-done.8.far_cross = f32[32,128]{1,0:T(8,128)S(1)} collective-permute-done((f32[32,128]{1,0:T(8,128)S(1)}, f32[32,128]{1,0:T(8,128)S(1)}, u32[]{:S(2)}, u32[]{:S(2)}) %collective-permute-start.8) | collective-permute-done | bytes 16416 | tf_op jit(solution)/shard_map/ppermute | solution.py:364
  26.5 0.0 collective-permute-done.9.near
  26.5 1.0 %shard_map.95 = f32[64,64]{1,0:T(8,128)} custom-call(f32[64,64]{1,0:T(8,128)S(1)} %get-tuple-element.30.inverse, f32[32,128]{1,0:T(8,128)S(1)} %get-tuple-element.31.proj, f32[32,128]{1,0:T(8,128)S(1)} %collective-permute-done.8.far_cross, f32[64,128]{1,0:T(8,128)S(1)} %collective-permute-done.7.far, f32[32,128]{1,0:T(8,128)S(1)} %collective-permute-done.9.near), custom_call_target="tpu_custom_call" | custom-call | tf_op jit(solution)/shard_map/pallas_call | solution.py:352
  (3 shorter events, 0.0 us)
Async XLA Ops:
  0.6 1.0 %copy-start = (f32[64,3,1,4,128]{4,3,2,1,0:T(4,128)S(1)}, f32[64,3,1,4,128]{4,3,2,1,0:T(4,128)}, u32[]{:S(2)}) copy-start(f32[64,3,1,4,128]{4,3,2,1,0:T(4,128)} %param.5) | copy-start | bytes 1179652
  1.7 8.7 %collective-permute-start.1 = (f32[512,128]{1,0:T(8,128)S(1)}, f32[512,128]{1,0:T(8,128)S(1)}, u32[]{:S(2)}, u32[]{:S(2)}) collective-permute-start(f32[512,128]{1,0:T(8,128)S(1)} %get-tuple-element.22), channel_id=1, source_target_pairs={{2,0},{4,2},{6,4},{8,6},{10,8},{12,10},{14,12},{0,1},{1,3},{3,5},{... | collective-permute-start | bytes 786440 | tf_op jit(solution)/shard_map/ppermute | solution.py:386
  2.8 2.8 %copy-start.1 = (s32[1,4,128]{2,1,0:T(4,128)S(1)}, s32[1,4,128]{2,1,0:T(4,128)}, u32[]{:S(2)}) copy-start(s32[1,4,128]{2,1,0:T(4,128)} %param.6) | copy-start | bytes 6148
  2.8 4.0 %collective-permute-start = (f32[160,128]{1,0:T(8,128)S(1)}, f32[160,128]{1,0:T(8,128)S(1)}, u32[]{:S(2)}, u32[]{:S(2)}) collective-permute-start(f32[160,128]{1,0:T(8,128)S(1)} %shard_map.85.gram_edge), channel_id=1, source_target_pairs={{0,1},{1,0},{2,3},{3,2},{4,5},{5,4},{6,7},{7,6},{8,9},{9,8},{10,11... | collective-permute-start | bytes 245768 | tf_op jit(solution)/shard_map/ppermute | solution.py:364
  5.5 0.7 %copy-start.2 = (f32[8]{0:T(128)S(1)}, f32[8]{0:T(128)}, u32[]{:S(2)}) copy-start(f32[8]{0:T(128)} %mu_table.1) | copy-start | bytes 100
  5.5 0.7 %copy-start.3 = (f32[8]{0:T(128)S(1)}, f32[8]{0:T(128)}, u32[]{:S(2)}) copy-start(f32[8]{0:T(128)} %eps_table.1) | copy-start | bytes 100
  6.7 3.7 %collective-permute-start.2 = (f32[8,128]{1,0:T(8,128)S(1)}, f32[8,128]{1,0:T(8,128)S(1)}, u32[]{:S(2)}, u32[]{:S(2)}) collective-permute-start(f32[8,128]{1,0:T(8,128)S(1)} %shard_map.86.material), channel_id=1, source_target_pairs={{2,0},{4,2},{6,4},{8,6},{10,8},{12,10},{14,12},{0,1},{1,3},{3,5},{... | collective-permute-start | bytes 12296 | tf_op jit(solution)/shard_map/ppermute | solution.py:391
  6.9 5.0 %collective-permute-start.5 = (f32[32,128]{1,0:T(8,128)S(1)}, f32[32,128]{1,0:T(8,128)S(1)}, u32[]{:S(2)}, u32[]{:S(2)}) collective-permute-start(f32[32,128]{1,0:T(8,128)S(1)} %get-tuple-element.25.left), channel_id=1, source_target_pairs={{0,2},{2,0},{4,6},{6,4},{8,10},{10,8},{12,14},{14,12},{1,3},{3,1},... | collective-permute-start | bytes 49160 | tf_op jit(solution)/shard_map/ppermute | solution.py:364
  10.0 14.6 %collective-permute-start.3 = (f32[520,128]{1,0:T(8,128)S(1)}, f32[520,128]{1,0:T(8,128)S(1)}, u32[]{:S(2)}, u32[]{:S(2)}) collective-permute-start(f32[520,128]{1,0:T(8,128)S(1)} %get-tuple-element.23), channel_id=1, source_target_pairs={{0,2},{2,4},{4,6},{6,8},{8,10},{10,12},{12,14},{1,0},{3,1},{5,3},{... | collective-permute-start | bytes 798728 | tf_op jit(solution)/shard_map/ppermute | solution.py:407
  11.0 1.8 %collective-permute-start.4 = (f32[160,128]{1,0:T(8,128)S(1)}, f32[160,128]{1,0:T(8,128)S(1)}, u32[]{:S(2)}, u32[]{:S(2)}) collective-permute-start(f32[160,128]{1,0:T(8,128)S(1)} %shard_map.89.edge), channel_id=1, source_target_pairs={{0,1},{1,0},{2,3},{3,2},{4,5},{5,4},{6,7},{7,6},{8,9},{9,8},{10,11... | collective-permute-start | bytes 245768 | tf_op jit(solution)/shard_map/ppermute | solution.py:364
  12.8 4.9 %collective-permute-start.6 = (f32[64,128]{1,0:T(8,128)S(1)}, f32[64,128]{1,0:T(8,128)S(1)}, u32[]{:S(2)}, u32[]{:S(2)}) collective-permute-start(f32[64,128]{1,0:T(8,128)S(1)} %shard_map.91.own), channel_id=1, source_target_pairs={{0,4},{2,6},{4,0},{6,2},{8,12},{10,14},{12,8},{14,10},{1,5},{3,7},... | collective-permute-start | bytes 98312 | tf_op jit(solution)/shard_map/ppermute | solution.py:364
  17.8 5.4 %collective-permute-start.7 = (f32[64,128]{1,0:T(8,128)S(1)}, f32[64,128]{1,0:T(8,128)S(1)}, u32[]{:S(2)}, u32[]{:S(2)}) collective-permute-start(f32[64,128]{1,0:T(8,128)S(1)} %get-tuple-element.26.sums), channel_id=1, source_target_pairs={{0,8},{2,10},{4,12},{6,14},{8,0},{10,2},{12,4},{14,6},{1,9},{3,11}... | collective-permute-start | bytes 98312 | tf_op jit(solution)/shard_map/ppermute | solution.py:364
  21.0 5.5 %collective-permute-start.8 = (f32[32,128]{1,0:T(8,128)S(1)}, f32[32,128]{1,0:T(8,128)S(1)}, u32[]{:S(2)}, u32[]{:S(2)}) collective-permute-start(f32[32,128]{1,0:T(8,128)S(1)} %get-tuple-element.31.proj), channel_id=1, source_target_pairs={{0,10},{2,8},{4,14},{6,12},{8,2},{10,0},{12,6},{14,4},{1,11},{3,9}... | collective-permute-start | bytes 49160 | tf_op jit(solution)/shard_map/ppermute | solution.py:364
  21.5 5.0 %collective-permute-start.9 = (f32[32,128]{1,0:T(8,128)S(1)}, f32[32,128]{1,0:T(8,128)S(1)}, u32[]{:S(2)}, u32[]{:S(2)}) collective-permute-start(f32[32,128]{1,0:T(8,128)S(1)} %get-tuple-element.31.proj), channel_id=1, source_target_pairs={{0,2},{2,0},{4,6},{6,4},{8,10},{10,8},{12,14},{14,12},{1,3},{3,1},... | collective-permute-start | bytes 49160 | tf_op jit(solution)/shard_map/ppermute | solution.py:364

commit v10 on v9

--- a/solution.py
+++ b/solution.py
@@ -416,16 +416,16 @@
     behind_y = swapped(proj_edge, "col", 1)
     both = (2 * half, 2 * columns)
     (own,) = call(join_kernel, (), (gram, proj_edge, behind_y), (both,), flops=0)
-    next_both = swapped(own, "row", 2)
+    next_both = swapped(own, "row", outer)
     sums, proj = call(sum_kernel, (), (own, next_both), (both, pair), flops=0)
     step = 4
     while step < outer:
         sums = sums + swapped(sums, "row", step)
         proj = sums[half:]
         step *= 2
-    far = swapped(sums, "row", outer)
+    far = swapped(sums, "row", 2)
     proj_near = swapped(proj, "row", 1)
-    far_cross = swapped(proj, "row", outer + 1)
+    far_cross = swapped(proj, "row", 3)
     (factors,) = call(
         functools.partial(factor_kernel, total), (), (sums, far), ((columns, 2 * columns),), flops=0
     )

time: 27.7 us -> 27.1 us (0.978)
  waiting for transfers between devices: 4.38 us -> 3.75 us
    ppermute x7, waiting for transfers between devices: 3.98 us -> 3.35 us  [swapped(): lax.ppermute(x, axis, [(i, i ^ step) for i in range(lax.axis_size(axis))])]
  transfers between devices with their start and end apart: 10 -> 10, of which waited for: 5 -> 4; matrix products, arithmetic and copies ran while one was open for 0% -> 0% of each run, Pallas kernels for 20% -> 21%
where the time goes in v10:
time: 27.1 us; the launch traced here: 26.9 us
  starting transfers between devices  13.4 us (49%)
  Pallas kernels  6.69 us (25%)
  waiting for transfers between devices  3.75 us (14%)
  local copies, waits for them, and re-layouts  1.64 us (6%)
  between operations  1.4 us (5%)
    ppermute x7, starting transfers between devices, swapped(): lax.ppermute(x, axis, [(i, i ^ step) for i in range(lax.axis_size(axis))])  12.8 us
    pallas_call x12, Pallas kernels, call(): pl.pallas_call(body, out_shape=shapes, in_specs=[SMEM] * len(scalars) + [...  6.69 us
    ppermute x7, waiting for transfers between devices, swapped(): lax.ppermute(x, axis, [(i, i ^ step) for i in range(lax.axis_size(axis))])  3.35 us
    unnamed x8, local copies, waits for them, and re-layouts  1.64 us
  transfers between devices with their start and end apart: 10, of which 4 were waited for; matrix products, arithmetic and copies ran while one was open for 0% of the time, Pallas kernels for 21%

profile of v10, /device:TPU:0, one launch (start us, length us, event | category | flops | bytes accessed | tf_op | source)
XLA Modules:
  0.0 26.9 jit_solution(9766964024237018543)
XLA Ops:
  0.6 0.0 copy-start
  0.6 1.0 %copy-done = f32[64,3,1,4,128]{4,3,2,1,0:T(4,128)S(1)} copy-done((f32[64,3,1,4,128]{4,3,2,1,0:T(4,128)S(1)}, f32[64,3,1,4,128]{4,3,2,1,0:T(4,128)}, u32[]{:S(2)}) %copy-start) | copy-done | bytes 393240
  1.6 0.1 shard_map.84
  1.7 0.5 %collective-permute-start.1 = (f32[512,128]{1,0:T(8,128)S(1)}, f32[512,128]{1,0:T(8,128)S(1)}, u32[]{:S(2)}, u32[]{:S(2)}) collective-permute-start(f32[512,128]{1,0:T(8,128)S(1)} %get-tuple-element.22), channel_id=1, source_target_pairs={{2,0},{4,2},{6,4},{8,6},{10,8},{12,10},{14,12},{0,1},{1,3},{3,5},{... | collective-permute-start | bytes 786440 | tf_op jit(solution)/shard_map/ppermute | solution.py:386
  2.2 0.5 %shard_map.85.gram_edge = f32[160,128]{1,0:T(8,128)S(1)} custom-call(f32[256,128]{1,0:T(8,128)S(1)} %get-tuple-element.18.field_x, f32[512,128]{1,0:T(8,128)S(1)} %get-tuple-element.19.field_yz), custom_call_target="tpu_custom_call" | custom-call | tf_op jit(solution)/shard_map/pallas_call | solution.py:352
  2.8 0.0 copy-start.1
  2.8 2.1 %collective-permute-start = (f32[160,128]{1,0:T(8,128)S(1)}, f32[160,128]{1,0:T(8,128)S(1)}, u32[]{:S(2)}, u32[]{:S(2)}) collective-permute-start(f32[160,128]{1,0:T(8,128)S(1)} %shard_map.85.gram_edge), channel_id=1, source_target_pairs={{0,1},{1,0},{2,3},{3,2},{4,5},{5,4},{6,7},{7,6},{8,9},{9,8},{10,11... | collective-permute-start | bytes 245768 | tf_op jit(solution)/shard_map/ppermute | solution.py:364
  5.5 0.0 copy-start.2
  5.5 0.0 copy-start.3
  5.5 0.0 copy-done.1
  5.5 0.6 %copy-done.2 = f32[8]{0:T(128)S(1)} copy-done((f32[8]{0:T(128)S(1)}, f32[8]{0:T(128)}, u32[]{:S(2)}) %copy-start.2) | copy-done | bytes 56
  6.2 0.0 copy-done.3
  6.2 0.6 %shard_map.86.material = f32[8,128]{1,0:T(8,128)S(1)} custom-call(f32[8]{0:T(128)S(1)} %copy-done.2, f32[8]{0:T(128)S(1)} %copy-done.3, f32[1]{0:T(128)S(6)} %copy.11.shift, s32[4,128]{1,0:T(4,128)S(1)} %bitcast.9), custom_call_target="tpu_custom_call" | custom-call | tf_op jit(solution)/shard_map/pallas_call | solution.py:352
  6.7 0.1 collective-permute-start.2
  6.8 0.0 collective-permute-done.ahead_y
  6.8 0.1 shard_map.87
  6.9 2.1 %collective-permute-start.5 = (f32[32,128]{1,0:T(8,128)S(1)}, f32[32,128]{1,0:T(8,128)S(1)}, u32[]{:S(2)}, u32[]{:S(2)}) collective-permute-start(f32[32,128]{1,0:T(8,128)S(1)} %get-tuple-element.25.left), channel_id=1, source_target_pairs={{0,2},{2,0},{4,6},{6,4},{8,10},{10,8},{12,14},{14,12},{1,3},{3,1},... | collective-permute-start | bytes 49160 | tf_op jit(solution)/shard_map/ppermute | solution.py:364
  9.0 1.0 %shard_map.88 = (f32[256,128]{1,0:T(8,128)S(1)}, f32[32,128]{1,0:T(8,128)S(1)}, f32[520,128]{1,0:T(8,128)S(1)}) custom-call(f32[256,128]{1,0:T(8,128)S(1)} %get-tuple-element.18.field_x, f32[512,128]{1,0:T(8,128)S(1)} %get-tuple-element.19.field_yz, f32[160,128]{1,0:T(8,128)S(1)} %collective-permute-done.ahead_y, f32[8,128]{1,0:T(8,128)S(1)} %shard_map.86.material, ...), custom_call_target="tpu_custom_call" | custom-call | tf_op jit(solution)/shard_map/pallas_call | solution.py:352
  10.0 0.0 collective-permute-start.3
  10.0 0.4 %collective-permute-done.2.mu_received = f32[8,128]{1,0:T(8,128)S(1)} collective-permute-done((f32[8,128]{1,0:T(8,128)S(1)}, f32[8,128]{1,0:T(8,128)S(1)}, u32[]{:S(2)}, u32[]{:S(2)}) %collective-permute-start.2) | collective-permute-done | bytes 4128 | tf_op jit(solution)/shard_map/ppermute | solution.py:391
  10.4 0.0 collective-permute-done.1.received.first_got
  10.4 0.6 %shard_map.89.edge = f32[160,128]{1,0:T(8,128)S(1)} custom-call(f32[512,128]{1,0:T(8,128)S(1)} %get-tuple-element.19.field_yz, f32[512,128]{1,0:T(8,128)S(1)} %collective-permute-done.1.received.first_got, f32[8,128]{1,0:T(8,128)S(1)} %collective-permute-done.2.mu_received, f32[512,128]{1,0:T(8,128)S(1)} %get-tuple-element.20.open_yz, ...), custom_call_target="tpu_custom_call" | custom-call | flops 10000000000 | tf_op jit(solution)/shard_map/pallas_call | solution.py:352
  11.0 0.9 %collective-permute-start.4 = (f32[160,128]{1,0:T(8,128)S(1)}, f32[160,128]{1,0:T(8,128)S(1)}, u32[]{:S(2)}, u32[]{:S(2)}) collective-permute-start(f32[160,128]{1,0:T(8,128)S(1)} %shard_map.89.edge), channel_id=1, source_target_pairs={{0,1},{1,0},{2,3},{3,2},{4,5},{5,4},{6,7},{7,6},{8,9},{9,8},{10,11... | collective-permute-start | bytes 245768 | tf_op jit(solution)/shard_map/ppermute | solution.py:364
  11.9 0.0 collective-permute-done.5.right
  11.9 0.9 %collective-permute-done.4.edge_other.behind_y = f32[160,128]{1,0:T(8,128)S(1)} collective-permute-done((f32[160,128]{1,0:T(8,128)S(1)}, f32[160,128]{1,0:T(8,128)S(1)}, u32[]{:S(2)}, u32[]{:S(2)}) %collective-permute-start.4) | collective-permute-done | bytes 81952 | tf_op jit(solution)/shard_map/ppermute | solution.py:364
  12.8 4.1 %collective-permute-start.6 = (f32[64,128]{1,0:T(8,128)S(1)}, f32[64,128]{1,0:T(8,128)S(1)}, u32[]{:S(2)}, u32[]{:S(2)}) collective-permute-start(f32[64,128]{1,0:T(8,128)S(1)} %shard_map.91.own), channel_id=1, source_target_pairs={{0,8},{2,10},{4,12},{6,14},{8,0},{10,2},{12,4},{14,6},{1,9},{3,11}... | collective-permute-start | bytes 98312 | tf_op jit(solution)/shard_map/ppermute | solution.py:364
  16.9 1.9 %collective-permute-done.6.both = f32[64,128]{1,0:T(8,128)S(1)} collective-permute-done((f32[64,128]{1,0:T(8,128)S(1)}, f32[64,128]{1,0:T(8,128)S(1)}, u32[]{:S(2)}, u32[]{:S(2)}) %collective-permute-start.6) | collective-permute-done | bytes 32800 | tf_op jit(solution)/shard_map/ppermute | solution.py:364
  18.8 2.2 %collective-permute-start.7 = (f32[64,128]{1,0:T(8,128)S(1)}, f32[64,128]{1,0:T(8,128)S(1)}, u32[]{:S(2)}, u32[]{:S(2)}) collective-permute-start(f32[64,128]{1,0:T(8,128)S(1)} %get-tuple-element.26.sums), channel_id=1, source_target_pairs={{0,4},{2,6},{4,0},{6,2},{8,12},{10,14},{12,8},{14,10},{1,5},{3,7},... | collective-permute-start | bytes 98312 | tf_op jit(solution)/shard_map/ppermute | solution.py:364
  21.0 0.9 %collective-permute-start.8 = (f32[32,128]{1,0:T(8,128)S(1)}, f32[32,128]{1,0:T(8,128)S(1)}, u32[]{:S(2)}, u32[]{:S(2)}) collective-permute-start(f32[32,128]{1,0:T(8,128)S(1)} %get-tuple-element.31.proj), channel_id=1, source_target_pairs={{0,6},{2,4},{4,2},{6,0},{8,14},{10,12},{12,10},{14,8},{1,7},{3,5},... | collective-permute-start | bytes 49160 | tf_op jit(solution)/shard_map/ppermute | solution.py:364
  21.9 0.6 %collective-permute-start.9 = (f32[32,128]{1,0:T(8,128)S(1)}, f32[32,128]{1,0:T(8,128)S(1)}, u32[]{:S(2)}, u32[]{:S(2)}) collective-permute-start(f32[32,128]{1,0:T(8,128)S(1)} %get-tuple-element.31.proj), channel_id=1, source_target_pairs={{0,2},{2,0},{4,6},{6,4},{8,10},{10,8},{12,14},{14,12},{1,3},{3,1},... | collective-permute-start | bytes 49160 | tf_op jit(solution)/shard_map/ppermute | solution.py:364
  22.5 0.5 %collective-permute-done.7.far = f32[64,128]{1,0:T(8,128)S(1)} collective-permute-done((f32[64,128]{1,0:T(8,128)S(1)}, f32[64,128]{1,0:T(8,128)S(1)}, u32[]{:S(2)}, u32[]{:S(2)}) %collective-permute-start.7) | collective-permute-done | bytes 32800 | tf_op jit(solution)/shard_map/ppermute | solution.py:364
  23.0 1.4 %shard_map.93.factors = f32[64,128]{1,0:T(8,128)S(1)} custom-call(f32[64,128]{1,0:T(8,128)S(1)} %get-tuple-element.26.sums, f32[64,128]{1,0:T(8,128)S(1)} %collective-permute-done.7.far), custom_call_target="tpu_custom_call" | custom-call | tf_op jit(solution)/shard_map/pallas_call | solution.py:352
  24.4 0.0 collective-permute-done.3.second_got
  24.5 1.4 %shard_map.94 = (f32[768,128]{1,0:T(8,128)}, f32[768,128]{1,0:T(8,128)}, f32[64,64]{1,0:T(8,128)}, f32[64,64]{1,0:T(8,128)S(1)}) custom-call(f32[256,128]{1,0:T(8,128)S(1)} %get-tuple-element.18.field_x, f32[512,128]{1,0:T(8,128)S(1)} %get-tuple-element.19.field_yz, f32[256,128]{1,0:T(8,128)S(1)} %get-tuple-element.21.m_x, ...), custom_call_target="tpu_custom_call" | custom-call | tf_op jit(solution)/shard_map/pallas_call | solution.py:352
  25.9 0.0 collective-permute-done.8.far_cross
  25.9 0.0 collective-permute-done.9.near
  25.9 1.0 %shard_map.95 = f32[64,64]{1,0:T(8,128)} custom-call(f32[64,64]{1,0:T(8,128)S(1)} %get-tuple-element.30.inverse, f32[32,128]{1,0:T(8,128)S(1)} %get-tuple-element.31.proj, f32[32,128]{1,0:T(8,128)S(1)} %collective-permute-done.8.far_cross, f32[64,128]{1,0:T(8,128)S(1)} %collective-permute-done.7.far, f32[32,128]{1,0:T(8,128)S(1)} %collective-permute-done.9.near), custom_call_target="tpu_custom_call" | custom-call | tf_op jit(solution)/shard_map/pallas_call | solution.py:352
  (3 shorter events, 0.0 us)
Async XLA Ops:
  0.6 1.0 %copy-start = (f32[64,3,1,4,128]{4,3,2,1,0:T(4,128)S(1)}, f32[64,3,1,4,128]{4,3,2,1,0:T(4,128)}, u32[]{:S(2)}) copy-start(f32[64,3,1,4,128]{4,3,2,1,0:T(4,128)} %param.5) | copy-start | bytes 1179652
  1.7 8.7 %collective-permute-start.1 = (f32[512,128]{1,0:T(8,128)S(1)}, f32[512,128]{1,0:T(8,128)S(1)}, u32[]{:S(2)}, u32[]{:S(2)}) collective-permute-start(f32[512,128]{1,0:T(8,128)S(1)} %get-tuple-element.22), channel_id=1, source_target_pairs={{2,0},{4,2},{6,4},{8,6},{10,8},{12,10},{14,12},{0,1},{1,3},{3,5},{... | collective-permute-start | bytes 786440 | tf_op jit(solution)/shard_map/ppermute | solution.py:386
  2.8 2.8 %copy-start.1 = (s32[1,4,128]{2,1,0:T(4,128)S(1)}, s32[1,4,128]{2,1,0:T(4,128)}, u32[]{:S(2)}) copy-start(s32[1,4,128]{2,1,0:T(4,128)} %param.6) | copy-start | bytes 6148
  2.8 4.0 %collective-permute-start = (f32[160,128]{1,0:T(8,128)S(1)}, f32[160,128]{1,0:T(8,128)S(1)}, u32[]{:S(2)}, u32[]{:S(2)}) collective-permute-start(f32[160,128]{1,0:T(8,128)S(1)} %shard_map.85.gram_edge), channel_id=1, source_target_pairs={{0,1},{1,0},{2,3},{3,2},{4,5},{5,4},{6,7},{7,6},{8,9},{9,8},{10,11... | collective-permute-start | bytes 245768 | tf_op jit(solution)/shard_map/ppermute | solution.py:364
  5.5 0.7 %copy-start.2 = (f32[8]{0:T(128)S(1)}, f32[8]{0:T(128)}, u32[]{:S(2)}) copy-start(f32[8]{0:T(128)} %mu_table.1) | copy-start | bytes 100
  5.5 0.7 %copy-start.3 = (f32[8]{0:T(128)S(1)}, f32[8]{0:T(128)}, u32[]{:S(2)}) copy-start(f32[8]{0:T(128)} %eps_table.1) | copy-start | bytes 100
  6.7 3.7 %collective-permute-start.2 = (f32[8,128]{1,0:T(8,128)S(1)}, f32[8,128]{1,0:T(8,128)S(1)}, u32[]{:S(2)}, u32[]{:S(2)}) collective-permute-start(f32[8,128]{1,0:T(8,128)S(1)} %shard_map.86.material), channel_id=1, source_target_pairs={{2,0},{4,2},{6,4},{8,6},{10,8},{12,10},{14,12},{0,1},{1,3},{3,5},{... | collective-permute-start | bytes 12296 | tf_op jit(solution)/shard_map/ppermute | solution.py:391
  6.9 5.0 %collective-permute-start.5 = (f32[32,128]{1,0:T(8,128)S(1)}, f32[32,128]{1,0:T(8,128)S(1)}, u32[]{:S(2)}, u32[]{:S(2)}) collective-permute-start(f32[32,128]{1,0:T(8,128)S(1)} %get-tuple-element.25.left), channel_id=1, source_target_pairs={{0,2},{2,0},{4,6},{6,4},{8,10},{10,8},{12,14},{14,12},{1,3},{3,1},... | collective-permute-start | bytes 49160 | tf_op jit(solution)/shard_map/ppermute | solution.py:364
  10.0 14.5 %collective-permute-start.3 = (f32[520,128]{1,0:T(8,128)S(1)}, f32[520,128]{1,0:T(8,128)S(1)}, u32[]{:S(2)}, u32[]{:S(2)}) collective-permute-start(f32[520,128]{1,0:T(8,128)S(1)} %get-tuple-element.23), channel_id=1, source_target_pairs={{0,2},{2,4},{4,6},{6,8},{8,10},{10,12},{12,14},{1,0},{3,1},{5,3},{... | collective-permute-start | bytes 798728 | tf_op jit(solution)/shard_map/ppermute | solution.py:407
  11.0 1.8 %collective-permute-start.4 = (f32[160,128]{1,0:T(8,128)S(1)}, f32[160,128]{1,0:T(8,128)S(1)}, u32[]{:S(2)}, u32[]{:S(2)}) collective-permute-start(f32[160,128]{1,0:T(8,128)S(1)} %shard_map.89.edge), channel_id=1, source_target_pairs={{0,1},{1,0},{2,3},{3,2},{4,5},{5,4},{6,7},{7,6},{8,9},{9,8},{10,11... | collective-permute-start | bytes 245768 | tf_op jit(solution)/shard_map/ppermute | solution.py:364
  12.8 6.0 %collective-permute-start.6 = (f32[64,128]{1,0:T(8,128)S(1)}, f32[64,128]{1,0:T(8,128)S(1)}, u32[]{:S(2)}, u32[]{:S(2)}) collective-permute-start(f32[64,128]{1,0:T(8,128)S(1)} %shard_map.91.own), channel_id=1, source_target_pairs={{0,8},{2,10},{4,12},{6,14},{8,0},{10,2},{12,4},{14,6},{1,9},{3,11}... | collective-permute-start | bytes 98312 | tf_op jit(solution)/shard_map/ppermute | solution.py:364
  18.8 4.2 %collective-permute-start.7 = (f32[64,128]{1,0:T(8,128)S(1)}, f32[64,128]{1,0:T(8,128)S(1)}, u32[]{:S(2)}, u32[]{:S(2)}) collective-permute-start(f32[64,128]{1,0:T(8,128)S(1)} %get-tuple-element.26.sums), channel_id=1, source_target_pairs={{0,4},{2,6},{4,0},{6,2},{8,12},{10,14},{12,8},{14,10},{1,5},{3,7},... | collective-permute-start | bytes 98312 | tf_op jit(solution)/shard_map/ppermute | solution.py:364
  21.0 4.9 %collective-permute-start.8 = (f32[32,128]{1,0:T(8,128)S(1)}, f32[32,128]{1,0:T(8,128)S(1)}, u32[]{:S(2)}, u32[]{:S(2)}) collective-permute-start(f32[32,128]{1,0:T(8,128)S(1)} %get-tuple-element.31.proj), channel_id=1, source_target_pairs={{0,6},{2,4},{4,2},{6,0},{8,14},{10,12},{12,10},{14,8},{1,7},{3,5},... | collective-permute-start | bytes 49160 | tf_op jit(solution)/shard_map/ppermute | solution.py:364
  21.9 4.0 %collective-permute-start.9 = (f32[32,128]{1,0:T(8,128)S(1)}, f32[32,128]{1,0:T(8,128)S(1)}, u32[]{:S(2)}, u32[]{:S(2)}) collective-permute-start(f32[32,128]{1,0:T(8,128)S(1)} %get-tuple-element.31.proj), channel_id=1, source_target_pairs={{0,2},{2,0},{4,6},{6,4},{8,10},{10,8},{12,14},{14,12},{1,3},{3,1},... | collective-permute-start | bytes 49160 | tf_op jit(solution)/shard_map/ppermute | solution.py:364

commit v11 on v10

--- a/solution.py
+++ b/solution.py
@@ -37,7 +37,7 @@
     )
 
 
-def product(left, right):
+def product(left, right_thirds):
     rows = left.shape[0]
     high, middle, low = three(left)
     none = jnp.zeros_like(high)
@@ -45,8 +45,7 @@
         [wide([high, high, high]), wide([middle, middle, none]), wide([low, none, none])], axis=0
     )
     blocks = lax.dot_general(
-        stacked, jnp.concatenate(three(right), axis=0), (((1,), (0,)), ((), ())),
-        preferred_element_type=F32,
+        stacked, right_thirds, (((1,), (0,)), ((), ())), preferred_element_type=F32
     )
     return blocks[:rows, :] + (blocks[rows : 2 * rows, :] + blocks[2 * rows :, :])
 
@@ -137,7 +136,8 @@
 
 
 def near_kernel(
-    columns, cells, field_x, field_yz, ahead_y, material, open_yz, out_x, out_proj, out_send
+    columns, cells, field_x, field_yz, ahead_y, material, open_yz, out_x, out_proj, out_send,
+    out_thirds,
 ):
     half = columns // 2
     inside = first_core()
@@ -161,6 +161,10 @@
         out_send[other : other + columns, :] = jnp.where(inside, open_z, e_z)
         left += [curl_x, e_x, e_y, e_z, open_y, open_z]
         right += [m_x, eps * e_x, eps * e_y, eps * e_z, mu * open_y, mu * open_z]
+    fields = [part(field_x, y, columns) for y in range(cells)]
+    fields += [part(field_yz, k, columns) for k in range(2 * cells)]
+    for i, values in enumerate(three(wide(fields))):
+        out_thirds[i * columns : (i + 1) * columns, :] = values
     out_send[2 * cells * columns :, :] = material[...]
     out_proj[...] = packed(inner(wide(left), wide(right)))
 
@@ -266,7 +270,7 @@
 
 def basis_kernel(
     columns, cells, field_x, field_yz, m_x, open_yz, first_got, mu_received, second_got, behind_y,
-    material, factors,
+    material, thirds_ref, factors,
     out_basis, out_image, out_upper, out_inverse, basis, image, upper, sems,
 ):
     half = columns // 2
@@ -277,18 +281,16 @@
     third = pltpu.make_async_copy(upper, out_upper, sems.at[2])
     third.start()
 
-    def write(chunks, places, held, target, sem):
-        lanes = chunks[0].shape[1]
-        whole = product(inverse, wide(chunks))
+    def write(thirds, places, held, target, sem):
+        lanes = held.shape[1]
+        whole = product(inverse, thirds)
         for i, k in enumerate(places):
             held[pl.ds(k, columns, stride=stride), :] = whole[:, i * lanes : (i + 1) * lanes]
         copy = pltpu.make_async_copy(held, target, sem)
         copy.start()
         return copy
 
-    fields = [part(field_x, y, columns) for y in range(cells)]
-    fields += [part(field_yz, k, columns) for k in range(2 * cells)]
-    first_copy = write(fields, range(stride), basis, out_basis, sems.at[0])
+    first_copy = write(thirds_ref[...], range(stride), basis, out_basis, sems.at[0])
     ahead = first_core()
     top, bottom = below_top(), above_bottom()
     scaled_eps = material[cells:, :]
@@ -323,7 +325,7 @@
         ]
         places += [y, cells + y, 2 * cells + y]
         m_z_down = m[2]
-    second_copy = write(images, places, image, out_image, sems.at[1])
+    second_copy = write(jnp.concatenate(three(wide(images)), axis=0), places, image, out_image, sems.at[1])
     first_copy.wait()
     second_copy.wait()
     third.wait()
@@ -345,7 +347,8 @@
 
 
 def call(body, scalars, arrays, outs, flops=None, far=0, scratch=()):
-    shapes = [jax.ShapeDtypeStruct(shape, F32) for shape in outs]
+    outs = [out if isinstance(out[0], tuple) else (out, F32) for out in outs]
+    shapes = [jax.ShapeDtypeStruct(shape, dtype) for shape, dtype in outs]
     cost = None
     if flops is not None:
         cost = pl.CostEstimate(flops=flops, bytes_accessed=0, transcendentals=0)
@@ -397,11 +400,14 @@
         flops=0,
     )
     gram_other = swapped(gram, "row", 1)
-    m_x, near, send = call(
+    m_x, near, send, thirds = call(
         functools.partial(near_kernel, columns, cells),
         (),
         (field_x, field_yz, ahead_y, material, open_yz),
-        (small, pair, (2 * cells * (columns + 1), lanes)),
+        (
+            small, pair, (2 * cells * (columns + 1), lanes),
+            ((3 * columns, 3 * cells * lanes), BF16),
+        ),
         flops=0,
     )
     second_got = lax.ppermute(send, ("row", "col"), halo_ring(rows, True))
@@ -434,7 +440,7 @@
         (),
         (
             field_x, field_yz, m_x, open_yz, first_got, mu_received, second_got, behind_y, material,
-            factors,
+            thirds, factors,
         ),
         (basis.shape, basis.shape, square, square),
         flops=0,

time: 27.1 us -> 26.9 us (level)
  no operation moved by 1% of the time
where the time goes in v11:
time: 26.9 us; the launch traced here: 26.8 us
  starting transfers between devices  13.4 us (50%)
  Pallas kernels  6.75 us (25%)
  waiting for transfers between devices  3.63 us (13%)
  local copies, waits for them, and re-layouts  1.64 us (6%)
  between operations  1.4 us (5%)
    ppermute x7, starting transfers between devices, swapped(): lax.ppermute(x, axis, [(i, i ^ step) for i in range(lax.axis_size(axis))])  12.7 us
    pallas_call x12, Pallas kernels, call(): pl.pallas_call(body, out_shape=shapes, in_specs=[SMEM] * len(scalars) + [...  6.75 us
    ppermute x7, waiting for transfers between devices, swapped(): lax.ppermute(x, axis, [(i, i ^ step) for i in range(lax.axis_size(axis))])  3.32 us
    unnamed x8, local copies, waits for them, and re-layouts  1.64 us
  transfers between devices with their start and end apart: 10, of which 4 were waited for; matrix products, arithmetic and copies ran while one was open for 0% of the time, Pallas kernels for 21%

profile of v11, /device:TPU:0, one launch (start us, length us, event | category | flops | bytes accessed | tf_op | source)
XLA Modules:
  0.0 26.8 jit_solution(5860876726872104565)
XLA Ops:
  0.6 0.0 copy-start
  0.6 1.0 %copy-done = f32[64,3,1,4,128]{4,3,2,1,0:T(4,128)S(1)} copy-done((f32[64,3,1,4,128]{4,3,2,1,0:T(4,128)S(1)}, f32[64,3,1,4,128]{4,3,2,1,0:T(4,128)}, u32[]{:S(2)}) %copy-start) | copy-done | bytes 393240
  1.6 0.1 shard_map.84
  1.7 0.5 %collective-permute-start.1 = (f32[512,128]{1,0:T(8,128)S(1)}, f32[512,128]{1,0:T(8,128)S(1)}, u32[]{:S(2)}, u32[]{:S(2)}) collective-permute-start(f32[512,128]{1,0:T(8,128)S(1)} %get-tuple-element.23), channel_id=1, source_target_pairs={{2,0},{4,2},{6,4},{8,6},{10,8},{12,10},{14,12},{0,1},{1,3},{3,5},{... | collective-permute-start | bytes 786440 | tf_op jit(solution)/shard_map/ppermute | solution.py:389
  2.2 0.5 %shard_map.85.gram_edge = f32[160,128]{1,0:T(8,128)S(1)} custom-call(f32[256,128]{1,0:T(8,128)S(1)} %get-tuple-element.19.field_x, f32[512,128]{1,0:T(8,128)S(1)} %get-tuple-element.20.field_yz), custom_call_target="tpu_custom_call" | custom-call | tf_op jit(solution)/shard_map/pallas_call | solution.py:355
  2.8 0.0 copy-start.1
  2.8 2.1 %collective-permute-start = (f32[160,128]{1,0:T(8,128)S(1)}, f32[160,128]{1,0:T(8,128)S(1)}, u32[]{:S(2)}, u32[]{:S(2)}) collective-permute-start(f32[160,128]{1,0:T(8,128)S(1)} %shard_map.85.gram_edge), channel_id=1, source_target_pairs={{0,1},{1,0},{2,3},{3,2},{4,5},{5,4},{6,7},{7,6},{8,9},{9,8},{10,11... | collective-permute-start | bytes 245768 | tf_op jit(solution)/shard_map/ppermute | solution.py:367
  5.5 0.0 copy-start.2
  5.5 0.0 copy-start.3
  5.5 0.0 copy-done.1
  5.5 0.6 %copy-done.2 = f32[8]{0:T(128)S(1)} copy-done((f32[8]{0:T(128)S(1)}, f32[8]{0:T(128)}, u32[]{:S(2)}) %copy-start.2) | copy-done | bytes 56
  6.2 0.0 copy-done.3
  6.2 0.6 %shard_map.86.material = f32[8,128]{1,0:T(8,128)S(1)} custom-call(f32[8]{0:T(128)S(1)} %copy-done.2, f32[8]{0:T(128)S(1)} %copy-done.3, f32[1]{0:T(128)S(6)} %copy.11.shift, s32[4,128]{1,0:T(4,128)S(1)} %bitcast.9), custom_call_target="tpu_custom_call" | custom-call | tf_op jit(solution)/shard_map/pallas_call | solution.py:355
  6.7 0.1 collective-permute-start.2
  6.8 0.0 collective-permute-done.ahead_y
  6.8 0.1 shard_map.87
  6.9 2.1 %collective-permute-start.5 = (f32[32,128]{1,0:T(8,128)S(1)}, f32[32,128]{1,0:T(8,128)S(1)}, u32[]{:S(2)}, u32[]{:S(2)}) collective-permute-start(f32[32,128]{1,0:T(8,128)S(1)} %get-tuple-element.27.left), channel_id=1, source_target_pairs={{0,2},{2,0},{4,6},{6,4},{8,10},{10,8},{12,14},{14,12},{1,3},{3,1},... | collective-permute-start | bytes 49160 | tf_op jit(solution)/shard_map/ppermute | solution.py:367
  9.0 1.1 %shard_map.88 = (f32[256,128]{1,0:T(8,128)S(1)}, f32[32,128]{1,0:T(8,128)S(1)}, f32[520,128]{1,0:T(8,128)S(1)}, bf16[192,1536]{1,0:T(8,128)(2,1)S(1)}) custom-call(f32[256,128]{1,0:T(8,128)S(1)} %get-tuple-element.19.field_x, f32[512,128]{1,0:T(8,128)S(1)} %get-tuple-element.20.field_yz, f32[160,128]{1,0:T(8,128)S(1)} %collective-permute-done.ahead_y, ...), custom_call_target="tpu_custom_call" | custom-call | tf_op jit(solution)/shard_map/pallas_call | solution.py:355
  10.1 0.0 collective-permute-start.3
  10.1 0.3 %collective-permute-done.2.mu_received = f32[8,128]{1,0:T(8,128)S(1)} collective-permute-done((f32[8,128]{1,0:T(8,128)S(1)}, f32[8,128]{1,0:T(8,128)S(1)}, u32[]{:S(2)}, u32[]{:S(2)}) %collective-permute-start.2) | collective-permute-done | bytes 4128 | tf_op jit(solution)/shard_map/ppermute | solution.py:394
  10.4 0.0 collective-permute-done.1.received.first_got
  10.4 0.6 %shard_map.89.edge = f32[160,128]{1,0:T(8,128)S(1)} custom-call(f32[512,128]{1,0:T(8,128)S(1)} %get-tuple-element.20.field_yz, f32[512,128]{1,0:T(8,128)S(1)} %collective-permute-done.1.received.first_got, f32[8,128]{1,0:T(8,128)S(1)} %collective-permute-done.2.mu_received, f32[512,128]{1,0:T(8,128)S(1)} %get-tuple-element.21.open_yz, ...), custom_call_target="tpu_custom_call" | custom-call | flops 10000000000 | tf_op jit(solution)/shard_map/pallas_call | solution.py:355
  11.0 1.0 %collective-permute-start.4 = (f32[160,128]{1,0:T(8,128)S(1)}, f32[160,128]{1,0:T(8,128)S(1)}, u32[]{:S(2)}, u32[]{:S(2)}) collective-permute-start(f32[160,128]{1,0:T(8,128)S(1)} %shard_map.89.edge), channel_id=1, source_target_pairs={{0,1},{1,0},{2,3},{3,2},{4,5},{5,4},{6,7},{7,6},{8,9},{9,8},{10,11... | collective-permute-start | bytes 245768 | tf_op jit(solution)/shard_map/ppermute | solution.py:367
  12.0 0.0 collective-permute-done.5.right
  12.0 0.9 %collective-permute-done.4.edge_other.behind_y = f32[160,128]{1,0:T(8,128)S(1)} collective-permute-done((f32[160,128]{1,0:T(8,128)S(1)}, f32[160,128]{1,0:T(8,128)S(1)}, u32[]{:S(2)}, u32[]{:S(2)}) %collective-permute-start.4) | collective-permute-done | bytes 81952 | tf_op jit(solution)/shard_map/ppermute | solution.py:367
  12.9 4.0 %collective-permute-start.6 = (f32[64,128]{1,0:T(8,128)S(1)}, f32[64,128]{1,0:T(8,128)S(1)}, u32[]{:S(2)}, u32[]{:S(2)}) collective-permute-start(f32[64,128]{1,0:T(8,128)S(1)} %shard_map.91.own), channel_id=1, source_target_pairs={{0,8},{2,10},{4,12},{6,14},{8,0},{10,2},{12,4},{14,6},{1,9},{3,11}... | collective-permute-start | bytes 98312 | tf_op jit(solution)/shard_map/ppermute | solution.py:367
  16.9 1.9 %collective-permute-done.6.both = f32[64,128]{1,0:T(8,128)S(1)} collective-permute-done((f32[64,128]{1,0:T(8,128)S(1)}, f32[64,128]{1,0:T(8,128)S(1)}, u32[]{:S(2)}, u32[]{:S(2)}) %collective-permute-start.6) | collective-permute-done | bytes 32800 | tf_op jit(solution)/shard_map/ppermute | solution.py:367
  18.8 2.1 %collective-permute-start.7 = (f32[64,128]{1,0:T(8,128)S(1)}, f32[64,128]{1,0:T(8,128)S(1)}, u32[]{:S(2)}, u32[]{:S(2)}) collective-permute-start(f32[64,128]{1,0:T(8,128)S(1)} %get-tuple-element.28.sums), channel_id=1, source_target_pairs={{0,4},{2,6},{4,0},{6,2},{8,12},{10,14},{12,8},{14,10},{1,5},{3,7},... | collective-permute-start | bytes 98312 | tf_op jit(solution)/shard_map/ppermute | solution.py:367
  20.9 1.1 %collective-permute-start.8 = (f32[32,128]{1,0:T(8,128)S(1)}, f32[32,128]{1,0:T(8,128)S(1)}, u32[]{:S(2)}, u32[]{:S(2)}) collective-permute-start(f32[32,128]{1,0:T(8,128)S(1)} %get-tuple-element.33.proj), channel_id=1, source_target_pairs={{0,6},{2,4},{4,2},{6,0},{8,14},{10,12},{12,10},{14,8},{1,7},{3,5},... | collective-permute-start | bytes 49160 | tf_op jit(solution)/shard_map/ppermute | solution.py:367
  22.0 0.4 %collective-permute-start.9 = (f32[32,128]{1,0:T(8,128)S(1)}, f32[32,128]{1,0:T(8,128)S(1)}, u32[]{:S(2)}, u32[]{:S(2)}) collective-permute-start(f32[32,128]{1,0:T(8,128)S(1)} %get-tuple-element.33.proj), channel_id=1, source_target_pairs={{0,2},{2,0},{4,6},{6,4},{8,10},{10,8},{12,14},{14,12},{1,3},{3,1},... | collective-permute-start | bytes 49160 | tf_op jit(solution)/shard_map/ppermute | solution.py:367
  22.4 0.5 %collective-permute-done.7.far = f32[64,128]{1,0:T(8,128)S(1)} collective-permute-done((f32[64,128]{1,0:T(8,128)S(1)}, f32[64,128]{1,0:T(8,128)S(1)}, u32[]{:S(2)}, u32[]{:S(2)}) %collective-permute-start.7) | collective-permute-done | bytes 32800 | tf_op jit(solution)/shard_map/ppermute | solution.py:367
  22.9 1.4 %shard_map.93.factors = f32[64,128]{1,0:T(8,128)S(1)} custom-call(f32[64,128]{1,0:T(8,128)S(1)} %get-tuple-element.28.sums, f32[64,128]{1,0:T(8,128)S(1)} %collective-permute-done.7.far), custom_call_target="tpu_custom_call" | custom-call | tf_op jit(solution)/shard_map/pallas_call | solution.py:355
  24.3 0.0 collective-permute-done.3.second_got
  24.3 1.4 %shard_map.94 = (f32[768,128]{1,0:T(8,128)}, f32[768,128]{1,0:T(8,128)}, f32[64,64]{1,0:T(8,128)}, f32[64,64]{1,0:T(8,128)S(1)}) custom-call(f32[256,128]{1,0:T(8,128)S(1)} %get-tuple-element.19.field_x, f32[512,128]{1,0:T(8,128)S(1)} %get-tuple-element.20.field_yz, f32[256,128]{1,0:T(8,128)S(1)} %get-tuple-element.22.m_x, ...), custom_call_target="tpu_custom_call" | custom-call | tf_op jit(solution)/shard_map/pallas_call | solution.py:355
  25.7 0.0 collective-permute-done.8.far_cross
  25.7 0.0 collective-permute-done.9.near
  25.7 1.0 %shard_map.95 = f32[64,64]{1,0:T(8,128)} custom-call(f32[64,64]{1,0:T(8,128)S(1)} %get-tuple-element.32.inverse, f32[32,128]{1,0:T(8,128)S(1)} %get-tuple-element.33.proj, f32[32,128]{1,0:T(8,128)S(1)} %collective-permute-done.8.far_cross, f32[64,128]{1,0:T(8,128)S(1)} %collective-permute-done.7.far, f32[32,128]{1,0:T(8,128)S(1)} %collective-permute-done.9.near), custom_call_target="tpu_custom_call" | custom-call | tf_op jit(solution)/shard_map/pallas_call | solution.py:355
  (3 shorter events, 0.0 us)
Async XLA Ops:
  0.6 1.0 %copy-start = (f32[64,3,1,4,128]{4,3,2,1,0:T(4,128)S(1)}, f32[64,3,1,4,128]{4,3,2,1,0:T(4,128)}, u32[]{:S(2)}) copy-start(f32[64,3,1,4,128]{4,3,2,1,0:T(4,128)} %param.5) | copy-start | bytes 1179652
  1.7 8.7 %collective-permute-start.1 = (f32[512,128]{1,0:T(8,128)S(1)}, f32[512,128]{1,0:T(8,128)S(1)}, u32[]{:S(2)}, u32[]{:S(2)}) collective-permute-start(f32[512,128]{1,0:T(8,128)S(1)} %get-tuple-element.23), channel_id=1, source_target_pairs={{2,0},{4,2},{6,4},{8,6},{10,8},{12,10},{14,12},{0,1},{1,3},{3,5},{... | collective-permute-start | bytes 786440 | tf_op jit(solution)/shard_map/ppermute | solution.py:389
  2.8 2.8 %copy-start.1 = (s32[1,4,128]{2,1,0:T(4,128)S(1)}, s32[1,4,128]{2,1,0:T(4,128)}, u32[]{:S(2)}) copy-start(s32[1,4,128]{2,1,0:T(4,128)} %param.6) | copy-start | bytes 6148
  2.8 4.0 %collective-permute-start = (f32[160,128]{1,0:T(8,128)S(1)}, f32[160,128]{1,0:T(8,128)S(1)}, u32[]{:S(2)}, u32[]{:S(2)}) collective-permute-start(f32[160,128]{1,0:T(8,128)S(1)} %shard_map.85.gram_edge), channel_id=1, source_target_pairs={{0,1},{1,0},{2,3},{3,2},{4,5},{5,4},{6,7},{7,6},{8,9},{9,8},{10,11... | collective-permute-start | bytes 245768 | tf_op jit(solution)/shard_map/ppermute | solution.py:367
  5.5 0.7 %copy-start.2 = (f32[8]{0:T(128)S(1)}, f32[8]{0:T(128)}, u32[]{:S(2)}) copy-start(f32[8]{0:T(128)} %mu_table.1) | copy-start | bytes 100
  5.5 0.7 %copy-start.3 = (f32[8]{0:T(128)S(1)}, f32[8]{0:T(128)}, u32[]{:S(2)}) copy-start(f32[8]{0:T(128)} %eps_table.1) | copy-start | bytes 100
  6.7 3.7 %collective-permute-start.2 = (f32[8,128]{1,0:T(8,128)S(1)}, f32[8,128]{1,0:T(8,128)S(1)}, u32[]{:S(2)}, u32[]{:S(2)}) collective-permute-start(f32[8,128]{1,0:T(8,128)S(1)} %shard_map.86.material), channel_id=1, source_target_pairs={{2,0},{4,2},{6,4},{8,6},{10,8},{12,10},{14,12},{0,1},{1,3},{3,5},{... | collective-permute-start | bytes 12296 | tf_op jit(solution)/shard_map/ppermute | solution.py:394
  6.9 5.1 %collective-permute-start.5 = (f32[32,128]{1,0:T(8,128)S(1)}, f32[32,128]{1,0:T(8,128)S(1)}, u32[]{:S(2)}, u32[]{:S(2)}) collective-permute-start(f32[32,128]{1,0:T(8,128)S(1)} %get-tuple-element.27.left), channel_id=1, source_target_pairs={{0,2},{2,0},{4,6},{6,4},{8,10},{10,8},{12,14},{14,12},{1,3},{3,1},... | collective-permute-start | bytes 49160 | tf_op jit(solution)/shard_map/ppermute | solution.py:367
  10.1 14.2 %collective-permute-start.3 = (f32[520,128]{1,0:T(8,128)S(1)}, f32[520,128]{1,0:T(8,128)S(1)}, u32[]{:S(2)}, u32[]{:S(2)}) collective-permute-start(f32[520,128]{1,0:T(8,128)S(1)} %get-tuple-element.24), channel_id=1, source_target_pairs={{0,2},{2,4},{4,6},{6,8},{8,10},{10,12},{12,14},{1,0},{3,1},{5,3},{... | collective-permute-start | bytes 798728 | tf_op jit(solution)/shard_map/ppermute | solution.py:413
  11.0 1.9 %collective-permute-start.4 = (f32[160,128]{1,0:T(8,128)S(1)}, f32[160,128]{1,0:T(8,128)S(1)}, u32[]{:S(2)}, u32[]{:S(2)}) collective-permute-start(f32[160,128]{1,0:T(8,128)S(1)} %shard_map.89.edge), channel_id=1, source_target_pairs={{0,1},{1,0},{2,3},{3,2},{4,5},{5,4},{6,7},{7,6},{8,9},{9,8},{10,11... | collective-permute-start | bytes 245768 | tf_op jit(solution)/shard_map/ppermute | solution.py:367
  12.9 5.9 %collective-permute-start.6 = (f32[64,128]{1,0:T(8,128)S(1)}, f32[64,128]{1,0:T(8,128)S(1)}, u32[]{:S(2)}, u32[]{:S(2)}) collective-permute-start(f32[64,128]{1,0:T(8,128)S(1)} %shard_map.91.own), channel_id=1, source_target_pairs={{0,8},{2,10},{4,12},{6,14},{8,0},{10,2},{12,4},{14,6},{1,9},{3,11}... | collective-permute-start | bytes 98312 | tf_op jit(solution)/shard_map/ppermute | solution.py:367
  18.8 4.1 %collective-permute-start.7 = (f32[64,128]{1,0:T(8,128)S(1)}, f32[64,128]{1,0:T(8,128)S(1)}, u32[]{:S(2)}, u32[]{:S(2)}) collective-permute-start(f32[64,128]{1,0:T(8,128)S(1)} %get-tuple-element.28.sums), channel_id=1, source_target_pairs={{0,4},{2,6},{4,0},{6,2},{8,12},{10,14},{12,8},{14,10},{1,5},{3,7},... | collective-permute-start | bytes 98312 | tf_op jit(solution)/shard_map/ppermute | solution.py:367
  20.9 4.9 %collective-permute-start.8 = (f32[32,128]{1,0:T(8,128)S(1)}, f32[32,128]{1,0:T(8,128)S(1)}, u32[]{:S(2)}, u32[]{:S(2)}) collective-permute-start(f32[32,128]{1,0:T(8,128)S(1)} %get-tuple-element.33.proj), channel_id=1, source_target_pairs={{0,6},{2,4},{4,2},{6,0},{8,14},{10,12},{12,10},{14,8},{1,7},{3,5},... | collective-permute-start | bytes 49160 | tf_op jit(solution)/shard_map/ppermute | solution.py:367
  22.0 3.7 %collective-permute-start.9 = (f32[32,128]{1,0:T(8,128)S(1)}, f32[32,128]{1,0:T(8,128)S(1)}, u32[]{:S(2)}, u32[]{:S(2)}) collective-permute-start(f32[32,128]{1,0:T(8,128)S(1)} %get-tuple-element.33.proj), channel_id=1, source_target_pairs={{0,2},{2,0},{4,6},{6,4},{8,10},{10,8},{12,14},{14,12},{1,3},{3,1},... | collective-permute-start | bytes 49160 | tf_op jit(solution)/shard_map/ppermute | solution.py:367

commit v12 on v11

--- a/solution.py
+++ b/solution.py
@@ -178,9 +178,9 @@
 
 
 def curl_kernel(
-    columns, cells, field_yz, received, mu_received, open_yz, material, m_x, near, out_edge
+    columns, cells, field_yz, received, mu_received, open_yz, material, m_x, near, out_edge,
+    out_proj,
 ):
-    half = columns // 2
     ahead = first_core()
     behind = jnp.logical_and(jnp.logical_not(ahead), above_bottom())
     ahead_here = jnp.logical_and(ahead, below_top())
@@ -198,20 +198,20 @@
         left += [e_z, e_y]
         right += [mu * (0.5 * e_z - open_y), mu * (0.5 * e_y + open_z)]
         if y + 1 == cells:
-            out_edge[half + columns :, :] = mu * (open_z + e_y)
-    out_edge[half : half + columns, :] = part(m_x, cells - 1, columns)
+            out_edge[columns:, :] = mu * (open_z + e_y)
+    out_edge[:columns, :] = part(m_x, cells - 1, columns)
     crossing = inner(wide(left), wide(right))
-    out_edge[:half, :] = near[...] + packed(crossing + crossing.T)
+    out_proj[...] = near[...] + packed(crossing + crossing.T)
 
 
 def add_kernel(left, right, out):
     out[...] = left[...] + right[...]
 
 
-def join_kernel(gram, edge, edge_other, out):
+def join_kernel(gram, proj, proj_other, out):
     half = gram.shape[0]
     out[:half, :] = gram[...]
-    out[half:, :] = edge[:half, :] + edge_other[:half, :]
+    out[half:, :] = proj[...] + proj_other[...]
 
 
 def sum_kernel(own, both, out, out_proj):
@@ -273,7 +273,6 @@
     material, thirds_ref, factors,
     out_basis, out_image, out_upper, out_inverse, basis, image, upper, sems,
 ):
-    half = columns // 2
     stride = 3 * cells
     inverse = factors[:, columns:]
     out_inverse[...] = inverse
@@ -312,8 +311,8 @@
         if y > 0:
             m_x_down = part(m_x, y - 1, columns)
         else:
-            m_x_down = jnp.where(ahead, 0.0, behind_y[half : half + columns, :])
-            m_z_down = jnp.where(ahead, 0.0, behind_y[half + columns :, :])
+            m_x_down = jnp.where(ahead, 0.0, behind_y[:columns, :])
+            m_z_down = jnp.where(ahead, 0.0, behind_y[columns:, :])
         mu_last = jnp.where(ahead, second_got[last : last + 1, :], mu_received[y : y + 1, :])
         m_y_last = jnp.where(bottom, mu_last * (jnp.where(ahead, second[0], first[0]) - e[2]), 0.0)
         m_z_last = jnp.where(bottom, mu_last * (jnp.where(ahead, second[1], first[1]) + e[1]), 0.0)
@@ -331,7 +330,7 @@
     third.wait()
 
 
-def proj_kernel(total, inverse, proj, far_cross, far, near, out):
+def proj_kernel(total, inverse, proj, near, far, far_cross, out):
     half = proj.shape[0]
     raw = (proj[...] + near[...]) + (far[half:, :] + far_cross[...])
     left = lax.dot_general(
@@ -411,17 +410,18 @@
         flops=0,
     )
     second_got = lax.ppermute(send, ("row", "col"), halo_ring(rows, True))
-    (proj_edge,) = call(
+    edge_m, proj = call(
         functools.partial(curl_kernel, columns, cells),
         (),
         (field_yz, first_got, mu_received, open_yz, material, m_x, near),
-        (edge,),
+        ((2 * columns, lanes), pair),
         flops=10**10,
     )
     (gram,) = call(add_kernel, (), (gram, gram_other), (pair,), flops=10**10)
-    behind_y = swapped(proj_edge, "col", 1)
+    proj_other = swapped(proj, "col", 1)
+    behind_y = swapped(edge_m, "col", 1)
     both = (2 * half, 2 * columns)
-    (own,) = call(join_kernel, (), (gram, proj_edge, behind_y), (both,), flops=0)
+    (own,) = call(join_kernel, (), (gram, proj, proj_other), (both,), flops=0)
     next_both = swapped(own, "row", outer)
     sums, proj = call(sum_kernel, (), (own, next_both), (both, pair), flops=0)
     step = 4
@@ -455,7 +455,7 @@
     (projected,) = call(
         functools.partial(proj_kernel, total),
         (),
-        (inverse, proj, far_cross, far, proj_near),
+        (inverse, proj, proj_near, far, far_cross),
         (square,),
         flops=0,
     )

time: 26.9 us -> 26.8 us (level)
    ppermute x7 -> x8, waiting for transfers between devices: 3.32 us -> 3.22 us  [swapped(): lax.ppermute(x, axis, [(i, i ^ step) for i in range(lax.axis_size(axis))])]
    ppermute x7 -> x8, starting transfers between devices: 12.7 us -> 12.7 us  [swapped(): lax.ppermute(x, axis, [(i, i ^ step) for i in range(lax.axis_size(axis))])]
  transfers between devices with their start and end apart: 10 -> 11, of which waited for: 4 -> 4; matrix products, arithmetic and copies ran while one was open for 0% -> 0% of each run, Pallas kernels for 21% -> 21%
where the time goes in v12:
time: 26.8 us; the launch traced here: 26.7 us
  starting transfers between devices  13.3 us (50%)
  Pallas kernels  6.76 us (25%)
  waiting for transfers between devices  3.52 us (13%)
  local copies, waits for them, and re-layouts  1.64 us (6%)
  between operations  1.4 us (5%)
    ppermute x8, starting transfers between devices, swapped(): lax.ppermute(x, axis, [(i, i ^ step) for i in range(lax.axis_size(axis))])  12.7 us
    pallas_call x12, Pallas kernels, call(): pl.pallas_call(body, out_shape=shapes, in_specs=[SMEM] * len(scalars) + [...  6.76 us
    ppermute x8, waiting for transfers between devices, swapped(): lax.ppermute(x, axis, [(i, i ^ step) for i in range(lax.axis_size(axis))])  3.22 us
    unnamed x8, local copies, waits for them, and re-layouts  1.64 us
  transfers between devices with their start and end apart: 11, of which 4 were waited for; matrix products, arithmetic and copies ran while one was open for 0% of the time, Pallas kernels for 21%

profile of v12, /device:TPU:0, one launch (start us, length us, event | category | flops | bytes accessed | tf_op | source)
XLA Modules:
  0.0 26.7 jit_solution(5940532104111964141)
XLA Ops:
  0.6 0.0 copy-start
  0.6 1.0 %copy-done = f32[64,3,1,4,128]{4,3,2,1,0:T(4,128)S(1)} copy-done((f32[64,3,1,4,128]{4,3,2,1,0:T(4,128)S(1)}, f32[64,3,1,4,128]{4,3,2,1,0:T(4,128)}, u32[]{:S(2)}) %copy-start) | copy-done | bytes 393240
  1.6 0.1 shard_map.84
  1.7 0.5 %collective-permute-start.1 = (f32[512,128]{1,0:T(8,128)S(1)}, f32[512,128]{1,0:T(8,128)S(1)}, u32[]{:S(2)}, u32[]{:S(2)}) collective-permute-start(f32[512,128]{1,0:T(8,128)S(1)} %get-tuple-element.25), channel_id=1, source_target_pairs={{2,0},{4,2},{6,4},{8,6},{10,8},{12,10},{14,12},{0,1},{1,3},{3,5},{... | collective-permute-start | bytes 786440 | tf_op jit(solution)/shard_map/ppermute | solution.py:388
  2.2 0.5 %shard_map.85.gram_edge = f32[160,128]{1,0:T(8,128)S(1)} custom-call(f32[256,128]{1,0:T(8,128)S(1)} %get-tuple-element.21.field_x, f32[512,128]{1,0:T(8,128)S(1)} %get-tuple-element.22.field_yz), custom_call_target="tpu_custom_call" | custom-call | tf_op jit(solution)/shard_map/pallas_call | solution.py:354
  2.8 0.0 copy-start.1
  2.8 2.1 %collective-permute-start = (f32[160,128]{1,0:T(8,128)S(1)}, f32[160,128]{1,0:T(8,128)S(1)}, u32[]{:S(2)}, u32[]{:S(2)}) collective-permute-start(f32[160,128]{1,0:T(8,128)S(1)} %shard_map.85.gram_edge), channel_id=1, source_target_pairs={{0,1},{1,0},{2,3},{3,2},{4,5},{5,4},{6,7},{7,6},{8,9},{9,8},{10,11... | collective-permute-start | bytes 245768 | tf_op jit(solution)/shard_map/ppermute | solution.py:366
  5.5 0.0 copy-start.2
  5.5 0.0 copy-start.3
  5.5 0.0 copy-done.1
  5.5 0.6 %copy-done.2 = f32[8]{0:T(128)S(1)} copy-done((f32[8]{0:T(128)S(1)}, f32[8]{0:T(128)}, u32[]{:S(2)}) %copy-start.2) | copy-done | bytes 56
  6.2 0.0 copy-done.3
  6.2 0.6 %shard_map.86.material = f32[8,128]{1,0:T(8,128)S(1)} custom-call(f32[8]{0:T(128)S(1)} %copy-done.2, f32[8]{0:T(128)S(1)} %copy-done.3, f32[1]{0:T(128)S(6)} %copy.11.shift, s32[4,128]{1,0:T(4,128)S(1)} %bitcast.9), custom_call_target="tpu_custom_call" | custom-call | tf_op jit(solution)/shard_map/pallas_call | solution.py:354
  6.7 0.1 collective-permute-start.2
  6.8 0.0 collective-permute-done.ahead_y
  6.8 0.1 shard_map.87
  6.9 2.1 %collective-permute-start.5 = (f32[32,128]{1,0:T(8,128)S(1)}, f32[32,128]{1,0:T(8,128)S(1)}, u32[]{:S(2)}, u32[]{:S(2)}) collective-permute-start(f32[32,128]{1,0:T(8,128)S(1)} %get-tuple-element.30.left), channel_id=1, source_target_pairs={{0,2},{2,0},{4,6},{6,4},{8,10},{10,8},{12,14},{14,12},{1,3},{3,1},... | collective-permute-start | bytes 49160 | tf_op jit(solution)/shard_map/ppermute | solution.py:366
  9.0 1.1 %shard_map.88 = (f32[256,128]{1,0:T(8,128)S(1)}, f32[32,128]{1,0:T(8,128)S(1)}, f32[520,128]{1,0:T(8,128)S(1)}, bf16[192,1536]{1,0:T(8,128)(2,1)S(1)}) custom-call(f32[256,128]{1,0:T(8,128)S(1)} %get-tuple-element.21.field_x, f32[512,128]{1,0:T(8,128)S(1)} %get-tuple-element.22.field_yz, f32[160,128]{1,0:T(8,128)S(1)} %collective-permute-done.ahead_y, ...), custom_call_target="tpu_custom_call" | custom-call | tf_op jit(solution)/shard_map/pallas_call | solution.py:354
  10.1 0.0 collective-permute-start.3
  10.1 0.3 %collective-permute-done.2.mu_received = f32[8,128]{1,0:T(8,128)S(1)} collective-permute-done((f32[8,128]{1,0:T(8,128)S(1)}, f32[8,128]{1,0:T(8,128)S(1)}, u32[]{:S(2)}, u32[]{:S(2)}) %collective-permute-start.2) | collective-permute-done | bytes 4128 | tf_op jit(solution)/shard_map/ppermute | solution.py:393
  10.4 0.0 collective-permute-done.1.received.first_got
  10.4 0.6 %shard_map.89 = (f32[128,128]{1,0:T(8,128)S(1)}, f32[32,128]{1,0:T(8,128)S(1)}) custom-call(f32[512,128]{1,0:T(8,128)S(1)} %get-tuple-element.22.field_yz, f32[512,128]{1,0:T(8,128)S(1)} %collective-permute-done.1.received.first_got, f32[8,128]{1,0:T(8,128)S(1)} %collective-permute-done.2.mu_received, f32[512,128]{1,0:T(8,128)S(1)} %get-tuple-element.23.open_yz, ...), custom_call_target="tpu_custom_call" | custom-call | flops 10000000000 | tf_op jit(solution)/shard_map/pallas_call | solution.py:354
  11.0 1.0 %collective-permute-start.6 = (f32[32,128]{1,0:T(8,128)S(1)}, f32[32,128]{1,0:T(8,128)S(1)}, u32[]{:S(2)}, u32[]{:S(2)}) collective-permute-start(f32[32,128]{1,0:T(8,128)S(1)} %get-tuple-element.31.proj), channel_id=1, source_target_pairs={{0,1},{1,0},{2,3},{3,2},{4,5},{5,4},{6,7},{7,6},{8,9},{9,8},{10,11... | collective-permute-start | bytes 49160 | tf_op jit(solution)/shard_map/ppermute | solution.py:366
  12.0 0.0 collective-permute-done.5.right
  12.0 0.8 %collective-permute-done.6.proj_other = f32[32,128]{1,0:T(8,128)S(1)} collective-permute-done((f32[32,128]{1,0:T(8,128)S(1)}, f32[32,128]{1,0:T(8,128)S(1)}, u32[]{:S(2)}, u32[]{:S(2)}) %collective-permute-start.6) | collective-permute-done | bytes 16416 | tf_op jit(solution)/shard_map/ppermute | solution.py:366
  12.8 4.0 %collective-permute-start.7 = (f32[64,128]{1,0:T(8,128)S(1)}, f32[64,128]{1,0:T(8,128)S(1)}, u32[]{:S(2)}, u32[]{:S(2)}) collective-permute-start(f32[64,128]{1,0:T(8,128)S(1)} %shard_map.91.own), channel_id=1, source_target_pairs={{0,8},{2,10},{4,12},{6,14},{8,0},{10,2},{12,4},{14,6},{1,9},{3,11}... | collective-permute-start | bytes 98312 | tf_op jit(solution)/shard_map/ppermute | solution.py:366
  16.8 0.0 collective-permute-start.4
  16.8 1.9 %collective-permute-done.7.both = f32[64,128]{1,0:T(8,128)S(1)} collective-permute-done((f32[64,128]{1,0:T(8,128)S(1)}, f32[64,128]{1,0:T(8,128)S(1)}, u32[]{:S(2)}, u32[]{:S(2)}) %collective-permute-start.7) | collective-permute-done | bytes 32800 | tf_op jit(solution)/shard_map/ppermute | solution.py:366
  18.7 2.1 %collective-permute-start.8 = (f32[64,128]{1,0:T(8,128)S(1)}, f32[64,128]{1,0:T(8,128)S(1)}, u32[]{:S(2)}, u32[]{:S(2)}) collective-permute-start(f32[64,128]{1,0:T(8,128)S(1)} %get-tuple-element.32.sums), channel_id=1, source_target_pairs={{0,4},{2,6},{4,0},{6,2},{8,12},{10,14},{12,8},{14,10},{1,5},{3,7},... | collective-permute-start | bytes 98312 | tf_op jit(solution)/shard_map/ppermute | solution.py:366
  20.8 1.1 %collective-permute-start.10 = (f32[32,128]{1,0:T(8,128)S(1)}, f32[32,128]{1,0:T(8,128)S(1)}, u32[]{:S(2)}, u32[]{:S(2)}) collective-permute-start(f32[32,128]{1,0:T(8,128)S(1)} %get-tuple-element.37.proj), channel_id=1, source_target_pairs={{0,6},{2,4},{4,2},{6,0},{8,14},{10,12},{12,10},{14,8},{1,7},{3,5},... | collective-permute-start | bytes 49160 | tf_op jit(solution)/shard_map/ppermute | solution.py:366
  21.9 0.4 %collective-permute-start.9 = (f32[32,128]{1,0:T(8,128)S(1)}, f32[32,128]{1,0:T(8,128)S(1)}, u32[]{:S(2)}, u32[]{:S(2)}) collective-permute-start(f32[32,128]{1,0:T(8,128)S(1)} %get-tuple-element.37.proj), channel_id=1, source_target_pairs={{0,2},{2,0},{4,6},{6,4},{8,10},{10,8},{12,14},{14,12},{1,3},{3,1},... | collective-permute-start | bytes 49160 | tf_op jit(solution)/shard_map/ppermute | solution.py:366
  22.3 0.5 %collective-permute-done.8.far = f32[64,128]{1,0:T(8,128)S(1)} collective-permute-done((f32[64,128]{1,0:T(8,128)S(1)}, f32[64,128]{1,0:T(8,128)S(1)}, u32[]{:S(2)}, u32[]{:S(2)}) %collective-permute-start.8) | collective-permute-done | bytes 32800 | tf_op jit(solution)/shard_map/ppermute | solution.py:366
  22.8 1.4 %shard_map.93.factors = f32[64,128]{1,0:T(8,128)S(1)} custom-call(f32[64,128]{1,0:T(8,128)S(1)} %get-tuple-element.32.sums, f32[64,128]{1,0:T(8,128)S(1)} %collective-permute-done.8.far), custom_call_target="tpu_custom_call" | custom-call | tf_op jit(solution)/shard_map/pallas_call | solution.py:354
  24.2 0.0 collective-permute-done.4.behind_y
  24.2 0.0 collective-permute-done.3.second_got
  24.2 1.4 %shard_map.94 = (f32[768,128]{1,0:T(8,128)}, f32[768,128]{1,0:T(8,128)}, f32[64,64]{1,0:T(8,128)}, f32[64,64]{1,0:T(8,128)S(1)}) custom-call(f32[256,128]{1,0:T(8,128)S(1)} %get-tuple-element.21.field_x, f32[512,128]{1,0:T(8,128)S(1)} %get-tuple-element.22.field_yz, f32[256,128]{1,0:T(8,128)S(1)} %get-tuple-element.24.m_x, ...), custom_call_target="tpu_custom_call" | custom-call | tf_op jit(solution)/shard_map/pallas_call | solution.py:354
  25.6 0.0 collective-permute-done.10.far_cross
  25.6 0.0 collective-permute-done.9.near
  25.6 1.0 %shard_map.95 = f32[64,64]{1,0:T(8,128)} custom-call(f32[64,64]{1,0:T(8,128)S(1)} %get-tuple-element.36.inverse, f32[32,128]{1,0:T(8,128)S(1)} %get-tuple-element.37.proj, f32[32,128]{1,0:T(8,128)S(1)} %collective-permute-done.9.near, f32[64,128]{1,0:T(8,128)S(1)} %collective-permute-done.8.far, f32[32,128]{1,0:T(8,128)S(1)} %collective-permute-done.10.far_cross), custom_call_target="tpu_custom_call" | custom-call | tf_op jit(solution)/shard_map/pallas_call | solution.py:354
  (3 shorter events, 0.0 us)
Async XLA Ops:
  0.6 1.0 %copy-start = (f32[64,3,1,4,128]{4,3,2,1,0:T(4,128)S(1)}, f32[64,3,1,4,128]{4,3,2,1,0:T(4,128)}, u32[]{:S(2)}) copy-start(f32[64,3,1,4,128]{4,3,2,1,0:T(4,128)} %param.5) | copy-start | bytes 1179652
  1.7 8.7 %collective-permute-start.1 = (f32[512,128]{1,0:T(8,128)S(1)}, f32[512,128]{1,0:T(8,128)S(1)}, u32[]{:S(2)}, u32[]{:S(2)}) collective-permute-start(f32[512,128]{1,0:T(8,128)S(1)} %get-tuple-element.25), channel_id=1, source_target_pairs={{2,0},{4,2},{6,4},{8,6},{10,8},{12,10},{14,12},{0,1},{1,3},{3,5},{... | collective-permute-start | bytes 786440 | tf_op jit(solution)/shard_map/ppermute | solution.py:388
  2.8 2.8 %copy-start.1 = (s32[1,4,128]{2,1,0:T(4,128)S(1)}, s32[1,4,128]{2,1,0:T(4,128)}, u32[]{:S(2)}) copy-start(s32[1,4,128]{2,1,0:T(4,128)} %param.6) | copy-start | bytes 6148
  2.8 4.0 %collective-permute-start = (f32[160,128]{1,0:T(8,128)S(1)}, f32[160,128]{1,0:T(8,128)S(1)}, u32[]{:S(2)}, u32[]{:S(2)}) collective-permute-start(f32[160,128]{1,0:T(8,128)S(1)} %shard_map.85.gram_edge), channel_id=1, source_target_pairs={{0,1},{1,0},{2,3},{3,2},{4,5},{5,4},{6,7},{7,6},{8,9},{9,8},{10,11... | collective-permute-start | bytes 245768 | tf_op jit(solution)/shard_map/ppermute | solution.py:366
  5.5 0.7 %copy-start.2 = (f32[8]{0:T(128)S(1)}, f32[8]{0:T(128)}, u32[]{:S(2)}) copy-start(f32[8]{0:T(128)} %mu_table.1) | copy-start | bytes 100
  5.5 0.7 %copy-start.3 = (f32[8]{0:T(128)S(1)}, f32[8]{0:T(128)}, u32[]{:S(2)}) copy-start(f32[8]{0:T(128)} %eps_table.1) | copy-start | bytes 100
  6.7 3.7 %collective-permute-start.2 = (f32[8,128]{1,0:T(8,128)S(1)}, f32[8,128]{1,0:T(8,128)S(1)}, u32[]{:S(2)}, u32[]{:S(2)}) collective-permute-start(f32[8,128]{1,0:T(8,128)S(1)} %shard_map.86.material), channel_id=1, source_target_pairs={{2,0},{4,2},{6,4},{8,6},{10,8},{12,10},{14,12},{0,1},{1,3},{3,5},{... | collective-permute-start | bytes 12296 | tf_op jit(solution)/shard_map/ppermute | solution.py:393
  6.9 5.1 %collective-permute-start.5 = (f32[32,128]{1,0:T(8,128)S(1)}, f32[32,128]{1,0:T(8,128)S(1)}, u32[]{:S(2)}, u32[]{:S(2)}) collective-permute-start(f32[32,128]{1,0:T(8,128)S(1)} %get-tuple-element.30.left), channel_id=1, source_target_pairs={{0,2},{2,0},{4,6},{6,4},{8,10},{10,8},{12,14},{14,12},{1,3},{3,1},... | collective-permute-start | bytes 49160 | tf_op jit(solution)/shard_map/ppermute | solution.py:366
  10.1 14.1 %collective-permute-start.3 = (f32[520,128]{1,0:T(8,128)S(1)}, f32[520,128]{1,0:T(8,128)S(1)}, u32[]{:S(2)}, u32[]{:S(2)}) collective-permute-start(f32[520,128]{1,0:T(8,128)S(1)} %get-tuple-element.26), channel_id=1, source_target_pairs={{0,2},{2,4},{4,6},{6,8},{8,10},{10,12},{12,14},{1,0},{3,1},{5,3},{... | collective-permute-start | bytes 798728 | tf_op jit(solution)/shard_map/ppermute | solution.py:412
  11.0 1.9 %collective-permute-start.6 = (f32[32,128]{1,0:T(8,128)S(1)}, f32[32,128]{1,0:T(8,128)S(1)}, u32[]{:S(2)}, u32[]{:S(2)}) collective-permute-start(f32[32,128]{1,0:T(8,128)S(1)} %get-tuple-element.31.proj), channel_id=1, source_target_pairs={{0,1},{1,0},{2,3},{3,2},{4,5},{5,4},{6,7},{7,6},{8,9},{9,8},{10,11... | collective-permute-start | bytes 49160 | tf_op jit(solution)/shard_map/ppermute | solution.py:366
  12.8 5.8 %collective-permute-start.7 = (f32[64,128]{1,0:T(8,128)S(1)}, f32[64,128]{1,0:T(8,128)S(1)}, u32[]{:S(2)}, u32[]{:S(2)}) collective-permute-start(f32[64,128]{1,0:T(8,128)S(1)} %shard_map.91.own), channel_id=1, source_target_pairs={{0,8},{2,10},{4,12},{6,14},{8,0},{10,2},{12,4},{14,6},{1,9},{3,11}... | collective-permute-start | bytes 98312 | tf_op jit(solution)/shard_map/ppermute | solution.py:366
  16.8 7.4 %collective-permute-start.4 = (f32[128,128]{1,0:T(8,128)S(1)}, f32[128,128]{1,0:T(8,128)S(1)}, u32[]{:S(2)}, u32[]{:S(2)}) collective-permute-start(f32[128,128]{1,0:T(8,128)S(1)} %get-tuple-element.28), channel_id=1, source_target_pairs={{0,1},{1,0},{2,3},{3,2},{4,5},{5,4},{6,7},{7,6},{8,9},{9,8},{10,11... | collective-permute-start | bytes 196616 | tf_op jit(solution)/shard_map/ppermute | solution.py:366
  18.7 4.1 %collective-permute-start.8 = (f32[64,128]{1,0:T(8,128)S(1)}, f32[64,128]{1,0:T(8,128)S(1)}, u32[]{:S(2)}, u32[]{:S(2)}) collective-permute-start(f32[64,128]{1,0:T(8,128)S(1)} %get-tuple-element.32.sums), channel_id=1, source_target_pairs={{0,4},{2,6},{4,0},{6,2},{8,12},{10,14},{12,8},{14,10},{1,5},{3,7},... | collective-permute-start | bytes 98312 | tf_op jit(solution)/shard_map/ppermute | solution.py:366
  20.8 4.8 %collective-permute-start.10 = (f32[32,128]{1,0:T(8,128)S(1)}, f32[32,128]{1,0:T(8,128)S(1)}, u32[]{:S(2)}, u32[]{:S(2)}) collective-permute-start(f32[32,128]{1,0:T(8,128)S(1)} %get-tuple-element.37.proj), channel_id=1, source_target_pairs={{0,6},{2,4},{4,2},{6,0},{8,14},{10,12},{12,10},{14,8},{1,7},{3,5},... | collective-permute-start | bytes 49160 | tf_op jit(solution)/shard_map/ppermute | solution.py:366
  21.9 3.7 %collective-permute-start.9 = (f32[32,128]{1,0:T(8,128)S(1)}, f32[32,128]{1,0:T(8,128)S(1)}, u32[]{:S(2)}, u32[]{:S(2)}) collective-permute-start(f32[32,128]{1,0:T(8,128)S(1)} %get-tuple-element.37.proj), channel_id=1, source_target_pairs={{0,2},{2,0},{4,6},{6,4},{8,10},{10,8},{12,14},{14,12},{1,3},{3,1},... | collective-permute-start | bytes 49160 | tf_op jit(solution)/shard_map/ppermute | solution.py:366

commit v13 on v12

--- a/solution.py
+++ b/solution.py
@@ -398,7 +398,7 @@
         (large, pair),
         flops=0,
     )
-    gram_other = swapped(gram, "row", 1)
+    gram_other = swapped(gram, "row", 2)
     m_x, near, send, thirds = call(
         functools.partial(near_kernel, columns, cells),
         (),
@@ -429,8 +429,8 @@
         sums = sums + swapped(sums, "row", step)
         proj = sums[half:]
         step *= 2
-    far = swapped(sums, "row", 2)
-    proj_near = swapped(proj, "row", 1)
+    far = swapped(sums, "row", 1)
+    proj_near = swapped(proj, "row", 2)
     far_cross = swapped(proj, "row", 3)
     (factors,) = call(
         functools.partial(factor_kernel, total), (), (sums, far), ((columns, 2 * columns),), flops=0

time: 26.8 us -> 26.9 us (level)
    ppermute x8, starting transfers between devices: 12.7 us -> 11.7 us  [swapped(): lax.ppermute(x, axis, [(i, i ^ step) for i in range(lax.axis_size(axis))])]
    ppermute x1, starting transfers between devices: 0.03 us -> 0.94 us  [local(): second_got = lax.ppermute(send, ('row', 'col'), halo_ring(rows, True))]
    ppermute x8, waiting for transfers between devices: 3.22 us -> 3.64 us  [swapped(): lax.ppermute(x, axis, [(i, i ^ step) for i in range(lax.axis_size(axis))])]
    ppermute x1, waiting for transfers between devices: 0.3 us -> 0.01 us  [local(): mu_received = lax.ppermute(material, ('row', 'col'), halo_ring(rows, False))]
where the time goes in v13:
time: 26.9 us; the launch traced here: 26.7 us
  starting transfers between devices  13.2 us (49%)
  Pallas kernels  6.76 us (25%)
  waiting for transfers between devices  3.65 us (14%)
  local copies, waits for them, and re-layouts  1.64 us (6%)
  between operations  1.42 us (5%)
    ppermute x8, starting transfers between devices, swapped(): lax.ppermute(x, axis, [(i, i ^ step) for i in range(lax.axis_size(axis))])  11.7 us
    pallas_call x12, Pallas kernels, call(): pl.pallas_call(body, out_shape=shapes, in_specs=[SMEM] * len(scalars) + [...  6.76 us
    ppermute x8, waiting for transfers between devices, swapped(): lax.ppermute(x, axis, [(i, i ^ step) for i in range(lax.axis_size(axis))])  3.64 us
    unnamed x8, local copies, waits for them, and re-layouts  1.64 us
    ppermute x1, starting transfers between devices, local(): second_got = lax.ppermute(send, ('row', 'col'), halo_ring(rows, True))  0.94 us
  transfers between devices with their start and end apart: 11, of which 4 were waited for; matrix products, arithmetic and copies ran while one was open for 0% of the time, Pallas kernels for 21%

profile of v13, /device:TPU:0, one launch (start us, length us, event | category | flops | bytes accessed | tf_op | source)
XLA Modules:
  0.0 26.7 jit_solution(4686519468517818536)
XLA Ops:
  0.6 0.0 copy-start
  0.6 1.0 %copy-done = f32[64,3,1,4,128]{4,3,2,1,0:T(4,128)S(1)} copy-done((f32[64,3,1,4,128]{4,3,2,1,0:T(4,128)S(1)}, f32[64,3,1,4,128]{4,3,2,1,0:T(4,128)}, u32[]{:S(2)}) %copy-start) | copy-done | bytes 393240
  1.6 0.1 shard_map.84
  1.7 0.5 %collective-permute-start.1 = (f32[512,128]{1,0:T(8,128)S(1)}, f32[512,128]{1,0:T(8,128)S(1)}, u32[]{:S(2)}, u32[]{:S(2)}) collective-permute-start(f32[512,128]{1,0:T(8,128)S(1)} %get-tuple-element.25), channel_id=1, source_target_pairs={{2,0},{4,2},{6,4},{8,6},{10,8},{12,10},{14,12},{0,1},{1,3},{3,5},{... | collective-permute-start | bytes 786440 | tf_op jit(solution)/shard_map/ppermute | solution.py:388
  2.2 0.5 %shard_map.85.gram_edge = f32[160,128]{1,0:T(8,128)S(1)} custom-call(f32[256,128]{1,0:T(8,128)S(1)} %get-tuple-element.21.field_x, f32[512,128]{1,0:T(8,128)S(1)} %get-tuple-element.22.field_yz), custom_call_target="tpu_custom_call" | custom-call | tf_op jit(solution)/shard_map/pallas_call | solution.py:354
  2.8 0.0 copy-start.1
  2.8 2.1 %collective-permute-start = (f32[160,128]{1,0:T(8,128)S(1)}, f32[160,128]{1,0:T(8,128)S(1)}, u32[]{:S(2)}, u32[]{:S(2)}) collective-permute-start(f32[160,128]{1,0:T(8,128)S(1)} %shard_map.85.gram_edge), channel_id=1, source_target_pairs={{0,1},{1,0},{2,3},{3,2},{4,5},{5,4},{6,7},{7,6},{8,9},{9,8},{10,11... | collective-permute-start | bytes 245768 | tf_op jit(solution)/shard_map/ppermute | solution.py:366
  5.5 0.0 copy-start.2
  5.5 0.0 copy-start.3
  5.5 0.0 copy-done.1
  5.5 0.6 %copy-done.2 = f32[8]{0:T(128)S(1)} copy-done((f32[8]{0:T(128)S(1)}, f32[8]{0:T(128)}, u32[]{:S(2)}) %copy-start.2) | copy-done | bytes 56
  6.2 0.0 copy-done.3
  6.2 0.6 %shard_map.86.material = f32[8,128]{1,0:T(8,128)S(1)} custom-call(f32[8]{0:T(128)S(1)} %copy-done.2, f32[8]{0:T(128)S(1)} %copy-done.3, f32[1]{0:T(128)S(6)} %copy.11.shift, s32[4,128]{1,0:T(4,128)S(1)} %bitcast.9), custom_call_target="tpu_custom_call" | custom-call | tf_op jit(solution)/shard_map/pallas_call | solution.py:354
  6.7 0.1 collective-permute-start.2
  6.8 0.0 collective-permute-done.ahead_y
  6.8 0.1 shard_map.87
  6.9 3.1 %collective-permute-start.5 = (f32[32,128]{1,0:T(8,128)S(1)}, f32[32,128]{1,0:T(8,128)S(1)}, u32[]{:S(2)}, u32[]{:S(2)}) collective-permute-start(f32[32,128]{1,0:T(8,128)S(1)} %get-tuple-element.30.left), channel_id=1, source_target_pairs={{0,4},{2,6},{4,0},{6,2},{8,12},{10,14},{12,8},{14,10},{1,5},{3,7},... | collective-permute-start | bytes 49160 | tf_op jit(solution)/shard_map/ppermute | solution.py:366
  10.0 1.1 %shard_map.88 = (f32[256,128]{1,0:T(8,128)S(1)}, f32[32,128]{1,0:T(8,128)S(1)}, f32[520,128]{1,0:T(8,128)S(1)}, bf16[192,1536]{1,0:T(8,128)(2,1)S(1)}) custom-call(f32[256,128]{1,0:T(8,128)S(1)} %get-tuple-element.21.field_x, f32[512,128]{1,0:T(8,128)S(1)} %get-tuple-element.22.field_yz, f32[160,128]{1,0:T(8,128)S(1)} %collective-permute-done.ahead_y, ...), custom_call_target="tpu_custom_call" | custom-call | tf_op jit(solution)/shard_map/pallas_call | solution.py:354
  11.1 0.9 %collective-permute-start.3 = (f32[520,128]{1,0:T(8,128)S(1)}, f32[520,128]{1,0:T(8,128)S(1)}, u32[]{:S(2)}, u32[]{:S(2)}) collective-permute-start(f32[520,128]{1,0:T(8,128)S(1)} %get-tuple-element.26), channel_id=1, source_target_pairs={{0,2},{2,4},{4,6},{6,8},{8,10},{10,12},{12,14},{1,0},{3,1},{5,3},{... | collective-permute-start | bytes 798728 | tf_op jit(solution)/shard_map/ppermute | solution.py:412
  12.0 0.0 collective-permute-done.2.mu_received
  12.0 0.0 collective-permute-done.1.received.first_got
  12.0 0.6 %shard_map.89 = (f32[128,128]{1,0:T(8,128)S(1)}, f32[32,128]{1,0:T(8,128)S(1)}) custom-call(f32[512,128]{1,0:T(8,128)S(1)} %get-tuple-element.22.field_yz, f32[512,128]{1,0:T(8,128)S(1)} %collective-permute-done.1.received.first_got, f32[8,128]{1,0:T(8,128)S(1)} %collective-permute-done.2.mu_received, f32[512,128]{1,0:T(8,128)S(1)} %get-tuple-element.23.open_yz, ...), custom_call_target="tpu_custom_call" | custom-call | flops 10000000000 | tf_op jit(solution)/shard_map/pallas_call | solution.py:354
  12.6 0.0 collective-permute-start.6
  12.6 0.0 collective-permute-done.5.right
  12.6 1.1 %collective-permute-done.6.proj_other = f32[32,128]{1,0:T(8,128)S(1)} collective-permute-done((f32[32,128]{1,0:T(8,128)S(1)}, f32[32,128]{1,0:T(8,128)S(1)}, u32[]{:S(2)}, u32[]{:S(2)}) %collective-permute-start.6) | collective-permute-done | bytes 16416 | tf_op jit(solution)/shard_map/ppermute | solution.py:366
  13.8 2.8 %collective-permute-start.7 = (f32[64,128]{1,0:T(8,128)S(1)}, f32[64,128]{1,0:T(8,128)S(1)}, u32[]{:S(2)}, u32[]{:S(2)}) collective-permute-start(f32[64,128]{1,0:T(8,128)S(1)} %shard_map.91.own), channel_id=1, source_target_pairs={{0,8},{2,10},{4,12},{6,14},{8,0},{10,2},{12,4},{14,6},{1,9},{3,11}... | collective-permute-start | bytes 98312 | tf_op jit(solution)/shard_map/ppermute | solution.py:366
  16.6 0.0 collective-permute-start.4
  16.6 2.0 %collective-permute-done.7.both = f32[64,128]{1,0:T(8,128)S(1)} collective-permute-done((f32[64,128]{1,0:T(8,128)S(1)}, f32[64,128]{1,0:T(8,128)S(1)}, u32[]{:S(2)}, u32[]{:S(2)}) %collective-permute-start.7) | collective-permute-done | bytes 32800 | tf_op jit(solution)/shard_map/ppermute | solution.py:366
  18.6 0.8 %collective-permute-start.8 = (f32[64,128]{1,0:T(8,128)S(1)}, f32[64,128]{1,0:T(8,128)S(1)}, u32[]{:S(2)}, u32[]{:S(2)}) collective-permute-start(f32[64,128]{1,0:T(8,128)S(1)} %get-tuple-element.32.sums), channel_id=1, source_target_pairs={{0,2},{2,0},{4,6},{6,4},{8,10},{10,8},{12,14},{14,12},{1,3},{3,1},... | collective-permute-start | bytes 98312 | tf_op jit(solution)/shard_map/ppermute | solution.py:366
  19.5 2.4 %collective-permute-start.10 = (f32[32,128]{1,0:T(8,128)S(1)}, f32[32,128]{1,0:T(8,128)S(1)}, u32[]{:S(2)}, u32[]{:S(2)}) collective-permute-start(f32[32,128]{1,0:T(8,128)S(1)} %get-tuple-element.37.proj), channel_id=1, source_target_pairs={{0,6},{2,4},{4,2},{6,0},{8,14},{10,12},{12,10},{14,8},{1,7},{3,5},... | collective-permute-start | bytes 49160 | tf_op jit(solution)/shard_map/ppermute | solution.py:366
  21.9 0.4 %collective-permute-start.9 = (f32[32,128]{1,0:T(8,128)S(1)}, f32[32,128]{1,0:T(8,128)S(1)}, u32[]{:S(2)}, u32[]{:S(2)}) collective-permute-start(f32[32,128]{1,0:T(8,128)S(1)} %get-tuple-element.37.proj), channel_id=1, source_target_pairs={{0,4},{2,6},{4,0},{6,2},{8,12},{10,14},{12,8},{14,10},{1,5},{3,7},... | collective-permute-start | bytes 49160 | tf_op jit(solution)/shard_map/ppermute | solution.py:366
  22.3 0.2 collective-permute-done.8.far
  22.5 1.4 %shard_map.93.factors = f32[64,128]{1,0:T(8,128)S(1)} custom-call(f32[64,128]{1,0:T(8,128)S(1)} %get-tuple-element.32.sums, f32[64,128]{1,0:T(8,128)S(1)} %collective-permute-done.8.far), custom_call_target="tpu_custom_call" | custom-call | tf_op jit(solution)/shard_map/pallas_call | solution.py:354
  23.9 0.0 collective-permute-done.4.behind_y
  24.0 0.0 collective-permute-done.3.second_got
  24.0 1.4 %shard_map.94 = (f32[768,128]{1,0:T(8,128)}, f32[768,128]{1,0:T(8,128)}, f32[64,64]{1,0:T(8,128)}, f32[64,64]{1,0:T(8,128)S(1)}) custom-call(f32[256,128]{1,0:T(8,128)S(1)} %get-tuple-element.21.field_x, f32[512,128]{1,0:T(8,128)S(1)} %get-tuple-element.22.field_yz, f32[256,128]{1,0:T(8,128)S(1)} %get-tuple-element.24.m_x, ...), custom_call_target="tpu_custom_call" | custom-call | tf_op jit(solution)/shard_map/pallas_call | solution.py:354
  25.3 0.0 collective-permute-done.10.far_cross
  25.3 0.3 %collective-permute-done.9.near = f32[32,128]{1,0:T(8,128)S(1)} collective-permute-done((f32[32,128]{1,0:T(8,128)S(1)}, f32[32,128]{1,0:T(8,128)S(1)}, u32[]{:S(2)}, u32[]{:S(2)}) %collective-permute-start.9) | collective-permute-done | bytes 16416 | tf_op jit(solution)/shard_map/ppermute | solution.py:366
  25.6 1.0 %shard_map.95 = f32[64,64]{1,0:T(8,128)} custom-call(f32[64,64]{1,0:T(8,128)S(1)} %get-tuple-element.36.inverse, f32[32,128]{1,0:T(8,128)S(1)} %get-tuple-element.37.proj, f32[32,128]{1,0:T(8,128)S(1)} %collective-permute-done.9.near, f32[64,128]{1,0:T(8,128)S(1)} %collective-permute-done.8.far, f32[32,128]{1,0:T(8,128)S(1)} %collective-permute-done.10.far_cross), custom_call_target="tpu_custom_call" | custom-call | tf_op jit(solution)/shard_map/pallas_call | solution.py:354
  (3 shorter events, 0.0 us)
Async XLA Ops:
  0.6 1.0 %copy-start = (f32[64,3,1,4,128]{4,3,2,1,0:T(4,128)S(1)}, f32[64,3,1,4,128]{4,3,2,1,0:T(4,128)}, u32[]{:S(2)}) copy-start(f32[64,3,1,4,128]{4,3,2,1,0:T(4,128)} %param.5) | copy-start | bytes 1179652
  1.7 10.3 %collective-permute-start.1 = (f32[512,128]{1,0:T(8,128)S(1)}, f32[512,128]{1,0:T(8,128)S(1)}, u32[]{:S(2)}, u32[]{:S(2)}) collective-permute-start(f32[512,128]{1,0:T(8,128)S(1)} %get-tuple-element.25), channel_id=1, source_target_pairs={{2,0},{4,2},{6,4},{8,6},{10,8},{12,10},{14,12},{0,1},{1,3},{3,5},{... | collective-permute-start | bytes 786440 | tf_op jit(solution)/shard_map/ppermute | solution.py:388
  2.8 2.8 %copy-start.1 = (s32[1,4,128]{2,1,0:T(4,128)S(1)}, s32[1,4,128]{2,1,0:T(4,128)}, u32[]{:S(2)}) copy-start(s32[1,4,128]{2,1,0:T(4,128)} %param.6) | copy-start | bytes 6148
  2.8 4.0 %collective-permute-start = (f32[160,128]{1,0:T(8,128)S(1)}, f32[160,128]{1,0:T(8,128)S(1)}, u32[]{:S(2)}, u32[]{:S(2)}) collective-permute-start(f32[160,128]{1,0:T(8,128)S(1)} %shard_map.85.gram_edge), channel_id=1, source_target_pairs={{0,1},{1,0},{2,3},{3,2},{4,5},{5,4},{6,7},{7,6},{8,9},{9,8},{10,11... | collective-permute-start | bytes 245768 | tf_op jit(solution)/shard_map/ppermute | solution.py:366
  5.5 0.7 %copy-start.2 = (f32[8]{0:T(128)S(1)}, f32[8]{0:T(128)}, u32[]{:S(2)}) copy-start(f32[8]{0:T(128)} %mu_table.1) | copy-start | bytes 100
  5.5 0.7 %copy-start.3 = (f32[8]{0:T(128)S(1)}, f32[8]{0:T(128)}, u32[]{:S(2)}) copy-start(f32[8]{0:T(128)} %eps_table.1) | copy-start | bytes 100
  6.7 5.3 %collective-permute-start.2 = (f32[8,128]{1,0:T(8,128)S(1)}, f32[8,128]{1,0:T(8,128)S(1)}, u32[]{:S(2)}, u32[]{:S(2)}) collective-permute-start(f32[8,128]{1,0:T(8,128)S(1)} %shard_map.86.material), channel_id=1, source_target_pairs={{2,0},{4,2},{6,4},{8,6},{10,8},{12,10},{14,12},{0,1},{1,3},{3,5},{... | collective-permute-start | bytes 12296 | tf_op jit(solution)/shard_map/ppermute | solution.py:393
  6.9 5.7 %collective-permute-start.5 = (f32[32,128]{1,0:T(8,128)S(1)}, f32[32,128]{1,0:T(8,128)S(1)}, u32[]{:S(2)}, u32[]{:S(2)}) collective-permute-start(f32[32,128]{1,0:T(8,128)S(1)} %get-tuple-element.30.left), channel_id=1, source_target_pairs={{0,4},{2,6},{4,0},{6,2},{8,12},{10,14},{12,8},{14,10},{1,5},{3,7},... | collective-permute-start | bytes 49160 | tf_op jit(solution)/shard_map/ppermute | solution.py:366
  11.1 12.9 %collective-permute-start.3 = (f32[520,128]{1,0:T(8,128)S(1)}, f32[520,128]{1,0:T(8,128)S(1)}, u32[]{:S(2)}, u32[]{:S(2)}) collective-permute-start(f32[520,128]{1,0:T(8,128)S(1)} %get-tuple-element.26), channel_id=1, source_target_pairs={{0,2},{2,4},{4,6},{6,8},{8,10},{10,12},{12,14},{1,0},{3,1},{5,3},{... | collective-permute-start | bytes 798728 | tf_op jit(solution)/shard_map/ppermute | solution.py:412
  12.6 1.2 %collective-permute-start.6 = (f32[32,128]{1,0:T(8,128)S(1)}, f32[32,128]{1,0:T(8,128)S(1)}, u32[]{:S(2)}, u32[]{:S(2)}) collective-permute-start(f32[32,128]{1,0:T(8,128)S(1)} %get-tuple-element.31.proj), channel_id=1, source_target_pairs={{0,1},{1,0},{2,3},{3,2},{4,5},{5,4},{6,7},{7,6},{8,9},{9,8},{10,11... | collective-permute-start | bytes 49160 | tf_op jit(solution)/shard_map/ppermute | solution.py:366
  13.8 4.8 %collective-permute-start.7 = (f32[64,128]{1,0:T(8,128)S(1)}, f32[64,128]{1,0:T(8,128)S(1)}, u32[]{:S(2)}, u32[]{:S(2)}) collective-permute-start(f32[64,128]{1,0:T(8,128)S(1)} %shard_map.91.own), channel_id=1, source_target_pairs={{0,8},{2,10},{4,12},{6,14},{8,0},{10,2},{12,4},{14,6},{1,9},{3,11}... | collective-permute-start | bytes 98312 | tf_op jit(solution)/shard_map/ppermute | solution.py:366
  16.6 7.3 %collective-permute-start.4 = (f32[128,128]{1,0:T(8,128)S(1)}, f32[128,128]{1,0:T(8,128)S(1)}, u32[]{:S(2)}, u32[]{:S(2)}) collective-permute-start(f32[128,128]{1,0:T(8,128)S(1)} %get-tuple-element.28), channel_id=1, source_target_pairs={{0,1},{1,0},{2,3},{3,2},{4,5},{5,4},{6,7},{7,6},{8,9},{9,8},{10,11... | collective-permute-start | bytes 196616 | tf_op jit(solution)/shard_map/ppermute | solution.py:366
  18.6 3.9 %collective-permute-start.8 = (f32[64,128]{1,0:T(8,128)S(1)}, f32[64,128]{1,0:T(8,128)S(1)}, u32[]{:S(2)}, u32[]{:S(2)}) collective-permute-start(f32[64,128]{1,0:T(8,128)S(1)} %get-tuple-element.32.sums), channel_id=1, source_target_pairs={{0,2},{2,0},{4,6},{6,4},{8,10},{10,8},{12,14},{14,12},{1,3},{3,1},... | collective-permute-start | bytes 98312 | tf_op jit(solution)/shard_map/ppermute | solution.py:366
  19.5 5.9 %collective-permute-start.10 = (f32[32,128]{1,0:T(8,128)S(1)}, f32[32,128]{1,0:T(8,128)S(1)}, u32[]{:S(2)}, u32[]{:S(2)}) collective-permute-start(f32[32,128]{1,0:T(8,128)S(1)} %get-tuple-element.37.proj), channel_id=1, source_target_pairs={{0,6},{2,4},{4,2},{6,0},{8,14},{10,12},{12,10},{14,8},{1,7},{3,5},... | collective-permute-start | bytes 49160 | tf_op jit(solution)/shard_map/ppermute | solution.py:366
  21.9 3.7 %collective-permute-start.9 = (f32[32,128]{1,0:T(8,128)S(1)}, f32[32,128]{1,0:T(8,128)S(1)}, u32[]{:S(2)}, u32[]{:S(2)}) collective-permute-start(f32[32,128]{1,0:T(8,128)S(1)} %get-tuple-element.37.proj), channel_id=1, source_target_pairs={{0,4},{2,6},{4,0},{6,2},{8,12},{10,14},{12,8},{14,10},{1,5},{3,7},... | collective-permute-start | bytes 49160 | tf_op jit(solution)/shard_map/ppermute | solution.py:366

commit v14 on v13

--- a/solution.py
+++ b/solution.py
@@ -269,13 +269,14 @@
 
 
 def basis_kernel(
-    columns, cells, field_x, field_yz, m_x, open_yz, first_got, mu_received, second_got, behind_y,
+    columns, cells, total, field_x, field_yz, m_x, open_yz, first_got, mu_received, second_got, behind_y,
     material, thirds_ref, factors,
-    out_basis, out_image, out_upper, out_inverse, basis, image, upper, sems,
+    out_basis, out_image, out_upper, out_inverse, out_turned, basis, image, upper, sems,
 ):
     stride = 3 * cells
     inverse = factors[:, columns:]
     out_inverse[...] = inverse
+    out_turned[...] = inverse.T / total
     upper[...] = factors[:, :columns]
     third = pltpu.make_async_copy(upper, out_upper, sems.at[2])
     third.start()
@@ -330,14 +331,17 @@
     third.wait()
 
 
-def proj_kernel(total, inverse, proj, near, far, far_cross, out):
+def proj_kernel(inverse, turned, proj, near, far, far_cross, out):
     half = proj.shape[0]
     raw = (proj[...] + near[...]) + (far[half:, :] + far_cross[...])
     left = lax.dot_general(
-        inverse[...], unpacked(raw) / total, (((1,), (0,)), ((), ())),
+        inverse[...], unpacked(raw), (((1,), (0,)), ((), ())),
         precision=lax.Precision.HIGHEST, preferred_element_type=F32,
     )
-    out[...] = inner(left, inverse[...])
+    out[...] = lax.dot_general(
+        left, turned[...], (((1,), (0,)), ((), ())), precision=lax.Precision.HIGHEST,
+        preferred_element_type=F32,
+    )
 
 
 SMEM = pl.BlockSpec(memory_space=pltpu.SMEM)
@@ -435,14 +439,14 @@
     (factors,) = call(
         functools.partial(factor_kernel, total), (), (sums, far), ((columns, 2 * columns),), flops=0
     )
-    basis_out, image_out, upper, inverse = call(
-        functools.partial(basis_kernel, columns, cells),
+    basis_out, image_out, upper, inverse, turned = call(
+        functools.partial(basis_kernel, columns, cells, total),
         (),
         (
             field_x, field_yz, m_x, open_yz, first_got, mu_received, second_got, behind_y, material,
             thirds, factors,
         ),
-        (basis.shape, basis.shape, square, square),
+        (basis.shape, basis.shape, square, square, square),
         flops=0,
         far=3,
         scratch=[
@@ -453,9 +457,9 @@
         ],
     )
     (projected,) = call(
-        functools.partial(proj_kernel, total),
+        proj_kernel,
         (),
-        (inverse, proj, proj_near, far, far_cross),
+        (inverse, turned, proj, proj_near, far, far_cross),
         (square,),
         flops=0,
     )

time: 26.9 us -> 26.8 us (level)
  no operation moved by 1% of the time
where the time goes in v14:
time: 26.8 us; the launch traced here: 26.7 us
  starting transfers between devices  13.2 us (49%)
  Pallas kernels  6.74 us (25%)
  waiting for transfers between devices  3.65 us (14%)
  local copies, waits for them, and re-layouts  1.64 us (6%)
  between operations  1.42 us (5%)
    ppermute x8, starting transfers between devices, swapped(): lax.ppermute(x, axis, [(i, i ^ step) for i in range(lax.axis_size(axis))])  11.7 us
    pallas_call x12, Pallas kernels, call(): pl.pallas_call(body, out_shape=shapes, in_specs=[SMEM] * len(scalars) + [...  6.74 us
    ppermute x8, waiting for transfers between devices, swapped(): lax.ppermute(x, axis, [(i, i ^ step) for i in range(lax.axis_size(axis))])  3.64 us
    unnamed x8, local copies, waits for them, and re-layouts  1.64 us
    ppermute x1, starting transfers between devices, local(): second_got = lax.ppermute(send, ('row', 'col'), halo_ring(rows, True))  0.94 us
  transfers between devices with their start and end apart: 11, of which 4 were waited for; matrix products, arithmetic and copies ran while one was open for 0% of the time, Pallas kernels for 21%

profile of v14, /device:TPU:0, one launch (start us, length us, event | category | flops | bytes accessed | tf_op | source)
XLA Modules:
  0.0 26.7 jit_solution(987243905431504010)
XLA Ops:
  0.6 0.0 copy-start
  0.6 1.0 %copy-done = f32[64,3,1,4,128]{4,3,2,1,0:T(4,128)S(1)} copy-done((f32[64,3,1,4,128]{4,3,2,1,0:T(4,128)S(1)}, f32[64,3,1,4,128]{4,3,2,1,0:T(4,128)}, u32[]{:S(2)}) %copy-start) | copy-done | bytes 393240
  1.6 0.1 shard_map.84
  1.7 0.5 %collective-permute-start.1 = (f32[512,128]{1,0:T(8,128)S(1)}, f32[512,128]{1,0:T(8,128)S(1)}, u32[]{:S(2)}, u32[]{:S(2)}) collective-permute-start(f32[512,128]{1,0:T(8,128)S(1)} %get-tuple-element.26), channel_id=1, source_target_pairs={{2,0},{4,2},{6,4},{8,6},{10,8},{12,10},{14,12},{0,1},{1,3},{3,5},{... | collective-permute-start | bytes 786440 | tf_op jit(solution)/shard_map/ppermute | solution.py:392
  2.2 0.5 %shard_map.85.gram_edge = f32[160,128]{1,0:T(8,128)S(1)} custom-call(f32[256,128]{1,0:T(8,128)S(1)} %get-tuple-element.22.field_x, f32[512,128]{1,0:T(8,128)S(1)} %get-tuple-element.23.field_yz), custom_call_target="tpu_custom_call" | custom-call | tf_op jit(solution)/shard_map/pallas_call | solution.py:358
  2.8 0.0 copy-start.1
  2.8 2.1 %collective-permute-start = (f32[160,128]{1,0:T(8,128)S(1)}, f32[160,128]{1,0:T(8,128)S(1)}, u32[]{:S(2)}, u32[]{:S(2)}) collective-permute-start(f32[160,128]{1,0:T(8,128)S(1)} %shard_map.85.gram_edge), channel_id=1, source_target_pairs={{0,1},{1,0},{2,3},{3,2},{4,5},{5,4},{6,7},{7,6},{8,9},{9,8},{10,11... | collective-permute-start | bytes 245768 | tf_op jit(solution)/shard_map/ppermute | solution.py:370
  5.5 0.0 copy-start.2
  5.5 0.0 copy-start.3
  5.5 0.0 copy-done.1
  5.5 0.6 %copy-done.2 = f32[8]{0:T(128)S(1)} copy-done((f32[8]{0:T(128)S(1)}, f32[8]{0:T(128)}, u32[]{:S(2)}) %copy-start.2) | copy-done | bytes 56
  6.2 0.0 copy-done.3
  6.2 0.6 %shard_map.86.material = f32[8,128]{1,0:T(8,128)S(1)} custom-call(f32[8]{0:T(128)S(1)} %copy-done.2, f32[8]{0:T(128)S(1)} %copy-done.3, f32[1]{0:T(128)S(6)} %copy.11.shift, s32[4,128]{1,0:T(4,128)S(1)} %bitcast.9), custom_call_target="tpu_custom_call" | custom-call | tf_op jit(solution)/shard_map/pallas_call | solution.py:358
  6.7 0.1 collective-permute-start.2
  6.8 0.0 collective-permute-done.ahead_y
  6.8 0.1 shard_map.87
  6.9 3.1 %collective-permute-start.5 = (f32[32,128]{1,0:T(8,128)S(1)}, f32[32,128]{1,0:T(8,128)S(1)}, u32[]{:S(2)}, u32[]{:S(2)}) collective-permute-start(f32[32,128]{1,0:T(8,128)S(1)} %get-tuple-element.31.left), channel_id=1, source_target_pairs={{0,4},{2,6},{4,0},{6,2},{8,12},{10,14},{12,8},{14,10},{1,5},{3,7},... | collective-permute-start | bytes 49160 | tf_op jit(solution)/shard_map/ppermute | solution.py:370
  10.0 1.1 %shard_map.88 = (f32[256,128]{1,0:T(8,128)S(1)}, f32[32,128]{1,0:T(8,128)S(1)}, f32[520,128]{1,0:T(8,128)S(1)}, bf16[192,1536]{1,0:T(8,128)(2,1)S(1)}) custom-call(f32[256,128]{1,0:T(8,128)S(1)} %get-tuple-element.22.field_x, f32[512,128]{1,0:T(8,128)S(1)} %get-tuple-element.23.field_yz, f32[160,128]{1,0:T(8,128)S(1)} %collective-permute-done.ahead_y, ...), custom_call_target="tpu_custom_call" | custom-call | tf_op jit(solution)/shard_map/pallas_call | solution.py:358
  11.1 0.9 %collective-permute-start.3 = (f32[520,128]{1,0:T(8,128)S(1)}, f32[520,128]{1,0:T(8,128)S(1)}, u32[]{:S(2)}, u32[]{:S(2)}) collective-permute-start(f32[520,128]{1,0:T(8,128)S(1)} %get-tuple-element.27), channel_id=1, source_target_pairs={{0,2},{2,4},{4,6},{6,8},{8,10},{10,12},{12,14},{1,0},{3,1},{5,3},{... | collective-permute-start | bytes 798728 | tf_op jit(solution)/shard_map/ppermute | solution.py:416
  12.0 0.0 collective-permute-done.2.mu_received
  12.0 0.0 collective-permute-done.1.received.first_got
  12.0 0.6 %shard_map.89 = (f32[128,128]{1,0:T(8,128)S(1)}, f32[32,128]{1,0:T(8,128)S(1)}) custom-call(f32[512,128]{1,0:T(8,128)S(1)} %get-tuple-element.23.field_yz, f32[512,128]{1,0:T(8,128)S(1)} %collective-permute-done.1.received.first_got, f32[8,128]{1,0:T(8,128)S(1)} %collective-permute-done.2.mu_received, f32[512,128]{1,0:T(8,128)S(1)} %get-tuple-element.24.open_yz, ...), custom_call_target="tpu_custom_call" | custom-call | flops 10000000000 | tf_op jit(solution)/shard_map/pallas_call | solution.py:358
  12.6 0.0 collective-permute-start.6
  12.6 0.0 collective-permute-done.5.right
  12.6 1.1 %collective-permute-done.6.proj_other = f32[32,128]{1,0:T(8,128)S(1)} collective-permute-done((f32[32,128]{1,0:T(8,128)S(1)}, f32[32,128]{1,0:T(8,128)S(1)}, u32[]{:S(2)}, u32[]{:S(2)}) %collective-permute-start.6) | collective-permute-done | bytes 16416 | tf_op jit(solution)/shard_map/ppermute | solution.py:370
  13.8 2.8 %collective-permute-start.7 = (f32[64,128]{1,0:T(8,128)S(1)}, f32[64,128]{1,0:T(8,128)S(1)}, u32[]{:S(2)}, u32[]{:S(2)}) collective-permute-start(f32[64,128]{1,0:T(8,128)S(1)} %shard_map.91.own), channel_id=1, source_target_pairs={{0,8},{2,10},{4,12},{6,14},{8,0},{10,2},{12,4},{14,6},{1,9},{3,11}... | collective-permute-start | bytes 98312 | tf_op jit(solution)/shard_map/ppermute | solution.py:370
  16.6 0.0 collective-permute-start.4
  16.6 2.0 %collective-permute-done.7.both = f32[64,128]{1,0:T(8,128)S(1)} collective-permute-done((f32[64,128]{1,0:T(8,128)S(1)}, f32[64,128]{1,0:T(8,128)S(1)}, u32[]{:S(2)}, u32[]{:S(2)}) %collective-permute-start.7) | collective-permute-done | bytes 32800 | tf_op jit(solution)/shard_map/ppermute | solution.py:370
  18.6 0.8 %collective-permute-start.8 = (f32[64,128]{1,0:T(8,128)S(1)}, f32[64,128]{1,0:T(8,128)S(1)}, u32[]{:S(2)}, u32[]{:S(2)}) collective-permute-start(f32[64,128]{1,0:T(8,128)S(1)} %get-tuple-element.33.sums), channel_id=1, source_target_pairs={{0,2},{2,0},{4,6},{6,4},{8,10},{10,8},{12,14},{14,12},{1,3},{3,1},... | collective-permute-start | bytes 98312 | tf_op jit(solution)/shard_map/ppermute | solution.py:370
  19.5 2.4 %collective-permute-start.10 = (f32[32,128]{1,0:T(8,128)S(1)}, f32[32,128]{1,0:T(8,128)S(1)}, u32[]{:S(2)}, u32[]{:S(2)}) collective-permute-start(f32[32,128]{1,0:T(8,128)S(1)} %get-tuple-element.39.proj), channel_id=1, source_target_pairs={{0,6},{2,4},{4,2},{6,0},{8,14},{10,12},{12,10},{14,8},{1,7},{3,5},... | collective-permute-start | bytes 49160 | tf_op jit(solution)/shard_map/ppermute | solution.py:370
  21.9 0.4 %collective-permute-start.9 = (f32[32,128]{1,0:T(8,128)S(1)}, f32[32,128]{1,0:T(8,128)S(1)}, u32[]{:S(2)}, u32[]{:S(2)}) collective-permute-start(f32[32,128]{1,0:T(8,128)S(1)} %get-tuple-element.39.proj), channel_id=1, source_target_pairs={{0,4},{2,6},{4,0},{6,2},{8,12},{10,14},{12,8},{14,10},{1,5},{3,7},... | collective-permute-start | bytes 49160 | tf_op jit(solution)/shard_map/ppermute | solution.py:370
  22.3 0.2 collective-permute-done.8.far
  22.5 1.4 %shard_map.93.factors = f32[64,128]{1,0:T(8,128)S(1)} custom-call(f32[64,128]{1,0:T(8,128)S(1)} %get-tuple-element.33.sums, f32[64,128]{1,0:T(8,128)S(1)} %collective-permute-done.8.far), custom_call_target="tpu_custom_call" | custom-call | tf_op jit(solution)/shard_map/pallas_call | solution.py:358
  23.9 0.0 collective-permute-done.4.behind_y
  24.0 0.0 collective-permute-done.3.second_got
  24.0 1.4 %shard_map.94 = (f32[768,128]{1,0:T(8,128)}, f32[768,128]{1,0:T(8,128)}, f32[64,64]{1,0:T(8,128)}, f32[64,64]{1,0:T(8,128)S(1)}, f32[64,64]{1,0:T(8,128)S(1)}) custom-call(f32[256,128]{1,0:T(8,128)S(1)} %get-tuple-element.22.field_x, f32[512,128]{1,0:T(8,128)S(1)} %get-tuple-element.23.field_yz, f32[256,128]{1,0:T(8,128)S(1)} %get-tuple-element.25.m_x, ...), custom_call_target="tpu_custom_call" | custom-call | tf_op jit(solution)/shard_map/pallas_call | solution.py:358
  25.3 0.0 collective-permute-done.10.far_cross
  25.3 0.3 %collective-permute-done.9.near = f32[32,128]{1,0:T(8,128)S(1)} collective-permute-done((f32[32,128]{1,0:T(8,128)S(1)}, f32[32,128]{1,0:T(8,128)S(1)}, u32[]{:S(2)}, u32[]{:S(2)}) %collective-permute-start.9) | collective-permute-done | bytes 16416 | tf_op jit(solution)/shard_map/ppermute | solution.py:370
  25.6 1.0 %shard_map.95 = f32[64,64]{1,0:T(8,128)} custom-call(f32[64,64]{1,0:T(8,128)S(1)} %get-tuple-element.37.inverse, f32[64,64]{1,0:T(8,128)S(1)} %get-tuple-element.38.turned, f32[32,128]{1,0:T(8,128)S(1)} %get-tuple-element.39.proj, f32[32,128]{1,0:T(8,128)S(1)} %collective-permute-done.9.near, f32[64,128]{1,0:T(8,128)S(1)} %collective-permute-done.8.far, ...), custom_call_target="tpu_custom_call" | custom-call | tf_op jit(solution)/shard_map/pallas_call | solution.py:358
  (3 shorter events, 0.0 us)
Async XLA Ops:
  0.6 1.0 %copy-start = (f32[64,3,1,4,128]{4,3,2,1,0:T(4,128)S(1)}, f32[64,3,1,4,128]{4,3,2,1,0:T(4,128)}, u32[]{:S(2)}) copy-start(f32[64,3,1,4,128]{4,3,2,1,0:T(4,128)} %param.5) | copy-start | bytes 1179652
  1.7 10.3 %collective-permute-start.1 = (f32[512,128]{1,0:T(8,128)S(1)}, f32[512,128]{1,0:T(8,128)S(1)}, u32[]{:S(2)}, u32[]{:S(2)}) collective-permute-start(f32[512,128]{1,0:T(8,128)S(1)} %get-tuple-element.26), channel_id=1, source_target_pairs={{2,0},{4,2},{6,4},{8,6},{10,8},{12,10},{14,12},{0,1},{1,3},{3,5},{... | collective-permute-start | bytes 786440 | tf_op jit(solution)/shard_map/ppermute | solution.py:392
  2.8 2.8 %copy-start.1 = (s32[1,4,128]{2,1,0:T(4,128)S(1)}, s32[1,4,128]{2,1,0:T(4,128)}, u32[]{:S(2)}) copy-start(s32[1,4,128]{2,1,0:T(4,128)} %param.6) | copy-start | bytes 6148
  2.8 4.0 %collective-permute-start = (f32[160,128]{1,0:T(8,128)S(1)}, f32[160,128]{1,0:T(8,128)S(1)}, u32[]{:S(2)}, u32[]{:S(2)}) collective-permute-start(f32[160,128]{1,0:T(8,128)S(1)} %shard_map.85.gram_edge), channel_id=1, source_target_pairs={{0,1},{1,0},{2,3},{3,2},{4,5},{5,4},{6,7},{7,6},{8,9},{9,8},{10,11... | collective-permute-start | bytes 245768 | tf_op jit(solution)/shard_map/ppermute | solution.py:370
  5.5 0.7 %copy-start.2 = (f32[8]{0:T(128)S(1)}, f32[8]{0:T(128)}, u32[]{:S(2)}) copy-start(f32[8]{0:T(128)} %mu_table.1) | copy-start | bytes 100
  5.5 0.7 %copy-start.3 = (f32[8]{0:T(128)S(1)}, f32[8]{0:T(128)}, u32[]{:S(2)}) copy-start(f32[8]{0:T(128)} %eps_table.1) | copy-start | bytes 100
  6.7 5.3 %collective-permute-start.2 = (f32[8,128]{1,0:T(8,128)S(1)}, f32[8,128]{1,0:T(8,128)S(1)}, u32[]{:S(2)}, u32[]{:S(2)}) collective-permute-start(f32[8,128]{1,0:T(8,128)S(1)} %shard_map.86.material), channel_id=1, source_target_pairs={{2,0},{4,2},{6,4},{8,6},{10,8},{12,10},{14,12},{0,1},{1,3},{3,5},{... | collective-permute-start | bytes 12296 | tf_op jit(solution)/shard_map/ppermute | solution.py:397
  6.9 5.7 %collective-permute-start.5 = (f32[32,128]{1,0:T(8,128)S(1)}, f32[32,128]{1,0:T(8,128)S(1)}, u32[]{:S(2)}, u32[]{:S(2)}) collective-permute-start(f32[32,128]{1,0:T(8,128)S(1)} %get-tuple-element.31.left), channel_id=1, source_target_pairs={{0,4},{2,6},{4,0},{6,2},{8,12},{10,14},{12,8},{14,10},{1,5},{3,7},... | collective-permute-start | bytes 49160 | tf_op jit(solution)/shard_map/ppermute | solution.py:370
  11.1 12.9 %collective-permute-start.3 = (f32[520,128]{1,0:T(8,128)S(1)}, f32[520,128]{1,0:T(8,128)S(1)}, u32[]{:S(2)}, u32[]{:S(2)}) collective-permute-start(f32[520,128]{1,0:T(8,128)S(1)} %get-tuple-element.27), channel_id=1, source_target_pairs={{0,2},{2,4},{4,6},{6,8},{8,10},{10,12},{12,14},{1,0},{3,1},{5,3},{... | collective-permute-start | bytes 798728 | tf_op jit(solution)/shard_map/ppermute | solution.py:416
  12.6 1.2 %collective-permute-start.6 = (f32[32,128]{1,0:T(8,128)S(1)}, f32[32,128]{1,0:T(8,128)S(1)}, u32[]{:S(2)}, u32[]{:S(2)}) collective-permute-start(f32[32,128]{1,0:T(8,128)S(1)} %get-tuple-element.32.proj), channel_id=1, source_target_pairs={{0,1},{1,0},{2,3},{3,2},{4,5},{5,4},{6,7},{7,6},{8,9},{9,8},{10,11... | collective-permute-start | bytes 49160 | tf_op jit(solution)/shard_map/ppermute | solution.py:370
  13.8 4.8 %collective-permute-start.7 = (f32[64,128]{1,0:T(8,128)S(1)}, f32[64,128]{1,0:T(8,128)S(1)}, u32[]{:S(2)}, u32[]{:S(2)}) collective-permute-start(f32[64,128]{1,0:T(8,128)S(1)} %shard_map.91.own), channel_id=1, source_target_pairs={{0,8},{2,10},{4,12},{6,14},{8,0},{10,2},{12,4},{14,6},{1,9},{3,11}... | collective-permute-start | bytes 98312 | tf_op jit(solution)/shard_map/ppermute | solution.py:370
  16.6 7.3 %collective-permute-start.4 = (f32[128,128]{1,0:T(8,128)S(1)}, f32[128,128]{1,0:T(8,128)S(1)}, u32[]{:S(2)}, u32[]{:S(2)}) collective-permute-start(f32[128,128]{1,0:T(8,128)S(1)} %get-tuple-element.29), channel_id=1, source_target_pairs={{0,1},{1,0},{2,3},{3,2},{4,5},{5,4},{6,7},{7,6},{8,9},{9,8},{10,11... | collective-permute-start | bytes 196616 | tf_op jit(solution)/shard_map/ppermute | solution.py:370
  18.6 3.9 %collective-permute-start.8 = (f32[64,128]{1,0:T(8,128)S(1)}, f32[64,128]{1,0:T(8,128)S(1)}, u32[]{:S(2)}, u32[]{:S(2)}) collective-permute-start(f32[64,128]{1,0:T(8,128)S(1)} %get-tuple-element.33.sums), channel_id=1, source_target_pairs={{0,2},{2,0},{4,6},{6,4},{8,10},{10,8},{12,14},{14,12},{1,3},{3,1},... | collective-permute-start | bytes 98312 | tf_op jit(solution)/shard_map/ppermute | solution.py:370
  19.5 5.9 %collective-permute-start.10 = (f32[32,128]{1,0:T(8,128)S(1)}, f32[32,128]{1,0:T(8,128)S(1)}, u32[]{:S(2)}, u32[]{:S(2)}) collective-permute-start(f32[32,128]{1,0:T(8,128)S(1)} %get-tuple-element.39.proj), channel_id=1, source_target_pairs={{0,6},{2,4},{4,2},{6,0},{8,14},{10,12},{12,10},{14,8},{1,7},{3,5},... | collective-permute-start | bytes 49160 | tf_op jit(solution)/shard_map/ppermute | solution.py:370
  21.9 3.7 %collective-permute-start.9 = (f32[32,128]{1,0:T(8,128)S(1)}, f32[32,128]{1,0:T(8,128)S(1)}, u32[]{:S(2)}, u32[]{:S(2)}) collective-permute-start(f32[32,128]{1,0:T(8,128)S(1)} %get-tuple-element.39.proj), channel_id=1, source_target_pairs={{0,4},{2,6},{4,0},{6,2},{8,12},{10,14},{12,8},{14,10},{1,5},{3,7},... | collective-permute-start | bytes 49160 | tf_op jit(solution)/shard_map/ppermute | solution.py:370

commit v15 on v13

--- a/solution.py
+++ b/solution.py
@@ -265,7 +265,10 @@
 
 def factor_kernel(total, sums, far, out):
     half = sums.shape[0] // 2
-    out[...] = factor(unpacked(sums[:half, :] + far[:half, :]) / total)
+    both = factor(unpacked(sums[:half, :] + far[:half, :]))
+    lane = lax.broadcasted_iota(jnp.int32, both.shape, 1)
+    root = float(total) ** 0.5
+    out[...] = both * jnp.where(lane < both.shape[0], 1.0 / root, root)
 
 
 def basis_kernel(

time: 26.9 us -> 26.9 us (level)
  no operation moved by 1% of the time
where the time goes in v15:
time: 26.9 us; the launch traced here: 26.7 us
  starting transfers between devices  13.2 us (49%)
  Pallas kernels  6.76 us (25%)
  waiting for transfers between devices  3.65 us (14%)
  local copies, waits for them, and re-layouts  1.64 us (6%)
  between operations  1.42 us (5%)
    ppermute x8, starting transfers between devices, swapped(): lax.ppermute(x, axis, [(i, i ^ step) for i in range(lax.axis_size(axis))])  11.7 us
    pallas_call x12, Pallas kernels, call(): pl.pallas_call(body, out_shape=shapes, in_specs=[SMEM] * len(scalars) + [...  6.76 us
    ppermute x8, waiting for transfers between devices, swapped(): lax.ppermute(x, axis, [(i, i ^ step) for i in range(lax.axis_size(axis))])  3.64 us
    unnamed x8, local copies, waits for them, and re-layouts  1.64 us
    ppermute x1, starting transfers between devices, local(): second_got = lax.ppermute(send, ('row', 'col'), halo_ring(rows, True))  0.94 us
  transfers between devices with their start and end apart: 11, of which 4 were waited for; matrix products, arithmetic and copies ran while one was open for 0% of the time, Pallas kernels for 21%

profile of v15, /device:TPU:0, one launch (start us, length us, event | category | flops | bytes accessed | tf_op | source)
XLA Modules:
  0.0 26.7 jit_solution(15238327483367757927)
XLA Ops:
  0.6 0.0 copy-start
  0.6 1.0 %copy-done = f32[64,3,1,4,128]{4,3,2,1,0:T(4,128)S(1)} copy-done((f32[64,3,1,4,128]{4,3,2,1,0:T(4,128)S(1)}, f32[64,3,1,4,128]{4,3,2,1,0:T(4,128)}, u32[]{:S(2)}) %copy-start) | copy-done | bytes 393240
  1.6 0.1 shard_map.84
  1.7 0.5 %collective-permute-start.1 = (f32[512,128]{1,0:T(8,128)S(1)}, f32[512,128]{1,0:T(8,128)S(1)}, u32[]{:S(2)}, u32[]{:S(2)}) collective-permute-start(f32[512,128]{1,0:T(8,128)S(1)} %get-tuple-element.25), channel_id=1, source_target_pairs={{2,0},{4,2},{6,4},{8,6},{10,8},{12,10},{14,12},{0,1},{1,3},{3,5},{... | collective-permute-start | bytes 786440 | tf_op jit(solution)/shard_map/ppermute | solution.py:391
  2.2 0.5 %shard_map.85.gram_edge = f32[160,128]{1,0:T(8,128)S(1)} custom-call(f32[256,128]{1,0:T(8,128)S(1)} %get-tuple-element.21.field_x, f32[512,128]{1,0:T(8,128)S(1)} %get-tuple-element.22.field_yz), custom_call_target="tpu_custom_call" | custom-call | tf_op jit(solution)/shard_map/pallas_call | solution.py:357
  2.8 0.0 copy-start.1
  2.8 2.1 %collective-permute-start = (f32[160,128]{1,0:T(8,128)S(1)}, f32[160,128]{1,0:T(8,128)S(1)}, u32[]{:S(2)}, u32[]{:S(2)}) collective-permute-start(f32[160,128]{1,0:T(8,128)S(1)} %shard_map.85.gram_edge), channel_id=1, source_target_pairs={{0,1},{1,0},{2,3},{3,2},{4,5},{5,4},{6,7},{7,6},{8,9},{9,8},{10,11... | collective-permute-start | bytes 245768 | tf_op jit(solution)/shard_map/ppermute | solution.py:369
  5.5 0.0 copy-start.2
  5.5 0.0 copy-start.3
  5.5 0.0 copy-done.1
  5.5 0.6 %copy-done.2 = f32[8]{0:T(128)S(1)} copy-done((f32[8]{0:T(128)S(1)}, f32[8]{0:T(128)}, u32[]{:S(2)}) %copy-start.2) | copy-done | bytes 56
  6.2 0.0 copy-done.3
  6.2 0.6 %shard_map.86.material = f32[8,128]{1,0:T(8,128)S(1)} custom-call(f32[8]{0:T(128)S(1)} %copy-done.2, f32[8]{0:T(128)S(1)} %copy-done.3, f32[1]{0:T(128)S(6)} %copy.11.shift, s32[4,128]{1,0:T(4,128)S(1)} %bitcast.9), custom_call_target="tpu_custom_call" | custom-call | tf_op jit(solution)/shard_map/pallas_call | solution.py:357
  6.7 0.1 collective-permute-start.2
  6.8 0.0 collective-permute-done.ahead_y
  6.8 0.1 shard_map.87
  6.9 3.1 %collective-permute-start.5 = (f32[32,128]{1,0:T(8,128)S(1)}, f32[32,128]{1,0:T(8,128)S(1)}, u32[]{:S(2)}, u32[]{:S(2)}) collective-permute-start(f32[32,128]{1,0:T(8,128)S(1)} %get-tuple-element.30.left), channel_id=1, source_target_pairs={{0,4},{2,6},{4,0},{6,2},{8,12},{10,14},{12,8},{14,10},{1,5},{3,7},... | collective-permute-start | bytes 49160 | tf_op jit(solution)/shard_map/ppermute | solution.py:369
  10.0 1.1 %shard_map.88 = (f32[256,128]{1,0:T(8,128)S(1)}, f32[32,128]{1,0:T(8,128)S(1)}, f32[520,128]{1,0:T(8,128)S(1)}, bf16[192,1536]{1,0:T(8,128)(2,1)S(1)}) custom-call(f32[256,128]{1,0:T(8,128)S(1)} %get-tuple-element.21.field_x, f32[512,128]{1,0:T(8,128)S(1)} %get-tuple-element.22.field_yz, f32[160,128]{1,0:T(8,128)S(1)} %collective-permute-done.ahead_y, ...), custom_call_target="tpu_custom_call" | custom-call | tf_op jit(solution)/shard_map/pallas_call | solution.py:357
  11.1 0.9 %collective-permute-start.3 = (f32[520,128]{1,0:T(8,128)S(1)}, f32[520,128]{1,0:T(8,128)S(1)}, u32[]{:S(2)}, u32[]{:S(2)}) collective-permute-start(f32[520,128]{1,0:T(8,128)S(1)} %get-tuple-element.26), channel_id=1, source_target_pairs={{0,2},{2,4},{4,6},{6,8},{8,10},{10,12},{12,14},{1,0},{3,1},{5,3},{... | collective-permute-start | bytes 798728 | tf_op jit(solution)/shard_map/ppermute | solution.py:415
  12.0 0.0 collective-permute-done.2.mu_received
  12.0 0.0 collective-permute-done.1.received.first_got
  12.0 0.6 %shard_map.89 = (f32[128,128]{1,0:T(8,128)S(1)}, f32[32,128]{1,0:T(8,128)S(1)}) custom-call(f32[512,128]{1,0:T(8,128)S(1)} %get-tuple-element.22.field_yz, f32[512,128]{1,0:T(8,128)S(1)} %collective-permute-done.1.received.first_got, f32[8,128]{1,0:T(8,128)S(1)} %collective-permute-done.2.mu_received, f32[512,128]{1,0:T(8,128)S(1)} %get-tuple-element.23.open_yz, ...), custom_call_target="tpu_custom_call" | custom-call | flops 10000000000 | tf_op jit(solution)/shard_map/pallas_call | solution.py:357
  12.6 0.0 collective-permute-start.6
  12.6 0.0 collective-permute-done.5.right
  12.6 1.1 %collective-permute-done.6.proj_other = f32[32,128]{1,0:T(8,128)S(1)} collective-permute-done((f32[32,128]{1,0:T(8,128)S(1)}, f32[32,128]{1,0:T(8,128)S(1)}, u32[]{:S(2)}, u32[]{:S(2)}) %collective-permute-start.6) | collective-permute-done | bytes 16416 | tf_op jit(solution)/shard_map/ppermute | solution.py:369
  13.8 2.8 %collective-permute-start.7 = (f32[64,128]{1,0:T(8,128)S(1)}, f32[64,128]{1,0:T(8,128)S(1)}, u32[]{:S(2)}, u32[]{:S(2)}) collective-permute-start(f32[64,128]{1,0:T(8,128)S(1)} %shard_map.91.own), channel_id=1, source_target_pairs={{0,8},{2,10},{4,12},{6,14},{8,0},{10,2},{12,4},{14,6},{1,9},{3,11}... | collective-permute-start | bytes 98312 | tf_op jit(solution)/shard_map/ppermute | solution.py:369
  16.6 0.0 collective-permute-start.4
  16.6 2.0 %collective-permute-done.7.both = f32[64,128]{1,0:T(8,128)S(1)} collective-permute-done((f32[64,128]{1,0:T(8,128)S(1)}, f32[64,128]{1,0:T(8,128)S(1)}, u32[]{:S(2)}, u32[]{:S(2)}) %collective-permute-start.7) | collective-permute-done | bytes 32800 | tf_op jit(solution)/shard_map/ppermute | solution.py:369
  18.6 0.8 %collective-permute-start.8 = (f32[64,128]{1,0:T(8,128)S(1)}, f32[64,128]{1,0:T(8,128)S(1)}, u32[]{:S(2)}, u32[]{:S(2)}) collective-permute-start(f32[64,128]{1,0:T(8,128)S(1)} %get-tuple-element.32.sums), channel_id=1, source_target_pairs={{0,2},{2,0},{4,6},{6,4},{8,10},{10,8},{12,14},{14,12},{1,3},{3,1},... | collective-permute-start | bytes 98312 | tf_op jit(solution)/shard_map/ppermute | solution.py:369
  19.5 2.4 %collective-permute-start.10 = (f32[32,128]{1,0:T(8,128)S(1)}, f32[32,128]{1,0:T(8,128)S(1)}, u32[]{:S(2)}, u32[]{:S(2)}) collective-permute-start(f32[32,128]{1,0:T(8,128)S(1)} %get-tuple-element.37.proj), channel_id=1, source_target_pairs={{0,6},{2,4},{4,2},{6,0},{8,14},{10,12},{12,10},{14,8},{1,7},{3,5},... | collective-permute-start | bytes 49160 | tf_op jit(solution)/shard_map/ppermute | solution.py:369
  21.9 0.4 %collective-permute-start.9 = (f32[32,128]{1,0:T(8,128)S(1)}, f32[32,128]{1,0:T(8,128)S(1)}, u32[]{:S(2)}, u32[]{:S(2)}) collective-permute-start(f32[32,128]{1,0:T(8,128)S(1)} %get-tuple-element.37.proj), channel_id=1, source_target_pairs={{0,4},{2,6},{4,0},{6,2},{8,12},{10,14},{12,8},{14,10},{1,5},{3,7},... | collective-permute-start | bytes 49160 | tf_op jit(solution)/shard_map/ppermute | solution.py:369
  22.3 0.2 collective-permute-done.8.far
  22.5 1.4 %shard_map.93.factors = f32[64,128]{1,0:T(8,128)S(1)} custom-call(f32[64,128]{1,0:T(8,128)S(1)} %get-tuple-element.32.sums, f32[64,128]{1,0:T(8,128)S(1)} %collective-permute-done.8.far), custom_call_target="tpu_custom_call" | custom-call | tf_op jit(solution)/shard_map/pallas_call | solution.py:357
  23.9 0.0 collective-permute-done.4.behind_y
  24.0 0.0 collective-permute-done.3.second_got
  24.0 1.4 %shard_map.94 = (f32[768,128]{1,0:T(8,128)}, f32[768,128]{1,0:T(8,128)}, f32[64,64]{1,0:T(8,128)}, f32[64,64]{1,0:T(8,128)S(1)}) custom-call(f32[256,128]{1,0:T(8,128)S(1)} %get-tuple-element.21.field_x, f32[512,128]{1,0:T(8,128)S(1)} %get-tuple-element.22.field_yz, f32[256,128]{1,0:T(8,128)S(1)} %get-tuple-element.24.m_x, ...), custom_call_target="tpu_custom_call" | custom-call | tf_op jit(solution)/shard_map/pallas_call | solution.py:357
  25.3 0.0 collective-permute-done.10.far_cross
  25.3 0.3 %collective-permute-done.9.near = f32[32,128]{1,0:T(8,128)S(1)} collective-permute-done((f32[32,128]{1,0:T(8,128)S(1)}, f32[32,128]{1,0:T(8,128)S(1)}, u32[]{:S(2)}, u32[]{:S(2)}) %collective-permute-start.9) | collective-permute-done | bytes 16416 | tf_op jit(solution)/shard_map/ppermute | solution.py:369
  25.6 1.0 %shard_map.95 = f32[64,64]{1,0:T(8,128)} custom-call(f32[64,64]{1,0:T(8,128)S(1)} %get-tuple-element.36.inverse, f32[32,128]{1,0:T(8,128)S(1)} %get-tuple-element.37.proj, f32[32,128]{1,0:T(8,128)S(1)} %collective-permute-done.9.near, f32[64,128]{1,0:T(8,128)S(1)} %collective-permute-done.8.far, f32[32,128]{1,0:T(8,128)S(1)} %collective-permute-done.10.far_cross), custom_call_target="tpu_custom_call" | custom-call | tf_op jit(solution)/shard_map/pallas_call | solution.py:357
  (3 shorter events, 0.0 us)
Async XLA Ops:
  0.6 1.0 %copy-start = (f32[64,3,1,4,128]{4,3,2,1,0:T(4,128)S(1)}, f32[64,3,1,4,128]{4,3,2,1,0:T(4,128)}, u32[]{:S(2)}) copy-start(f32[64,3,1,4,128]{4,3,2,1,0:T(4,128)} %param.5) | copy-start | bytes 1179652
  1.7 10.3 %collective-permute-start.1 = (f32[512,128]{1,0:T(8,128)S(1)}, f32[512,128]{1,0:T(8,128)S(1)}, u32[]{:S(2)}, u32[]{:S(2)}) collective-permute-start(f32[512,128]{1,0:T(8,128)S(1)} %get-tuple-element.25), channel_id=1, source_target_pairs={{2,0},{4,2},{6,4},{8,6},{10,8},{12,10},{14,12},{0,1},{1,3},{3,5},{... | collective-permute-start | bytes 786440 | tf_op jit(solution)/shard_map/ppermute | solution.py:391
  2.8 2.8 %copy-start.1 = (s32[1,4,128]{2,1,0:T(4,128)S(1)}, s32[1,4,128]{2,1,0:T(4,128)}, u32[]{:S(2)}) copy-start(s32[1,4,128]{2,1,0:T(4,128)} %param.6) | copy-start | bytes 6148
  2.8 4.0 %collective-permute-start = (f32[160,128]{1,0:T(8,128)S(1)}, f32[160,128]{1,0:T(8,128)S(1)}, u32[]{:S(2)}, u32[]{:S(2)}) collective-permute-start(f32[160,128]{1,0:T(8,128)S(1)} %shard_map.85.gram_edge), channel_id=1, source_target_pairs={{0,1},{1,0},{2,3},{3,2},{4,5},{5,4},{6,7},{7,6},{8,9},{9,8},{10,11... | collective-permute-start | bytes 245768 | tf_op jit(solution)/shard_map/ppermute | solution.py:369
  5.5 0.7 %copy-start.2 = (f32[8]{0:T(128)S(1)}, f32[8]{0:T(128)}, u32[]{:S(2)}) copy-start(f32[8]{0:T(128)} %mu_table.1) | copy-start | bytes 100
  5.5 0.7 %copy-start.3 = (f32[8]{0:T(128)S(1)}, f32[8]{0:T(128)}, u32[]{:S(2)}) copy-start(f32[8]{0:T(128)} %eps_table.1) | copy-start | bytes 100
  6.7 5.3 %collective-permute-start.2 = (f32[8,128]{1,0:T(8,128)S(1)}, f32[8,128]{1,0:T(8,128)S(1)}, u32[]{:S(2)}, u32[]{:S(2)}) collective-permute-start(f32[8,128]{1,0:T(8,128)S(1)} %shard_map.86.material), channel_id=1, source_target_pairs={{2,0},{4,2},{6,4},{8,6},{10,8},{12,10},{14,12},{0,1},{1,3},{3,5},{... | collective-permute-start | bytes 12296 | tf_op jit(solution)/shard_map/ppermute | solution.py:396
  6.9 5.7 %collective-permute-start.5 = (f32[32,128]{1,0:T(8,128)S(1)}, f32[32,128]{1,0:T(8,128)S(1)}, u32[]{:S(2)}, u32[]{:S(2)}) collective-permute-start(f32[32,128]{1,0:T(8,128)S(1)} %get-tuple-element.30.left), channel_id=1, source_target_pairs={{0,4},{2,6},{4,0},{6,2},{8,12},{10,14},{12,8},{14,10},{1,5},{3,7},... | collective-permute-start | bytes 49160 | tf_op jit(solution)/shard_map/ppermute | solution.py:369
  11.1 12.9 %collective-permute-start.3 = (f32[520,128]{1,0:T(8,128)S(1)}, f32[520,128]{1,0:T(8,128)S(1)}, u32[]{:S(2)}, u32[]{:S(2)}) collective-permute-start(f32[520,128]{1,0:T(8,128)S(1)} %get-tuple-element.26), channel_id=1, source_target_pairs={{0,2},{2,4},{4,6},{6,8},{8,10},{10,12},{12,14},{1,0},{3,1},{5,3},{... | collective-permute-start | bytes 798728 | tf_op jit(solution)/shard_map/ppermute | solution.py:415
  12.6 1.2 %collective-permute-start.6 = (f32[32,128]{1,0:T(8,128)S(1)}, f32[32,128]{1,0:T(8,128)S(1)}, u32[]{:S(2)}, u32[]{:S(2)}) collective-permute-start(f32[32,128]{1,0:T(8,128)S(1)} %get-tuple-element.31.proj), channel_id=1, source_target_pairs={{0,1},{1,0},{2,3},{3,2},{4,5},{5,4},{6,7},{7,6},{8,9},{9,8},{10,11... | collective-permute-start | bytes 49160 | tf_op jit(solution)/shard_map/ppermute | solution.py:369
  13.8 4.8 %collective-permute-start.7 = (f32[64,128]{1,0:T(8,128)S(1)}, f32[64,128]{1,0:T(8,128)S(1)}, u32[]{:S(2)}, u32[]{:S(2)}) collective-permute-start(f32[64,128]{1,0:T(8,128)S(1)} %shard_map.91.own), channel_id=1, source_target_pairs={{0,8},{2,10},{4,12},{6,14},{8,0},{10,2},{12,4},{14,6},{1,9},{3,11}... | collective-permute-start | bytes 98312 | tf_op jit(solution)/shard_map/ppermute | solution.py:369
  16.6 7.3 %collective-permute-start.4 = (f32[128,128]{1,0:T(8,128)S(1)}, f32[128,128]{1,0:T(8,128)S(1)}, u32[]{:S(2)}, u32[]{:S(2)}) collective-permute-start(f32[128,128]{1,0:T(8,128)S(1)} %get-tuple-element.28), channel_id=1, source_target_pairs={{0,1},{1,0},{2,3},{3,2},{4,5},{5,4},{6,7},{7,6},{8,9},{9,8},{10,11... | collective-permute-start | bytes 196616 | tf_op jit(solution)/shard_map/ppermute | solution.py:369
  18.6 3.9 %collective-permute-start.8 = (f32[64,128]{1,0:T(8,128)S(1)}, f32[64,128]{1,0:T(8,128)S(1)}, u32[]{:S(2)}, u32[]{:S(2)}) collective-permute-start(f32[64,128]{1,0:T(8,128)S(1)} %get-tuple-element.32.sums), channel_id=1, source_target_pairs={{0,2},{2,0},{4,6},{6,4},{8,10},{10,8},{12,14},{14,12},{1,3},{3,1},... | collective-permute-start | bytes 98312 | tf_op jit(solution)/shard_map/ppermute | solution.py:369
  19.5 5.9 %collective-permute-start.10 = (f32[32,128]{1,0:T(8,128)S(1)}, f32[32,128]{1,0:T(8,128)S(1)}, u32[]{:S(2)}, u32[]{:S(2)}) collective-permute-start(f32[32,128]{1,0:T(8,128)S(1)} %get-tuple-element.37.proj), channel_id=1, source_target_pairs={{0,6},{2,4},{4,2},{6,0},{8,14},{10,12},{12,10},{14,8},{1,7},{3,5},... | collective-permute-start | bytes 49160 | tf_op jit(solution)/shard_map/ppermute | solution.py:369
  21.9 3.7 %collective-permute-start.9 = (f32[32,128]{1,0:T(8,128)S(1)}, f32[32,128]{1,0:T(8,128)S(1)}, u32[]{:S(2)}, u32[]{:S(2)}) collective-permute-start(f32[32,128]{1,0:T(8,128)S(1)} %get-tuple-element.37.proj), channel_id=1, source_target_pairs={{0,4},{2,6},{4,0},{6,2},{8,12},{10,14},{12,8},{14,10},{1,5},{3,7},... | collective-permute-start | bytes 49160 | tf_op jit(solution)/shard_map/ppermute | solution.py:369
